TPU v7x, 32 devices: a whole 2x2x4 slice. The times are simulated.
32 devices in a mesh: dp: 8 (over z, x), seq: 4 (over y, core).
Axes of the slice: x: 2, y: 2, z: 4, core: 2. Of those that a mesh axis runs over, the one named last changes fastest.
Arguments:
- qx: bfloat16 [4096, 1024], P(('dp', 'seq')), may hold values from -6 to 6
- queries: bfloat16 [4096, 1024], P(('dp', 'seq')), may hold values from -8 to 8
- keys: bfloat16 [1536, 1024], P('seq'), may hold values from -6 to 6
- values: bfloat16 [1536, 1024], P('seq'), may hold values from -6 to 6
- attn_out: bfloat16 [4096, 1024], P(('dp', 'seq')), may hold values from -3 to 3
- grad_out: bfloat16 [4096, 1024], P(('dp', 'seq')), may hold values from -24 to 24
- wq: bfloat16 [1024, 1024], replicated, may hold values from -0.1875 to 0.1875
Outputs:
- grad_input: bfloat16 [4096, 1024], P(('dp', 'seq'))
- grad_keys: bfloat16 [1536, 1024], P('seq')
- grad_values: bfloat16 [1536, 1024], P('seq')
- grad_weight: float32 [1024, 1024], P('dp', 'seq')
All inputs are finite; a program needn't handle non-finite values.
Results may differ from a plain program's by a relative error of at most 0.014.
Values may be sent and summed in bfloat16 or wider, within the bound.
No kernel may reach another device: no remote copies, remote signals or barrier semaphores. Data moves between devices by JAX's collectives and lax.ppermute only.
A program may use at most 64 MiB of HBM per device.

v0:
```python
import math

import jax
import jax.numpy as jnp
from jax import lax
from jax.sharding import PartitionSpec as P

HD = 64


def local(qx, queries, keys, values, attn_out, grad_out, wq):
    query_part, grad_part, output_part, key_part, val_part = (
        lax.all_to_all(queries, "seq", split_axis=1, concat_axis=0, tiled=True),
        lax.all_to_all(grad_out, "seq", split_axis=1, concat_axis=0, tiled=True),
        lax.all_to_all(attn_out, "seq", split_axis=1, concat_axis=0, tiled=True),
        lax.all_to_all(keys, "seq", split_axis=1, concat_axis=0, tiled=True),
        lax.all_to_all(values, "seq", split_axis=1, concat_axis=0, tiled=True),
    )
    slab_rows = query_part.shape[0]
    key_total = key_part.shape[0]
    col_count = query_part.shape[1]
    head_count = col_count // HD
    score_scale = 1.0 / math.sqrt(HD)
    query_heads = query_part.reshape(slab_rows, head_count, HD)
    grad_heads = grad_part.reshape(slab_rows, head_count, HD)
    output_heads = output_part.reshape(slab_rows, head_count, HD)
    key_heads = key_part.reshape(key_total, head_count, HD)
    val_heads = val_part.reshape(key_total, head_count, HD)
    block_len = math.gcd(key_total, 512)
    block_count = key_total // block_len

    def block_scores(step_index):
        key_block = lax.dynamic_slice_in_dim(key_heads, step_index * block_len, block_len, 0)
        scores = jnp.einsum(
            "qhd,khd->hqk", query_heads, key_block, preferred_element_type=jnp.float32
        )
        return (key_block, scores * score_scale)

    def first_pass(step_index, carry):
        run_max, run_sum = carry
        unused, scores = block_scores(step_index)
        new_max = jnp.maximum(run_max, jnp.max(scores, axis=2))
        run_sum = run_sum * jnp.exp(run_max - new_max) + jnp.sum(
            jnp.exp(scores - new_max[:, :, None]), axis=2
        )
        return (new_max, run_sum)

    start_max = jnp.full((head_count, slab_rows), -jnp.inf, jnp.float32)
    start_sum = jnp.zeros((head_count, slab_rows), jnp.float32)
    run_max, run_sum = lax.fori_loop(0, block_count, first_pass, (start_max, start_sum))
    lse = run_max + jnp.log(run_sum)
    delta = jnp.sum(grad_heads.astype(jnp.float32) * output_heads.astype(jnp.float32), axis=2).T

    def second_pass(step_index, carry):
        grad_query, grad_key, grad_val = carry
        key_block, scores = block_scores(step_index)
        val_block = lax.dynamic_slice_in_dim(val_heads, step_index * block_len, block_len, 0)
        probs = jnp.exp(scores - lse[:, :, None])
        probs_b = probs.astype(jnp.bfloat16)
        grad_probs = jnp.einsum(
            "qhd,khd->hqk", grad_heads, val_block, preferred_element_type=jnp.float32
        )
        grad_scores = (probs * (grad_probs - delta[:, :, None]) * score_scale).astype(jnp.bfloat16)
        val_grad_block = jnp.einsum(
            "hqk,qhd->khd", probs_b, grad_heads, preferred_element_type=jnp.float32
        )
        key_grad_block = jnp.einsum(
            "hqk,qhd->khd", grad_scores, query_heads, preferred_element_type=jnp.float32
        )
        grad_query = grad_query + jnp.einsum(
            "hqk,khd->hqd", grad_scores, key_block, preferred_element_type=jnp.float32
        )
        grad_key = lax.dynamic_update_slice_in_dim(
            grad_key, key_grad_block.astype(jnp.bfloat16), step_index * block_len, 0
        )
        grad_val = lax.dynamic_update_slice_in_dim(
            grad_val, val_grad_block.astype(jnp.bfloat16), step_index * block_len, 0
        )
        return (grad_query, grad_key, grad_val)

    start_query = jnp.zeros((head_count, slab_rows, HD), jnp.float32)
    start_keys = jnp.zeros((key_total, head_count, HD), jnp.bfloat16)
    grad_query, grad_key, grad_val = lax.fori_loop(
        0, block_count, second_pass, (start_query, start_keys, start_keys)
    )
    query_grad_heads = (
        grad_query.transpose(1, 0, 2).reshape(slab_rows, col_count).astype(jnp.bfloat16)
    )
    key_grad_heads = grad_key.reshape(key_total, col_count)
    val_grad_heads = grad_val.reshape(key_total, col_count)
    query_grad_rows = lax.all_to_all(
        query_grad_heads, "seq", split_axis=0, concat_axis=1, tiled=True
    )
    grad_input = lax.dot_general(
        query_grad_rows, wq, (((1,), (1,)), ((), ())), preferred_element_type=jnp.float32
    ).astype(jnp.bfloat16)
    key_back, val_back = (
        lax.all_to_all(key_grad_heads, "seq", split_axis=0, concat_axis=1, tiled=True),
        lax.all_to_all(val_grad_heads, "seq", split_axis=0, concat_axis=1, tiled=True),
    )
    key_sums, val_sums = (
        lax.psum(key_back, "dp").astype(jnp.float32),
        lax.psum(val_back, "dp").astype(jnp.float32),
    )
    grad_keys = key_sums.astype(jnp.bfloat16)
    grad_values = val_sums.astype(jnp.bfloat16)
    slab_weight = lax.psum_scatter(
        lax.dot_general(
            qx, query_grad_rows, (((0,), (0,)), ((), ())), preferred_element_type=jnp.float32
        ).astype(jnp.bfloat16),
        "dp",
        scatter_dimension=0,
        tiled=True,
    )
    grad_weight = lax.psum_scatter(slab_weight, "seq", scatter_dimension=1, tiled=True).astype(
        jnp.float32
    )
    return (grad_input, grad_keys, grad_values, grad_weight)


def solution(mesh):
    return jax.shard_map(
        local,
        mesh=mesh,
        in_specs=(
            P(("dp", "seq"), None),
            P(("dp", "seq"), None),
            P("seq", None),
            P("seq", None),
            P(("dp", "seq"), None),
            P(("dp", "seq"), None),
            P(),
        ),
        out_specs=(P(("dp", "seq"), None), P("seq", None), P("seq", None), P("dp", "seq")),
        check_vma=False,
    )
```

profile of v0, /device:TPU:0, one launch (start us, length us, event | category | flops | bytes accessed | tf_op | source)
XLA Modules:
  0.0 304.9 jit_solution(11012092780772330732)
XLA Ops:
  7.2 1.9 copy.47
  9.1 4.2 %all-to-all-start.1 = ((bf16[128,4,256]{0,2,1:T(8,128)(2,1)}), bf16[128,4,256]{0,2,1:T(8,128)(2,1)S(1)}, u32[]{:S(2)}, u32[]{:S(2)}) async-start(bf16[128,4,256]{0,2,1:T(8,128)(2,1)} %bitcast.2), calls=%async_computation.1 | async-start | bytes 524288 | tf_op jit(solution)/shard_map/all_to_all | solution.py:13
  13.4 1.8 copy.53
  15.1 4.2 %all-to-all-done.1 = bf16[128,4,256]{0,2,1:T(8,128)(2,1)S(1)} async-done(((bf16[128,4,256]{0,2,1:T(8,128)(2,1)}), bf16[128,4,256]{0,2,1:T(8,128)(2,1)S(1)}, u32[]{:S(2)}, u32[]{:S(2)}) %all-to-all-start.1) | async-done | bytes 262176 | tf_op jit(solution)/shard_map/all_to_all | solution.py:13
  19.4 3.4 %all-to-all-start.4 = ((bf16[128,4,256]{0,2,1:T(8,128)(2,1)}), bf16[128,4,256]{0,2,1:T(8,128)(2,1)S(1)}, u32[]{:S(2)}, u32[]{:S(2)}) async-start(bf16[128,4,256]{0,2,1:T(8,128)(2,1)} %bitcast.8), calls=%async_computation.4 | async-start | bytes 524288 | tf_op jit(solution)/shard_map/all_to_all | solution.py:15
  22.8 1.8 copy.51
  24.6 4.2 %all-to-all-done.4 = bf16[128,4,256]{0,2,1:T(8,128)(2,1)S(1)} async-done(((bf16[128,4,256]{0,2,1:T(8,128)(2,1)}), bf16[128,4,256]{0,2,1:T(8,128)(2,1)S(1)}, u32[]{:S(2)}, u32[]{:S(2)}) %all-to-all-start.4) | async-done | bytes 262176 | tf_op jit(solution)/shard_map/all_to_all | solution.py:15
  28.8 3.4 %all-to-all-start.3 = ((bf16[128,4,256]{0,2,1:T(8,128)(2,1)}), bf16[128,4,256]{0,2,1:T(8,128)(2,1)S(1)}, u32[]{:S(2)}, u32[]{:S(2)}) async-start(bf16[128,4,256]{0,2,1:T(8,128)(2,1)} %bitcast.6), calls=%async_computation.3 | async-start | bytes 524288 | tf_op jit(solution)/shard_map/all_to_all | solution.py:14
  32.2 2.3 copy.45
  34.5 3.7 %all-to-all-done.3 = bf16[128,4,256]{0,2,1:T(8,128)(2,1)S(1)} async-done(((bf16[128,4,256]{0,2,1:T(8,128)(2,1)}), bf16[128,4,256]{0,2,1:T(8,128)(2,1)S(1)}, u32[]{:S(2)}, u32[]{:S(2)}) %all-to-all-start.3) | async-done | bytes 262176 | tf_op jit(solution)/shard_map/all_to_all | solution.py:14
  38.9 3.5 %all-to-all-start = ((bf16[384,4,256]{0,2,1:T(8,128)(2,1)}), bf16[384,4,256]{0,2,1:T(8,128)(2,1)S(1)}, u32[]{:S(2)}, u32[]{:S(2)}) async-start(bf16[384,4,256]{0,2,1:T(8,128)(2,1)} %bitcast.92), calls=%async_computation | async-start | bytes 1572864 | tf_op jit(solution)/shard_map/all_to_all | solution.py:16
  42.5 2.3 copy.49
  44.8 0.9 copy.48
  45.7 1.1 reshape.63
  46.8 1.2 copy.54
  47.9 2.0 reshape.66
  50.0 1.9 copy.52
  51.8 1.1 reshape.65
  52.9 1.1 multiply_reduce_fusion
  54.1 4.2 %all-to-all-start.2 = ((bf16[384,4,256]{0,2,1:T(8,128)(2,1)}), bf16[384,4,256]{0,2,1:T(8,128)(2,1)}, u32[]{:S(2)}, u32[]{:S(2)}) async-start(bf16[384,4,256]{0,2,1:T(8,128)(2,1)} %bitcast.4), calls=%async_computation.2 | async-start | bytes 1572864 | tf_op jit(solution)/shard_map/all_to_all | solution.py:17
  58.3 1.5 copy.46
  59.8 1.7 reshape.62
  61.5 4.7 %while.34 = (s32[]{:T(128)}, f32[4,512]{1,0:T(4,128)S(1)}, f32[4,512]{1,0:T(4,128)S(1)}, bf16[1536,4,64]{0,2,1:T(8,128)(2,1)S(1)}, bf16[512,4,64]{0,2,1:T(8,128)...) while((s32[]{:T(128)}, f32[4,512]{1,0:T(4,128)S(1)}, f32[4,512]{1,0:T(4,128)S(1)}, ...), condition=%wide.region_3.0_spmd.clone, body=%wide.region_0.0_spmd.clone.sunk | while | flops 139470848 | bytes 9019554 | solution.py:50
  61.5 0.8 bitcast_reduce_fusion.2
  63.0 0.8 bitcast_reduce_fusion.2
  64.6 0.8 bitcast_reduce_fusion.2
  66.1 3.8 %all-to-all-done.2 = bf16[384,4,256]{0,2,1:T(8,128)(2,1)} async-done(((bf16[384,4,256]{0,2,1:T(8,128)(2,1)}), bf16[384,4,256]{0,2,1:T(8,128)(2,1)}, u32[]{:S(2)}, u32[]{:S(2)}) %all-to-all-start.2) | async-done | bytes 786464 | tf_op jit(solution)/shard_map/all_to_all | solution.py:17
  70.0 2.6 copy.50
  72.6 2.4 reshape.64
  75.0 0.9 broadcast_in_dim.22.clone
  75.9 0.9 broadcast_in_dim.22
  76.9 20.0 %while.35 = (s32[]{:T(128)}, f32[4,512,64]{1,2,0:T(8,128)}, bf16[1536,4,64]{0,2,1:T(8,128)(2,1)}, bf16[1536,4,64]{0,2,1:T(8,128)(2,1)}, bf16[1536,4,64]{0,2,1:T(...) while((s32[]{:T(128)}, f32[4,512,64]{1,2,0:T(8,128)}, ...), condition=%wide.region_6.0_spmd.clone, body=%wide.region_5.0_spmd.clone.sunk | while | flops 681050112 | bytes 26501392 | solution.py:83
  76.9 0.8 fusion.70
  77.6 1.6 fusion.72
  79.2 2.3 multiply_convert_fusion.2
  82.0 1.5 fusion.71
  84.3 1.6 fusion.72
  85.8 2.3 multiply_convert_fusion.2
  88.7 1.5 fusion.71
  90.9 1.6 fusion.72
  92.5 2.3 multiply_convert_fusion.2
  95.3 1.5 fusion.71
  96.8 1.1 convert_bitcast_fusion.2
  98.0 8.4 %all_to_all.131 = bf16[4,128,256]{1,2,0:T(8,128)(2,1)S(1)} all-to-all(bf16[4,128,256]{1,2,0:T(8,128)(2,1)S(1)} %copy.55), channel_id=1, replica_groups=mesh['dp'=8,'seq'=4] {'seq'}, dimensions={0} | all-to-all | bytes 524288 | tf_op jit(solution)/shard_map/all_to_all | solution.py:91
  106.4 3.0 convert_bitcast_fusion
  109.5 4.0 %copy.63 = bf16[1024,1024]{1,0:T(8,128)(2,1)} copy(bf16[1024,1024]{0,1:T(8,128)(2,1)} %convert_bitcast_fusion) | data formatting | bytes 4194304
  113.5 1.1 all_to_all.119
  114.5 2.2 copy.58
  116.7 3.5 %all-to-all-start.7 = ((bf16[4,384,256]{2,1,0:T(8,128)(2,1)}), bf16[4,384,256]{2,1,0:T(8,128)(2,1)S(1)}, u32[]{:S(2)}, u32[]{:S(2)}) async-start(bf16[4,384,256]{2,1,0:T(8,128)(2,1)} %copy.58), calls=%async_computation.7 | async-start | bytes 1572864 | tf_op jit(solution)/shard_map/all_to_all | solution.py:99
  120.2 2.4 all_to_all.115
  122.7 2.2 copy.56
  124.8 7.0 %all-to-all-done.7 = bf16[4,384,256]{2,1,0:T(8,128)(2,1)S(1)} async-done(((bf16[4,384,256]{2,1,0:T(8,128)(2,1)}), bf16[4,384,256]{2,1,0:T(8,128)(2,1)S(1)}, u32[]{:S(2)}, u32[]{:S(2)}) %all-to-all-start.7) | async-done | bytes 786464 | tf_op jit(solution)/shard_map/all_to_all | solution.py:99
  131.8 4.2 %all-to-all-start.6 = ((bf16[4,384,256]{2,1,0:T(8,128)(2,1)}), bf16[4,384,256]{2,1,0:T(8,128)(2,1)}, u32[]{:S(2)}, u32[]{:S(2)}) async-start(bf16[4,384,256]{2,1,0:T(8,128)(2,1)} %copy.56), calls=%async_computation.6 | async-start | bytes 1572864 | tf_op jit(solution)/shard_map/all_to_all | solution.py:98
  136.1 1.2 copy.59
  137.2 10.5 %all-to-all-done.6 = bf16[4,384,256]{2,1,0:T(8,128)(2,1)} async-done(((bf16[4,384,256]{2,1,0:T(8,128)(2,1)}), bf16[4,384,256]{2,1,0:T(8,128)(2,1)}, u32[]{:S(2)}, u32[]{:S(2)}) %all-to-all-start.6) | async-done | bytes 786464 | tf_op jit(solution)/shard_map/all_to_all | solution.py:98
  147.8 2.3 copy.57
  150.1 32.1 %reduce-scatter.7.cloned.1.call-done = bf16[128,1024]{1,0:T(8,128)(2,1)} async-done(((bf16[1024,1024]{1,0:T(8,128)(2,1)}), bf16[128,1024]{1,0:T(8,128)(2,1)}) %reduce-scatter.7.cloned.1.call-update) | async-done | bytes 262160
  182.2 1.8 copy.64
  184.1 1.5 convolution_convert_fusion.1
  185.6 89.2 %all-reduce.3.cloned.1.call-done = (bf16[384,1024]{0,1:T(8,128)(2,1)}, bf16[384,1024]{0,1:T(8,128)(2,1)}) async-done(((bf16[384,1024]{0,1:T(8,128)(2,1)}, bf16[384,1024]{0,1:T(8,128)(2,1)}), (bf16[384,1024]{0,1:T(8,128)(2,1)}, bf16[384,1024]{0,1:T(8,128)(2,1)})) %all-reduce.3.cloned.1.call-update) | async-done | bytes 1572880 | tf_op jit(solution)/shard_map/psum | solution.py:102
  274.8 2.3 copy.60
  277.1 2.3 copy.61
  279.4 17.3 %reduce-scatter.5.cloned.1.call-done = bf16[128,256]{0,1:T(8,128)(2,1)} async-done(((bf16[128,1024]{0,1:T(8,128)(2,1)}), bf16[128,256]{0,1:T(8,128)(2,1)}) %reduce-scatter.5.cloned.1.call-update) | async-done | bytes 65552 | tf_op jit(solution)/shard_map/reduce_scatter | solution.py:115
  296.7 1.6 copy.62
  (49 shorter events, 6.4 us)
Async XLA Ops:
  7.2 176.9 %copy-start = (bf16[1024,1024]{1,0:T(8,128)(2,1)S(1)}, bf16[1024,1024]{1,0:T(8,128)(2,1)}, u32[]{:S(2)}) copy-start(bf16[1024,1024]{1,0:T(8,128)(2,1)} %param.17) | copy-start | bytes 6291460
  9.1 10.3 %all-to-all-start.1 = ((bf16[128,4,256]{0,2,1:T(8,128)(2,1)}), bf16[128,4,256]{0,2,1:T(8,128)(2,1)S(1)}, u32[]{:S(2)}, u32[]{:S(2)}) async-start(bf16[128,4,256]{0,2,1:T(8,128)(2,1)} %bitcast.2), calls=%async_computation.1 | async-start | bytes 524288 | tf_op jit(solution)/shard_map/all_to_all | solution.py:13
  19.4 9.4 %all-to-all-start.4 = ((bf16[128,4,256]{0,2,1:T(8,128)(2,1)}), bf16[128,4,256]{0,2,1:T(8,128)(2,1)S(1)}, u32[]{:S(2)}, u32[]{:S(2)}) async-start(bf16[128,4,256]{0,2,1:T(8,128)(2,1)} %bitcast.8), calls=%async_computation.4 | async-start | bytes 524288 | tf_op jit(solution)/shard_map/all_to_all | solution.py:15
  28.8 9.4 %all-to-all-start.3 = ((bf16[128,4,256]{0,2,1:T(8,128)(2,1)}), bf16[128,4,256]{0,2,1:T(8,128)(2,1)S(1)}, u32[]{:S(2)}, u32[]{:S(2)}) async-start(bf16[128,4,256]{0,2,1:T(8,128)(2,1)} %bitcast.6), calls=%async_computation.3 | async-start | bytes 524288 | tf_op jit(solution)/shard_map/all_to_all | solution.py:14
  38.2 0.7 copy-start.4
  38.9 15.1 %all-to-all-start = ((bf16[384,4,256]{0,2,1:T(8,128)(2,1)}), bf16[384,4,256]{0,2,1:T(8,128)(2,1)S(1)}, u32[]{:S(2)}, u32[]{:S(2)}) async-start(bf16[384,4,256]{0,2,1:T(8,128)(2,1)} %bitcast.92), calls=%async_computation | async-start | bytes 1572864 | tf_op jit(solution)/shard_map/all_to_all | solution.py:16
  54.1 15.9 %all-to-all-start.2 = ((bf16[384,4,256]{0,2,1:T(8,128)(2,1)}), bf16[384,4,256]{0,2,1:T(8,128)(2,1)}, u32[]{:S(2)}, u32[]{:S(2)}) async-start(bf16[384,4,256]{0,2,1:T(8,128)(2,1)} %bitcast.4), calls=%async_computation.2 | async-start | bytes 1572864 | tf_op jit(solution)/shard_map/all_to_all | solution.py:17
  58.3 124.0 %reduce-scatter.7.cloned.1.call-start = ((), (), s32[]{:S(2)}) async-start(), calls=%async_computation.11 | async-start | bytes 2359296
  79.2 2.3 copy-start.1
  82.0 1.5 copy-start.2
  85.8 2.3 copy-start.1
  88.7 1.5 copy-start.2
  92.5 2.3 copy-start.1
  95.3 1.5 copy-start.2
  106.4 7.0 %copy-start.3 = (bf16[1536,4,64]{0,2,1:T(8,128)(2,1)S(1)}, bf16[1536,4,64]{0,2,1:T(8,128)(2,1)}, u32[]{:S(2)}) copy-start(bf16[1536,4,64]{0,2,1:T(8,128)(2,1)} %get-tuple-element.274) | copy-start | bytes 2359300
  116.7 15.1 %all-to-all-start.7 = ((bf16[4,384,256]{2,1,0:T(8,128)(2,1)}), bf16[4,384,256]{2,1,0:T(8,128)(2,1)S(1)}, u32[]{:S(2)}, u32[]{:S(2)}) async-start(bf16[4,384,256]{2,1,0:T(8,128)(2,1)} %copy.58), calls=%async_computation.7 | async-start | bytes 1572864 | tf_op jit(solution)/shard_map/all_to_all | solution.py:99
  131.8 15.9 %all-to-all-start.6 = ((bf16[4,384,256]{2,1,0:T(8,128)(2,1)}), bf16[4,384,256]{2,1,0:T(8,128)(2,1)}, u32[]{:S(2)}, u32[]{:S(2)}) async-start(bf16[4,384,256]{2,1,0:T(8,128)(2,1)} %copy.56), calls=%async_computation.6 | async-start | bytes 1572864 | tf_op jit(solution)/shard_map/all_to_all | solution.py:98
  136.0 138.8 %all-reduce.3.cloned.1.call-start = ((), (), s32[]{:S(2)}) async-start(), calls=%async_computation.12 | async-start | bytes 3145728 | tf_op jit(solution)/shard_map/psum | solution.py:102
  150.1 146.7 %reduce-scatter.5.cloned.1.call-start = ((), (), s32[]{:S(2)}) async-start(), calls=%async_computation.10 | async-start | bytes 327680 | tf_op jit(solution)/shard_map/reduce_scatter | solution.py:115
Sparse Core Ops, SparseCore 0:
  113.6 68.6 reduce-scatter.6
  186.4 88.3 all-reduce.2
  277.3 19.4 reduce-scatter.4
where the time goes:
time: 306 us; the launch traced here: 305 us
  waiting for transfers between devices  172 us (56%)
  local copies, waits for them, and re-layouts  52.2 us (17%)
  matrix products  26.7 us (9%)
  starting transfers between devices  26.6 us (9%)
  between operations  13.9 us (5%)
  blocking collectives  8.42 us (3%)
  other arithmetic  4.45 us (1%)
    psum x1, waiting for transfers between devices, local(): lax.psum(key_back, 'dp').astype(jnp.float32)  89.2 us
    unnamed x4, waiting for transfers between devices  32.2 us
    unnamed x16, local copies, waits for them, and re-layouts  22.7 us
    reduce_scatter x1, waiting for transfers between devices, local(): lax.psum_scatter(slab_weight, 'seq', scatter_dimension=1, tiled=True)  17.3 us
    all_to_all x1, waiting for transfers between devices, local(): lax.all_to_all(key_grad_heads, 'seq', split_axis=0, concat_axis=1, tiled=...  10.5 us
    all_to_all x1, blocking collectives, local(): lax.all_to_all(query_grad_heads, 'seq', split_axis=0, concat_axis=1, tile...  8.42 us
    all_to_all x1, waiting for transfers between devices, local(): lax.all_to_all(val_grad_heads, 'seq', split_axis=0, concat_axis=1, tiled=...  7 us
    dot_general x3, matrix products, second_pass(): jnp.einsum('qhd,khd->hqk', grad_heads, val_block, preferred_element_type=...  6.93 us
  transfers between devices with their start and end apart: 10, of which 10 were waited for; matrix products, arithmetic and copies ran while one was open for 13% of the time, Pallas kernels for 0%

commit v1 on v0

v1 whole, which is shorter than its diff:
```python
import functools
import math

import jax
import jax.numpy as jnp
from jax import lax
from jax.experimental import pallas as pl
from jax.experimental.pallas import tpu as pltpu
from jax.sharding import PartitionSpec as P

HD = 64
PAIR = 2 * HD
SCALE = 1.0 / math.sqrt(HD)
BF = jnp.bfloat16
F32 = jnp.float32
VMEM_LIMIT = 56 * 1024 * 1024


def dot(a, b, ca, cb):
    return lax.dot_general(a, b, (((ca,), (cb,)), ((), ())), preferred_element_type=F32)


def own_lanes(x, head):
    lane = lax.broadcasted_iota(jnp.int32, x.shape, 1)
    mine = lane < HD if head == 0 else lane >= HD
    return jnp.where(mine, x, jnp.zeros_like(x))


def delta_kernel(grad_ref, out_ref, delta_ref):
    prod = grad_ref[...].astype(F32) * out_ref[...].astype(F32)
    cols = prod.T
    heads = cols.shape[0] // HD
    for head in range(heads):
        part = jnp.sum(cols[head * HD : (head + 1) * HD], axis=0, keepdims=True)
        delta_ref[head // 2, head % 2] = part[0]


def delta_of(grad_out, attn_out):
    rows, cols = grad_out.shape
    return pl.pallas_call(
        delta_kernel,
        out_shape=jax.ShapeDtypeStruct((cols // PAIR, 2, rows), F32),
        compiler_params=pltpu.CompilerParams(vmem_limit_bytes=VMEM_LIMIT),
        cost_estimate=pl.CostEstimate(flops=4 * rows * cols, bytes_accessed=4 * rows * cols, transcendentals=0),
    )(grad_out, attn_out)


def probs_kernel(count, *refs):
    q_refs, k_ref = refs[:count], refs[count]
    p_ref, m_ref, lse_ref = refs[count + 1 :]
    q = jnp.concatenate([r[...] for r in q_refs], axis=0) * jnp.asarray(SCALE, BF)
    k = k_ref[...]
    for head in range(2):
        s = dot(own_lanes(k, head), q, 1, 1)
        top = jnp.max(s, axis=0, keepdims=True)
        p = jnp.exp(s - top)
        total = jnp.sum(p, axis=0, keepdims=True)
        p_ref[head] = p.astype(BF)
        m_ref[0, head] = top[0]
        lse_ref[0, head] = (top + jnp.log(total))[0]


def probs_of(q_pieces, keys):
    count = len(q_pieces)
    piece, cols = q_pieces[0].shape
    tokens = keys.shape[0]
    rows = piece * count
    pairs = cols // PAIR
    return pl.pallas_call(
        functools.partial(probs_kernel, count),
        grid=(pairs,),
        in_specs=[pl.BlockSpec((piece, PAIR), lambda i: (0, i))] * count
        + [pl.BlockSpec((tokens, PAIR), lambda i: (0, i))],
        out_specs=[
            pl.BlockSpec((2, tokens, rows), lambda i: (i, 0, 0)),
            pl.BlockSpec((1, 2, rows), lambda i: (i, 0, 0)),
            pl.BlockSpec((1, 2, rows), lambda i: (i, 0, 0)),
        ],
        out_shape=[
            jax.ShapeDtypeStruct((2 * pairs, tokens, rows), BF),
            jax.ShapeDtypeStruct((pairs, 2, rows), F32),
            jax.ShapeDtypeStruct((pairs, 2, rows), F32),
        ],
        compiler_params=pltpu.CompilerParams(vmem_limit_bytes=VMEM_LIMIT),
        cost_estimate=pl.CostEstimate(
            flops=2 * rows * tokens * cols,
            bytes_accessed=2 * rows * tokens * 2 * pairs,
            transcendentals=rows * tokens * 2 * pairs,
        ),
    )(*q_pieces, keys)


def grads_kernel(count, half_ref, *refs):
    q_refs, g_refs = refs[:count], refs[count : 2 * count]
    pa_ref, pb_ref, v_ref, kt_ref, w_ref, delta_ref, dkv_ref, dqt_ref = refs[2 * count :]
    rows = w_ref.shape[2]
    side = rows // 2
    w = w_ref[0]
    delta = delta_ref[0]
    v = v_ref[...]
    first = lax.broadcasted_iota(jnp.int32, (PAIR, rows), 0) < HD
    wide = jnp.where(first, w[0:1], w[1:2]).T
    q = jnp.concatenate([r[...] for r in q_refs], axis=0)
    g = jnp.concatenate([r[...] for r in g_refs], axis=0)
    qw = (q.astype(F32) * (wide * SCALE)).astype(BF)
    gw = (g.astype(F32) * wide).astype(BF)
    dk = jnp.zeros((v.shape[0], PAIR), F32)
    dv = jnp.zeros((v.shape[0], PAIR), F32)
    for half, p_ref in ((0, pa_ref), (1, pb_ref)):
        at = slice(half * side, (half + 1) * side)
        for head in range(2):
            p = p_ref[head]
            dp = dot(v, own_lanes(g[at], head), 1, 1)
            t = (p.astype(F32) * (dp - delta[head : head + 1, at])).astype(BF)
            dv = dv + dot(p, own_lanes(gw[at], head), 1, 0)
            dk = dk + dot(t, own_lanes(qw[at], head), 1, 0)
            dq = dot(kt_ref[head * HD : (head + 1) * HD], t, 1, 0)
            dq = dq * (w[head : head + 1, at] * SCALE)
            dqt_ref[head * HD : (head + 1) * HD, at] = dq.astype(BF)
    dkv_ref[0] = dk.astype(BF)
    dkv_ref[1] = dv.astype(BF)


def grads_of(half, q_pieces, g_pieces, pa, pb, values, keys_t, w, delta):
    count = len(q_pieces)
    piece, cols = q_pieces[0].shape
    tokens = values.shape[0]
    rows = piece * count
    steps = cols // PAIR // 2
    at = lambda i, h: h[0] * steps + i
    row_spec = pl.BlockSpec((piece, PAIR), lambda i, h: (0, at(i, h)))
    p_spec = pl.BlockSpec((2, tokens, rows // 2), lambda i, h: (at(i, h), 0, 0))
    stat_spec = pl.BlockSpec((1, 2, rows), lambda i, h: (at(i, h), 0, 0))
    return pl.pallas_call(
        functools.partial(grads_kernel, count),
        grid_spec=pltpu.PrefetchScalarGridSpec(
            num_scalar_prefetch=1,
            grid=(steps,),
            in_specs=[row_spec] * (2 * count)
            + [
                p_spec,
                p_spec,
                pl.BlockSpec((tokens, PAIR), lambda i, h: (0, at(i, h))),
                pl.BlockSpec((PAIR, tokens), lambda i, h: (at(i, h), 0)),
                stat_spec,
                stat_spec,
            ],
            out_specs=[
                pl.BlockSpec((2, tokens, PAIR), lambda i, h: (0, 0, i)),
                pl.BlockSpec((PAIR, rows), lambda i, h: (i, 0)),
            ],
        ),
        out_shape=[
            jax.ShapeDtypeStruct((2, tokens, cols // 2), BF),
            jax.ShapeDtypeStruct((cols // 2, rows), BF),
        ],
        compiler_params=pltpu.CompilerParams(vmem_limit_bytes=VMEM_LIMIT),
        cost_estimate=pl.CostEstimate(
            flops=4 * rows * tokens * cols,
            bytes_accessed=2 * rows * tokens * 2 * steps,
            transcendentals=0,
        ),
    )(half, *q_pieces, *g_pieces, pa, pb, values, keys_t, w, delta)


def weight_kernel(count, *refs):
    x = jnp.concatenate([r[...] for r in refs[:count]], axis=0)
    refs[count + 1][...] = dot(x, refs[count][...], 0, 1).astype(BF)


def weight_of(x_pieces, dq_cols):
    count = len(x_pieces)
    piece, cols = x_pieces[0].shape
    width, rows = dq_cols.shape
    step = min(cols, 256)
    return pl.pallas_call(
        functools.partial(weight_kernel, count),
        grid=(cols // step,),
        in_specs=[pl.BlockSpec((piece, step), lambda i: (0, i))] * count
        + [pl.BlockSpec((width, rows), lambda i: (0, 0))],
        out_specs=pl.BlockSpec((step, width), lambda i: (i, 0)),
        out_shape=jax.ShapeDtypeStruct((cols, width), BF),
        compiler_params=pltpu.CompilerParams(vmem_limit_bytes=VMEM_LIMIT),
        cost_estimate=pl.CostEstimate(
            flops=2 * rows * cols * width, bytes_accessed=2 * rows * cols, transcendentals=0
        ),
    )(*x_pieces, dq_cols)


def swap(x, axis, size, mask):
    return lax.ppermute(x, axis, [(i, i ^ mask) for i in range(size)])


def gather_pieces(x, axis, size):
    pieces = {0: x}
    bit = size // 2
    while bit:
        for k in list(pieces):
            pieces[k | bit] = swap(pieces[k], axis, size, bit)
        bit //= 2
    return [pieces[k] for k in range(size)]


def flip_pieces(x, count, bit):
    lead, piece = x.shape[:-1], x.shape[-1] // count
    y = x.reshape(lead + (count // (2 * bit), 2, bit * piece))
    return jnp.flip(y, axis=-2).reshape(x.shape)


def pick(blocks, index):
    return lax.dynamic_index_in_dim(blocks, index, 0, keepdims=False)


def exchange_sum(x, axis, size, stride, group, wide=False):
    me = (lax.axis_index(axis) // stride) % group
    total = pick(x, me).astype(F32)
    for k in range(1, group):
        total = total + swap(pick(x, me ^ k), axis, size, k * stride).astype(F32)
    return total if wide else total.astype(BF)


def exchange_gather(x, axis, size, stride, group):
    me = (lax.axis_index(axis) // stride) % group
    out = jnp.zeros((group,) + x.shape, x.dtype)
    for k in range(group):
        got = x if k == 0 else swap(x, axis, size, k * stride)
        out = lax.dynamic_update_index_in_dim(out, got, me ^ k, 0)
    return out


def local(n_dp, n_seq, qx, queries, keys, values, attn_out, grad_out, wq):
    low = max(n_dp // 4, 1)
    high = n_dp // low
    cols = queries.shape[1]
    me = lax.axis_index("seq")
    top = n_seq // 2
    q_pieces = gather_pieces(queries, "seq", n_seq)
    g_pieces = gather_pieces(grad_out, "seq", n_seq)
    x_pieces = gather_pieces(qx, "seq", n_seq)
    keys_t = keys.T
    delta = delta_of(grad_out, attn_out)
    pa, ma, la = probs_of(q_pieces[:top], keys)
    pb, mb, lb = probs_of(q_pieces[top:], keys)
    rows = 2 * la.shape[2]
    peak = jnp.concatenate([ma, mb], axis=2)
    lse = jnp.concatenate([la, lb], axis=2)
    bit = 1
    while bit < n_seq:
        got = swap(jnp.concatenate([lse, delta], axis=2), "seq", n_seq, bit)
        lse = jnp.logaddexp(lse, flip_pieces(got[:, :, :rows], n_seq, bit))
        delta = jnp.concatenate([delta, got[:, :, rows:]], axis=2)
        bit *= 2
    w = jnp.exp(peak - lse)

    mine = (me // top).astype(jnp.int32)
    shards, dqs = [], []
    for half in (1 - mine, mine):
        dkv, dqt = grads_of(half.reshape(1), q_pieces, g_pieces, pa, pb, values, keys_t, w, delta)
        tokens = dkv.shape[1]
        part = dkv.reshape(low, 2 * tokens // low, cols // 2)
        part = exchange_sum(part, "dp", n_dp, 1, low)
        part = part.reshape(high, part.shape[0] // high, cols // 2)
        shards.append(exchange_sum(part, "dp", n_dp, low, high))
        dqs.append(dqt)

    def narrow(dqt):
        blocks = dqt.reshape(top, dqt.shape[0] // top, rows)
        bit = 1
        base = me % top
        while bit < top:
            view = blocks.reshape((blocks.shape[0] // 2, 2) + blocks.shape[1:])
            own = (base // bit) % 2
            keep = lax.dynamic_index_in_dim(view, own, 1, keepdims=False)
            send = lax.dynamic_index_in_dim(view, 1 - own, 1, keepdims=False)
            got = swap(send, "seq", n_seq, bit)
            got = flip_pieces(got, n_seq, bit)
            blocks = (keep.astype(F32) + got.astype(F32)).astype(BF)
            bit *= 2
        return blocks[0]

    other, own = narrow(dqs[0]), narrow(dqs[1])
    got = flip_pieces(swap(other, "seq", n_seq, top), n_seq, top)
    dq_cols = (own.astype(F32) + got.astype(F32)).astype(BF)

    weight = weight_of(x_pieces, dq_cols)
    weight = weight.reshape(high, low, weight.shape[0] // n_dp, weight.shape[1])
    weight = exchange_sum(weight, "dp", n_dp, low, high)
    grad_weight = exchange_sum(weight, "dp", n_dp, 1, low, wide=True)

    piece = rows // n_seq
    width = cols // n_seq
    dq_rows = jnp.zeros((n_seq, width, piece), BF)
    for k in range(n_seq):
        block = dq_cols[:, k * piece : (k + 1) * piece]
        block = block if k == 0 else swap(block, "seq", n_seq, k)
        dq_rows = lax.dynamic_update_index_in_dim(dq_rows, block, me ^ k, 0)
    grad_input = dot(dq_rows.reshape(cols, piece), wq, 0, 1).astype(BF)

    halves = []
    for shard in shards:
        part = exchange_gather(shard, "dp", n_dp, low, high)
        part = part.reshape((-1,) + part.shape[2:])
        part = exchange_gather(part, "dp", n_dp, 1, low)
        halves.append(part.reshape(2, -1, cols // 2))
    other, own = halves
    left = jnp.where(mine == 0, own, other)
    right = jnp.where(mine == 0, other, own)
    both = jnp.concatenate([left, right], axis=2)
    return (grad_input, both[0], both[1], grad_weight)


def solution(mesh):
    n_dp, n_seq = mesh.shape["dp"], mesh.shape["seq"]
    return jax.shard_map(
        functools.partial(local, n_dp, n_seq),
        mesh=mesh,
        in_specs=(
            P(("dp", "seq"), None),
            P(("dp", "seq"), None),
            P("seq", None),
            P("seq", None),
            P(("dp", "seq"), None),
            P(("dp", "seq"), None),
            P(),
        ),
        out_specs=(P(("dp", "seq"), None), P("seq", None), P("seq", None), P("dp", "seq")),
        check_vma=False,
    )
```

time: 306 us -> 155 us (0.51)
  waiting for transfers between devices: 172 us -> 35 us
  Pallas kernels: 0 us -> 35.6 us
  local copies, waits for them, and re-layouts: 52.2 us -> 26.7 us
  matrix products: 26.7 us -> 1.54 us
  starting transfers between devices: 26.6 us -> 42.9 us
  between operations: 13.9 us -> 1.2 us
  blocking collectives: 8.42 us -> 0 us
  other arithmetic: 4.45 us -> 10.3 us
    psum x1 -> x0, waiting for transfers between devices: 89.2 us -> none  [local(): lax.psum(key_back, 'dp').astype(jnp.float32)]
    ppermute x0 -> x37, starting transfers between devices: none -> 42.9 us  [swap(): return lax.ppermute(x, axis, [(i, i ^ mask) for i in range(size)])]
    pallas_call x0 -> x6, Pallas kernels: none -> 35.6 us  [the longest x2 15.3 us: grads_of(): pl.pallas_call(functools.partial(grads_kernel, count), grid_spec=pltpu.Pr...]
    ppermute x0 -> x37, waiting for transfers between devices: none -> 35 us  [swap(): return lax.ppermute(x, axis, [(i, i ^ mask) for i in range(size)])]
    all_to_all x7 -> x0, waiting for transfers between devices: 33.6 us -> none  [the longest x1 10.5 us: local(): lax.all_to_all(key_grad_heads, 'seq', split_axis=0, concat_axis=1, tiled=...]
    unnamed x4 -> x0, waiting for transfers between devices: 32.2 us -> none
    all_to_all x7 -> x0, starting transfers between devices: 26.4 us -> none  [the longest x1 4.24 us: local(): lax.all_to_all(queries, 'seq', split_axis=1, concat_axis=0, tiled=True)]
    dot_general x20 -> x1, matrix products: 26.7 us -> 1.54 us  [dot(): lax.dot_general(a, b, (((ca,), (cb,)), ((), ())), preferred_element_type=...]
  transfers between devices with their start and end apart: 10 -> 37, of which waited for: 10 -> 11; matrix products, arithmetic and copies ran while one was open for 13% -> 22% of each run, Pallas kernels for 0% -> 23%
where the time goes in v1:
time: 155 us; the launch traced here: 153 us
  starting transfers between devices  42.9 us (28%)
  Pallas kernels  35.6 us (23%)
  waiting for transfers between devices  35 us (23%)
  local copies, waits for them, and re-layouts  26.7 us (17%)
  other arithmetic  10.3 us (7%)
    ppermute x37, starting transfers between devices, swap(): return lax.ppermute(x, axis, [(i, i ^ mask) for i in range(size)])  42.9 us
    ppermute x37, waiting for transfers between devices, swap(): return lax.ppermute(x, axis, [(i, i ^ mask) for i in range(size)])  35 us
    pallas_call x2, Pallas kernels, grads_of(): pl.pallas_call(functools.partial(grads_kernel, count), grid_spec=pltpu.Pr...  15.3 us
    pallas_call x2, Pallas kernels, probs_of(): pl.pallas_call(functools.partial(probs_kernel, count), grid=(pairs,), in_...  14.4 us
    unnamed x35, local copies, waits for them, and re-layouts  6.75 us
    rev x5, local copies, waits for them, and re-layouts, flip_pieces(): return jnp.flip(y, axis=-2).reshape(x.shape)  6.42 us
    squeeze x6, local copies, waits for them, and re-layouts, pick(): return lax.dynamic_index_in_dim(blocks, index, 0, keepdims=False)  4.69 us
    pallas_call x1, Pallas kernels, weight_of(): pl.pallas_call(functools.partial(weight_kernel, count), grid=(cols // ste...  3.95 us
  transfers between devices with their start and end apart: 37, of which 11 were waited for; matrix products, arithmetic and copies ran while one was open for 22% of the time, Pallas kernels for 23%

profile of v1, /device:TPU:0, one launch (start us, length us, event | category | flops | bytes accessed | tf_op | source)
XLA Modules:
  0.0 153.3 jit_solution(2279449577598928692)
XLA Ops:
  0.6 3.0 %collective-permute-start.1 = (bf16[128,1024]{1,0:T(8,128)(2,1)}, bf16[128,1024]{1,0:T(8,128)(2,1)S(1)}, u32[]{:S(2)}, u32[]{:S(2)}) collective-permute-start(bf16[128,1024]{1,0:T(8,128)(2,1)} %refs_0_.6), channel_id=1, source_target_pairs={{0,2},{1,3},{2,0},{3,1},{4,6},{5,7},{6,4},{7,5},{8,10},{9,11},{10,... | collective-permute-start | bytes 786440 | tf_op jit(solution)/shard_map/ppermute | solution.py:191
  3.7 6.5 %collective-permute-done.1.refs_0_.refs_2_ = bf16[128,1024]{1,0:T(8,128)(2,1)S(1)} collective-permute-done((bf16[128,1024]{1,0:T(8,128)(2,1)}, bf16[128,1024]{1,0:T(8,128)(2,1)S(1)}, u32[]{:S(2)}, u32[]{:S(2)}) %collective-permute-start.1) | collective-permute-done | bytes 262176 | tf_op jit(solution)/shard_map/ppermute | solution.py:191
  10.2 1.7 %collective-permute-start.4 = (bf16[128,1024]{1,0:T(8,128)(2,1)}, bf16[128,1024]{1,0:T(8,128)(2,1)S(1)}, u32[]{:S(2)}, u32[]{:S(2)}) collective-permute-start(bf16[128,1024]{1,0:T(8,128)(2,1)} %refs_4_.3), channel_id=1, source_target_pairs={{0,2},{1,3},{2,0},{3,1},{4,6},{5,7},{6,4},{7,5},{8,10},{9,11},{10,... | collective-permute-start | bytes 786440 | tf_op jit(solution)/shard_map/ppermute | solution.py:191
  11.9 1.8 %shard_map.104 = f32[8,2,128]{2,1,0:T(2,128)} custom-call(bf16[128,1024]{1,0:T(8,128)(2,1)} %refs_4_.3, bf16[128,1024]{1,0:T(8,128)(2,1)} %out_ref.1), custom_call_target="tpu_custom_call" | custom-call | flops 524288 | bytes 524288 | tf_op jit(solution)/shard_map/pallas_call | solution.py:40
  13.8 0.7 copy-done.4
  14.5 7.2 %shard_map.102 = (bf16[16,384,256]{2,1,0:T(8,128)(2,1)}, f32[8,2,256]{2,1,0:T(2,128)}, f32[8,2,256]{2,1,0:T(2,128)}) custom-call(bf16[128,1024]{1,0:T(8,128)(2,1)} %refs_0_.6, bf16[128,1024]{1,0:T(8,128)(2,1)} %copy-done.4, bf16[384,1024]{1,0:T(8,128)(2,1)} %refs_2_.3), custom_call_target="tpu_custom_call" | custom-call | flops 201326592 | bytes 3145728 | tf_op jit(solution)/shard_map/pallas_call | solution.py:69
  21.7 0.8 constant_dynamic-update-slice_fusion.1
  22.5 0.7 copy-done.5
  23.3 7.2 %shard_map.103 = (bf16[16,384,256]{2,1,0:T(8,128)(2,1)}, f32[8,2,256]{2,1,0:T(2,128)}, f32[8,2,256]{2,1,0:T(2,128)}) custom-call(bf16[128,1024]{1,0:T(8,128)(2,1)} %copy-done.3, bf16[128,1024]{1,0:T(8,128)(2,1)} %copy-done.5, bf16[384,1024]{1,0:T(8,128)(2,1)} %refs_2_.3), custom_call_target="tpu_custom_call" | custom-call | flops 201326592 | bytes 3145728 | tf_op jit(solution)/shard_map/pallas_call | solution.py:69
  30.5 0.7 pad_maximum_fusion.2
  31.5 0.7 constant_dynamic-update-slice_fusion
  33.8 1.7 %collective-permute-start.31 = (bf16[128,1024]{1,0:T(8,128)(2,1)}, bf16[128,1024]{1,0:T(8,128)(2,1)}, u32[]{:S(2)}, u32[]{:S(2)}) collective-permute-start(bf16[128,1024]{1,0:T(8,128)(2,1)} %refs_0_.7), channel_id=1, source_target_pairs={{0,2},{1,3},{2,0},{3,1},{4,6},{5,7},{6,4},{7,5},{8,10},{9,11},{10,... | collective-permute-start | bytes 786440 | tf_op jit(solution)/shard_map/ppermute | solution.py:191
  35.5 2.3 %copy.11 = bf16[384,1024]{0,1:T(8,128)(2,1)} copy(bf16[384,1024]{1,0:T(8,128)(2,1)} %refs_2_.3) | data formatting | bytes 1572864 | tf_op args[2]
  38.0 0.7 fusion.18
  38.8 0.7 copy-done.7
  39.6 7.7 %shard_map.106 = (bf16[2,384,512]{2,1,0:T(8,128)(2,1)}, bf16[512,512]{1,0:T(8,128)(2,1)}) custom-call(s32[1]{0:T(128)} %bitcast.5.half_ref, bf16[128,1024]{1,0:T(8,128)(2,1)} %refs_0_.6, bf16[128,1024]{1,0:T(8,128)(2,1)} %copy-done.4, bf16[128,1024]{1,0:T(8,128)(2,1)} %copy-done.3, bf16[128,1024]{1,0:T(8,128)(2,1)} %copy-done.5, bf16[128,1024]{1,0:T(8,128)(2,1)} %refs_4_.3, ...), custom_call_target="tpu_custom_call" | custom-call | flops 805306368 | bytes 3145728 | tf_op jit(solution)/shard_map/pallas_call | solution.py:134
  47.2 1.0 dynamic-slice_bitcast_fusion.2
  48.3 1.8 %dynamic-slice_bitcast_fusion = bf16[384,512]{1,0:T(8,128)(2,1)} fusion(bf16[2,384,512]{2,1,0:T(8,128)(2,1)} %get-tuple-element.23, s32[]{:T(128)S(6)} %select_n.159), kind=kLoop, calls=%fused_computation.22 | loop fusion | bytes 786436 | tf_op jit(solution)/shard_map/jit(dynamic_index_in_dim)/squeeze | solution.py:211
  50.1 1.5 collective-permute-start.22
  51.6 7.7 %shard_map.105 = (bf16[2,384,512]{2,1,0:T(8,128)(2,1)}, bf16[512,512]{1,0:T(8,128)(2,1)}) custom-call(s32[1]{0:T(128)} %bitcast.half_ref, bf16[128,1024]{1,0:T(8,128)(2,1)} %refs_0_.6, bf16[128,1024]{1,0:T(8,128)(2,1)} %copy-done.4, bf16[128,1024]{1,0:T(8,128)(2,1)} %copy-done.3, bf16[128,1024]{1,0:T(8,128)(2,1)} %copy-done.5, bf16[128,1024]{1,0:T(8,128)(2,1)} %refs_4_.3, ...), custom_call_target="tpu_custom_call" | custom-call | flops 805306368 | bytes 3145728 | tf_op jit(solution)/shard_map/pallas_call | solution.py:134
  59.3 1.7 %dynamic-slice_bitcast_fusion.3 = bf16[1,256,512]{2,1,0:T(8,128)(2,1)} fusion(bf16[1,2,256,512]{3,2,1,0:T(8,128)(2,1)} %bitcast.129, s32[]{:T(128)S(6)} %select_n.151), kind=kLoop, calls=%fused_computation.29 | loop fusion | bytes 524292 | tf_op jit(solution)/shard_map/jit(dynamic_index_in_dim)/squeeze | solution.py:274
  61.2 1.8 %dynamic-slice_bitcast_fusion.1 = bf16[384,512]{1,0:T(8,128)(2,1)} fusion(bf16[2,384,512]{2,1,0:T(8,128)(2,1)} %get-tuple-element.22, s32[]{:T(128)S(6)} %select_n.159), kind=kLoop, calls=%fused_computation.23 | loop fusion | bytes 786436 | tf_op jit(solution)/shard_map/jit(dynamic_index_in_dim)/squeeze | solution.py:211
  63.0 0.5 collective-permute-start.14
  63.6 1.4 rev.22
  65.1 0.8 fusion.5
  66.2 1.0 reshape.105
  67.2 1.4 rev.21
  68.7 1.3 fusion.3
  70.0 3.9 %collective-permute-start.25 = (bf16[96,512]{1,0:T(8,128)(2,1)S(1)}, bf16[96,512]{1,0:T(8,128)(2,1)S(1)}, u32[]{:S(2)}, u32[]{:S(2)}) collective-permute-start(bf16[96,512]{1,0:T(8,128)(2,1)S(1)} %get-tuple-element.36), channel_id=1, source_target_pairs={{0,24},{4,28},{8,16},{12,20},{16,8},{20,12},{24,0},{28,4},{1,25},{... | collective-permute-start | bytes 294920 | tf_op jit(solution)/shard_map/ppermute | solution.py:191
  73.9 0.7 collective-permute-done.14
  74.6 1.6 %collective-permute-start.23 = (bf16[96,512]{1,0:T(8,128)(2,1)S(1)}, bf16[96,512]{1,0:T(8,128)(2,1)S(1)}, u32[]{:S(2)}, u32[]{:S(2)}) collective-permute-start(bf16[96,512]{1,0:T(8,128)(2,1)S(1)} %get-tuple-element.35), channel_id=1, source_target_pairs={{0,8},{4,12},{8,0},{12,4},{16,24},{20,28},{24,16},{28,20},{1,9},{5... | collective-permute-start | bytes 294920 | tf_op jit(solution)/shard_map/ppermute | solution.py:191
  76.2 1.1 fusion.4
  77.5 4.0 %collective-permute-start.17 = (bf16[96,512]{1,0:T(8,128)(2,1)S(1)}, bf16[96,512]{1,0:T(8,128)(2,1)S(1)}, u32[]{:S(2)}, u32[]{:S(2)}) collective-permute-start(bf16[96,512]{1,0:T(8,128)(2,1)S(1)} %get-tuple-element.39), channel_id=1, source_target_pairs={{0,24},{4,28},{8,16},{12,20},{16,8},{20,12},{24,0},{28,4},{1,25},{... | collective-permute-start | bytes 294920 | tf_op jit(solution)/shard_map/ppermute | solution.py:191
  81.4 4.5 %collective-permute-done.24 = bf16[96,512]{1,0:T(8,128)(2,1)S(1)} collective-permute-done((bf16[96,512]{1,0:T(8,128)(2,1)S(1)}, bf16[96,512]{1,0:T(8,128)(2,1)S(1)}, u32[]{:S(2)}, u32[]{:S(2)}) %collective-permute-start.24) | collective-permute-done | bytes 98336 | tf_op jit(solution)/shard_map/ppermute | solution.py:191
  86.0 3.5 %collective-permute-start.15 = (bf16[96,512]{1,0:T(8,128)(2,1)S(1)}, bf16[96,512]{1,0:T(8,128)(2,1)S(1)}, u32[]{:S(2)}, u32[]{:S(2)}) collective-permute-start(bf16[96,512]{1,0:T(8,128)(2,1)S(1)} %get-tuple-element.38), channel_id=1, source_target_pairs={{0,8},{4,12},{8,0},{12,4},{16,24},{20,28},{24,16},{28,20},{1,9},{5... | collective-permute-start | bytes 294920 | tf_op jit(solution)/shard_map/ppermute | solution.py:191
  89.5 0.7 bitcast_dynamic-update-slice_fusion.7
  90.2 0.5 collective-permute-start.32
  90.7 1.9 %collective-permute-done.16 = bf16[96,512]{1,0:T(8,128)(2,1)S(1)} collective-permute-done((bf16[96,512]{1,0:T(8,128)(2,1)S(1)}, bf16[96,512]{1,0:T(8,128)(2,1)S(1)}, u32[]{:S(2)}, u32[]{:S(2)}) %collective-permute-start.16) | collective-permute-done | bytes 98336 | tf_op jit(solution)/shard_map/ppermute | solution.py:191
  93.0 2.1 %collective-permute-start.27 = (bf16[96,512]{1,0:T(8,128)(2,1)}, bf16[96,512]{1,0:T(8,128)(2,1)S(1)}, u32[]{:S(2)}, u32[]{:S(2)}) collective-permute-start(bf16[96,512]{1,0:T(8,128)(2,1)} %get-tuple-element.25), channel_id=1, source_target_pairs={{0,16},{4,20},{8,24},{12,28},{16,0},{20,4},{24,8},{28,12},{1,17},{... | collective-permute-start | bytes 294920 | tf_op jit(solution)/shard_map/ppermute | solution.py:191
  95.2 0.7 bitcast_dynamic-update-slice_fusion.11
  95.9 1.9 %collective-permute-start.28 = (bf16[96,512]{1,0:T(8,128)(2,1)}, bf16[96,512]{1,0:T(8,128)(2,1)}, u32[]{:S(2)}, u32[]{:S(2)}) collective-permute-start(bf16[96,512]{1,0:T(8,128)(2,1)} %get-tuple-element.25), channel_id=1, source_target_pairs={{0,24},{4,28},{8,16},{12,20},{16,8},{20,12},{24,0},{28,4},{1,25},{... | collective-permute-start | bytes 294920 | tf_op jit(solution)/shard_map/ppermute | solution.py:191
  97.8 1.7 %reshape.108 = bf16[256,1,2,256]{3,2,0,1:T(2,128)(2,1)} reshape(bf16[256,512]{1,0:T(8,128)(2,1)} %collective-permute-done.10) | data formatting | bytes 524288 | tf_op jit(solution)/shard_map/reshape | solution.py:206
  99.5 3.4 %rev.23 = bf16[256,1,2,256]{3,2,0,1:T(2,128)(2,1)} reverse(bf16[256,1,2,256]{3,2,0,1:T(2,128)(2,1)} %reshape.108), dimensions={2} | reverse | bytes 524288 | tf_op jit(solution)/shard_map/jit(_flip)/rev | solution.py:207
  102.9 1.0 copy.12
  104.0 1.1 add_convert_fusion.refs_4_
  105.8 4.0 %shard_map.107 = bf16[1024,256]{1,0:T(8,128)(2,1)} custom-call(bf16[128,1024]{1,0:T(8,128)(2,1)} %refs_0_.7, bf16[128,1024]{1,0:T(8,128)(2,1)} %collective-permute-done.30.refs_1_, bf16[128,1024]{1,0:T(8,128)(2,1)} %collective-permute-done.31.refs_2_, bf16[128,1024]{1,0:T(8,128)(2,1)} %collective-permute-done.32.refs_3_, bf16[256,512]{1,0:T(8,128)(2,1)} %copy-done.2), custom_call_target="tpu_custom_call" | custom-call | flops 268435456 | bytes 1048576 | tf_op jit(solution)/shard_map/pallas_call | solution.py:176
  109.7 1.1 dynamic-slice_bitcast_fusion.6
  110.8 0.8 collective-permute-start.12
  111.6 3.5 %collective-permute-done.12 = bf16[256,128]{1,0:T(8,128)(2,1)S(1)} collective-permute-done((bf16[256,128]{1,0:T(8,128)(2,1)S(1)}, bf16[256,128]{1,0:T(8,128)(2,1)S(1)}, u32[]{:S(2)}, u32[]{:S(2)}) %collective-permute-start.12) | collective-permute-done | bytes 65568 | tf_op jit(solution)/shard_map/ppermute | solution.py:191
  115.1 3.7 %collective-permute-done.13 = bf16[256,128]{1,0:T(8,128)(2,1)S(1)} collective-permute-done((bf16[256,128]{1,0:T(8,128)(2,1)S(1)}, bf16[256,128]{1,0:T(8,128)(2,1)S(1)}, u32[]{:S(2)}, u32[]{:S(2)}) %collective-permute-start.13) | collective-permute-done | bytes 65568 | tf_op jit(solution)/shard_map/ppermute | solution.py:191
  118.8 2.8 %collective-permute-start.19 = (bf16[96,512]{1,0:T(8,128)(2,1)S(1)}, bf16[96,512]{1,0:T(8,128)(2,1)S(1)}, u32[]{:S(2)}, u32[]{:S(2)}) collective-permute-start(bf16[96,512]{1,0:T(8,128)(2,1)S(1)} %copy-done.12), channel_id=1, source_target_pairs={{0,16},{4,20},{8,24},{12,28},{16,0},{20,4},{24,8},{28,12},{1,17},{... | collective-permute-start | bytes 294920 | tf_op jit(solution)/shard_map/ppermute | solution.py:191
  121.6 1.5 %convolution_convert_fusion = bf16[128,1024]{1,0:T(8,128)(2,1)} fusion(bf16[1024,128]{1,0:T(8,128)(2,1)S(1)} %bitcast.128, bf16[1024,1024]{1,0:T(8,128)(2,1)S(1)} %copy-done), kind=kOutput, calls=%fused_computation.2 | convolution fusion | flops 268566528 | bytes 2621440 | tf_op jit(solution)/shard_map/dot_general | solution.py:20
  123.2 1.9 %collective-permute-start.20 = (bf16[96,512]{1,0:T(8,128)(2,1)S(1)}, bf16[96,512]{1,0:T(8,128)(2,1)S(1)}, u32[]{:S(2)}, u32[]{:S(2)}) collective-permute-start(bf16[96,512]{1,0:T(8,128)(2,1)S(1)} %copy-done.12), channel_id=1, source_target_pairs={{0,24},{4,28},{8,16},{12,20},{16,8},{20,12},{24,0},{28,4},{1,25},{... | collective-permute-start | bytes 294920 | tf_op jit(solution)/shard_map/ppermute | solution.py:191
  125.1 0.9 bitcast_dynamic-update-slice_fusion.6
  126.0 1.9 %collective-permute-start.35 = (bf16[2,128,256]{2,1,0:T(8,128)(2,1)S(1)}, bf16[2,128,256]{2,1,0:T(8,128)(2,1)S(1)}, u32[]{:S(2)}, u32[]{:S(2)}) collective-permute-start(bf16[2,128,256]{2,1,0:T(8,128)(2,1)S(1)} %get-tuple-element.33), channel_id=1, source_target_pairs={{0,24},{4,28},{8,16},{12,20},{16,8},{20,12},{24,0},{28,4},{1,25},{... | collective-permute-start | bytes 393224 | tf_op jit(solution)/shard_map/ppermute | solution.py:191
  128.1 0.9 bitcast_dynamic-update-slice_fusion.4
  129.0 2.6 %collective-permute-start.33 = (bf16[2,128,256]{2,1,0:T(8,128)(2,1)S(1)}, bf16[2,128,256]{2,1,0:T(8,128)(2,1)S(1)}, u32[]{:S(2)}, u32[]{:S(2)}) collective-permute-start(bf16[2,128,256]{2,1,0:T(8,128)(2,1)S(1)} %get-tuple-element.32), channel_id=1, source_target_pairs={{0,8},{4,12},{8,0},{12,4},{16,24},{20,28},{24,16},{28,20},{1,9},{5... | collective-permute-start | bytes 393224 | tf_op jit(solution)/shard_map/ppermute | solution.py:191
  131.6 3.5 %collective-permute-start.29 = (bf16[384,512]{1,0:T(8,128)(2,1)S(1)}, bf16[384,512]{1,0:T(8,128)(2,1)S(1)}, u32[]{:S(2)}, u32[]{:S(2)}) collective-permute-start(bf16[384,512]{1,0:T(8,128)(2,1)S(1)} %bitcast.119), channel_id=1, source_target_pairs={{0,4},{4,0},{8,12},{12,8},{16,20},{20,16},{24,28},{28,24},{1,5},{5... | collective-permute-start | bytes 1179656 | tf_op jit(solution)/shard_map/ppermute | solution.py:191
  135.3 6.8 %collective-permute-done.34 = bf16[2,128,256]{2,1,0:T(8,128)(2,1)S(1)} collective-permute-done((bf16[2,128,256]{2,1,0:T(8,128)(2,1)S(1)}, bf16[2,128,256]{2,1,0:T(8,128)(2,1)S(1)}, u32[]{:S(2)}, u32[]{:S(2)}) %collective-permute-start.34) | collective-permute-done | bytes 131104 | tf_op jit(solution)/shard_map/ppermute | solution.py:191
  142.1 1.0 fusion.9
  143.1 1.3 collective-permute-start.36
  144.5 6.5 %collective-permute-done.36 = bf16[128,256]{1,0:T(8,128)(2,1)S(1)} collective-permute-done((bf16[128,256]{1,0:T(8,128)(2,1)S(1)}, bf16[128,256]{1,0:T(8,128)(2,1)S(1)}, u32[]{:S(2)}, u32[]{:S(2)}) %collective-permute-start.36) | collective-permute-done | bytes 65568 | tf_op jit(solution)/shard_map/ppermute | solution.py:191
  151.1 0.7 convert_add_fusion.7
  152.0 1.3 fusion.2
  (113 shorter events, 4.8 us)
Async XLA Ops:
  0.6 121.0 %copy-start = (bf16[1024,1024]{1,0:T(8,128)(2,1)S(1)}, bf16[1024,1024]{1,0:T(8,128)(2,1)}, u32[]{:S(2)}) copy-start(bf16[1024,1024]{1,0:T(8,128)(2,1)} %param.13) | copy-start | bytes 6291460
  0.6 9.6 %collective-permute-start.1 = (bf16[128,1024]{1,0:T(8,128)(2,1)}, bf16[128,1024]{1,0:T(8,128)(2,1)S(1)}, u32[]{:S(2)}, u32[]{:S(2)}) collective-permute-start(bf16[128,1024]{1,0:T(8,128)(2,1)} %refs_0_.6), channel_id=1, source_target_pairs={{0,2},{1,3},{2,0},{3,1},{4,6},{5,7},{6,4},{7,5},{8,10},{9,11},{10,... | collective-permute-start | bytes 786440 | tf_op jit(solution)/shard_map/ppermute | solution.py:191
  3.7 10.1 %collective-permute-start = (bf16[128,1024]{1,0:T(8,128)(2,1)}, bf16[128,1024]{1,0:T(8,128)(2,1)S(1)}, u32[]{:S(2)}, u32[]{:S(2)}) collective-permute-start(bf16[128,1024]{1,0:T(8,128)(2,1)} %refs_0_.6), channel_id=1, source_target_pairs={{0,1},{1,0},{2,3},{3,2},{4,5},{5,4},{6,7},{7,6},{8,9},{9,8},{10,11... | collective-permute-start | bytes 786440 | tf_op jit(solution)/shard_map/ppermute | solution.py:191
  10.2 11.5 %copy-start.3 = (bf16[128,1024]{1,0:T(8,128)(2,1)}, bf16[128,1024]{1,0:T(8,128)(2,1)S(1)}, u32[]{:S(2)}) copy-start(bf16[128,1024]{1,0:T(8,128)(2,1)S(1)} %collective-permute-done.1.refs_0_.refs_2_) | copy-start | bytes 786436
  10.2 12.3 %collective-permute-start.2 = (bf16[128,1024]{1,0:T(8,128)(2,1)S(1)}, bf16[128,1024]{1,0:T(8,128)(2,1)S(1)}, u32[]{:S(2)}, u32[]{:S(2)}) collective-permute-start(bf16[128,1024]{1,0:T(8,128)(2,1)S(1)} %collective-permute-done.1.refs_0_.refs_2_), channel_id=1, source_target_pairs={{0,1},{1,0},{2,3},{3,2},{4,5},{5,4},{6,7},{7,6},{8,9},{9,8},{10,11... | collective-permute-start | bytes 786440 | tf_op jit(solution)/shard_map/ppermute | solution.py:191
  10.2 23.0 %collective-permute-start.4 = (bf16[128,1024]{1,0:T(8,128)(2,1)}, bf16[128,1024]{1,0:T(8,128)(2,1)S(1)}, u32[]{:S(2)}, u32[]{:S(2)}) collective-permute-start(bf16[128,1024]{1,0:T(8,128)(2,1)} %refs_4_.3), channel_id=1, source_target_pairs={{0,2},{1,3},{2,0},{3,1},{4,6},{5,7},{6,4},{7,5},{8,10},{9,11},{10,... | collective-permute-start | bytes 786440 | tf_op jit(solution)/shard_map/ppermute | solution.py:191
  13.8 0.7 copy-start.4
  21.7 8.8 %copy-start.11 = (f32[8,2,128]{2,1,0:T(2,128)S(1)}, f32[8,2,128]{2,1,0:T(2,128)}, u32[]{:S(2)}) copy-start(f32[8,2,128]{2,1,0:T(2,128)} %shard_map.104) | copy-start | bytes 24580
  21.7 8.8 %copy-start.13 = (f32[8,2,256]{2,1,0:T(2,128)S(1)}, f32[8,2,256]{2,1,0:T(2,128)}, u32[]{:S(2)}) copy-start(f32[8,2,256]{2,1,0:T(2,128)} %get-tuple-element.18) | copy-start | bytes 49156
  22.5 10.7 %copy-start.1 = (bf16[128,1024]{1,0:T(8,128)(2,1)S(1)}, bf16[128,1024]{1,0:T(8,128)(2,1)}, u32[]{:S(2)}) copy-start(bf16[128,1024]{1,0:T(8,128)(2,1)} %refs_4_.3) | copy-start | bytes 786436
  22.5 0.7 copy-start.5
  30.5 7.6 %copy-start.14 = (f32[8,2,256]{2,1,0:T(2,128)S(1)}, f32[8,2,256]{2,1,0:T(2,128)}, u32[]{:S(2)}) copy-start(f32[8,2,256]{2,1,0:T(2,128)} %get-tuple-element.16) | copy-start | bytes 49156
  30.5 7.6 %copy-start.15 = (f32[8,2,256]{2,1,0:T(2,128)S(1)}, f32[8,2,256]{2,1,0:T(2,128)}, u32[]{:S(2)}) copy-start(f32[8,2,256]{2,1,0:T(2,128)} %get-tuple-element.17) | copy-start | bytes 49156
  31.3 1.3 collective-permute-start.6
  32.9 4.9 %collective-permute-start.7 = (f32[8,2,768]{2,1,0:T(2,128)S(1)}, f32[8,2,768]{2,1,0:T(2,128)S(1)}, u32[]{:S(2)}, u32[]{:S(2)}) collective-permute-start(f32[8,2,768]{2,1,0:T(2,128)S(1)} %pad_maximum_fusion.1), channel_id=1, source_target_pairs={{0,2},{1,3},{2,0},{3,1},{4,6},{5,7},{6,4},{7,5},{8,10},{9,11},{10,... | collective-permute-start | bytes 147464 | tf_op jit(solution)/shard_map/ppermute | solution.py:191
  33.2 5.6 %collective-permute-start.3 = (bf16[128,1024]{1,0:T(8,128)(2,1)S(1)}, bf16[128,1024]{1,0:T(8,128)(2,1)S(1)}, u32[]{:S(2)}, u32[]{:S(2)}) collective-permute-start(bf16[128,1024]{1,0:T(8,128)(2,1)S(1)} %copy-done.1), channel_id=1, source_target_pairs={{0,1},{1,0},{2,3},{3,2},{4,5},{5,4},{6,7},{7,6},{8,9},{9,8},{10,11... | collective-permute-start | bytes 786440 | tf_op jit(solution)/shard_map/ppermute | solution.py:191
  33.2 5.6 %copy-start.6 = (bf16[128,1024]{1,0:T(8,128)(2,1)}, bf16[128,1024]{1,0:T(8,128)(2,1)S(1)}, u32[]{:S(2)}) copy-start(bf16[128,1024]{1,0:T(8,128)(2,1)S(1)} %collective-permute-done.4.refs_6_) | copy-start | bytes 786436
  33.3 5.5 %collective-permute-start.5 = (bf16[128,1024]{1,0:T(8,128)(2,1)S(1)}, bf16[128,1024]{1,0:T(8,128)(2,1)S(1)}, u32[]{:S(2)}, u32[]{:S(2)}) collective-permute-start(bf16[128,1024]{1,0:T(8,128)(2,1)S(1)} %collective-permute-done.4.refs_6_), channel_id=1, source_target_pairs={{0,1},{1,0},{2,3},{3,2},{4,5},{5,4},{6,7},{7,6},{8,9},{9,8},{10,11... | collective-permute-start | bytes 786440 | tf_op jit(solution)/shard_map/ppermute | solution.py:191
  33.8 56.5 %collective-permute-start.31 = (bf16[128,1024]{1,0:T(8,128)(2,1)}, bf16[128,1024]{1,0:T(8,128)(2,1)}, u32[]{:S(2)}, u32[]{:S(2)}) collective-permute-start(bf16[128,1024]{1,0:T(8,128)(2,1)} %refs_0_.7), channel_id=1, source_target_pairs={{0,2},{1,3},{2,0},{3,1},{4,6},{5,7},{6,4},{7,5},{8,10},{9,11},{10,... | collective-permute-start | bytes 786440 | tf_op jit(solution)/shard_map/ppermute | solution.py:191
  38.8 0.7 copy-start.7
  38.8 0.8 copy-start.8
  48.2 15.3 %collective-permute-start.9 = (bf16[1,256,512]{2,1,0:T(8,128)(2,1)S(1)}, bf16[1,256,512]{2,1,0:T(8,128)(2,1)S(1)}, u32[]{:S(2)}, u32[]{:S(2)}) collective-permute-start(bf16[1,256,512]{2,1,0:T(8,128)(2,1)S(1)} %dynamic-slice_bitcast_fusion.2), channel_id=1, source_target_pairs={{0,1},{1,0},{2,3},{3,2},{4,5},{5,4},{6,7},{7,6},{8,9},{9,8},{10,11... | collective-permute-start | bytes 786440 | tf_op jit(solution)/shard_map/ppermute | solution.py:191
  50.1 18.6 %collective-permute-start.22 = (bf16[384,512]{1,0:T(8,128)(2,1)}, bf16[384,512]{1,0:T(8,128)(2,1)}, u32[]{:S(2)}, u32[]{:S(2)}) collective-permute-start(bf16[384,512]{1,0:T(8,128)(2,1)} %dynamic-slice_bitcast_fusion), channel_id=1, source_target_pairs={{0,4},{4,0},{8,12},{12,8},{16,20},{20,16},{24,28},{28,24},{1,5},{5... | collective-permute-start | bytes 1179656 | tf_op jit(solution)/shard_map/ppermute | solution.py:191
  59.3 5.8 %copy-start.10 = (bf16[512,512]{1,0:T(8,128)(2,1)S(1)}, bf16[512,512]{1,0:T(8,128)(2,1)}, u32[]{:S(2)}) copy-start(bf16[512,512]{1,0:T(8,128)(2,1)} %get-tuple-element.21) | copy-start | bytes 1572868
  61.0 5.2 %collective-permute-start.8 = (bf16[1,256,512]{2,1,0:T(8,128)(2,1)}, bf16[1,256,512]{2,1,0:T(8,128)(2,1)}, u32[]{:S(2)}, u32[]{:S(2)}) collective-permute-start(bf16[1,256,512]{2,1,0:T(8,128)(2,1)} %dynamic-slice_bitcast_fusion.3), channel_id=1, source_target_pairs={{0,1},{1,0},{2,3},{3,2},{4,5},{5,4},{6,7},{7,6},{8,9},{9,8},{10,11... | collective-permute-start | bytes 786440 | tf_op jit(solution)/shard_map/ppermute | solution.py:191
  63.0 11.6 %collective-permute-start.14 = (bf16[384,512]{1,0:T(8,128)(2,1)}, bf16[384,512]{1,0:T(8,128)(2,1)}, u32[]{:S(2)}, u32[]{:S(2)}) collective-permute-start(bf16[384,512]{1,0:T(8,128)(2,1)} %dynamic-slice_bitcast_fusion.1), channel_id=1, source_target_pairs={{0,4},{4,0},{8,12},{12,8},{16,20},{20,16},{24,28},{28,24},{1,5},{5... | collective-permute-start | bytes 1179656 | tf_op jit(solution)/shard_map/ppermute | solution.py:191
  65.9 30.0 %collective-permute-start.10 = (bf16[256,512]{1,0:T(8,128)(2,1)}, bf16[256,512]{1,0:T(8,128)(2,1)}, u32[]{:S(2)}, u32[]{:S(2)}) collective-permute-start(bf16[256,512]{1,0:T(8,128)(2,1)} %fusion.5), channel_id=1, source_target_pairs={{0,2},{1,3},{2,0},{3,1},{4,6},{5,7},{6,4},{7,5},{8,10},{9,11},{10,... | collective-permute-start | bytes 786440 | tf_op jit(solution)/shard_map/ppermute | solution.py:191
  68.7 7.5 %copy-start.9 = (bf16[2,384,512]{2,1,0:T(8,128)(2,1)S(1)}, bf16[2,384,512]{2,1,0:T(8,128)(2,1)}, u32[]{:S(2)}) copy-start(bf16[2,384,512]{2,1,0:T(8,128)(2,1)} %get-tuple-element.22) | copy-start | bytes 2359300
  70.0 7.4 %collective-permute-start.25 = (bf16[96,512]{1,0:T(8,128)(2,1)S(1)}, bf16[96,512]{1,0:T(8,128)(2,1)S(1)}, u32[]{:S(2)}, u32[]{:S(2)}) collective-permute-start(bf16[96,512]{1,0:T(8,128)(2,1)S(1)} %get-tuple-element.36), channel_id=1, source_target_pairs={{0,24},{4,28},{8,16},{12,20},{16,8},{20,12},{24,0},{28,4},{1,25},{... | collective-permute-start | bytes 294920 | tf_op jit(solution)/shard_map/ppermute | solution.py:191
  73.9 12.1 %collective-permute-start.24 = (bf16[96,512]{1,0:T(8,128)(2,1)S(1)}, bf16[96,512]{1,0:T(8,128)(2,1)S(1)}, u32[]{:S(2)}, u32[]{:S(2)}) collective-permute-start(bf16[96,512]{1,0:T(8,128)(2,1)S(1)} %get-tuple-element.37), channel_id=1, source_target_pairs={{0,16},{4,20},{8,24},{12,28},{16,0},{20,4},{24,8},{28,12},{1,17},{... | collective-permute-start | bytes 294920 | tf_op jit(solution)/shard_map/ppermute | solution.py:191
  74.6 11.4 %collective-permute-start.23 = (bf16[96,512]{1,0:T(8,128)(2,1)S(1)}, bf16[96,512]{1,0:T(8,128)(2,1)S(1)}, u32[]{:S(2)}, u32[]{:S(2)}) collective-permute-start(bf16[96,512]{1,0:T(8,128)(2,1)S(1)} %get-tuple-element.35), channel_id=1, source_target_pairs={{0,8},{4,12},{8,0},{12,4},{16,24},{20,28},{24,16},{28,20},{1,9},{5... | collective-permute-start | bytes 294920 | tf_op jit(solution)/shard_map/ppermute | solution.py:191
  77.5 12.8 %collective-permute-start.17 = (bf16[96,512]{1,0:T(8,128)(2,1)S(1)}, bf16[96,512]{1,0:T(8,128)(2,1)S(1)}, u32[]{:S(2)}, u32[]{:S(2)}) collective-permute-start(bf16[96,512]{1,0:T(8,128)(2,1)S(1)} %get-tuple-element.39), channel_id=1, source_target_pairs={{0,24},{4,28},{8,16},{12,20},{16,8},{20,12},{24,0},{28,4},{1,25},{... | collective-permute-start | bytes 294920 | tf_op jit(solution)/shard_map/ppermute | solution.py:191
  86.0 6.7 %collective-permute-start.16 = (bf16[96,512]{1,0:T(8,128)(2,1)S(1)}, bf16[96,512]{1,0:T(8,128)(2,1)S(1)}, u32[]{:S(2)}, u32[]{:S(2)}) collective-permute-start(bf16[96,512]{1,0:T(8,128)(2,1)S(1)} %get-tuple-element.40), channel_id=1, source_target_pairs={{0,16},{4,20},{8,24},{12,28},{16,0},{20,4},{24,8},{28,12},{1,17},{... | collective-permute-start | bytes 294920 | tf_op jit(solution)/shard_map/ppermute | solution.py:191
  86.0 7.0 %collective-permute-start.15 = (bf16[96,512]{1,0:T(8,128)(2,1)S(1)}, bf16[96,512]{1,0:T(8,128)(2,1)S(1)}, u32[]{:S(2)}, u32[]{:S(2)}) collective-permute-start(bf16[96,512]{1,0:T(8,128)(2,1)S(1)} %get-tuple-element.38), channel_id=1, source_target_pairs={{0,8},{4,12},{8,0},{12,4},{16,24},{20,28},{24,16},{28,20},{1,9},{5... | collective-permute-start | bytes 294920 | tf_op jit(solution)/shard_map/ppermute | solution.py:191
  90.2 14.9 %collective-permute-start.30 = (bf16[128,1024]{1,0:T(8,128)(2,1)}, bf16[128,1024]{1,0:T(8,128)(2,1)}, u32[]{:S(2)}, u32[]{:S(2)}) collective-permute-start(bf16[128,1024]{1,0:T(8,128)(2,1)} %refs_0_.7), channel_id=1, source_target_pairs={{0,1},{1,0},{2,3},{3,2},{4,5},{5,4},{6,7},{7,6},{8,9},{9,8},{10,11... | collective-permute-start | bytes 786440 | tf_op jit(solution)/shard_map/ppermute | solution.py:191
  90.2 15.0 %collective-permute-start.32 = (bf16[128,1024]{1,0:T(8,128)(2,1)}, bf16[128,1024]{1,0:T(8,128)(2,1)}, u32[]{:S(2)}, u32[]{:S(2)}) collective-permute-start(bf16[128,1024]{1,0:T(8,128)(2,1)} %collective-permute-done.31.refs_2_), channel_id=1, source_target_pairs={{0,1},{1,0},{2,3},{3,2},{4,5},{5,4},{6,7},{7,6},{8,9},{9,8},{10,11... | collective-permute-start | bytes 786440 | tf_op jit(solution)/shard_map/ppermute | solution.py:191
  92.7 30.5 %collective-permute-start.26 = (bf16[96,512]{1,0:T(8,128)(2,1)}, bf16[96,512]{1,0:T(8,128)(2,1)}, u32[]{:S(2)}, u32[]{:S(2)}) collective-permute-start(bf16[96,512]{1,0:T(8,128)(2,1)} %get-tuple-element.25), channel_id=1, source_target_pairs={{0,8},{4,12},{8,0},{12,4},{16,24},{20,28},{24,16},{28,20},{1,9},{5... | collective-permute-start | bytes 294920 | tf_op jit(solution)/shard_map/ppermute | solution.py:191
  93.0 33.0 %collective-permute-start.27 = (bf16[96,512]{1,0:T(8,128)(2,1)}, bf16[96,512]{1,0:T(8,128)(2,1)S(1)}, u32[]{:S(2)}, u32[]{:S(2)}) collective-permute-start(bf16[96,512]{1,0:T(8,128)(2,1)} %get-tuple-element.25), channel_id=1, source_target_pairs={{0,16},{4,20},{8,24},{12,28},{16,0},{20,4},{24,8},{28,12},{1,17},{... | collective-permute-start | bytes 294920 | tf_op jit(solution)/shard_map/ppermute | solution.py:191
  95.9 32.1 %collective-permute-start.28 = (bf16[96,512]{1,0:T(8,128)(2,1)}, bf16[96,512]{1,0:T(8,128)(2,1)}, u32[]{:S(2)}, u32[]{:S(2)}) collective-permute-start(bf16[96,512]{1,0:T(8,128)(2,1)} %get-tuple-element.25), channel_id=1, source_target_pairs={{0,24},{4,28},{8,16},{12,20},{16,8},{20,12},{24,0},{28,4},{1,25},{... | collective-permute-start | bytes 294920 | tf_op jit(solution)/shard_map/ppermute | solution.py:191
  102.9 2.3 %copy-start.12 = (bf16[96,512]{1,0:T(8,128)(2,1)S(1)}, bf16[96,512]{1,0:T(8,128)(2,1)}, u32[]{:S(2)}) copy-start(bf16[96,512]{1,0:T(8,128)(2,1)} %get-tuple-element.27) | copy-start | bytes 294916
  105.0 0.7 copy-start.2
  105.2 23.8 %collective-permute-start.18 = (bf16[96,512]{1,0:T(8,128)(2,1)S(1)}, bf16[96,512]{1,0:T(8,128)(2,1)S(1)}, u32[]{:S(2)}, u32[]{:S(2)}) collective-permute-start(bf16[96,512]{1,0:T(8,128)(2,1)S(1)} %copy-done.12), channel_id=1, source_target_pairs={{0,8},{4,12},{8,0},{12,4},{16,24},{20,28},{24,16},{28,20},{1,9},{5... | collective-permute-start | bytes 294920 | tf_op jit(solution)/shard_map/ppermute | solution.py:191
  105.3 5.5 %collective-permute-start.11 = (bf16[256,128]{1,0:T(8,128)(2,1)S(1)}, bf16[256,128]{1,0:T(8,128)(2,1)S(1)}, u32[]{:S(2)}, u32[]{:S(2)}) collective-permute-start(bf16[256,128]{1,0:T(8,128)(2,1)S(1)} %get-tuple-element.43), channel_id=1, source_target_pairs={{0,1},{1,0},{2,3},{3,2},{4,5},{5,4},{6,7},{7,6},{8,9},{9,8},{10,11... | collective-permute-start | bytes 196616 | tf_op jit(solution)/shard_map/ppermute | solution.py:191
  110.8 4.3 %collective-permute-start.12 = (bf16[256,128]{1,0:T(8,128)(2,1)S(1)}, bf16[256,128]{1,0:T(8,128)(2,1)S(1)}, u32[]{:S(2)}, u32[]{:S(2)}) collective-permute-start(bf16[256,128]{1,0:T(8,128)(2,1)S(1)} %get-tuple-element.42), channel_id=1, source_target_pairs={{0,2},{1,3},{2,0},{3,1},{4,6},{5,7},{6,4},{7,5},{8,10},{9,11},{10,... | collective-permute-start | bytes 196616 | tf_op jit(solution)/shard_map/ppermute | solution.py:191
  115.1 3.7 %collective-permute-start.13 = (bf16[256,128]{1,0:T(8,128)(2,1)S(1)}, bf16[256,128]{1,0:T(8,128)(2,1)S(1)}, u32[]{:S(2)}, u32[]{:S(2)}) collective-permute-start(bf16[256,128]{1,0:T(8,128)(2,1)S(1)} %get-tuple-element.41), channel_id=1, source_target_pairs={{0,3},{1,2},{2,1},{3,0},{4,7},{5,6},{6,5},{7,4},{8,11},{9,10},{10,... | collective-permute-start | bytes 196616 | tf_op jit(solution)/shard_map/ppermute | solution.py:191
  118.8 12.8 %collective-permute-start.19 = (bf16[96,512]{1,0:T(8,128)(2,1)S(1)}, bf16[96,512]{1,0:T(8,128)(2,1)S(1)}, u32[]{:S(2)}, u32[]{:S(2)}) collective-permute-start(bf16[96,512]{1,0:T(8,128)(2,1)S(1)} %copy-done.12), channel_id=1, source_target_pairs={{0,16},{4,20},{8,24},{12,28},{16,0},{20,4},{24,8},{28,12},{1,17},{... | collective-permute-start | bytes 294920 | tf_op jit(solution)/shard_map/ppermute | solution.py:191
  123.2 11.9 %collective-permute-start.20 = (bf16[96,512]{1,0:T(8,128)(2,1)S(1)}, bf16[96,512]{1,0:T(8,128)(2,1)S(1)}, u32[]{:S(2)}, u32[]{:S(2)}) collective-permute-start(bf16[96,512]{1,0:T(8,128)(2,1)S(1)} %copy-done.12), channel_id=1, source_target_pairs={{0,24},{4,28},{8,16},{12,20},{16,8},{20,12},{24,0},{28,4},{1,25},{... | collective-permute-start | bytes 294920 | tf_op jit(solution)/shard_map/ppermute | solution.py:191
  126.0 9.3 %collective-permute-start.35 = (bf16[2,128,256]{2,1,0:T(8,128)(2,1)S(1)}, bf16[2,128,256]{2,1,0:T(8,128)(2,1)S(1)}, u32[]{:S(2)}, u32[]{:S(2)}) collective-permute-start(bf16[2,128,256]{2,1,0:T(8,128)(2,1)S(1)} %get-tuple-element.33), channel_id=1, source_target_pairs={{0,24},{4,28},{8,16},{12,20},{16,8},{20,12},{24,0},{28,4},{1,25},{... | collective-permute-start | bytes 393224 | tf_op jit(solution)/shard_map/ppermute | solution.py:191
  128.0 14.1 %collective-permute-start.34 = (bf16[2,128,256]{2,1,0:T(8,128)(2,1)S(1)}, bf16[2,128,256]{2,1,0:T(8,128)(2,1)S(1)}, u32[]{:S(2)}, u32[]{:S(2)}) collective-permute-start(bf16[2,128,256]{2,1,0:T(8,128)(2,1)S(1)} %get-tuple-element.34), channel_id=1, source_target_pairs={{0,16},{4,20},{8,24},{12,28},{16,0},{20,4},{24,8},{28,12},{1,17},{... | collective-permute-start | bytes 393224 | tf_op jit(solution)/shard_map/ppermute | solution.py:191
  129.0 13.1 %collective-permute-start.33 = (bf16[2,128,256]{2,1,0:T(8,128)(2,1)S(1)}, bf16[2,128,256]{2,1,0:T(8,128)(2,1)S(1)}, u32[]{:S(2)}, u32[]{:S(2)}) collective-permute-start(bf16[2,128,256]{2,1,0:T(8,128)(2,1)S(1)} %get-tuple-element.32), channel_id=1, source_target_pairs={{0,8},{4,12},{8,0},{12,4},{16,24},{20,28},{24,16},{28,20},{1,9},{5... | collective-permute-start | bytes 393224 | tf_op jit(solution)/shard_map/ppermute | solution.py:191
  131.6 20.2 %collective-permute-start.29 = (bf16[384,512]{1,0:T(8,128)(2,1)S(1)}, bf16[384,512]{1,0:T(8,128)(2,1)S(1)}, u32[]{:S(2)}, u32[]{:S(2)}) collective-permute-start(bf16[384,512]{1,0:T(8,128)(2,1)S(1)} %bitcast.119), channel_id=1, source_target_pairs={{0,4},{4,0},{8,12},{12,8},{16,20},{20,16},{24,28},{28,24},{1,5},{5... | collective-permute-start | bytes 1179656 | tf_op jit(solution)/shard_map/ppermute | solution.py:191
  135.1 16.7 %collective-permute-start.21 = (bf16[384,512]{1,0:T(8,128)(2,1)S(1)}, bf16[384,512]{1,0:T(8,128)(2,1)S(1)}, u32[]{:S(2)}, u32[]{:S(2)}) collective-permute-start(bf16[384,512]{1,0:T(8,128)(2,1)S(1)} %bitcast.121), channel_id=1, source_target_pairs={{0,4},{4,0},{8,12},{12,8},{16,20},{20,16},{24,28},{28,24},{1,5},{5... | collective-permute-start | bytes 1179656 | tf_op jit(solution)/shard_map/ppermute | solution.py:191
  143.1 8.0 %collective-permute-start.36 = (bf16[128,256]{1,0:T(8,128)(2,1)S(1)}, bf16[128,256]{1,0:T(8,128)(2,1)S(1)}, u32[]{:S(2)}, u32[]{:S(2)}) collective-permute-start(bf16[128,256]{1,0:T(8,128)(2,1)S(1)} %dynamic-slice_bitcast_fusion.13), channel_id=1, source_target_pairs={{0,4},{4,0},{8,12},{12,8},{16,20},{20,16},{24,28},{28,24},{1,5},{5... | collective-permute-start | bytes 196616 | tf_op jit(solution)/shard_map/ppermute | solution.py:191

commit v2 on v1

--- a/solution.py
+++ b/solution.py
@@ -309,20 +309,467 @@
     return (grad_input, both[0], both[1], grad_weight)
 
 
+def params(limit=24):
+    return pltpu.CompilerParams(vmem_limit_bytes=limit * 1024 * 1024)
+
+
+def cost(flops, nbytes, exps=0):
+    return pl.CostEstimate(flops=flops, bytes_accessed=nbytes, transcendentals=exps)
+
+
+def like(shape, dtype=BF):
+    return jax.ShapeDtypeStruct(shape, dtype)
+
+
+SMEM = pl.BlockSpec(memory_space=pltpu.SMEM)
+VMEM = pl.BlockSpec(memory_space=pltpu.VMEM)
+
+
+def span(i, size=PAIR):
+    return slice(i * size, (i + 1) * size)
+
+
+def flip_core(x):
+    n = x.shape[-1] // PAIR
+    return jnp.concatenate([x[..., span(i ^ 1)] for i in range(n)], axis=-1)
+
+
+def pack_kernel(at_ref, q_ref, g_ref, o_ref, qk_ref, qs_ref, gk_ref, gs_ref, dk_ref, ds_ref):
+    low = at_ref[0] == 0
+    pairs = qk_ref.shape[1] // PAIR
+    for ref, keep, send, scale in ((q_ref, qk_ref, qs_ref, SCALE), (g_ref, gk_ref, gs_ref, 1.0)):
+        for p in range(pairs):
+            a, b = ref[:, span(2 * p)], ref[:, span(2 * p + 1)]
+            if scale != 1.0:
+                a, b = a * jnp.asarray(scale, BF), b * jnp.asarray(scale, BF)
+            keep[:, span(p)] = jnp.where(low, a, b)
+            send[:, span(p)] = jnp.where(low, b, a)
+    cols = (g_ref[...].astype(F32) * o_ref[...].astype(F32)).T
+    for p in range(pairs):
+        for h in range(2):
+            a = jnp.sum(cols[span(4 * p + h, HD)], axis=0)
+            b = jnp.sum(cols[span(4 * p + 2 + h, HD)], axis=0)
+            dk_ref[p, h] = jnp.where(low, a, b)
+            ds_ref[p, h] = jnp.where(low, b, a)
+
+
+def pack(at, queries, grad_out, attn_out):
+    rows, cols = queries.shape
+    half, stat = like((rows, cols // 2)), like((cols // PAIR // 2, 2, rows), F32)
+    return pl.pallas_call(
+        pack_kernel,
+        in_specs=[SMEM] + [VMEM] * 3,
+        out_specs=[VMEM] * 6,
+        out_shape=[half] * 4 + [stat] * 2,
+        compiler_params=params(),
+        cost_estimate=cost(4 * rows * cols, 10 * rows * cols),
+    )(at, queries, grad_out, attn_out)
+
+
+def pack_tokens_kernel(at_ref, k_ref, v_ref, kp_ref, vp_ref, kt_ref):
+    low = at_ref[0] == 0
+    for p in range(kp_ref.shape[1] // PAIR):
+        k = jnp.where(low, k_ref[:, span(2 * p)], k_ref[:, span(2 * p + 1)])
+        kp_ref[:, span(p)] = k
+        kt_ref[span(p)] = k.T
+        vp_ref[:, span(p)] = jnp.where(low, v_ref[:, span(2 * p)], v_ref[:, span(2 * p + 1)])
+
+
+def pack_tokens(at, keys, values):
+    tokens, cols = keys.shape
+    return pl.pallas_call(
+        pack_tokens_kernel,
+        in_specs=[SMEM, VMEM, VMEM],
+        out_specs=[VMEM] * 3,
+        out_shape=[like((tokens, cols // 2))] * 2 + [like((cols // 2, tokens))],
+        compiler_params=params(),
+        cost_estimate=cost(tokens * cols, 7 * tokens * cols),
+    )(at, keys, values)
+
+
+def side_kernel(count, step, last, *refs):
+    q_refs, k_ref = refs[:count], refs[count]
+    if last:
+        la_ref, own_ref, got_ref, p_ref, m_ref, lse_ref, send_ref = refs[count + 1 :]
+    else:
+        p_ref, m_ref, lse_ref = refs[count + 1 :]
+    for j in range(step):
+        q = jnp.concatenate([r[:, span(j)] for r in q_refs], axis=0)
+        k = k_ref[:, span(j)]
+        for head in range(2):
+            s = dot(own_lanes(k, head), q, 1, 1)
+            top = jnp.max(s, axis=0, keepdims=True)
+            p = jnp.exp(s - top)
+            total = jnp.sum(p, axis=0, keepdims=True)
+            p_ref[2 * j + head] = p.astype(BF)
+            m_ref[j, head] = top[0]
+            lse_ref[j, head] = (top + jnp.log(total))[0]
+    if last:
+        send_ref[...] = jnp.concatenate(
+            [flip_core(la_ref[...]), flip_core(lse_ref[...]), own_ref[...], got_ref[...]], axis=-1
+        )
+
+
+def side_of(pieces, keys, extra=None, step=2):
+    count = len(pieces)
+    piece, cols = pieces[0].shape
+    tokens = keys.shape[0]
+    rows, pairs = piece * count, cols // PAIR
+    stat_spec = lambda n: pl.BlockSpec((step, 2, n), lambda i: (i, 0, 0))
+    in_specs = [pl.BlockSpec((piece, step * PAIR), lambda i: (0, i))] * count
+    in_specs += [pl.BlockSpec((tokens, step * PAIR), lambda i: (0, i))]
+    out_specs = [pl.BlockSpec((2 * step, tokens, rows), lambda i: (i, 0, 0)), stat_spec(rows), stat_spec(rows)]
+    out_shape = [like((2 * pairs, tokens, rows)), like((pairs, 2, rows), F32), like((pairs, 2, rows), F32)]
+    args = [*pieces, keys]
+    if extra is not None:
+        in_specs += [stat_spec(rows), stat_spec(piece), stat_spec(piece)]
+        out_specs += [stat_spec(2 * rows + 2 * piece)]
+        out_shape += [like((pairs, 2, 2 * rows + 2 * piece), F32)]
+        args += extra
+    return pl.pallas_call(
+        functools.partial(side_kernel, count, step, extra is not None),
+        grid=(pairs // step,),
+        in_specs=in_specs,
+        out_specs=out_specs,
+        out_shape=out_shape,
+        compiler_params=params(),
+        cost_estimate=cost(2 * rows * tokens * cols, 4 * rows * tokens * pairs, 2 * rows * tokens * pairs),
+    )(*args)
+
+
+def log_add(a, b):
+    top = jnp.maximum(a, b)
+    return top + jnp.log(jnp.exp(a - top) + jnp.exp(b - top))
+
+
+def merge_kernel(la_ref, lb_ref, sent_ref, got_ref, send_ref):
+    side = la_ref.shape[2]
+    lb = log_add(lb_ref[...], got_ref[:, :, side : 2 * side])
+    la = log_add(la_ref[...], got_ref[:, :, :side])
+    own, other = sent_ref[:, :, 2 * side :], got_ref[:, :, 2 * side :]
+    deltas = [own[..., span(0)], other[..., span(0)], own[..., span(1)], other[..., span(1)]]
+    send_ref[...] = jnp.concatenate([lb, la] + deltas, axis=-1)
+
+
+def merge(la, lb, sent, got):
+    pairs, two, side = la.shape
+    return pl.pallas_call(
+        merge_kernel,
+        in_specs=[VMEM] * 4,
+        out_specs=VMEM,
+        out_shape=like((pairs, two, 3 * side), F32),
+        compiler_params=params(),
+        cost_estimate=cost(1000, 100000),
+    )(la, lb, sent, got)
+
+
+def half_kernel(count, at_ref, *refs):
+    q_refs, g_refs = refs[:count], refs[count : 2 * count]
+    pa_ref, pb_ref, v_ref, kt_ref, ma_ref, mb_ref, sent_ref, got_ref = refs[2 * count : 2 * count + 8]
+    kv_refs, dqs_ref, dqk_ref = refs[2 * count + 8 : -2], refs[-2], refs[-1]
+    side = ma_ref.shape[2]
+    z = at_ref[2]
+    v = v_ref[...]
+    tokens = v.shape[0]
+    dk = jnp.zeros((tokens, PAIR), F32)
+    dv = jnp.zeros((tokens, PAIR), F32)
+    first = lax.broadcasted_iota(jnp.int32, (PAIR, side), 0) < HD
+    halves = []
+    for b, p_ref, m_ref in ((0, pa_ref, ma_ref), (1, pb_ref, mb_ref)):
+        lse = log_add(sent_ref[0, :, span(1 - b, side)], got_ref[0, :, span(b, side)])
+        w = jnp.exp(m_ref[0] - lse)
+        delta = (got_ref if b else sent_ref)[0, :, 2 * side :]
+        wide = jnp.where(first, w[0:1], w[1:2]).T
+        at = slice(b * count // 2, (b + 1) * count // 2)
+        q = jnp.concatenate([r[...] for r in q_refs[at]], axis=0)
+        g = jnp.concatenate([r[...] for r in g_refs[at]], axis=0)
+        qw = (q.astype(F32) * wide).astype(BF)
+        gw = (g.astype(F32) * wide).astype(BF)
+        parts = []
+        for head in range(2):
+            p = p_ref[head]
+            dp = dot(v, own_lanes(g, head), 1, 1)
+            t = (p.astype(F32) * (dp - delta[head : head + 1])).astype(BF)
+            dv = dv + dot(p, own_lanes(gw, head), 1, 0)
+            dk = dk + dot(t, own_lanes(qw, head), 1, 0)
+            dq = dot(kt_ref[span(head, HD)], t, 1, 0)
+            parts.append((dq * (w[head : head + 1] * SCALE)).astype(BF))
+        halves.append(jnp.concatenate(parts, axis=0))
+    dq = jnp.concatenate(halves, axis=1)
+
+    @pl.when(pl.program_id(0) == 0)
+    def _():
+        dqs_ref[...] = flip_core(dq)
+
+    @pl.when(pl.program_id(0) == 1)
+    def _():
+        dqk_ref[...] = dq
+
+    both = jnp.concatenate([dk.astype(BF), dv.astype(BF)], axis=0)
+    size = both.shape[0] // len(kv_refs)
+    for k, ref in enumerate(kv_refs):
+        out = both[:size]
+        for j in range(1, len(kv_refs)):
+            out = jnp.where((z ^ k) == j, both[span(j, size)], out)
+        ref[...] = out
+
+
+def half_of(at, high, q_pieces, g_pieces, pa, pb, vp, kt, ma, mb, sent, got):
+    count = len(q_pieces)
+    piece, cols = q_pieces[0].shape
+    tokens = vp.shape[0]
+    side = ma.shape[2]
+    bit = lambda i, a: (i + 1 + a[1]) % 2
+    pair = lambda i, a: 2 * a[0] + bit(i, a)
+    row_spec = pl.BlockSpec((piece, PAIR), lambda i, a: (0, pair(i, a)))
+    p_spec = pl.BlockSpec((2, tokens, side), lambda i, a: (pair(i, a), 0, 0))
+    stat_spec = lambda n: pl.BlockSpec((1, 2, n), lambda i, a: (pair(i, a), 0, 0))
+    block = 2 * tokens // high
+    return pl.pallas_call(
+        functools.partial(half_kernel, count),
+        grid_spec=pltpu.PrefetchScalarGridSpec(
+            num_scalar_prefetch=1,
+            grid=(2,),
+            in_specs=[row_spec] * (2 * count)
+            + [
+                p_spec,
+                p_spec,
+                pl.BlockSpec((tokens, PAIR), lambda i, a: (0, pair(i, a))),
+                pl.BlockSpec((PAIR, tokens), lambda i, a: (pair(i, a), 0)),
+                stat_spec(side),
+                stat_spec(side),
+                stat_spec(3 * side),
+                stat_spec(3 * side),
+            ],
+            out_specs=[pl.BlockSpec((block, PAIR), lambda i, a: (0, bit(i, a)))] * high
+            + [pl.BlockSpec((PAIR, 2 * side), lambda i, a: (0, 0))] * 2,
+        ),
+        out_shape=[like((block, 2 * PAIR))] * high + [like((PAIR, 2 * side))] * 2,
+        compiler_params=params(),
+        cost_estimate=cost(16 * side * tokens * 2 * PAIR * 2, 8 * side * tokens * 2, 0),
+    )(at, *q_pieces, *g_pieces, pa, pb, vp, kt, ma, mb, sent, got)
+
+
+def columns_kernel(count, high, at_ref, *refs):
+    x_refs = refs[:count]
+    keep_ref, core_ref, y_ref = refs[count : count + 3]
+    w_refs, back_ref, send_ref, all_ref = refs[count + 3 : -3], refs[-3], refs[-2], refs[-1]
+    side = keep_ref.shape[1] // 2
+    far = jnp.concatenate([y_ref[:, side:], y_ref[:, :side]], axis=1)
+    dq = (keep_ref[...].astype(F32) + core_ref[...].astype(F32) + far.astype(F32)).astype(BF)
+    quarter = side // 2
+    back_ref[...] = jnp.concatenate([dq[:, span(0, quarter)], dq[:, span(2, quarter)]], axis=1)
+    send_ref[...] = jnp.concatenate([dq[:, span(1, quarter)], dq[:, span(3, quarter)]], axis=1)
+    x = jnp.concatenate([r[...] for r in x_refs], axis=0)
+    all_ref[...] = dot(dq, x, 1, 0)
+    width = x.shape[1] // high
+    for k, ref in enumerate(w_refs):
+        start = pl.multiple_of((at_ref[0] ^ k) * width, PAIR)
+        ref[...] = all_ref[:, pl.ds(start, width)].astype(BF)
+
+
+def columns_of(at, high, x_pieces, keep, core, y):
+    count = len(x_pieces)
+    piece, cols = x_pieces[0].shape
+    width, rows = keep.shape
+    return pl.pallas_call(
+        functools.partial(columns_kernel, count, high),
+        in_specs=[SMEM] + [VMEM] * (count + 3),
+        out_specs=[VMEM] * (high + 2),
+        out_shape=[like((width, cols // high))] * high + [like((width, rows // 2))] * 2,
+        scratch_shapes=[pltpu.VMEM((width, cols), F32)],
+        compiler_params=params(),
+        cost_estimate=cost(2 * rows * cols * width, 2 * rows * cols),
+    )(at, *x_pieces, keep, core, y)
+
+
+def input_kernel(at_ref, back_ref, x_ref, y_ref, core_ref, wq_ref, out_ref, dq_ref):
+    me, x = at_ref[0], at_ref[1]
+    size = back_ref.shape[0]
+
+    def put(group, odd, block):
+        row = pl.multiple_of((2 * group + (x ^ odd)) * size, PAIR)
+        dq_ref[pl.ds(row, size), :] = block
+
+    put(me, 0, back_ref[:, :size])
+    put(me, 1, x_ref[:, :size])
+    for odd in range(2):
+        put(me ^ 2, odd, y_ref[span(odd, size), :size])
+        put(me ^ 1, odd, core_ref[span(odd, size), :])
+        put(me ^ 3, odd, core_ref[span(2 + odd, size), :])
+    out_ref[...] = dot(dq_ref[...], wq_ref[...], 0, 1).astype(BF)
+
+
+def input_of(at, back, x, y, core, wq):
+    size, cols = back.shape[0], wq.shape[1]
+    return pl.pallas_call(
+        input_kernel,
+        in_specs=[SMEM] + [VMEM] * 5,
+        out_specs=VMEM,
+        out_shape=like((size, cols)),
+        scratch_shapes=[pltpu.VMEM((cols, size), BF)],
+        compiler_params=params(),
+        cost_estimate=cost(2 * size * cols * cols, 2 * cols * cols),
+    )(at, back, x, y, core, wq)
+
+
+def weight_sum_kernel(at_ref, *refs):
+    total = refs[0][...].astype(F32)
+    for r in refs[1:-2]:
+        total = total + r[...].astype(F32)
+    keep_ref, send_ref = refs[-2:]
+    size = keep_ref.shape[1]
+    a, b = total[:, :size], total[:, size:]
+    low = at_ref[0] == 0
+    keep_ref[...] = jnp.where(low, a, b)
+    send_ref[...] = jnp.where(low, b, a).astype(BF)
+
+
+def weight_sum(at, parts):
+    rows, cols = parts[0].shape
+    return pl.pallas_call(
+        weight_sum_kernel,
+        in_specs=[SMEM] + [VMEM] * len(parts),
+        out_specs=[VMEM] * 2,
+        out_shape=[like((rows, cols // 2), F32), like((rows, cols // 2))],
+        compiler_params=params(),
+        cost_estimate=cost(1000, 300000),
+    )(at, *parts)
+
+
+def weight_out_kernel(at_ref, keep_ref, got_ref, out_ref):
+    size = keep_ref.shape[0]
+    a, b = keep_ref[...].T, got_ref[...].astype(F32).T
+    low = at_ref[0] == 0
+    out_ref[:, :size] = jnp.where(low, a, b)
+    out_ref[:, size:] = jnp.where(low, b, a)
+
+
+def weight_out(at, keep, got):
+    size, rows = keep.shape
+    return pl.pallas_call(
+        weight_out_kernel,
+        in_specs=[SMEM, VMEM, VMEM],
+        out_specs=VMEM,
+        out_shape=like((rows, 2 * size), F32),
+        compiler_params=params(),
+        cost_estimate=cost(1000, 300000),
+    )(at, keep, got)
+
+
+def tokens_kernel(high, at_ref, *refs):
+    y, x, z = at_ref[0], at_ref[1], at_ref[2]
+    key_ref, val_ref = refs[-2:]
+    size = refs[0].shape[0]
+    each = high + 1
+    for half in range(2):
+        group = 2 * (y ^ (1 - half))
+        own, got = refs[half * each : half * each + high], refs[half * each + high]
+        for k in range(high):
+            b = z ^ k
+            row = pl.multiple_of((b % (high // 2)) * size, 16)
+            for out_ref, which in ((key_ref, 0), (val_ref, 1)):
+
+                @pl.when(b // (high // 2) == which)
+                def _():
+                    for c in range(2):
+                        for odd, block in ((0, own[k][:, span(c)]), (1, got[span(k, size), span(c)])):
+                            col = pl.multiple_of((2 * (group + c) + (x ^ odd)) * PAIR, PAIR)
+                            out_ref[pl.ds(row, size), pl.ds(col, PAIR)] = block
+
+
+def tokens_out(at, high, tokens, cols, parts):
+    return pl.pallas_call(
+        functools.partial(tokens_kernel, high),
+        in_specs=[SMEM] + [VMEM] * len(parts),
+        out_specs=[VMEM] * 2,
+        out_shape=[like((tokens, cols))] * 2,
+        compiler_params=params(),
+        cost_estimate=cost(1000, 8 * tokens * cols),
+    )(at, *parts)
+
+
+def local_split(n_dp, n_seq, qx, queries, keys, values, attn_out, grad_out, wq):
+    high = n_dp // 2
+    dp, me = lax.axis_index("dp").astype(jnp.int32), lax.axis_index("seq").astype(jnp.int32)
+    x, z, y, c = dp % 2, dp // 2, me // 2, me % 2
+    over_x = lambda t: swap(t, "dp", n_dp, 1)
+    over_y = lambda t: swap(t, "seq", n_seq, 2)
+    over_core = lambda t: swap(t, "seq", n_seq, 1)
+    over_z = lambda t, k: swap(t, "dp", n_dp, 2 * k)
+    scalars = lambda *t: jnp.stack(t)
+
+    def rows_of(own, from_x):
+        from_y, from_xy = over_y(own), over_y(from_x)
+        a = [own, over_core(own), from_x, over_core(from_x)]
+        return a, [from_y, over_core(from_y), from_xy, over_core(from_xy)]
+
+    qk, qs, gk, gs, delta, delta_s = pack(scalars(x), queries, grad_out, attn_out)
+    kp, vp, kt = pack_tokens(scalars(x), keys, values)
+    qa, qb = rows_of(qk, over_x(qs))
+    ga, gb = rows_of(gk, over_x(gs))
+    delta_x = over_x(delta_s)
+    pa, ma, la = side_of(qa, kp)
+    pb, mb, lb, sent = side_of(qb, kp, [la, delta, delta_x])
+    send = merge(la, lb, sent, over_core(sent))
+    got = over_y(send)
+
+    sums, dqs = [], []
+    for half in (1 - y, y):
+        out = half_of(scalars(half, c, z), high, qa + qb, ga + gb, pa, pb, vp, kt, ma, mb, send, got)
+        total = out[0].astype(F32)
+        for k in range(1, high):
+            total = total + over_z(out[k], k).astype(F32)
+        sums.append(total.astype(BF))
+        dqs.append((out[high + 1], over_core(out[high])))
+
+    keep, core = dqs[0]
+    far = over_y((keep.astype(F32) + core.astype(F32)).astype(BF))
+    qx, got = lax.optimization_barrier((qx, got))
+    xa, xb = rows_of(qx, over_x(qx))
+    *parts, back, back_s = columns_of(scalars(z), high, xa + xb, *dqs[1], far)
+    parts = parts[:1] + [over_z(parts[k], k) for k in range(1, high)]
+    keep, send_w = weight_sum(scalars(x), parts)
+    grad_weight = weight_out(scalars(x), keep, over_x(send_w))
+
+    size = back.shape[0]
+    from_x = over_x(back_s)
+    from_y = over_y(jnp.concatenate([back[:, 2 * size :], from_x[:, 2 * size :]], axis=0))
+    near = [back[:, size : 2 * size], from_x[:, size : 2 * size], from_y[:, size:]]
+    from_core = over_core(jnp.concatenate(near, axis=0))
+    grad_input = input_of(scalars(me, x), back, from_x, from_y, from_core, wq)
+
+    parts = []
+    for total in sums:
+        blocks = [total] + [over_z(total, k) for k in range(1, high)]
+        parts += blocks + [over_x(jnp.concatenate(blocks, axis=0))]
+    grad_keys, grad_values = tokens_out(scalars(y, x, z), high, *keys.shape, parts)
+    return (grad_input, grad_keys, grad_values, grad_weight)
+
+
 def solution(mesh):
     n_dp, n_seq = mesh.shape["dp"], mesh.shape["seq"]
-    return jax.shard_map(
-        functools.partial(local, n_dp, n_seq),
-        mesh=mesh,
-        in_specs=(
-            P(("dp", "seq"), None),
-            P(("dp", "seq"), None),
-            P("seq", None),
-            P("seq", None),
-            P(("dp", "seq"), None),
-            P(("dp", "seq"), None),
-            P(),
-        ),
-        out_specs=(P(("dp", "seq"), None), P("seq", None), P("seq", None), P("dp", "seq")),
-        check_vma=False,
-    )
+
+    def run(qx, queries, keys, *rest):
+        pairs = queries.shape[1] == 2 * n_seq * PAIR and queries.shape[0] == n_dp * n_seq * PAIR
+        split = n_seq == 4 and n_dp == 8 and pairs and (2 * keys.shape[0] // n_seq) % (16 * n_dp // 2) == 0
+        return shard(local_split if split else local)(qx, queries, keys, *rest)
+
+    def shard(f):
+        return jax.shard_map(
+            functools.partial(f, n_dp, n_seq),
+            mesh=mesh,
+            in_specs=(
+                P(("dp", "seq"), None),
+                P(("dp", "seq"), None),
+                P("seq", None),
+                P("seq", None),
+                P(("dp", "seq"), None),
+                P(("dp", "seq"), None),
+                P(),
+            ),
+            out_specs=(P(("dp", "seq"), None), P("seq", None), P("seq", None), P("dp", "seq")),
+            check_vma=False,
+        )
+
+    return run

time: 155 us -> 133 us (0.86)
  Pallas kernels: 35.6 us -> 24.5 us
  other arithmetic: 10.3 us -> 0.48 us
  starting transfers between devices: 42.9 us -> 50.1 us
  local copies, waits for them, and re-layouts: 26.7 us -> 20.3 us
    unnamed x35 -> x66, local copies, waits for them, and re-layouts: 6.75 us -> 20.2 us
    pallas_call x6 -> x12, Pallas kernels: 35.6 us -> 24.5 us  [the longest x2 11.7 us: half_of(): pl.pallas_call(functools.partial(half_kernel, count), grid_spec=pltpu.Pre...]
    squeeze x8 -> x0, local copies, waits for them, and re-layouts: 7.39 us -> none  [the longest x6 4.69 us: pick(): return lax.dynamic_index_in_dim(blocks, index, 0, keepdims=False)]
    ppermute x37 -> x48, starting transfers between devices: 42.9 us -> 50.1 us  [swap(): return lax.ppermute(x, axis, [(i, i ^ mask) for i in range(size)])]
    rev x5 -> x0, local copies, waits for them, and re-layouts: 6.42 us -> none  [flip_pieces(): return jnp.flip(y, axis=-2).reshape(x.shape)]
    convert_element_type x5 -> x3, other arithmetic: 5.22 us -> 0.17 us  [the longest x2 0.11 us: local_split(): sums.append(total.astype(BF))]
    reshape x7 -> x0, local copies, waits for them, and re-layouts: 2.96 us -> none  [the longest x5 2.88 us: flip_pieces(): y = x.reshape(lead + (count // (2 * bit), 2, bit * piece))]
    dynamic_update_slice x14 -> x0, local copies, waits for them, and re-layouts: 2.04 us -> none  [the longest x10 1.98 us: exchange_gather(): out = lax.dynamic_update_index_in_dim(out, got, me ^ k, 0)]
  transfers between devices with their start and end apart: 37 -> 48, of which waited for: 11 -> 15; matrix products, arithmetic and copies ran while one was open for 22% -> 0% of each run, Pallas kernels for 23% -> 12%
where the time goes in v2:
time: 133 us
  starting transfers between devices  50.1 us (38%)
  waiting for transfers between devices  36.1 us (27%)
  Pallas kernels  24.5 us (18%)
  local copies, waits for them, and re-layouts  20.3 us (15%)
    ppermute x48, starting transfers between devices, swap(): return lax.ppermute(x, axis, [(i, i ^ mask) for i in range(size)])  50.1 us
    ppermute x48, waiting for transfers between devices, swap(): return lax.ppermute(x, axis, [(i, i ^ mask) for i in range(size)])  36.1 us
    unnamed x66, local copies, waits for them, and re-layouts  20.2 us
    pallas_call x2, Pallas kernels, half_of(): pl.pallas_call(functools.partial(half_kernel, count), grid_spec=pltpu.Pre...  11.7 us
    pallas_call x2, Pallas kernels, side_of(): pl.pallas_call(functools.partial(side_kernel, count, step, extra is not N...  5.26 us
  transfers between devices with their start and end apart: 48, of which 15 were waited for; matrix products, arithmetic and copies ran while one was open for 0% of the time, Pallas kernels for 12%

profile of v2, /device:TPU:0, one launch (start us, length us, event | category | flops | bytes accessed | tf_op | source)
XLA Modules:
  0.0 132.5 jit_solution(2250498473629110644)
XLA Ops:
  0.7 0.9 copy-done.24
  1.6 0.9 copy-done.25
  2.6 0.9 copy-done.26
  3.5 0.9 shard_map.102
  4.4 2.9 %collective-permute-start.1 = (bf16[128,512]{1,0:T(8,128)(2,1)S(1)}, bf16[128,512]{1,0:T(8,128)(2,1)S(1)}, u32[]{:S(2)}, u32[]{:S(2)}) collective-permute-start(bf16[128,512]{1,0:T(8,128)(2,1)S(1)} %get-tuple-element.44), channel_id=1, source_target_pairs={{0,4},{4,0},{8,12},{12,8},{16,20},{20,16},{24,28},{28,24},{1,5},{5... | collective-permute-start | bytes 393224 | tf_op jit(solution)/shard_map/ppermute | solution.py:191
  7.4 1.5 %collective-permute-start.3 = (bf16[128,512]{1,0:T(8,128)(2,1)S(1)}, bf16[128,512]{1,0:T(8,128)(2,1)S(1)}, u32[]{:S(2)}, u32[]{:S(2)}) collective-permute-start(bf16[128,512]{1,0:T(8,128)(2,1)S(1)} %get-tuple-element.43.refs_0_), channel_id=1, source_target_pairs={{0,2},{1,3},{2,0},{3,1},{4,6},{5,7},{6,4},{7,5},{8,10},{9,11},{10,... | collective-permute-start | bytes 393224 | tf_op jit(solution)/shard_map/ppermute | solution.py:191
  8.9 2.0 %collective-permute-done.1.refs_2_ = bf16[128,512]{1,0:T(8,128)(2,1)S(1)} collective-permute-done((bf16[128,512]{1,0:T(8,128)(2,1)S(1)}, bf16[128,512]{1,0:T(8,128)(2,1)S(1)}, u32[]{:S(2)}, u32[]{:S(2)}) %collective-permute-start.1) | collective-permute-done | bytes 131104 | tf_op jit(solution)/shard_map/ppermute | solution.py:191
  10.9 1.8 %collective-permute-start.5 = (bf16[128,512]{1,0:T(8,128)(2,1)S(1)}, bf16[128,512]{1,0:T(8,128)(2,1)S(1)}, u32[]{:S(2)}, u32[]{:S(2)}) collective-permute-start(bf16[128,512]{1,0:T(8,128)(2,1)S(1)} %collective-permute-done.1.refs_2_), channel_id=1, source_target_pairs={{0,2},{1,3},{2,0},{3,1},{4,6},{5,7},{6,4},{7,5},{8,10},{9,11},{10,... | collective-permute-start | bytes 393224 | tf_op jit(solution)/shard_map/ppermute | solution.py:191
  12.6 1.5 %collective-permute-start.18 = (bf16[128,512]{1,0:T(8,128)(2,1)S(1)}, bf16[128,512]{1,0:T(8,128)(2,1)}, u32[]{:S(2)}, u32[]{:S(2)}) collective-permute-start(bf16[128,512]{1,0:T(8,128)(2,1)S(1)} %get-tuple-element.53), channel_id=1, source_target_pairs={{0,4},{4,0},{8,12},{12,8},{16,20},{20,16},{24,28},{28,24},{1,5},{5... | collective-permute-start | bytes 393224 | tf_op jit(solution)/shard_map/ppermute | solution.py:191
  14.6 1.2 collective-permute-done.5.refs_2_.refs_6_
  15.8 1.8 %collective-permute-start.20 = (bf16[128,512]{1,0:T(8,128)(2,1)}, bf16[128,512]{1,0:T(8,128)(2,1)}, u32[]{:S(2)}, u32[]{:S(2)}) collective-permute-start(bf16[128,512]{1,0:T(8,128)(2,1)} %get-tuple-element.52.refs_8_), channel_id=1, source_target_pairs={{0,2},{1,3},{2,0},{3,1},{4,6},{5,7},{6,4},{7,5},{8,10},{9,11},{10,... | collective-permute-start | bytes 393224 | tf_op jit(solution)/shard_map/ppermute | solution.py:191
  17.7 1.0 collective-permute-done.18.refs_10_
  18.9 1.1 copy-done.5
  20.0 1.1 copy-done.6
  21.4 1.8 %collective-permute-start.7 = (f32[4,2,128]{2,1,0:T(2,128)S(1)}, f32[4,2,128]{2,1,0:T(2,128)S(1)}, u32[]{:S(2)}, u32[]{:S(2)}) collective-permute-start(f32[4,2,128]{2,1,0:T(2,128)S(1)} %get-tuple-element.48), channel_id=1, source_target_pairs={{0,4},{4,0},{8,12},{12,8},{16,20},{20,16},{24,28},{28,24},{1,5},{5... | collective-permute-start | bytes 12296 | tf_op jit(solution)/shard_map/ppermute | solution.py:191
  23.3 2.3 %shard_map.104 = (bf16[8,384,512]{2,1,0:T(8,128)(2,1)S(1)}, f32[4,2,512]{2,1,0:T(2,128)S(1)}, f32[4,2,512]{2,1,0:T(2,128)S(1)}) custom-call(bf16[128,512]{1,0:T(8,128)(2,1)S(1)} %get-tuple-element.43.refs_0_, bf16[128,512]{1,0:T(8,128)(2,1)S(1)} %collective-permute-done.refs_1_, bf16[128,512]{1,0:T(8,128)(2,1)S(1)} %collective-permute-done.1.refs_2_, ...), custom_call_target="tpu_custom_call" | custom-call | flops 201326592 | bytes 3145728 | tf_op jit(solution)/shard_map/pallas_call | solution.py:429
  25.7 2.9 %shard_map.105 = (bf16[8,384,512]{2,1,0:T(8,128)(2,1)S(1)}, f32[4,2,512]{2,1,0:T(2,128)S(1)}, f32[4,2,512]{2,1,0:T(2,128)S(1)}, f32[4,2,1280]{2,1,0:T(2,128)}) custom-call(bf16[128,512]{1,0:T(8,128)(2,1)S(1)} %collective-permute-done.3.refs_0_.refs_4_, bf16[128,512]{1,0:T(8,128)(2,1)S(1)} %collective-permute-done.4.refs_1_.refs_5_, ...), custom_call_target="tpu_custom_call" | custom-call | flops 201326592 | bytes 3145728 | tf_op jit(solution)/shard_map/pallas_call | solution.py:429
  28.6 1.6 %copy-done = bf16[8,384,512]{2,1,0:T(8,128)(2,1)} copy-done((bf16[8,384,512]{2,1,0:T(8,128)(2,1)}, bf16[8,384,512]{2,1,0:T(8,128)(2,1)S(1)}, u32[]{:S(2)}) %copy-start) | copy-done | bytes 3145752
  34.5 0.8 shard_map.106.refs_22_
  35.3 1.6 %collective-permute-start.9 = (f32[4,2,1536]{2,1,0:T(2,128)S(1)}, f32[4,2,1536]{2,1,0:T(2,128)S(1)}, u32[]{:S(2)}, u32[]{:S(2)}) collective-permute-start(f32[4,2,1536]{2,1,0:T(2,128)S(1)} %shard_map.106.refs_22_), channel_id=1, source_target_pairs={{0,2},{1,3},{2,0},{3,1},{4,6},{5,7},{6,4},{7,5},{8,10},{9,11},{10,... | collective-permute-start | bytes 147464 | tf_op jit(solution)/shard_map/ppermute | solution.py:191
  37.0 2.5 %collective-permute-done.9.refs_23_ = f32[4,2,1536]{2,1,0:T(2,128)S(1)} collective-permute-done((f32[4,2,1536]{2,1,0:T(2,128)S(1)}, f32[4,2,1536]{2,1,0:T(2,128)S(1)}, u32[]{:S(2)}, u32[]{:S(2)}) %collective-permute-start.9) | collective-permute-done | bytes 49184 | tf_op jit(solution)/shard_map/ppermute | solution.py:191
  39.5 1.9 %copy-done.1 = bf16[8,384,512]{2,1,0:T(8,128)(2,1)S(1)} copy-done((bf16[8,384,512]{2,1,0:T(8,128)(2,1)S(1)}, bf16[8,384,512]{2,1,0:T(8,128)(2,1)}, u32[]{:S(2)}) %copy-start.1) | copy-done | bytes 3145752
  41.4 1.0 copy-done.4
  42.4 0.9 copy-done.8
  43.3 0.9 copy-done.10
  44.2 0.9 copy-done.12
  45.1 0.9 copy-done.14
  46.0 0.9 copy-done.16
  46.9 0.9 copy-done.18
  47.8 0.9 copy-done.20
  48.7 0.9 copy-done.22
  50.3 5.9 %shard_map.108 = (bf16[192,256]{1,0:T(8,128)(2,1)S(1)}, bf16[192,256]{1,0:T(8,128)(2,1)S(1)}, bf16[192,256]{1,0:T(8,128)(2,1)S(1)}, bf16[192,256]{1,0:T(8,128)(2...) custom-call(s32[3]{0:T(128)S(1)} %get-tuple-element.83.at_ref, bf16[128,512]{1,0:T(8,128)(2,1)S(1)} %copy-done.8, ...), custom_call_target="tpu_custom_call" | custom-call | flops 1610612736 | bytes 3145728 | tf_op jit(solution)/shard_map/pallas_call | solution.py:528
  56.3 1.3 collective-permute-start.11
  57.6 5.9 %shard_map.107 = (bf16[192,256]{1,0:T(8,128)(2,1)S(1)}, bf16[192,256]{1,0:T(8,128)(2,1)S(1)}, bf16[192,256]{1,0:T(8,128)(2,1)S(1)}, bf16[192,256]{1,0:T(8,128)(2...) custom-call(s32[3]{0:T(128)S(1)} %get-tuple-element.82.at_ref, bf16[128,512]{1,0:T(8,128)(2,1)S(1)} %copy-done.8, ...), custom_call_target="tpu_custom_call" | custom-call | flops 1610612736 | bytes 3145728 | tf_op jit(solution)/shard_map/pallas_call | solution.py:528
  63.4 1.6 %collective-permute-start.37 = (bf16[192,256]{1,0:T(8,128)(2,1)S(1)}, bf16[192,256]{1,0:T(8,128)(2,1)S(1)}, u32[]{:S(2)}, u32[]{:S(2)}) collective-permute-start(bf16[192,256]{1,0:T(8,128)(2,1)S(1)} %get-tuple-element.71), channel_id=1, source_target_pairs={{0,8},{4,12},{8,0},{12,4},{16,24},{20,28},{24,16},{28,20},{1,9},{5... | collective-permute-start | bytes 294920 | tf_op jit(solution)/shard_map/ppermute | solution.py:191
  65.1 2.6 %collective-permute-start.38 = (bf16[192,256]{1,0:T(8,128)(2,1)S(1)}, bf16[192,256]{1,0:T(8,128)(2,1)S(1)}, u32[]{:S(2)}, u32[]{:S(2)}) collective-permute-start(bf16[192,256]{1,0:T(8,128)(2,1)S(1)} %get-tuple-element.72), channel_id=1, source_target_pairs={{0,16},{4,20},{8,24},{12,28},{16,0},{20,4},{24,8},{28,12},{1,17},{... | collective-permute-start | bytes 294920 | tf_op jit(solution)/shard_map/ppermute | solution.py:191
  68.4 1.5 %collective-permute-start.13 = (bf16[128,1024]{1,0:T(8,128)(2,1)S(1)}, bf16[128,1024]{1,0:T(8,128)(2,1)S(1)}, u32[]{:S(2)}, u32[]{:S(2)}) collective-permute-start(bf16[128,1024]{1,0:T(8,128)(2,1)S(1)} %copy-done.23), channel_id=1, source_target_pairs={{0,2},{1,3},{2,0},{3,1},{4,6},{5,7},{6,4},{7,5},{8,10},{9,11},{10,... | collective-permute-start | bytes 786440 | tf_op jit(solution)/shard_map/ppermute | solution.py:191
  69.9 2.8 %collective-permute-done.38 = bf16[192,256]{1,0:T(8,128)(2,1)S(1)} collective-permute-done((bf16[192,256]{1,0:T(8,128)(2,1)S(1)}, bf16[192,256]{1,0:T(8,128)(2,1)S(1)}, u32[]{:S(2)}, u32[]{:S(2)}) %collective-permute-start.38) | collective-permute-done | bytes 98336 | tf_op jit(solution)/shard_map/ppermute | solution.py:191
  72.7 2.5 %collective-permute-start.39 = (bf16[192,256]{1,0:T(8,128)(2,1)S(1)}, bf16[192,256]{1,0:T(8,128)(2,1)S(1)}, u32[]{:S(2)}, u32[]{:S(2)}) collective-permute-start(bf16[192,256]{1,0:T(8,128)(2,1)S(1)} %get-tuple-element.73), channel_id=1, source_target_pairs={{0,24},{4,28},{8,16},{12,20},{16,8},{20,12},{24,0},{28,4},{1,25},{... | collective-permute-start | bytes 294920 | tf_op jit(solution)/shard_map/ppermute | solution.py:191
  75.2 1.6 %collective-permute-start.15 = (bf16[128,1024]{1,0:T(8,128)(2,1)S(1)}, bf16[128,1024]{1,0:T(8,128)(2,1)S(1)}, u32[]{:S(2)}, u32[]{:S(2)}) collective-permute-start(bf16[128,1024]{1,0:T(8,128)(2,1)S(1)} %collective-permute-done.11.refs_2_), channel_id=1, source_target_pairs={{0,2},{1,3},{2,0},{3,1},{4,6},{5,7},{6,4},{7,5},{8,10},{9,11},{10,... | collective-permute-start | bytes 786440 | tf_op jit(solution)/shard_map/ppermute | solution.py:191
  76.8 3.0 %collective-permute-done.39 = bf16[192,256]{1,0:T(8,128)(2,1)S(1)} collective-permute-done((bf16[192,256]{1,0:T(8,128)(2,1)S(1)}, bf16[192,256]{1,0:T(8,128)(2,1)S(1)}, u32[]{:S(2)}, u32[]{:S(2)}) %collective-permute-start.39) | collective-permute-done | bytes 98336 | tf_op jit(solution)/shard_map/ppermute | solution.py:191
  79.8 1.5 %collective-permute-start.26 = (bf16[128,1024]{1,0:T(8,128)(2,1)S(1)}, bf16[128,1024]{1,0:T(8,128)(2,1)S(1)}, u32[]{:S(2)}, u32[]{:S(2)}) collective-permute-start(bf16[128,1024]{1,0:T(8,128)(2,1)S(1)} %add_convert_fusion), channel_id=1, source_target_pairs={{0,2},{1,3},{2,0},{3,1},{4,6},{5,7},{6,4},{7,5},{8,10},{9,11},{10,... | collective-permute-start | bytes 786440 | tf_op jit(solution)/shard_map/ppermute | solution.py:191
  81.9 2.5 %collective-permute-done.15.refs_6_ = bf16[128,1024]{1,0:T(8,128)(2,1)S(1)} collective-permute-done((bf16[128,1024]{1,0:T(8,128)(2,1)S(1)}, bf16[128,1024]{1,0:T(8,128)(2,1)S(1)}, u32[]{:S(2)}, u32[]{:S(2)}) %collective-permute-start.15) | collective-permute-done | bytes 262176 | tf_op jit(solution)/shard_map/ppermute | solution.py:191
  84.4 4.9 %collective-permute-done.26.refs_10_ = bf16[128,1024]{1,0:T(8,128)(2,1)S(1)} collective-permute-done((bf16[128,1024]{1,0:T(8,128)(2,1)S(1)}, bf16[128,1024]{1,0:T(8,128)(2,1)S(1)}, u32[]{:S(2)}, u32[]{:S(2)}) %collective-permute-start.26) | collective-permute-done | bytes 262176 | tf_op jit(solution)/shard_map/ppermute | solution.py:191
  89.8 2.1 %collective-permute-start.32 = (bf16[192,256]{1,0:T(8,128)(2,1)S(1)}, bf16[192,256]{1,0:T(8,128)(2,1)S(1)}, u32[]{:S(2)}, u32[]{:S(2)}) collective-permute-start(bf16[192,256]{1,0:T(8,128)(2,1)S(1)} %get-tuple-element.69), channel_id=1, source_target_pairs={{0,24},{4,28},{8,16},{12,20},{16,8},{20,12},{24,0},{28,4},{1,25},{... | collective-permute-start | bytes 294920 | tf_op jit(solution)/shard_map/ppermute | solution.py:191
  91.9 1.0 collective-permute-start.40
  92.9 1.4 %collective-permute-start.41 = (bf16[192,256]{1,0:T(8,128)(2,1)S(1)}, bf16[192,256]{1,0:T(8,128)(2,1)S(1)}, u32[]{:S(2)}, u32[]{:S(2)}) collective-permute-start(bf16[192,256]{1,0:T(8,128)(2,1)S(1)} %add_convert_fusion.1.refs_5_), channel_id=1, source_target_pairs={{0,16},{4,20},{8,24},{12,28},{16,0},{20,4},{24,8},{28,12},{1,17},{... | collective-permute-start | bytes 294920 | tf_op jit(solution)/shard_map/ppermute | solution.py:191
  94.8 2.1 %collective-permute-start.42 = (bf16[192,256]{1,0:T(8,128)(2,1)S(1)}, bf16[192,256]{1,0:T(8,128)(2,1)S(1)}, u32[]{:S(2)}, u32[]{:S(2)}) collective-permute-start(bf16[192,256]{1,0:T(8,128)(2,1)S(1)} %add_convert_fusion.1.refs_5_), channel_id=1, source_target_pairs={{0,24},{4,28},{8,16},{12,20},{16,8},{20,12},{24,0},{28,4},{1,25},{... | collective-permute-start | bytes 294920 | tf_op jit(solution)/shard_map/ppermute | solution.py:191
  96.9 5.7 %collective-permute-done.31 = bf16[192,256]{1,0:T(8,128)(2,1)S(1)} collective-permute-done((bf16[192,256]{1,0:T(8,128)(2,1)S(1)}, bf16[192,256]{1,0:T(8,128)(2,1)S(1)}, u32[]{:S(2)}, u32[]{:S(2)}) %collective-permute-start.31) | collective-permute-done | bytes 98336 | tf_op jit(solution)/shard_map/ppermute | solution.py:191
  102.6 0.8 collective-permute-start.27
  103.5 1.9 %collective-permute-start.33 = (bf16[192,256]{1,0:T(8,128)(2,1)S(1)}, bf16[192,256]{1,0:T(8,128)(2,1)S(1)}, u32[]{:S(2)}, u32[]{:S(2)}) collective-permute-start(bf16[192,256]{1,0:T(8,128)(2,1)S(1)} %add_convert_fusion.2.refs_0_), channel_id=1, source_target_pairs={{0,8},{4,12},{8,0},{12,4},{16,24},{20,28},{24,16},{28,20},{1,9},{5... | collective-permute-start | bytes 294920 | tf_op jit(solution)/shard_map/ppermute | solution.py:191
  105.4 0.8 collective-permute-start.34
  106.8 2.1 %collective-permute-start.35 = (bf16[192,256]{1,0:T(8,128)(2,1)S(1)}, bf16[192,256]{1,0:T(8,128)(2,1)S(1)}, u32[]{:S(2)}, u32[]{:S(2)}) collective-permute-start(bf16[192,256]{1,0:T(8,128)(2,1)S(1)} %add_convert_fusion.2.refs_0_), channel_id=1, source_target_pairs={{0,24},{4,28},{8,16},{12,20},{16,8},{20,12},{24,0},{28,4},{1,25},{... | collective-permute-start | bytes 294920 | tf_op jit(solution)/shard_map/ppermute | solution.py:191
  109.0 0.9 collective-permute-start.43
  109.9 1.5 %collective-permute-start.28 = (bf16[256,256]{1,0:T(8,128)(2,1)S(1)}, bf16[256,256]{1,0:T(8,128)(2,1)S(1)}, u32[]{:S(2)}, u32[]{:S(2)}) collective-permute-start(bf16[256,256]{1,0:T(8,128)(2,1)S(1)} %pad_maximum_fusion.2), channel_id=1, source_target_pairs={{0,2},{1,3},{2,0},{3,1},{4,6},{5,7},{6,4},{7,5},{8,10},{9,11},{10,... | collective-permute-start | bytes 393224 | tf_op jit(solution)/shard_map/ppermute | solution.py:191
  111.4 3.8 %collective-permute-done.34.refs_2_ = bf16[192,256]{1,0:T(8,128)(2,1)S(1)} collective-permute-done((bf16[192,256]{1,0:T(8,128)(2,1)S(1)}, bf16[192,256]{1,0:T(8,128)(2,1)S(1)}, u32[]{:S(2)}, u32[]{:S(2)}) %collective-permute-start.34) | collective-permute-done | bytes 98336 | tf_op jit(solution)/shard_map/ppermute | solution.py:191
  115.3 0.9 collective-permute-start.36
  116.2 2.2 %collective-permute-start.44 = (bf16[128,256]{1,0:T(8,128)(2,1)S(1)}, bf16[128,256]{1,0:T(8,128)(2,1)S(1)}, u32[]{:S(2)}, u32[]{:S(2)}) collective-permute-start(bf16[128,256]{1,0:T(8,128)(2,1)S(1)} %get-tuple-element.77), channel_id=1, source_target_pairs={{0,8},{4,12},{8,0},{12,4},{16,24},{20,28},{24,16},{28,20},{1,9},{5... | collective-permute-start | bytes 196616 | tf_op jit(solution)/shard_map/ppermute | solution.py:191
  118.9 2.0 %collective-permute-start.46 = (bf16[128,256]{1,0:T(8,128)(2,1)S(1)}, bf16[128,256]{1,0:T(8,128)(2,1)S(1)}, u32[]{:S(2)}, u32[]{:S(2)}) collective-permute-start(bf16[128,256]{1,0:T(8,128)(2,1)S(1)} %get-tuple-element.79), channel_id=1, source_target_pairs={{0,24},{4,28},{8,16},{12,20},{16,8},{20,12},{24,0},{28,4},{1,25},{... | collective-permute-start | bytes 196616 | tf_op jit(solution)/shard_map/ppermute | solution.py:191
  121.1 4.6 %collective-permute-done.45.refs_2_ = bf16[128,256]{1,0:T(8,128)(2,1)S(1)} collective-permute-done((bf16[128,256]{1,0:T(8,128)(2,1)S(1)}, bf16[128,256]{1,0:T(8,128)(2,1)S(1)}, u32[]{:S(2)}, u32[]{:S(2)}) %collective-permute-start.45) | collective-permute-done | bytes 65568 | tf_op jit(solution)/shard_map/ppermute | solution.py:191
  125.7 1.3 %collective-permute-start.47 = (bf16[128,128]{1,0:T(8,128)(2,1)S(1)}, bf16[128,128]{1,0:T(8,128)(2,1)S(1)}, u32[]{:S(2)}, u32[]{:S(2)}) collective-permute-start(bf16[128,128]{1,0:T(8,128)(2,1)S(1)} %get-tuple-element.81), channel_id=1, source_target_pairs={{0,4},{4,0},{8,12},{12,8},{16,20},{20,16},{24,28},{28,24},{1,5},{5... | collective-permute-start | bytes 98312 | tf_op jit(solution)/shard_map/ppermute | solution.py:191
  127.1 2.1 %shard_map.111 = (bf16[384,1024]{1,0:T(8,128)(2,1)}, bf16[384,1024]{1,0:T(8,128)(2,1)}) custom-call(s32[3]{0:T(128)S(1)} %add_add_fusion.2.at_ref, bf16[192,256]{1,0:T(8,128)(2,1)S(1)} %add_convert_fusion.2.refs_0_, bf16[192,256]{1,0:T(8,128)(2,1)S(1)} %collective-permute-done.33.refs_1_, bf16[192,256]{1,0:T(8,128)(2,1)S(1)} %collective-permute-done.34.refs_2_, ...), custom_call_target="tpu_custom_call" | custom-call | flops 1000 | bytes 3145728 | tf_op jit(solution)/shard_map/pallas_call | solution.py:682
  129.7 0.8 shard_map.113
  130.4 2.1 %shard_map.110 = bf16[128,1024]{1,0:T(8,128)(2,1)} custom-call(s32[2]{0:T(128)S(1)} %pad_add_fusion.at_ref, bf16[128,512]{1,0:T(8,128)(2,1)S(1)} %get-tuple-element.64.back_ref, bf16[128,512]{1,0:T(8,128)(2,1)S(1)} %collective-permute-done.27.x_ref, bf16[256,256]{1,0:T(8,128)(2,1)S(1)} %collective-permute-done.28.y_ref, ...), custom_call_target="tpu_custom_call" | custom-call | flops 268435456 | bytes 2097152 | tf_op jit(solution)/shard_map/pallas_call | solution.py:605
  (125 shorter events, 10.5 us)
Async XLA Ops:
  4.4 21.2 %copy-start.7 = (bf16[128,512]{1,0:T(8,128)(2,1)}, bf16[128,512]{1,0:T(8,128)(2,1)S(1)}, u32[]{:S(2)}) copy-start(bf16[128,512]{1,0:T(8,128)(2,1)S(1)} %get-tuple-element.43.refs_0_) | copy-start | bytes 393220
  4.4 6.4 %collective-permute-start.1 = (bf16[128,512]{1,0:T(8,128)(2,1)S(1)}, bf16[128,512]{1,0:T(8,128)(2,1)S(1)}, u32[]{:S(2)}, u32[]{:S(2)}) collective-permute-start(bf16[128,512]{1,0:T(8,128)(2,1)S(1)} %get-tuple-element.44), channel_id=1, source_target_pairs={{0,4},{4,0},{8,12},{12,8},{16,20},{20,16},{24,28},{28,24},{1,5},{5... | collective-permute-start | bytes 393224 | tf_op jit(solution)/shard_map/ppermute | solution.py:191
  7.4 7.0 %collective-permute-start.3 = (bf16[128,512]{1,0:T(8,128)(2,1)S(1)}, bf16[128,512]{1,0:T(8,128)(2,1)S(1)}, u32[]{:S(2)}, u32[]{:S(2)}) collective-permute-start(bf16[128,512]{1,0:T(8,128)(2,1)S(1)} %get-tuple-element.43.refs_0_), channel_id=1, source_target_pairs={{0,2},{1,3},{2,0},{3,1},{4,6},{5,7},{6,4},{7,5},{8,10},{9,11},{10,... | collective-permute-start | bytes 393224 | tf_op jit(solution)/shard_map/ppermute | solution.py:191
  10.9 14.8 %copy-start.9 = (bf16[128,512]{1,0:T(8,128)(2,1)}, bf16[128,512]{1,0:T(8,128)(2,1)S(1)}, u32[]{:S(2)}) copy-start(bf16[128,512]{1,0:T(8,128)(2,1)S(1)} %collective-permute-done.1.refs_2_) | copy-start | bytes 393220
  10.9 5.0 %collective-permute-start.5 = (bf16[128,512]{1,0:T(8,128)(2,1)S(1)}, bf16[128,512]{1,0:T(8,128)(2,1)S(1)}, u32[]{:S(2)}, u32[]{:S(2)}) collective-permute-start(bf16[128,512]{1,0:T(8,128)(2,1)S(1)} %collective-permute-done.1.refs_2_), channel_id=1, source_target_pairs={{0,2},{1,3},{2,0},{3,1},{4,6},{5,7},{6,4},{7,5},{8,10},{9,11},{10,... | collective-permute-start | bytes 393224 | tf_op jit(solution)/shard_map/ppermute | solution.py:191
  12.6 3.2 %collective-permute-start = (bf16[128,512]{1,0:T(8,128)(2,1)S(1)}, bf16[128,512]{1,0:T(8,128)(2,1)S(1)}, u32[]{:S(2)}, u32[]{:S(2)}) collective-permute-start(bf16[128,512]{1,0:T(8,128)(2,1)S(1)} %get-tuple-element.43.refs_0_), channel_id=1, source_target_pairs={{0,1},{1,0},{2,3},{3,2},{4,5},{5,4},{6,7},{7,6},{8,9},{9,8},{10,11... | collective-permute-start | bytes 393224 | tf_op jit(solution)/shard_map/ppermute | solution.py:191
  12.6 6.0 %collective-permute-start.18 = (bf16[128,512]{1,0:T(8,128)(2,1)S(1)}, bf16[128,512]{1,0:T(8,128)(2,1)}, u32[]{:S(2)}, u32[]{:S(2)}) collective-permute-start(bf16[128,512]{1,0:T(8,128)(2,1)S(1)} %get-tuple-element.53), channel_id=1, source_target_pairs={{0,4},{4,0},{8,12},{12,8},{16,20},{20,16},{24,28},{28,24},{1,5},{5... | collective-permute-start | bytes 393224 | tf_op jit(solution)/shard_map/ppermute | solution.py:191
  14.1 7.3 %collective-permute-start.2 = (bf16[128,512]{1,0:T(8,128)(2,1)S(1)}, bf16[128,512]{1,0:T(8,128)(2,1)S(1)}, u32[]{:S(2)}, u32[]{:S(2)}) collective-permute-start(bf16[128,512]{1,0:T(8,128)(2,1)S(1)} %collective-permute-done.1.refs_2_), channel_id=1, source_target_pairs={{0,1},{1,0},{2,3},{3,2},{4,5},{5,4},{6,7},{7,6},{8,9},{9,8},{10,11... | collective-permute-start | bytes 393224 | tf_op jit(solution)/shard_map/ppermute | solution.py:191
  14.4 14.3 %copy-start.11 = (bf16[128,512]{1,0:T(8,128)(2,1)}, bf16[128,512]{1,0:T(8,128)(2,1)S(1)}, u32[]{:S(2)}) copy-start(bf16[128,512]{1,0:T(8,128)(2,1)S(1)} %collective-permute-done.3.refs_0_.refs_4_) | copy-start | bytes 393220
  14.4 11.2 %collective-permute-start.4 = (bf16[128,512]{1,0:T(8,128)(2,1)S(1)}, bf16[128,512]{1,0:T(8,128)(2,1)S(1)}, u32[]{:S(2)}, u32[]{:S(2)}) collective-permute-start(bf16[128,512]{1,0:T(8,128)(2,1)S(1)} %collective-permute-done.3.refs_0_.refs_4_), channel_id=1, source_target_pairs={{0,1},{1,0},{2,3},{3,2},{4,5},{5,4},{6,7},{7,6},{8,9},{9,8},{10,11... | collective-permute-start | bytes 393224 | tf_op jit(solution)/shard_map/ppermute | solution.py:191
  15.8 12.8 %copy-start.13 = (bf16[128,512]{1,0:T(8,128)(2,1)}, bf16[128,512]{1,0:T(8,128)(2,1)S(1)}, u32[]{:S(2)}) copy-start(bf16[128,512]{1,0:T(8,128)(2,1)S(1)} %collective-permute-done.5.refs_2_.refs_6_) | copy-start | bytes 393220
  15.8 9.8 %collective-permute-start.6 = (bf16[128,512]{1,0:T(8,128)(2,1)S(1)}, bf16[128,512]{1,0:T(8,128)(2,1)S(1)}, u32[]{:S(2)}, u32[]{:S(2)}) collective-permute-start(bf16[128,512]{1,0:T(8,128)(2,1)S(1)} %collective-permute-done.5.refs_2_.refs_6_), channel_id=1, source_target_pairs={{0,1},{1,0},{2,3},{3,2},{4,5},{5,4},{6,7},{7,6},{8,9},{9,8},{10,11... | collective-permute-start | bytes 393224 | tf_op jit(solution)/shard_map/ppermute | solution.py:191
  15.8 9.8 %copy-start.15 = (bf16[128,512]{1,0:T(8,128)(2,1)}, bf16[128,512]{1,0:T(8,128)(2,1)S(1)}, u32[]{:S(2)}) copy-start(bf16[128,512]{1,0:T(8,128)(2,1)S(1)} %collective-permute-done.refs_1_) | copy-start | bytes 393220
  15.8 16.2 %collective-permute-start.20 = (bf16[128,512]{1,0:T(8,128)(2,1)}, bf16[128,512]{1,0:T(8,128)(2,1)}, u32[]{:S(2)}, u32[]{:S(2)}) collective-permute-start(bf16[128,512]{1,0:T(8,128)(2,1)} %get-tuple-element.52.refs_8_), channel_id=1, source_target_pairs={{0,2},{1,3},{2,0},{3,1},{4,6},{5,7},{6,4},{7,5},{8,10},{9,11},{10,... | collective-permute-start | bytes 393224 | tf_op jit(solution)/shard_map/ppermute | solution.py:191
  18.6 13.9 %collective-permute-start.22 = (bf16[128,512]{1,0:T(8,128)(2,1)}, bf16[128,512]{1,0:T(8,128)(2,1)}, u32[]{:S(2)}, u32[]{:S(2)}) collective-permute-start(bf16[128,512]{1,0:T(8,128)(2,1)} %collective-permute-done.18.refs_10_), channel_id=1, source_target_pairs={{0,2},{1,3},{2,0},{3,1},{4,6},{5,7},{6,4},{7,5},{8,10},{9,11},{10,... | collective-permute-start | bytes 393224 | tf_op jit(solution)/shard_map/ppermute | solution.py:191
  18.9 1.1 copy-start.5
  20.0 1.1 copy-start.6
  21.4 4.3 %copy-start.3 = (bf16[512,384]{1,0:T(8,128)(2,1)}, bf16[512,384]{1,0:T(8,128)(2,1)S(1)}, u32[]{:S(2)}) copy-start(bf16[512,384]{1,0:T(8,128)(2,1)S(1)} %get-tuple-element.57.refs_19_) | copy-start | bytes 1179652
  21.4 4.2 %copy-start.17 = (bf16[128,512]{1,0:T(8,128)(2,1)}, bf16[128,512]{1,0:T(8,128)(2,1)S(1)}, u32[]{:S(2)}) copy-start(bf16[128,512]{1,0:T(8,128)(2,1)S(1)} %collective-permute-done.2.refs_3_) | copy-start | bytes 393220
  21.4 4.1 %collective-permute-start.7 = (f32[4,2,128]{2,1,0:T(2,128)S(1)}, f32[4,2,128]{2,1,0:T(2,128)S(1)}, u32[]{:S(2)}, u32[]{:S(2)}) collective-permute-start(f32[4,2,128]{2,1,0:T(2,128)S(1)} %get-tuple-element.48), channel_id=1, source_target_pairs={{0,4},{4,0},{8,12},{12,8},{16,20},{20,16},{24,28},{28,24},{1,5},{5... | collective-permute-start | bytes 12296 | tf_op jit(solution)/shard_map/ppermute | solution.py:191
  25.6 6.4 %copy-start.29 = (f32[4,2,512]{2,1,0:T(2,128)}, f32[4,2,512]{2,1,0:T(2,128)S(1)}, u32[]{:S(2)}) copy-start(f32[4,2,512]{2,1,0:T(2,128)S(1)} %get-tuple-element.46.refs_5_.la_ref) | copy-start | bytes 49156
  25.6 5.9 %copy-start.19 = (bf16[128,512]{1,0:T(8,128)(2,1)}, bf16[128,512]{1,0:T(8,128)(2,1)S(1)}, u32[]{:S(2)}) copy-start(bf16[128,512]{1,0:T(8,128)(2,1)S(1)} %collective-permute-done.4.refs_1_.refs_5_) | copy-start | bytes 393220
  25.6 5.8 %copy-start.21 = (bf16[128,512]{1,0:T(8,128)(2,1)}, bf16[128,512]{1,0:T(8,128)(2,1)S(1)}, u32[]{:S(2)}) copy-start(bf16[128,512]{1,0:T(8,128)(2,1)S(1)} %collective-permute-done.6.refs_3_.refs_7_) | copy-start | bytes 393220
  28.6 1.6 %copy-start = (bf16[8,384,512]{2,1,0:T(8,128)(2,1)}, bf16[8,384,512]{2,1,0:T(8,128)(2,1)S(1)}, u32[]{:S(2)}) copy-start(bf16[8,384,512]{2,1,0:T(8,128)(2,1)S(1)} %get-tuple-element.55.refs_17_) | copy-start | bytes 9437188
  31.5 1.6 %collective-permute-start.8 = (f32[4,2,1280]{2,1,0:T(2,128)}, f32[4,2,1280]{2,1,0:T(2,128)}, u32[]{:S(2)}, u32[]{:S(2)}) collective-permute-start(f32[4,2,1280]{2,1,0:T(2,128)} %get-tuple-element.50.sent_ref), channel_id=1, source_target_pairs={{0,1},{1,0},{2,3},{3,2},{4,5},{5,4},{6,7},{7,6},{8,9},{9,8},{10,11... | collective-permute-start | bytes 122888 | tf_op jit(solution)/shard_map/ppermute | solution.py:191
  31.5 5.5 %collective-permute-start.17 = (bf16[128,512]{1,0:T(8,128)(2,1)}, bf16[128,512]{1,0:T(8,128)(2,1)}, u32[]{:S(2)}, u32[]{:S(2)}) collective-permute-start(bf16[128,512]{1,0:T(8,128)(2,1)} %get-tuple-element.52.refs_8_), channel_id=1, source_target_pairs={{0,1},{1,0},{2,3},{3,2},{4,5},{5,4},{6,7},{7,6},{8,9},{9,8},{10,11... | collective-permute-start | bytes 393224 | tf_op jit(solution)/shard_map/ppermute | solution.py:191
  32.0 5.0 %collective-permute-start.19 = (bf16[128,512]{1,0:T(8,128)(2,1)}, bf16[128,512]{1,0:T(8,128)(2,1)}, u32[]{:S(2)}, u32[]{:S(2)}) collective-permute-start(bf16[128,512]{1,0:T(8,128)(2,1)} %collective-permute-done.18.refs_10_), channel_id=1, source_target_pairs={{0,1},{1,0},{2,3},{3,2},{4,5},{5,4},{6,7},{7,6},{8,9},{9,8},{10,11... | collective-permute-start | bytes 393224 | tf_op jit(solution)/shard_map/ppermute | solution.py:191
  32.1 4.9 %collective-permute-start.21 = (bf16[128,512]{1,0:T(8,128)(2,1)}, bf16[128,512]{1,0:T(8,128)(2,1)}, u32[]{:S(2)}, u32[]{:S(2)}) collective-permute-start(bf16[128,512]{1,0:T(8,128)(2,1)} %collective-permute-done.20.refs_12_), channel_id=1, source_target_pairs={{0,1},{1,0},{2,3},{3,2},{4,5},{5,4},{6,7},{7,6},{8,9},{9,8},{10,11... | collective-permute-start | bytes 393224 | tf_op jit(solution)/shard_map/ppermute | solution.py:191
  32.5 4.5 %collective-permute-start.23 = (bf16[128,512]{1,0:T(8,128)(2,1)}, bf16[128,512]{1,0:T(8,128)(2,1)}, u32[]{:S(2)}, u32[]{:S(2)}) collective-permute-start(bf16[128,512]{1,0:T(8,128)(2,1)} %collective-permute-done.22.refs_14_), channel_id=1, source_target_pairs={{0,1},{1,0},{2,3},{3,2},{4,5},{5,4},{6,7},{7,6},{8,9},{9,8},{10,11... | collective-permute-start | bytes 393224 | tf_op jit(solution)/shard_map/ppermute | solution.py:191
  35.3 4.2 %collective-permute-start.9 = (f32[4,2,1536]{2,1,0:T(2,128)S(1)}, f32[4,2,1536]{2,1,0:T(2,128)S(1)}, u32[]{:S(2)}, u32[]{:S(2)}) collective-permute-start(f32[4,2,1536]{2,1,0:T(2,128)S(1)} %shard_map.106.refs_22_), channel_id=1, source_target_pairs={{0,2},{1,3},{2,0},{3,1},{4,6},{5,7},{6,4},{7,5},{8,10},{9,11},{10,... | collective-permute-start | bytes 147464 | tf_op jit(solution)/shard_map/ppermute | solution.py:191
  39.5 1.9 %copy-start.1 = (bf16[8,384,512]{2,1,0:T(8,128)(2,1)S(1)}, bf16[8,384,512]{2,1,0:T(8,128)(2,1)}, u32[]{:S(2)}) copy-start(bf16[8,384,512]{2,1,0:T(8,128)(2,1)} %copy-done) | copy-start | bytes 9437188
  50.3 5.9 %copy-start.23 = (bf16[128,1024]{1,0:T(8,128)(2,1)S(1)}, bf16[128,1024]{1,0:T(8,128)(2,1)}, u32[]{:S(2)}) copy-start(bf16[128,1024]{1,0:T(8,128)(2,1)} %refs_0_) | copy-start | bytes 786436
  56.2 16.5 %collective-permute-start.25 = (bf16[128,1024]{1,0:T(8,128)(2,1)S(1)}, bf16[128,1024]{1,0:T(8,128)(2,1)S(1)}, u32[]{:S(2)}, u32[]{:S(2)}) collective-permute-start(bf16[128,1024]{1,0:T(8,128)(2,1)S(1)} %get-tuple-element.63), channel_id=1, source_target_pairs={{0,1},{1,0},{2,3},{3,2},{4,5},{5,4},{6,7},{7,6},{8,9},{9,8},{10,11... | collective-permute-start | bytes 786440 | tf_op jit(solution)/shard_map/ppermute | solution.py:191
  56.3 18.9 %collective-permute-start.11 = (bf16[128,1024]{1,0:T(8,128)(2,1)S(1)}, bf16[128,1024]{1,0:T(8,128)(2,1)S(1)}, u32[]{:S(2)}, u32[]{:S(2)}) collective-permute-start(bf16[128,1024]{1,0:T(8,128)(2,1)S(1)} %copy-done.23), channel_id=1, source_target_pairs={{0,4},{4,0},{8,12},{12,8},{16,20},{20,16},{24,28},{28,24},{1,5},{5... | collective-permute-start | bytes 786440 | tf_op jit(solution)/shard_map/ppermute | solution.py:191
  63.4 4.9 %collective-permute-start.37 = (bf16[192,256]{1,0:T(8,128)(2,1)S(1)}, bf16[192,256]{1,0:T(8,128)(2,1)S(1)}, u32[]{:S(2)}, u32[]{:S(2)}) collective-permute-start(bf16[192,256]{1,0:T(8,128)(2,1)S(1)} %get-tuple-element.71), channel_id=1, source_target_pairs={{0,8},{4,12},{8,0},{12,4},{16,24},{20,28},{24,16},{28,20},{1,9},{5... | collective-permute-start | bytes 294920 | tf_op jit(solution)/shard_map/ppermute | solution.py:191
  65.1 7.6 %collective-permute-start.38 = (bf16[192,256]{1,0:T(8,128)(2,1)S(1)}, bf16[192,256]{1,0:T(8,128)(2,1)S(1)}, u32[]{:S(2)}, u32[]{:S(2)}) collective-permute-start(bf16[192,256]{1,0:T(8,128)(2,1)S(1)} %get-tuple-element.72), channel_id=1, source_target_pairs={{0,16},{4,20},{8,24},{12,28},{16,0},{20,4},{24,8},{28,12},{1,17},{... | collective-permute-start | bytes 294920 | tf_op jit(solution)/shard_map/ppermute | solution.py:191
  67.7 13.7 %collective-permute-start.24 = (bf16[128,1024]{1,0:T(8,128)(2,1)S(1)}, bf16[128,1024]{1,0:T(8,128)(2,1)S(1)}, u32[]{:S(2)}, u32[]{:S(2)}) collective-permute-start(bf16[128,1024]{1,0:T(8,128)(2,1)S(1)} %get-tuple-element.61), channel_id=1, source_target_pairs={{0,1},{1,0},{2,3},{3,2},{4,5},{5,4},{6,7},{7,6},{8,9},{9,8},{10,11... | collective-permute-start | bytes 786440 | tf_op jit(solution)/shard_map/ppermute | solution.py:191
  68.4 13.0 %collective-permute-start.13 = (bf16[128,1024]{1,0:T(8,128)(2,1)S(1)}, bf16[128,1024]{1,0:T(8,128)(2,1)S(1)}, u32[]{:S(2)}, u32[]{:S(2)}) collective-permute-start(bf16[128,1024]{1,0:T(8,128)(2,1)S(1)} %copy-done.23), channel_id=1, source_target_pairs={{0,2},{1,3},{2,0},{3,1},{4,6},{5,7},{6,4},{7,5},{8,10},{9,11},{10,... | collective-permute-start | bytes 786440 | tf_op jit(solution)/shard_map/ppermute | solution.py:191
  72.7 11.6 %collective-permute-start.10 = (bf16[128,1024]{1,0:T(8,128)(2,1)S(1)}, bf16[128,1024]{1,0:T(8,128)(2,1)S(1)}, u32[]{:S(2)}, u32[]{:S(2)}) collective-permute-start(bf16[128,1024]{1,0:T(8,128)(2,1)S(1)} %copy-done.23), channel_id=1, source_target_pairs={{0,1},{1,0},{2,3},{3,2},{4,5},{5,4},{6,7},{7,6},{8,9},{9,8},{10,11... | collective-permute-start | bytes 786440 | tf_op jit(solution)/shard_map/ppermute | solution.py:191
  72.7 7.1 %collective-permute-start.39 = (bf16[192,256]{1,0:T(8,128)(2,1)S(1)}, bf16[192,256]{1,0:T(8,128)(2,1)S(1)}, u32[]{:S(2)}, u32[]{:S(2)}) collective-permute-start(bf16[192,256]{1,0:T(8,128)(2,1)S(1)} %get-tuple-element.73), channel_id=1, source_target_pairs={{0,24},{4,28},{8,16},{12,20},{16,8},{20,12},{24,0},{28,4},{1,25},{... | collective-permute-start | bytes 294920 | tf_op jit(solution)/shard_map/ppermute | solution.py:191
  75.2 9.1 %collective-permute-start.15 = (bf16[128,1024]{1,0:T(8,128)(2,1)S(1)}, bf16[128,1024]{1,0:T(8,128)(2,1)S(1)}, u32[]{:S(2)}, u32[]{:S(2)}) collective-permute-start(bf16[128,1024]{1,0:T(8,128)(2,1)S(1)} %collective-permute-done.11.refs_2_), channel_id=1, source_target_pairs={{0,2},{1,3},{2,0},{3,1},{4,6},{5,7},{6,4},{7,5},{8,10},{9,11},{10,... | collective-permute-start | bytes 786440 | tf_op jit(solution)/shard_map/ppermute | solution.py:191
  79.8 9.4 %collective-permute-start.26 = (bf16[128,1024]{1,0:T(8,128)(2,1)S(1)}, bf16[128,1024]{1,0:T(8,128)(2,1)S(1)}, u32[]{:S(2)}, u32[]{:S(2)}) collective-permute-start(bf16[128,1024]{1,0:T(8,128)(2,1)S(1)} %add_convert_fusion), channel_id=1, source_target_pairs={{0,2},{1,3},{2,0},{3,1},{4,6},{5,7},{6,4},{7,5},{8,10},{9,11},{10,... | collective-permute-start | bytes 786440 | tf_op jit(solution)/shard_map/ppermute | solution.py:191
  81.4 8.4 %collective-permute-start.12 = (bf16[128,1024]{1,0:T(8,128)(2,1)S(1)}, bf16[128,1024]{1,0:T(8,128)(2,1)S(1)}, u32[]{:S(2)}, u32[]{:S(2)}) collective-permute-start(bf16[128,1024]{1,0:T(8,128)(2,1)S(1)} %collective-permute-done.11.refs_2_), channel_id=1, source_target_pairs={{0,1},{1,0},{2,3},{3,2},{4,5},{5,4},{6,7},{7,6},{8,9},{9,8},{10,11... | collective-permute-start | bytes 786440 | tf_op jit(solution)/shard_map/ppermute | solution.py:191
  81.4 10.5 %collective-permute-start.14 = (bf16[128,1024]{1,0:T(8,128)(2,1)S(1)}, bf16[128,1024]{1,0:T(8,128)(2,1)S(1)}, u32[]{:S(2)}, u32[]{:S(2)}) collective-permute-start(bf16[128,1024]{1,0:T(8,128)(2,1)S(1)} %collective-permute-done.13.refs_4_), channel_id=1, source_target_pairs={{0,1},{1,0},{2,3},{3,2},{4,5},{5,4},{6,7},{7,6},{8,9},{9,8},{10,11... | collective-permute-start | bytes 786440 | tf_op jit(solution)/shard_map/ppermute | solution.py:191
  84.3 8.5 %collective-permute-start.16 = (bf16[128,1024]{1,0:T(8,128)(2,1)S(1)}, bf16[128,1024]{1,0:T(8,128)(2,1)S(1)}, u32[]{:S(2)}, u32[]{:S(2)}) collective-permute-start(bf16[128,1024]{1,0:T(8,128)(2,1)S(1)} %collective-permute-done.15.refs_6_), channel_id=1, source_target_pairs={{0,1},{1,0},{2,3},{3,2},{4,5},{5,4},{6,7},{7,6},{8,9},{9,8},{10,11... | collective-permute-start | bytes 786440 | tf_op jit(solution)/shard_map/ppermute | solution.py:191
  84.3 10.5 %collective-permute-start.30 = (bf16[192,256]{1,0:T(8,128)(2,1)S(1)}, bf16[192,256]{1,0:T(8,128)(2,1)S(1)}, u32[]{:S(2)}, u32[]{:S(2)}) collective-permute-start(bf16[192,256]{1,0:T(8,128)(2,1)S(1)} %get-tuple-element.67), channel_id=1, source_target_pairs={{0,8},{4,12},{8,0},{12,4},{16,24},{20,28},{24,16},{28,20},{1,9},{5... | collective-permute-start | bytes 294920 | tf_op jit(solution)/shard_map/ppermute | solution.py:191
  89.3 13.3 %collective-permute-start.31 = (bf16[192,256]{1,0:T(8,128)(2,1)S(1)}, bf16[192,256]{1,0:T(8,128)(2,1)S(1)}, u32[]{:S(2)}, u32[]{:S(2)}) collective-permute-start(bf16[192,256]{1,0:T(8,128)(2,1)S(1)} %get-tuple-element.68), channel_id=1, source_target_pairs={{0,16},{4,20},{8,24},{12,28},{16,0},{20,4},{24,8},{28,12},{1,17},{... | collective-permute-start | bytes 294920 | tf_op jit(solution)/shard_map/ppermute | solution.py:191
  89.8 13.7 %collective-permute-start.32 = (bf16[192,256]{1,0:T(8,128)(2,1)S(1)}, bf16[192,256]{1,0:T(8,128)(2,1)S(1)}, u32[]{:S(2)}, u32[]{:S(2)}) collective-permute-start(bf16[192,256]{1,0:T(8,128)(2,1)S(1)} %get-tuple-element.69), channel_id=1, source_target_pairs={{0,24},{4,28},{8,16},{12,20},{16,8},{20,12},{24,0},{28,4},{1,25},{... | collective-permute-start | bytes 294920 | tf_op jit(solution)/shard_map/ppermute | solution.py:191
  91.9 13.5 %collective-permute-start.40 = (bf16[192,256]{1,0:T(8,128)(2,1)S(1)}, bf16[192,256]{1,0:T(8,128)(2,1)S(1)}, u32[]{:S(2)}, u32[]{:S(2)}) collective-permute-start(bf16[192,256]{1,0:T(8,128)(2,1)S(1)} %add_convert_fusion.1.refs_5_), channel_id=1, source_target_pairs={{0,8},{4,12},{8,0},{12,4},{16,24},{20,28},{24,16},{28,20},{1,9},{5... | collective-permute-start | bytes 294920 | tf_op jit(solution)/shard_map/ppermute | solution.py:191
  92.9 13.9 %collective-permute-start.41 = (bf16[192,256]{1,0:T(8,128)(2,1)S(1)}, bf16[192,256]{1,0:T(8,128)(2,1)S(1)}, u32[]{:S(2)}, u32[]{:S(2)}) collective-permute-start(bf16[192,256]{1,0:T(8,128)(2,1)S(1)} %add_convert_fusion.1.refs_5_), channel_id=1, source_target_pairs={{0,16},{4,20},{8,24},{12,28},{16,0},{20,4},{24,8},{28,12},{1,17},{... | collective-permute-start | bytes 294920 | tf_op jit(solution)/shard_map/ppermute | solution.py:191
  94.8 35.6 %copy-start.2 = (bf16[1024,1024]{1,0:T(8,128)(2,1)S(1)}, bf16[1024,1024]{1,0:T(8,128)(2,1)}, u32[]{:S(2)}) copy-start(bf16[1024,1024]{1,0:T(8,128)(2,1)} %wq_ref.1) | copy-start | bytes 6291460
  94.8 14.2 %collective-permute-start.42 = (bf16[192,256]{1,0:T(8,128)(2,1)S(1)}, bf16[192,256]{1,0:T(8,128)(2,1)S(1)}, u32[]{:S(2)}, u32[]{:S(2)}) collective-permute-start(bf16[192,256]{1,0:T(8,128)(2,1)S(1)} %add_convert_fusion.1.refs_5_), channel_id=1, source_target_pairs={{0,24},{4,28},{8,16},{12,20},{16,8},{20,12},{24,0},{28,4},{1,25},{... | collective-permute-start | bytes 294920 | tf_op jit(solution)/shard_map/ppermute | solution.py:191
  102.6 7.3 %collective-permute-start.27 = (bf16[128,512]{1,0:T(8,128)(2,1)S(1)}, bf16[128,512]{1,0:T(8,128)(2,1)S(1)}, u32[]{:S(2)}, u32[]{:S(2)}) collective-permute-start(bf16[128,512]{1,0:T(8,128)(2,1)S(1)} %get-tuple-element.65), channel_id=1, source_target_pairs={{0,4},{4,0},{8,12},{12,8},{16,20},{20,16},{24,28},{28,24},{1,5},{5... | collective-permute-start | bytes 393224 | tf_op jit(solution)/shard_map/ppermute | solution.py:191
  103.5 8.0 %collective-permute-start.33 = (bf16[192,256]{1,0:T(8,128)(2,1)S(1)}, bf16[192,256]{1,0:T(8,128)(2,1)S(1)}, u32[]{:S(2)}, u32[]{:S(2)}) collective-permute-start(bf16[192,256]{1,0:T(8,128)(2,1)S(1)} %add_convert_fusion.2.refs_0_), channel_id=1, source_target_pairs={{0,8},{4,12},{8,0},{12,4},{16,24},{20,28},{24,16},{28,20},{1,9},{5... | collective-permute-start | bytes 294920 | tf_op jit(solution)/shard_map/ppermute | solution.py:191
  105.4 9.8 %collective-permute-start.34 = (bf16[192,256]{1,0:T(8,128)(2,1)S(1)}, bf16[192,256]{1,0:T(8,128)(2,1)S(1)}, u32[]{:S(2)}, u32[]{:S(2)}) collective-permute-start(bf16[192,256]{1,0:T(8,128)(2,1)S(1)} %add_convert_fusion.2.refs_0_), channel_id=1, source_target_pairs={{0,16},{4,20},{8,24},{12,28},{16,0},{20,4},{24,8},{28,12},{1,17},{... | collective-permute-start | bytes 294920 | tf_op jit(solution)/shard_map/ppermute | solution.py:191
  106.8 8.4 %collective-permute-start.35 = (bf16[192,256]{1,0:T(8,128)(2,1)S(1)}, bf16[192,256]{1,0:T(8,128)(2,1)S(1)}, u32[]{:S(2)}, u32[]{:S(2)}) collective-permute-start(bf16[192,256]{1,0:T(8,128)(2,1)S(1)} %add_convert_fusion.2.refs_0_), channel_id=1, source_target_pairs={{0,24},{4,28},{8,16},{12,20},{16,8},{20,12},{24,0},{28,4},{1,25},{... | collective-permute-start | bytes 294920 | tf_op jit(solution)/shard_map/ppermute | solution.py:191
  109.0 18.1 %collective-permute-start.43 = (bf16[768,256]{1,0:T(8,128)(2,1)S(1)}, bf16[768,256]{1,0:T(8,128)(2,1)S(1)}, u32[]{:S(2)}, u32[]{:S(2)}) collective-permute-start(bf16[768,256]{1,0:T(8,128)(2,1)S(1)} %pad_maximum_fusion.1), channel_id=1, source_target_pairs={{0,4},{4,0},{8,12},{12,8},{16,20},{20,16},{24,28},{28,24},{1,5},{5... | collective-permute-start | bytes 1179656 | tf_op jit(solution)/shard_map/ppermute | solution.py:191
  109.9 9.0 %collective-permute-start.28 = (bf16[256,256]{1,0:T(8,128)(2,1)S(1)}, bf16[256,256]{1,0:T(8,128)(2,1)S(1)}, u32[]{:S(2)}, u32[]{:S(2)}) collective-permute-start(bf16[256,256]{1,0:T(8,128)(2,1)S(1)} %pad_maximum_fusion.2), channel_id=1, source_target_pairs={{0,2},{1,3},{2,0},{3,1},{4,6},{5,7},{6,4},{7,5},{8,10},{9,11},{10,... | collective-permute-start | bytes 393224 | tf_op jit(solution)/shard_map/ppermute | solution.py:191
  115.3 11.8 %collective-permute-start.36 = (bf16[768,256]{1,0:T(8,128)(2,1)S(1)}, bf16[768,256]{1,0:T(8,128)(2,1)S(1)}, u32[]{:S(2)}, u32[]{:S(2)}) collective-permute-start(bf16[768,256]{1,0:T(8,128)(2,1)S(1)} %pad_maximum_fusion), channel_id=1, source_target_pairs={{0,4},{4,0},{8,12},{12,8},{16,20},{20,16},{24,28},{28,24},{1,5},{5... | collective-permute-start | bytes 1179656 | tf_op jit(solution)/shard_map/ppermute | solution.py:191
  116.2 4.7 %collective-permute-start.44 = (bf16[128,256]{1,0:T(8,128)(2,1)S(1)}, bf16[128,256]{1,0:T(8,128)(2,1)S(1)}, u32[]{:S(2)}, u32[]{:S(2)}) collective-permute-start(bf16[128,256]{1,0:T(8,128)(2,1)S(1)} %get-tuple-element.77), channel_id=1, source_target_pairs={{0,8},{4,12},{8,0},{12,4},{16,24},{20,28},{24,16},{28,20},{1,9},{5... | collective-permute-start | bytes 196616 | tf_op jit(solution)/shard_map/ppermute | solution.py:191
  118.4 7.3 %collective-permute-start.45 = (bf16[128,256]{1,0:T(8,128)(2,1)S(1)}, bf16[128,256]{1,0:T(8,128)(2,1)S(1)}, u32[]{:S(2)}, u32[]{:S(2)}) collective-permute-start(bf16[128,256]{1,0:T(8,128)(2,1)S(1)} %get-tuple-element.78), channel_id=1, source_target_pairs={{0,16},{4,20},{8,24},{12,28},{16,0},{20,4},{24,8},{28,12},{1,17},{... | collective-permute-start | bytes 196616 | tf_op jit(solution)/shard_map/ppermute | solution.py:191
  118.9 6.8 %collective-permute-start.46 = (bf16[128,256]{1,0:T(8,128)(2,1)S(1)}, bf16[128,256]{1,0:T(8,128)(2,1)S(1)}, u32[]{:S(2)}, u32[]{:S(2)}) collective-permute-start(bf16[128,256]{1,0:T(8,128)(2,1)S(1)} %get-tuple-element.79), channel_id=1, source_target_pairs={{0,24},{4,28},{8,16},{12,20},{16,8},{20,12},{24,0},{28,4},{1,25},{... | collective-permute-start | bytes 196616 | tf_op jit(solution)/shard_map/ppermute | solution.py:191
  120.9 9.5 %collective-permute-start.29 = (bf16[512,128]{1,0:T(8,128)(2,1)S(1)}, bf16[512,128]{1,0:T(8,128)(2,1)S(1)}, u32[]{:S(2)}, u32[]{:S(2)}) collective-permute-start(bf16[512,128]{1,0:T(8,128)(2,1)S(1)} %pad_maximum_fusion.3), channel_id=1, source_target_pairs={{0,1},{1,0},{2,3},{3,2},{4,5},{5,4},{6,7},{7,6},{8,9},{9,8},{10,11... | collective-permute-start | bytes 393224 | tf_op jit(solution)/shard_map/ppermute | solution.py:191
  125.7 4.0 %collective-permute-start.47 = (bf16[128,128]{1,0:T(8,128)(2,1)S(1)}, bf16[128,128]{1,0:T(8,128)(2,1)S(1)}, u32[]{:S(2)}, u32[]{:S(2)}) collective-permute-start(bf16[128,128]{1,0:T(8,128)(2,1)S(1)} %get-tuple-element.81), channel_id=1, source_target_pairs={{0,4},{4,0},{8,12},{12,8},{16,20},{20,16},{24,28},{28,24},{1,5},{5... | collective-permute-start | bytes 98312 | tf_op jit(solution)/shard_map/ppermute | solution.py:191
  (17 other events, 14.4 us)

commit v3 on v2

--- a/solution.py
+++ b/solution.py
@@ -313,8 +313,8 @@
     return pltpu.CompilerParams(vmem_limit_bytes=limit * 1024 * 1024)
 
 
-def cost(flops, nbytes, exps=0):
-    return pl.CostEstimate(flops=flops, bytes_accessed=nbytes, transcendentals=exps)
+def cost(flops=0, nbytes=0, exps=0):
+    return pl.CostEstimate(flops=1, bytes_accessed=1, transcendentals=0)
 
 
 def like(shape, dtype=BF):
@@ -334,40 +334,62 @@
     return jnp.concatenate([x[..., span(i ^ 1)] for i in range(n)], axis=-1)
 
 
-def pack_kernel(at_ref, q_ref, g_ref, o_ref, qk_ref, qs_ref, gk_ref, gs_ref, dk_ref, ds_ref):
-    low = at_ref[0] == 0
+def whole(shape):
+    return pl.BlockSpec(shape, lambda i: (0,) * len(shape))
+
+
+X, Y, Z, CORE, SEQ = range(5)
+EXTRA = 16
+
+
+def split_parts(d):
+    high = d.astype(BF).astype(F32)
+    mid = (d - high).astype(BF).astype(F32)
+    return high, mid, d - high - mid
+
+
+def pack_kernel(at_ref, q_ref, g_ref, o_ref, qk_ref, qs_ref, gk_ref, gs_ref):
+    low = at_ref[X] == 0
+    rows = q_ref.shape[0]
     pairs = qk_ref.shape[1] // PAIR
-    for ref, keep, send, scale in ((q_ref, qk_ref, qs_ref, SCALE), (g_ref, gk_ref, gs_ref, 1.0)):
-        for p in range(pairs):
-            a, b = ref[:, span(2 * p)], ref[:, span(2 * p + 1)]
-            if scale != 1.0:
-                a, b = a * jnp.asarray(scale, BF), b * jnp.asarray(scale, BF)
-            keep[:, span(p)] = jnp.where(low, a, b)
-            send[:, span(p)] = jnp.where(low, b, a)
+    for p in range(pairs):
+        scale = jnp.asarray(SCALE, BF)
+        a, b = q_ref[:, span(2 * p)] * scale, q_ref[:, span(2 * p + 1)] * scale
+        qk_ref[:, span(p)] = jnp.where(low, a, b)
+        qs_ref[:, span(p)] = jnp.where(low, b, a)
+        a, b = g_ref[:, span(2 * p)], g_ref[:, span(2 * p + 1)]
+        gk_ref[:rows, span(p)] = jnp.where(low, a, b)
+        gs_ref[:rows, span(p)] = jnp.where(low, b, a)
     cols = (g_ref[...].astype(F32) * o_ref[...].astype(F32)).T
     for p in range(pairs):
-        for h in range(2):
-            a = jnp.sum(cols[span(4 * p + h, HD)], axis=0)
-            b = jnp.sum(cols[span(4 * p + 2 + h, HD)], axis=0)
-            dk_ref[p, h] = jnp.where(low, a, b)
-            ds_ref[p, h] = jnp.where(low, b, a)
+        both = []
+        for h in range(4):
+            both.append(split_parts(jnp.sum(cols[span(4 * p + h, HD)], axis=0, keepdims=True)))
+        pad = [jnp.zeros((EXTRA - 6, rows), F32)]
+        a = jnp.concatenate([both[h][n] for n in range(3) for h in (0, 1)] + pad, axis=0).astype(BF)
+        b = jnp.concatenate([both[h][n] for n in range(3) for h in (2, 3)] + pad, axis=0).astype(BF)
+        gk_ref[rows:, span(p)] = jnp.where(low, a, b)
+        gs_ref[rows:, span(p)] = jnp.where(low, b, a)
 
 
 def pack(at, queries, grad_out, attn_out):
     rows, cols = queries.shape
-    half, stat = like((rows, cols // 2)), like((cols // PAIR // 2, 2, rows), F32)
+    steps = 2
+    block = pl.BlockSpec((rows, cols // steps), lambda i: (0, i))
+    half = lambda n: pl.BlockSpec((n, cols // 2 // steps), lambda i: (0, i))
     return pl.pallas_call(
         pack_kernel,
-        in_specs=[SMEM] + [VMEM] * 3,
-        out_specs=[VMEM] * 6,
-        out_shape=[half] * 4 + [stat] * 2,
-        compiler_params=params(),
-        cost_estimate=cost(4 * rows * cols, 10 * rows * cols),
+        grid=(steps,),
+        in_specs=[SMEM] + [block] * 3,
+        out_specs=[half(rows)] * 2 + [half(rows + EXTRA)] * 2,
+        out_shape=[like((rows, cols // 2))] * 2 + [like((rows + EXTRA, cols // 2))] * 2,
+        compiler_params=params(),
+        cost_estimate=cost(),
     )(at, queries, grad_out, attn_out)
 
 
 def pack_tokens_kernel(at_ref, k_ref, v_ref, kp_ref, vp_ref, kt_ref):
-    low = at_ref[0] == 0
+    low = at_ref[X] == 0
     for p in range(kp_ref.shape[1] // PAIR):
         k = jnp.where(low, k_ref[:, span(2 * p)], k_ref[:, span(2 * p + 1)])
         kp_ref[:, span(p)] = k
@@ -377,20 +399,64 @@
 
 def pack_tokens(at, keys, values):
     tokens, cols = keys.shape
+    steps = 2
+    block = pl.BlockSpec((tokens, cols // steps), lambda i: (0, i))
+    half = pl.BlockSpec((tokens, cols // 2 // steps), lambda i: (0, i))
     return pl.pallas_call(
         pack_tokens_kernel,
-        in_specs=[SMEM, VMEM, VMEM],
-        out_specs=[VMEM] * 3,
+        grid=(steps,),
+        in_specs=[SMEM, block, block],
+        out_specs=[half, half, pl.BlockSpec((cols // 2 // steps, tokens), lambda i: (i, 0))],
         out_shape=[like((tokens, cols // 2))] * 2 + [like((cols // 2, tokens))],
         compiler_params=params(),
-        cost_estimate=cost(tokens * cols, 7 * tokens * cols),
+        cost_estimate=cost(),
     )(at, keys, values)
+
+
+def add_kernel(*refs):
+    total = refs[0][...].astype(F32)
+    for r in refs[1:-1]:
+        total = total + r[...].astype(F32)
+    refs[-1][...] = total.astype(BF)
+
+
+def add(*parts):
+    return pl.pallas_call(
+        add_kernel,
+        in_specs=[VMEM] * len(parts),
+        out_specs=VMEM,
+        out_shape=like(parts[0].shape),
+        compiler_params=params(),
+        cost_estimate=cost(),
+    )(*parts)
+
+
+def stack_kernel(cuts, *refs):
+    out_ref, row = refs[-1], 0
+    for r, cut in zip(refs[:-1], cuts, strict=True):
+        block = r[...] if cut is None else r[:, cut]
+        out_ref[row : row + block.shape[0], :] = block
+        row += block.shape[0]
+
+
+def stack(parts, cuts=None):
+    cuts = cuts or [None] * len(parts)
+    rows = sum(t.shape[0] for t in parts)
+    width = parts[0].shape[1] if cuts[0] is None else cuts[0].stop - cuts[0].start
+    return pl.pallas_call(
+        functools.partial(stack_kernel, cuts),
+        in_specs=[VMEM] * len(parts),
+        out_specs=VMEM,
+        out_shape=like((rows, width)),
+        compiler_params=params(),
+        cost_estimate=cost(),
+    )(*parts)
 
 
 def side_kernel(count, step, last, *refs):
     q_refs, k_ref = refs[:count], refs[count]
     if last:
-        la_ref, own_ref, got_ref, p_ref, m_ref, lse_ref, send_ref = refs[count + 1 :]
+        la_ref, p_ref, m_ref, lse_ref, send_ref = refs[count + 1 :]
     else:
         p_ref, m_ref, lse_ref = refs[count + 1 :]
     for j in range(step):
@@ -405,9 +471,7 @@
             m_ref[j, head] = top[0]
             lse_ref[j, head] = (top + jnp.log(total))[0]
     if last:
-        send_ref[...] = jnp.concatenate(
-            [flip_core(la_ref[...]), flip_core(lse_ref[...]), own_ref[...], got_ref[...]], axis=-1
-        )
+        send_ref[...] = jnp.concatenate([flip_core(la_ref[...]), flip_core(lse_ref[...])], axis=-1)
 
 
 def side_of(pieces, keys, extra=None, step=2):
@@ -422,10 +486,10 @@
     out_shape = [like((2 * pairs, tokens, rows)), like((pairs, 2, rows), F32), like((pairs, 2, rows), F32)]
     args = [*pieces, keys]
     if extra is not None:
-        in_specs += [stat_spec(rows), stat_spec(piece), stat_spec(piece)]
-        out_specs += [stat_spec(2 * rows + 2 * piece)]
-        out_shape += [like((pairs, 2, 2 * rows + 2 * piece), F32)]
-        args += extra
+        in_specs += [stat_spec(rows)]
+        out_specs += [stat_spec(2 * rows)]
+        out_shape += [like((pairs, 2, 2 * rows), F32)]
+        args += [extra]
     return pl.pallas_call(
         functools.partial(side_kernel, count, step, extra is not None),
         grid=(pairs // step,),
@@ -442,25 +506,22 @@
     return top + jnp.log(jnp.exp(a - top) + jnp.exp(b - top))
 
 
-def merge_kernel(la_ref, lb_ref, sent_ref, got_ref, send_ref):
+def merge_kernel(la_ref, lb_ref, got_ref, send_ref):
     side = la_ref.shape[2]
-    lb = log_add(lb_ref[...], got_ref[:, :, side : 2 * side])
-    la = log_add(la_ref[...], got_ref[:, :, :side])
-    own, other = sent_ref[:, :, 2 * side :], got_ref[:, :, 2 * side :]
-    deltas = [own[..., span(0)], other[..., span(0)], own[..., span(1)], other[..., span(1)]]
-    send_ref[...] = jnp.concatenate([lb, la] + deltas, axis=-1)
-
-
-def merge(la, lb, sent, got):
+    send_ref[:, :, :side] = log_add(lb_ref[...], got_ref[:, :, side:])
+    send_ref[:, :, side:] = log_add(la_ref[...], got_ref[:, :, :side])
+
+
+def merge(la, lb, got):
     pairs, two, side = la.shape
     return pl.pallas_call(
         merge_kernel,
-        in_specs=[VMEM] * 4,
+        in_specs=[VMEM] * 3,
         out_specs=VMEM,
-        out_shape=like((pairs, two, 3 * side), F32),
+        out_shape=like((pairs, two, 2 * side), F32),
         compiler_params=params(),
         cost_estimate=cost(1000, 100000),
-    )(la, lb, sent, got)
+    )(la, lb, got)
 
 
 def half_kernel(count, at_ref, *refs):
@@ -468,7 +529,7 @@
     pa_ref, pb_ref, v_ref, kt_ref, ma_ref, mb_ref, sent_ref, got_ref = refs[2 * count : 2 * count + 8]
     kv_refs, dqs_ref, dqk_ref = refs[2 * count + 8 : -2], refs[-2], refs[-1]
     side = ma_ref.shape[2]
-    z = at_ref[2]
+    z = at_ref[Z]
     v = v_ref[...]
     tokens = v.shape[0]
     dk = jnp.zeros((tokens, PAIR), F32)
@@ -478,11 +539,12 @@
     for b, p_ref, m_ref in ((0, pa_ref, ma_ref), (1, pb_ref, mb_ref)):
         lse = log_add(sent_ref[0, :, span(1 - b, side)], got_ref[0, :, span(b, side)])
         w = jnp.exp(m_ref[0] - lse)
-        delta = (got_ref if b else sent_ref)[0, :, 2 * side :]
         wide = jnp.where(first, w[0:1], w[1:2]).T
         at = slice(b * count // 2, (b + 1) * count // 2)
         q = jnp.concatenate([r[...] for r in q_refs[at]], axis=0)
-        g = jnp.concatenate([r[...] for r in g_refs[at]], axis=0)
+        g = jnp.concatenate([r[: r.shape[0] - EXTRA] for r in g_refs[at]], axis=0)
+        parts = [r[r.shape[0] - EXTRA :].astype(F32) for r in g_refs[at]]
+        delta = jnp.concatenate([d[0:2] + d[2:4] + d[4:6] for d in parts], axis=1)
         qw = (q.astype(F32) * wide).astype(BF)
         gw = (g.astype(F32) * wide).astype(BF)
         parts = []
@@ -514,13 +576,14 @@
         ref[...] = out
 
 
-def half_of(at, high, q_pieces, g_pieces, pa, pb, vp, kt, ma, mb, sent, got):
+def half_of(at, own, high, q_pieces, g_pieces, pa, pb, vp, kt, ma, mb, sent, got):
     count = len(q_pieces)
     piece, cols = q_pieces[0].shape
     tokens = vp.shape[0]
     side = ma.shape[2]
-    bit = lambda i, a: (i + 1 + a[1]) % 2
-    pair = lambda i, a: 2 * a[0] + bit(i, a)
+    bit = lambda i, a: (i + 1 + a[CORE]) % 2
+    pair = lambda i, a: 2 * (a[Y] if own else 1 - a[Y]) + bit(i, a)
+    extra_spec = pl.BlockSpec((piece + EXTRA, PAIR), lambda i, a: (0, pair(i, a)))
     row_spec = pl.BlockSpec((piece, PAIR), lambda i, a: (0, pair(i, a)))
     p_spec = pl.BlockSpec((2, tokens, side), lambda i, a: (pair(i, a), 0, 0))
     stat_spec = lambda n: pl.BlockSpec((1, 2, n), lambda i, a: (pair(i, a), 0, 0))
@@ -530,7 +593,8 @@
         grid_spec=pltpu.PrefetchScalarGridSpec(
             num_scalar_prefetch=1,
             grid=(2,),
-            in_specs=[row_spec] * (2 * count)
+            in_specs=[row_spec] * count
+            + [extra_spec] * count
             + [
                 p_spec,
                 p_spec,
@@ -538,8 +602,8 @@
                 pl.BlockSpec((PAIR, tokens), lambda i, a: (pair(i, a), 0)),
                 stat_spec(side),
                 stat_spec(side),
-                stat_spec(3 * side),
-                stat_spec(3 * side),
+                stat_spec(2 * side),
+                stat_spec(2 * side),
             ],
             out_specs=[pl.BlockSpec((block, PAIR), lambda i, a: (0, bit(i, a)))] * high
             + [pl.BlockSpec((PAIR, 2 * side), lambda i, a: (0, 0))] * 2,
@@ -564,7 +628,7 @@
     all_ref[...] = dot(dq, x, 1, 0)
     width = x.shape[1] // high
     for k, ref in enumerate(w_refs):
-        start = pl.multiple_of((at_ref[0] ^ k) * width, PAIR)
+        start = pl.multiple_of((at_ref[Z] ^ k) * width, PAIR)
         ref[...] = all_ref[:, pl.ds(start, width)].astype(BF)
 
 
@@ -584,7 +648,7 @@
 
 
 def input_kernel(at_ref, back_ref, x_ref, y_ref, core_ref, wq_ref, out_ref, dq_ref):
-    me, x = at_ref[0], at_ref[1]
+    me, x = at_ref[SEQ], at_ref[X]
     size = back_ref.shape[0]
 
     def put(group, odd, block):
@@ -620,7 +684,7 @@
     keep_ref, send_ref = refs[-2:]
     size = keep_ref.shape[1]
     a, b = total[:, :size], total[:, size:]
-    low = at_ref[0] == 0
+    low = at_ref[X] == 0
     keep_ref[...] = jnp.where(low, a, b)
     send_ref[...] = jnp.where(low, b, a).astype(BF)
 
@@ -640,7 +704,7 @@
 def weight_out_kernel(at_ref, keep_ref, got_ref, out_ref):
     size = keep_ref.shape[0]
     a, b = keep_ref[...].T, got_ref[...].astype(F32).T
-    low = at_ref[0] == 0
+    low = at_ref[X] == 0
     out_ref[:, :size] = jnp.where(low, a, b)
     out_ref[:, size:] = jnp.where(low, b, a)
 
@@ -658,7 +722,7 @@
 
 
 def tokens_kernel(high, at_ref, *refs):
-    y, x, z = at_ref[0], at_ref[1], at_ref[2]
+    y, x, z = at_ref[Y], at_ref[X], at_ref[Z]
     key_ref, val_ref = refs[-2:]
     size = refs[0].shape[0]
     each = high + 1
@@ -692,58 +756,55 @@
 def local_split(n_dp, n_seq, qx, queries, keys, values, attn_out, grad_out, wq):
     high = n_dp // 2
     dp, me = lax.axis_index("dp").astype(jnp.int32), lax.axis_index("seq").astype(jnp.int32)
-    x, z, y, c = dp % 2, dp // 2, me // 2, me % 2
+    at = jnp.stack([dp % 2, me // 2, dp // 2, me % 2, me])
     over_x = lambda t: swap(t, "dp", n_dp, 1)
     over_y = lambda t: swap(t, "seq", n_seq, 2)
     over_core = lambda t: swap(t, "seq", n_seq, 1)
     over_z = lambda t, k: swap(t, "dp", n_dp, 2 * k)
-    scalars = lambda *t: jnp.stack(t)
+    after = lambda t, *deps: lax.optimization_barrier((t, *deps))[0]
 
     def rows_of(own, from_x):
         from_y, from_xy = over_y(own), over_y(from_x)
         a = [own, over_core(own), from_x, over_core(from_x)]
         return a, [from_y, over_core(from_y), from_xy, over_core(from_xy)]
 
-    qk, qs, gk, gs, delta, delta_s = pack(scalars(x), queries, grad_out, attn_out)
-    kp, vp, kt = pack_tokens(scalars(x), keys, values)
-    qa, qb = rows_of(qk, over_x(qs))
-    ga, gb = rows_of(gk, over_x(gs))
-    delta_x = over_x(delta_s)
+    qk, qs, gk, gs = pack(at, queries, grad_out, attn_out)
+    kp, vp, kt = pack_tokens(at, keys, values)
+    q_from_x = after(over_x(qs), kp)
+    qa, qb = rows_of(qk, q_from_x)
+    ga, gb = rows_of(after(gk, q_from_x), over_x(after(gs, q_from_x)))
     pa, ma, la = side_of(qa, kp)
-    pb, mb, lb, sent = side_of(qb, kp, [la, delta, delta_x])
-    send = merge(la, lb, sent, over_core(sent))
+    pb, mb, lb, sent = side_of(qb, kp, la)
+    send = merge(la, lb, over_core(sent))
     got = over_y(send)
 
     sums, dqs = [], []
-    for half in (1 - y, y):
-        out = half_of(scalars(half, c, z), high, qa + qb, ga + gb, pa, pb, vp, kt, ma, mb, send, got)
-        total = out[0].astype(F32)
-        for k in range(1, high):
-            total = total + over_z(out[k], k).astype(F32)
-        sums.append(total.astype(BF))
+    for own in (False, True):
+        out = half_of(at, own, high, qa + qb, ga + gb, pa, pb, vp, kt, ma, mb, send, got)
+        sums.append(add(out[0], *[over_z(out[k], k) for k in range(1, high)]))
         dqs.append((out[high + 1], over_core(out[high])))
 
-    keep, core = dqs[0]
-    far = over_y((keep.astype(F32) + core.astype(F32)).astype(BF))
-    qx, got = lax.optimization_barrier((qx, got))
-    xa, xb = rows_of(qx, over_x(qx))
-    *parts, back, back_s = columns_of(scalars(z), high, xa + xb, *dqs[1], far)
+    far = over_y(add(*dqs[0]))
+    qx_from_x = over_x(after(qx, la))
+    xa, xb = rows_of(after(qx, got), after(qx_from_x, got))
+    *parts, back, back_s = columns_of(at, high, xa + xb, *dqs[1], far)
     parts = parts[:1] + [over_z(parts[k], k) for k in range(1, high)]
-    keep, send_w = weight_sum(scalars(x), parts)
-    grad_weight = weight_out(scalars(x), keep, over_x(send_w))
+    keep, send_w = weight_sum(at, parts)
+    grad_weight = weight_out(at, keep, over_x(send_w))
 
     size = back.shape[0]
     from_x = over_x(back_s)
-    from_y = over_y(jnp.concatenate([back[:, 2 * size :], from_x[:, 2 * size :]], axis=0))
-    near = [back[:, size : 2 * size], from_x[:, size : 2 * size], from_y[:, size:]]
-    from_core = over_core(jnp.concatenate(near, axis=0))
-    grad_input = input_of(scalars(me, x), back, from_x, from_y, from_core, wq)
+    far_cut = slice(2 * size, 4 * size)
+    from_y = over_y(stack([back, from_x], [far_cut, far_cut]))
+    near = slice(size, 2 * size)
+    from_core = over_core(stack([back, from_x, from_y], [near, near, near]))
+    grad_input = input_of(at, back, from_x, from_y, from_core, wq)
 
     parts = []
     for total in sums:
         blocks = [total] + [over_z(total, k) for k in range(1, high)]
-        parts += blocks + [over_x(jnp.concatenate(blocks, axis=0))]
-    grad_keys, grad_values = tokens_out(scalars(y, x, z), high, *keys.shape, parts)
+        parts += blocks + [over_x(stack(blocks))]
+    grad_keys, grad_values = tokens_out(at, high, *keys.shape, parts)
     return (grad_input, grad_keys, grad_values, grad_weight)
 
 

time: 133 us -> 126 us (0.947)
  local copies, waits for them, and re-layouts: 20.3 us -> 5.21 us
  waiting for transfers between devices: 36.1 us -> 48.2 us
  starting transfers between devices: 50.1 us -> 46.4 us
    unnamed x66 -> x14, local copies, waits for them, and re-layouts: 20.2 us -> 5.13 us
    ppermute x48 -> x47, waiting for transfers between devices: 36.1 us -> 48.2 us  [swap(): return lax.ppermute(x, axis, [(i, i ^ mask) for i in range(size)])]
    ppermute x48 -> x47, starting transfers between devices: 50.1 us -> 46.4 us  [swap(): return lax.ppermute(x, axis, [(i, i ^ mask) for i in range(size)])]
  transfers between devices with their start and end apart: 48 -> 47, of which waited for: 15 -> 16; matrix products, arithmetic and copies ran while one was open for 0% -> 0% of each run, Pallas kernels for 12% -> 18%
where the time goes in v3:
time: 126 us
  waiting for transfers between devices  48.2 us (38%)
  starting transfers between devices  46.4 us (37%)
  Pallas kernels  25.2 us (20%)
  local copies, waits for them, and re-layouts  5.21 us (4%)
    ppermute x47, waiting for transfers between devices, swap(): return lax.ppermute(x, axis, [(i, i ^ mask) for i in range(size)])  48.2 us
    ppermute x47, starting transfers between devices, swap(): return lax.ppermute(x, axis, [(i, i ^ mask) for i in range(size)])  46.4 us
    pallas_call x2, Pallas kernels, half_of(): pl.pallas_call(functools.partial(half_kernel, count), grid_spec=pltpu.Pre...  11 us
    unnamed x14, local copies, waits for them, and re-layouts  5.13 us
    pallas_call x2, Pallas kernels, side_of(): pl.pallas_call(functools.partial(side_kernel, count, step, extra is not N...  4.73 us
  transfers between devices with their start and end apart: 47, of which 16 were waited for; matrix products, arithmetic and copies ran while one was open for 0% of the time, Pallas kernels for 18%

profile of v3, /device:TPU:0, one launch (start us, length us, event | category | flops | bytes accessed | tf_op | source)
XLA Modules:
  0.0 125.9 jit_solution(15075768088911397185)
XLA Ops:
  0.8 0.9 copy-done.4
  1.7 0.9 copy-done.5
  2.7 0.9 copy-done.6
  3.6 1.0 shard_map.102
  4.6 3.0 %collective-permute-start.1 = (bf16[128,512]{1,0:T(8,128)(2,1)S(1)}, bf16[128,512]{1,0:T(8,128)(2,1)S(1)}, u32[]{:S(2)}, u32[]{:S(2)}) collective-permute-start(bf16[128,512]{1,0:T(8,128)(2,1)S(1)} %get-tuple-element.47), channel_id=1, source_target_pairs={{0,4},{4,0},{8,12},{12,8},{16,20},{20,16},{24,28},{28,24},{1,5},{5... | collective-permute-start | bytes 393224 | tf_op jit(solution)/shard_map/ppermute | solution.py:191
  7.6 1.5 %collective-permute-start.3 = (bf16[128,512]{1,0:T(8,128)(2,1)S(1)}, bf16[128,512]{1,0:T(8,128)(2,1)S(1)}, u32[]{:S(2)}, u32[]{:S(2)}) collective-permute-start(bf16[128,512]{1,0:T(8,128)(2,1)S(1)} %get-tuple-element.46.refs_0_), channel_id=1, source_target_pairs={{0,2},{1,3},{2,0},{3,1},{4,6},{5,7},{6,4},{7,5},{8,10},{9,11},{10,... | collective-permute-start | bytes 393224 | tf_op jit(solution)/shard_map/ppermute | solution.py:191
  9.1 1.1 copy-done.1
  10.3 1.1 copy-done.2
  11.4 1.1 shard_map.103
  12.5 0.6 collective-permute-start.5
  13.0 1.3 %collective-permute-start.17 = (bf16[144,512]{1,0:T(8,128)(2,1)S(1)}, bf16[144,512]{1,0:T(8,128)(2,1)S(1)}, u32[]{:S(2)}, u32[]{:S(2)}) collective-permute-start(bf16[144,512]{1,0:T(8,128)(2,1)S(1)} %get-tuple-element.59), channel_id=1, source_target_pairs={{0,4},{4,0},{8,12},{12,8},{16,20},{20,16},{24,28},{28,24},{1,5},{5... | collective-permute-start | bytes 442376 | tf_op jit(solution)/shard_map/ppermute | solution.py:191
  14.4 0.5 collective-permute-start.2
  14.9 2.6 %collective-permute-done.5.refs_2_.refs_6_ = bf16[128,512]{1,0:T(8,128)(2,1)S(1)} collective-permute-done((bf16[128,512]{1,0:T(8,128)(2,1)S(1)}, bf16[128,512]{1,0:T(8,128)(2,1)S(1)}, u32[]{:S(2)}, u32[]{:S(2)}) %collective-permute-start.5) | collective-permute-done | bytes 131104 | tf_op jit(solution)/shard_map/ppermute | solution.py:191
  17.5 0.5 collective-permute-start.19
  18.2 1.5 %collective-permute-start.21 = (bf16[144,512]{1,0:T(8,128)(2,1)S(1)}, bf16[144,512]{1,0:T(8,128)(2,1)S(1)}, u32[]{:S(2)}, u32[]{:S(2)}) collective-permute-start(bf16[144,512]{1,0:T(8,128)(2,1)S(1)} %collective-permute-done.17.refs_10_), channel_id=1, source_target_pairs={{0,2},{1,3},{2,0},{3,1},{4,6},{5,7},{6,4},{7,5},{8,10},{9,11},{10,... | collective-permute-start | bytes 442376 | tf_op jit(solution)/shard_map/ppermute | solution.py:191
  19.7 2.4 %shard_map.104 = (bf16[8,384,512]{2,1,0:T(8,128)(2,1)S(1)}, f32[4,2,512]{2,1,0:T(2,128)S(1)}, f32[4,2,512]{2,1,0:T(2,128)S(1)}) custom-call(bf16[128,512]{1,0:T(8,128)(2,1)S(1)} %get-tuple-element.46.refs_0_, bf16[128,512]{1,0:T(8,128)(2,1)S(1)} %collective-permute-done.refs_1_, bf16[128,512]{1,0:T(8,128)(2,1)S(1)} %collective-permute-done.1.refs_2_, ...), custom_call_target="tpu_custom_call" | custom-call | flops 1 | bytes 1 | tf_op jit(solution)/shard_map/pallas_call | solution.py:493
  22.1 2.4 %shard_map.105 = (bf16[8,384,512]{2,1,0:T(8,128)(2,1)S(1)}, f32[4,2,512]{2,1,0:T(2,128)S(1)}, f32[4,2,512]{2,1,0:T(2,128)S(1)}, f32[4,2,1024]{2,1,0:T(2,128)S(1)}) custom-call(bf16[128,512]{1,0:T(8,128)(2,1)S(1)} %collective-permute-done.3.refs_0_.refs_4_, bf16[128,512]{1,0:T(8,128)(2,1)S(1)} %collective-permute-done.4.refs_1_.refs_5_, ...), custom_call_target="tpu_custom_call" | custom-call | flops 1 | bytes 1 | tf_op jit(solution)/shard_map/pallas_call | solution.py:493
  24.6 0.6 collective-permute-start.10
  25.2 0.6 collective-permute-done.7.got_ref
  25.8 0.8 collective-permute-start.8
  26.6 0.5 collective-permute-start.18
  27.1 2.6 %collective-permute-done.8.refs_23_ = f32[4,2,1024]{2,1,0:T(2,128)S(1)} collective-permute-done((f32[4,2,1024]{2,1,0:T(2,128)S(1)}, f32[4,2,1024]{2,1,0:T(2,128)S(1)}, u32[]{:S(2)}, u32[]{:S(2)}) %collective-permute-start.8) | collective-permute-done | bytes 32800 | tf_op jit(solution)/shard_map/ppermute | solution.py:191
  29.8 1.3 %collective-permute-done.22.refs_15_ = bf16[144,512]{1,0:T(8,128)(2,1)S(1)} collective-permute-done((bf16[144,512]{1,0:T(8,128)(2,1)S(1)}, bf16[144,512]{1,0:T(8,128)(2,1)S(1)}, u32[]{:S(2)}, u32[]{:S(2)}) %collective-permute-start.22) | collective-permute-done | bytes 147488 | tf_op jit(solution)/shard_map/ppermute | solution.py:191
  31.1 5.5 %shard_map.107 = (bf16[192,256]{1,0:T(8,128)(2,1)S(1)}, bf16[192,256]{1,0:T(8,128)(2,1)S(1)}, bf16[192,256]{1,0:T(8,128)(2,1)S(1)}, bf16[192,256]{1,0:T(8,128)(2...) custom-call(s32[5]{0:T(128)S(1)} %stack.23.at_ref, ...), custom_call_target="tpu_custom_call" | custom-call | flops 1 | bytes 1 | tf_op jit(solution)/shard_map/pallas_call | solution.py:591
  36.6 1.6 %collective-permute-start.36 = (bf16[192,256]{1,0:T(8,128)(2,1)S(1)}, bf16[192,256]{1,0:T(8,128)(2,1)S(1)}, u32[]{:S(2)}, u32[]{:S(2)}) collective-permute-start(bf16[192,256]{1,0:T(8,128)(2,1)S(1)} %get-tuple-element.77), channel_id=1, source_target_pairs={{0,8},{4,12},{8,0},{12,4},{16,24},{20,28},{24,16},{28,20},{1,9},{5... | collective-permute-start | bytes 294920 | tf_op jit(solution)/shard_map/ppermute | solution.py:191
  38.3 2.6 %collective-permute-start.37 = (bf16[192,256]{1,0:T(8,128)(2,1)S(1)}, bf16[192,256]{1,0:T(8,128)(2,1)S(1)}, u32[]{:S(2)}, u32[]{:S(2)}) collective-permute-start(bf16[192,256]{1,0:T(8,128)(2,1)S(1)} %get-tuple-element.78), channel_id=1, source_target_pairs={{0,16},{4,20},{8,24},{12,28},{16,0},{20,4},{24,8},{28,12},{1,17},{... | collective-permute-start | bytes 294920 | tf_op jit(solution)/shard_map/ppermute | solution.py:191
  40.9 0.7 collective-permute-start.12
  41.6 0.2 collective-permute-start.38
  41.8 5.5 %shard_map.108 = (bf16[192,256]{1,0:T(8,128)(2,1)S(1)}, bf16[192,256]{1,0:T(8,128)(2,1)S(1)}, bf16[192,256]{1,0:T(8,128)(2,1)S(1)}, bf16[192,256]{1,0:T(8,128)(2...) custom-call(s32[5]{0:T(128)S(1)} %stack.23.at_ref, ...), custom_call_target="tpu_custom_call" | custom-call | flops 1 | bytes 1 | tf_op jit(solution)/shard_map/pallas_call | solution.py:591
  47.3 0.8 collective-permute-start.29
  48.1 0.7 collective-permute-done.37.refs_2_
  48.7 2.9 %collective-permute-start.30 = (bf16[192,256]{1,0:T(8,128)(2,1)S(1)}, bf16[192,256]{1,0:T(8,128)(2,1)S(1)}, u32[]{:S(2)}, u32[]{:S(2)}) collective-permute-start(bf16[192,256]{1,0:T(8,128)(2,1)S(1)} %get-tuple-element.74), channel_id=1, source_target_pairs={{0,16},{4,20},{8,24},{12,28},{16,0},{20,4},{24,8},{28,12},{1,17},{... | collective-permute-start | bytes 294920 | tf_op jit(solution)/shard_map/ppermute | solution.py:191
  51.8 0.2 collective-permute-done.29.refs_1_
  52.0 4.9 %collective-permute-start.31 = (bf16[192,256]{1,0:T(8,128)(2,1)S(1)}, bf16[192,256]{1,0:T(8,128)(2,1)S(1)}, u32[]{:S(2)}, u32[]{:S(2)}) collective-permute-start(bf16[192,256]{1,0:T(8,128)(2,1)S(1)} %get-tuple-element.75), channel_id=1, source_target_pairs={{0,24},{4,28},{8,16},{12,20},{16,8},{20,12},{24,0},{28,4},{1,25},{... | collective-permute-start | bytes 294920 | tf_op jit(solution)/shard_map/ppermute | solution.py:191
  56.9 1.4 %collective-permute-done.30.refs_2_ = bf16[192,256]{1,0:T(8,128)(2,1)S(1)} collective-permute-done((bf16[192,256]{1,0:T(8,128)(2,1)S(1)}, bf16[192,256]{1,0:T(8,128)(2,1)S(1)}, u32[]{:S(2)}, u32[]{:S(2)}) %collective-permute-start.30) | collective-permute-done | bytes 98336 | tf_op jit(solution)/shard_map/ppermute | solution.py:191
  58.3 1.3 %collective-permute-start.14 = (bf16[128,1024]{1,0:T(8,128)(2,1)S(1)}, bf16[128,1024]{1,0:T(8,128)(2,1)S(1)}, u32[]{:S(2)}, u32[]{:S(2)}) collective-permute-start(bf16[128,1024]{1,0:T(8,128)(2,1)S(1)} %collective-permute-done.10.refs_2_), channel_id=1, source_target_pairs={{0,2},{1,3},{2,0},{3,1},{4,6},{5,7},{6,4},{7,5},{8,10},{9,11},{10,... | collective-permute-start | bytes 786440 | tf_op jit(solution)/shard_map/ppermute | solution.py:191
  59.7 2.2 %collective-permute-start.39 = (bf16[192,256]{1,0:T(8,128)(2,1)S(1)}, bf16[192,256]{1,0:T(8,128)(2,1)S(1)}, u32[]{:S(2)}, u32[]{:S(2)}) collective-permute-start(bf16[192,256]{1,0:T(8,128)(2,1)S(1)} %shard_map.116.refs_0_.refs_5_), channel_id=1, source_target_pairs={{0,8},{4,12},{8,0},{12,4},{16,24},{20,28},{24,16},{28,20},{1,9},{5... | collective-permute-start | bytes 294920 | tf_op jit(solution)/shard_map/ppermute | solution.py:191
  61.9 2.1 %collective-permute-start.40 = (bf16[192,256]{1,0:T(8,128)(2,1)S(1)}, bf16[192,256]{1,0:T(8,128)(2,1)S(1)}, u32[]{:S(2)}, u32[]{:S(2)}) collective-permute-start(bf16[192,256]{1,0:T(8,128)(2,1)S(1)} %shard_map.116.refs_0_.refs_5_), channel_id=1, source_target_pairs={{0,16},{4,20},{8,24},{12,28},{16,0},{20,4},{24,8},{28,12},{1,17},{... | collective-permute-start | bytes 294920 | tf_op jit(solution)/shard_map/ppermute | solution.py:191
  64.1 0.3 collective-permute-start.41
  64.4 0.7 collective-permute-done.39.refs_1_.refs_6_
  65.1 2.5 %collective-permute-start.32 = (bf16[192,256]{1,0:T(8,128)(2,1)S(1)}, bf16[192,256]{1,0:T(8,128)(2,1)S(1)}, u32[]{:S(2)}, u32[]{:S(2)}) collective-permute-start(bf16[192,256]{1,0:T(8,128)(2,1)S(1)} %shard_map.114.refs_0_), channel_id=1, source_target_pairs={{0,8},{4,12},{8,0},{12,4},{16,24},{20,28},{24,16},{28,20},{1,9},{5... | collective-permute-start | bytes 294920 | tf_op jit(solution)/shard_map/ppermute | solution.py:191
  67.5 5.0 %collective-permute-done.40.refs_2_.refs_7_ = bf16[192,256]{1,0:T(8,128)(2,1)S(1)} collective-permute-done((bf16[192,256]{1,0:T(8,128)(2,1)S(1)}, bf16[192,256]{1,0:T(8,128)(2,1)S(1)}, u32[]{:S(2)}, u32[]{:S(2)}) %collective-permute-start.40) | collective-permute-done | bytes 98336 | tf_op jit(solution)/shard_map/ppermute | solution.py:191
  72.6 1.7 %collective-permute-start.34 = (bf16[192,256]{1,0:T(8,128)(2,1)S(1)}, bf16[192,256]{1,0:T(8,128)(2,1)S(1)}, u32[]{:S(2)}, u32[]{:S(2)}) collective-permute-start(bf16[192,256]{1,0:T(8,128)(2,1)S(1)} %shard_map.114.refs_0_), channel_id=1, source_target_pairs={{0,24},{4,28},{8,16},{12,20},{16,8},{20,12},{24,0},{28,4},{1,25},{... | collective-permute-start | bytes 294920 | tf_op jit(solution)/shard_map/ppermute | solution.py:191
  74.5 0.5 collective-permute-start.23
  75.0 5.3 %collective-permute-done.33.refs_2_ = bf16[192,256]{1,0:T(8,128)(2,1)S(1)} collective-permute-done((bf16[192,256]{1,0:T(8,128)(2,1)S(1)}, bf16[192,256]{1,0:T(8,128)(2,1)S(1)}, u32[]{:S(2)}, u32[]{:S(2)}) %collective-permute-start.33) | collective-permute-done | bytes 98336 | tf_op jit(solution)/shard_map/ppermute | solution.py:191
  80.3 0.5 collective-permute-start.15
  80.8 1.3 %collective-permute-start.25 = (bf16[128,1024]{1,0:T(8,128)(2,1)S(1)}, bf16[128,1024]{1,0:T(8,128)(2,1)S(1)}, u32[]{:S(2)}, u32[]{:S(2)}) collective-permute-start(bf16[128,1024]{1,0:T(8,128)(2,1)S(1)} %shard_map.109), channel_id=1, source_target_pairs={{0,2},{1,3},{2,0},{3,1},{4,6},{5,7},{6,4},{7,5},{8,10},{9,11},{10,... | collective-permute-start | bytes 786440 | tf_op jit(solution)/shard_map/ppermute | solution.py:191
  82.2 1.0 collective-permute-start.42
  83.2 1.1 collective-permute-start.35
  84.3 4.8 %collective-permute-done.25.refs_10_ = bf16[128,1024]{1,0:T(8,128)(2,1)S(1)} collective-permute-done((bf16[128,1024]{1,0:T(8,128)(2,1)S(1)}, bf16[128,1024]{1,0:T(8,128)(2,1)S(1)}, u32[]{:S(2)}, u32[]{:S(2)}) %collective-permute-start.25) | collective-permute-done | bytes 262176 | tf_op jit(solution)/shard_map/ppermute | solution.py:191
  89.1 1.0 shard_map.110
  90.1 1.2 collective-permute-start.26
  91.3 13.0 %collective-permute-done.26.refs_1_.x_ref = bf16[128,512]{1,0:T(8,128)(2,1)S(1)} collective-permute-done((bf16[128,512]{1,0:T(8,128)(2,1)S(1)}, bf16[128,512]{1,0:T(8,128)(2,1)S(1)}, u32[]{:S(2)}, u32[]{:S(2)}) %collective-permute-start.26) | collective-permute-done | bytes 131104 | tf_op jit(solution)/shard_map/ppermute | solution.py:191
  104.3 0.8 collective-permute-start.27
  105.1 0.7 collective-permute-start.43
  105.8 3.5 %collective-permute-done.27.refs_2_.y_ref = bf16[256,256]{1,0:T(8,128)(2,1)S(1)} collective-permute-done((bf16[256,256]{1,0:T(8,128)(2,1)S(1)}, bf16[256,256]{1,0:T(8,128)(2,1)S(1)}, u32[]{:S(2)}, u32[]{:S(2)}) %collective-permute-start.27) | collective-permute-done | bytes 131104 | tf_op jit(solution)/shard_map/ppermute | solution.py:191
  109.6 3.0 %collective-permute-start.45 = (bf16[128,256]{1,0:T(8,128)(2,1)S(1)}, bf16[128,256]{1,0:T(8,128)(2,1)S(1)}, u32[]{:S(2)}, u32[]{:S(2)}) collective-permute-start(bf16[128,256]{1,0:T(8,128)(2,1)S(1)} %get-tuple-element.85), channel_id=1, source_target_pairs={{0,24},{4,28},{8,16},{12,20},{16,8},{20,12},{24,0},{28,4},{1,25},{... | collective-permute-start | bytes 196616 | tf_op jit(solution)/shard_map/ppermute | solution.py:191
  112.7 5.3 %collective-permute-done.44.refs_2_ = bf16[128,256]{1,0:T(8,128)(2,1)S(1)} collective-permute-done((bf16[128,256]{1,0:T(8,128)(2,1)S(1)}, bf16[128,256]{1,0:T(8,128)(2,1)S(1)}, u32[]{:S(2)}, u32[]{:S(2)}) %collective-permute-start.44) | collective-permute-done | bytes 65568 | tf_op jit(solution)/shard_map/ppermute | solution.py:191
  118.0 0.6 shard_map.119
  118.6 1.0 collective-permute-start.46
  119.6 2.1 %shard_map.118 = (bf16[384,1024]{1,0:T(8,128)(2,1)}, bf16[384,1024]{1,0:T(8,128)(2,1)}) custom-call(s32[5]{0:T(128)S(1)} %stack.23.at_ref, bf16[192,256]{1,0:T(8,128)(2,1)S(1)} %shard_map.114.refs_0_, bf16[192,256]{1,0:T(8,128)(2,1)S(1)} %collective-permute-done.32.refs_1_, bf16[192,256]{1,0:T(8,128)(2,1)S(1)} %collective-permute-done.33.refs_2_, ...), custom_call_target="tpu_custom_call" | custom-call | flops 1 | bytes 1 | tf_op jit(solution)/shard_map/pallas_call | solution.py:746
  121.7 0.8 collective-permute-done.46.got_ref
  122.5 1.3 %shard_map.120 = f32[128,256]{1,0:T(8,128)} custom-call(s32[5]{0:T(128)S(1)} %stack.23.at_ref, f32[128,128]{1,0:T(8,128)S(1)} %get-tuple-element.86.keep_ref, bf16[128,128]{1,0:T(8,128)(2,1)S(1)} %collective-permute-done.46.got_ref), custom_call_target="tpu_custom_call" | custom-call | flops 1 | bytes 1 | tf_op jit(solution)/shard_map/pallas_call | solution.py:714
  123.8 2.1 %shard_map.113 = bf16[128,1024]{1,0:T(8,128)(2,1)} custom-call(s32[5]{0:T(128)S(1)} %stack.23.at_ref, bf16[128,512]{1,0:T(8,128)(2,1)S(1)} %get-tuple-element.70.refs_0_.back_ref, bf16[128,512]{1,0:T(8,128)(2,1)S(1)} %collective-permute-done.26.refs_1_.x_ref, bf16[256,256]{1,0:T(8,128)(2,1)S(1)} %collective-permute-done.27.refs_2_.y_ref, ...), custom_call_target="tpu_custom_call" | custom-call | flops 1 | bytes 1 | tf_op jit(solution)/shard_map/pallas_call | solution.py:669
  (64 shorter events, 1.3 us)
Async XLA Ops:
  0.6 23.9 %copy-start.3 = (bf16[128,1024]{1,0:T(8,128)(2,1)S(1)}, bf16[128,1024]{1,0:T(8,128)(2,1)}, u32[]{:S(2)}) copy-start(bf16[128,1024]{1,0:T(8,128)(2,1)} %refs_0_) | copy-start | bytes 786436
  0.8 1.0 copy-start.4
  1.7 0.9 copy-start.5
  2.7 0.9 copy-start.6
  4.6 7.9 %collective-permute-start.1 = (bf16[128,512]{1,0:T(8,128)(2,1)S(1)}, bf16[128,512]{1,0:T(8,128)(2,1)S(1)}, u32[]{:S(2)}, u32[]{:S(2)}) collective-permute-start(bf16[128,512]{1,0:T(8,128)(2,1)S(1)} %get-tuple-element.47), channel_id=1, source_target_pairs={{0,4},{4,0},{8,12},{12,8},{16,20},{20,16},{24,28},{28,24},{1,5},{5... | collective-permute-start | bytes 393224 | tf_op jit(solution)/shard_map/ppermute | solution.py:191
  7.6 7.3 %collective-permute-start.3 = (bf16[128,512]{1,0:T(8,128)(2,1)S(1)}, bf16[128,512]{1,0:T(8,128)(2,1)S(1)}, u32[]{:S(2)}, u32[]{:S(2)}) collective-permute-start(bf16[128,512]{1,0:T(8,128)(2,1)S(1)} %get-tuple-element.46.refs_0_), channel_id=1, source_target_pairs={{0,2},{1,3},{2,0},{3,1},{4,6},{5,7},{6,4},{7,5},{8,10},{9,11},{10,... | collective-permute-start | bytes 393224 | tf_op jit(solution)/shard_map/ppermute | solution.py:191
  9.1 1.1 copy-start.1
  10.3 1.1 copy-start.2
  12.5 5.0 %collective-permute-start.5 = (bf16[128,512]{1,0:T(8,128)(2,1)S(1)}, bf16[128,512]{1,0:T(8,128)(2,1)S(1)}, u32[]{:S(2)}, u32[]{:S(2)}) collective-permute-start(bf16[128,512]{1,0:T(8,128)(2,1)S(1)} %collective-permute-done.1.refs_2_), channel_id=1, source_target_pairs={{0,2},{1,3},{2,0},{3,1},{4,6},{5,7},{6,4},{7,5},{8,10},{9,11},{10,... | collective-permute-start | bytes 393224 | tf_op jit(solution)/shard_map/ppermute | solution.py:191
  13.0 5.1 %collective-permute-start.17 = (bf16[144,512]{1,0:T(8,128)(2,1)S(1)}, bf16[144,512]{1,0:T(8,128)(2,1)S(1)}, u32[]{:S(2)}, u32[]{:S(2)}) collective-permute-start(bf16[144,512]{1,0:T(8,128)(2,1)S(1)} %get-tuple-element.59), channel_id=1, source_target_pairs={{0,4},{4,0},{8,12},{12,8},{16,20},{20,16},{24,28},{28,24},{1,5},{5... | collective-permute-start | bytes 442376 | tf_op jit(solution)/shard_map/ppermute | solution.py:191
  14.4 3.1 %collective-permute-start = (bf16[128,512]{1,0:T(8,128)(2,1)S(1)}, bf16[128,512]{1,0:T(8,128)(2,1)S(1)}, u32[]{:S(2)}, u32[]{:S(2)}) collective-permute-start(bf16[128,512]{1,0:T(8,128)(2,1)S(1)} %get-tuple-element.46.refs_0_), channel_id=1, source_target_pairs={{0,1},{1,0},{2,3},{3,2},{4,5},{5,4},{6,7},{7,6},{8,9},{9,8},{10,11... | collective-permute-start | bytes 393224 | tf_op jit(solution)/shard_map/ppermute | solution.py:191
  14.4 5.3 %collective-permute-start.2 = (bf16[128,512]{1,0:T(8,128)(2,1)S(1)}, bf16[128,512]{1,0:T(8,128)(2,1)S(1)}, u32[]{:S(2)}, u32[]{:S(2)}) collective-permute-start(bf16[128,512]{1,0:T(8,128)(2,1)S(1)} %collective-permute-done.1.refs_2_), channel_id=1, source_target_pairs={{0,1},{1,0},{2,3},{3,2},{4,5},{5,4},{6,7},{7,6},{8,9},{9,8},{10,11... | collective-permute-start | bytes 393224 | tf_op jit(solution)/shard_map/ppermute | solution.py:191
  14.9 7.2 %collective-permute-start.4 = (bf16[128,512]{1,0:T(8,128)(2,1)S(1)}, bf16[128,512]{1,0:T(8,128)(2,1)S(1)}, u32[]{:S(2)}, u32[]{:S(2)}) collective-permute-start(bf16[128,512]{1,0:T(8,128)(2,1)S(1)} %collective-permute-done.3.refs_0_.refs_4_), channel_id=1, source_target_pairs={{0,1},{1,0},{2,3},{3,2},{4,5},{5,4},{6,7},{7,6},{8,9},{9,8},{10,11... | collective-permute-start | bytes 393224 | tf_op jit(solution)/shard_map/ppermute | solution.py:191
  17.5 4.6 %collective-permute-start.6 = (bf16[128,512]{1,0:T(8,128)(2,1)S(1)}, bf16[128,512]{1,0:T(8,128)(2,1)S(1)}, u32[]{:S(2)}, u32[]{:S(2)}) collective-permute-start(bf16[128,512]{1,0:T(8,128)(2,1)S(1)} %collective-permute-done.5.refs_2_.refs_6_), channel_id=1, source_target_pairs={{0,1},{1,0},{2,3},{3,2},{4,5},{5,4},{6,7},{7,6},{8,9},{9,8},{10,11... | collective-permute-start | bytes 393224 | tf_op jit(solution)/shard_map/ppermute | solution.py:191
  17.5 9.0 %collective-permute-start.19 = (bf16[144,512]{1,0:T(8,128)(2,1)S(1)}, bf16[144,512]{1,0:T(8,128)(2,1)S(1)}, u32[]{:S(2)}, u32[]{:S(2)}) collective-permute-start(bf16[144,512]{1,0:T(8,128)(2,1)S(1)} %get-tuple-element.57.refs_8_), channel_id=1, source_target_pairs={{0,2},{1,3},{2,0},{3,1},{4,6},{5,7},{6,4},{7,5},{8,10},{9,11},{10,... | collective-permute-start | bytes 442376 | tf_op jit(solution)/shard_map/ppermute | solution.py:191
  18.2 8.9 %collective-permute-start.21 = (bf16[144,512]{1,0:T(8,128)(2,1)S(1)}, bf16[144,512]{1,0:T(8,128)(2,1)S(1)}, u32[]{:S(2)}, u32[]{:S(2)}) collective-permute-start(bf16[144,512]{1,0:T(8,128)(2,1)S(1)} %collective-permute-done.17.refs_10_), channel_id=1, source_target_pairs={{0,2},{1,3},{2,0},{3,1},{4,6},{5,7},{6,4},{7,5},{8,10},{9,11},{10,... | collective-permute-start | bytes 442376 | tf_op jit(solution)/shard_map/ppermute | solution.py:191
  24.5 1.3 %collective-permute-start.7 = (f32[4,2,1024]{2,1,0:T(2,128)S(1)}, f32[4,2,1024]{2,1,0:T(2,128)S(1)}, u32[]{:S(2)}, u32[]{:S(2)}) collective-permute-start(f32[4,2,1024]{2,1,0:T(2,128)S(1)} %get-tuple-element.52), channel_id=1, source_target_pairs={{0,1},{1,0},{2,3},{3,2},{4,5},{5,4},{6,7},{7,6},{8,9},{9,8},{10,11... | collective-permute-start | bytes 98312 | tf_op jit(solution)/shard_map/ppermute | solution.py:191
  24.6 22.8 %collective-permute-start.10 = (bf16[128,1024]{1,0:T(8,128)(2,1)S(1)}, bf16[128,1024]{1,0:T(8,128)(2,1)S(1)}, u32[]{:S(2)}, u32[]{:S(2)}) collective-permute-start(bf16[128,1024]{1,0:T(8,128)(2,1)S(1)} %copy-done.3), channel_id=1, source_target_pairs={{0,4},{4,0},{8,12},{12,8},{16,20},{20,16},{24,28},{28,24},{1,5},{5... | collective-permute-start | bytes 786440 | tf_op jit(solution)/shard_map/ppermute | solution.py:191
  25.8 4.0 %collective-permute-start.8 = (f32[4,2,1024]{2,1,0:T(2,128)S(1)}, f32[4,2,1024]{2,1,0:T(2,128)S(1)}, u32[]{:S(2)}, u32[]{:S(2)}) collective-permute-start(f32[4,2,1024]{2,1,0:T(2,128)S(1)} %shard_map.106.refs_22_), channel_id=1, source_target_pairs={{0,2},{1,3},{2,0},{3,1},{4,6},{5,7},{6,4},{7,5},{8,10},{9,11},{10,... | collective-permute-start | bytes 98312 | tf_op jit(solution)/shard_map/ppermute | solution.py:191
  26.6 3.2 %collective-permute-start.16 = (bf16[144,512]{1,0:T(8,128)(2,1)S(1)}, bf16[144,512]{1,0:T(8,128)(2,1)S(1)}, u32[]{:S(2)}, u32[]{:S(2)}) collective-permute-start(bf16[144,512]{1,0:T(8,128)(2,1)S(1)} %get-tuple-element.57.refs_8_), channel_id=1, source_target_pairs={{0,1},{1,0},{2,3},{3,2},{4,5},{5,4},{6,7},{7,6},{8,9},{9,8},{10,11... | collective-permute-start | bytes 442376 | tf_op jit(solution)/shard_map/ppermute | solution.py:191
  26.6 3.2 %collective-permute-start.18 = (bf16[144,512]{1,0:T(8,128)(2,1)S(1)}, bf16[144,512]{1,0:T(8,128)(2,1)S(1)}, u32[]{:S(2)}, u32[]{:S(2)}) collective-permute-start(bf16[144,512]{1,0:T(8,128)(2,1)S(1)} %collective-permute-done.17.refs_10_), channel_id=1, source_target_pairs={{0,1},{1,0},{2,3},{3,2},{4,5},{5,4},{6,7},{7,6},{8,9},{9,8},{10,11... | collective-permute-start | bytes 442376 | tf_op jit(solution)/shard_map/ppermute | solution.py:191
  27.1 2.7 %collective-permute-start.20 = (bf16[144,512]{1,0:T(8,128)(2,1)S(1)}, bf16[144,512]{1,0:T(8,128)(2,1)S(1)}, u32[]{:S(2)}, u32[]{:S(2)}) collective-permute-start(bf16[144,512]{1,0:T(8,128)(2,1)S(1)} %collective-permute-done.19.refs_12_), channel_id=1, source_target_pairs={{0,1},{1,0},{2,3},{3,2},{4,5},{5,4},{6,7},{7,6},{8,9},{9,8},{10,11... | collective-permute-start | bytes 442376 | tf_op jit(solution)/shard_map/ppermute | solution.py:191
  29.8 1.4 %collective-permute-start.22 = (bf16[144,512]{1,0:T(8,128)(2,1)S(1)}, bf16[144,512]{1,0:T(8,128)(2,1)S(1)}, u32[]{:S(2)}, u32[]{:S(2)}) collective-permute-start(bf16[144,512]{1,0:T(8,128)(2,1)S(1)} %collective-permute-done.21.refs_14_), channel_id=1, source_target_pairs={{0,1},{1,0},{2,3},{3,2},{4,5},{5,4},{6,7},{7,6},{8,9},{9,8},{10,11... | collective-permute-start | bytes 442376 | tf_op jit(solution)/shard_map/ppermute | solution.py:191
  36.6 11.4 %collective-permute-start.36 = (bf16[192,256]{1,0:T(8,128)(2,1)S(1)}, bf16[192,256]{1,0:T(8,128)(2,1)S(1)}, u32[]{:S(2)}, u32[]{:S(2)}) collective-permute-start(bf16[192,256]{1,0:T(8,128)(2,1)S(1)} %get-tuple-element.77), channel_id=1, source_target_pairs={{0,8},{4,12},{8,0},{12,4},{16,24},{20,28},{24,16},{28,20},{1,9},{5... | collective-permute-start | bytes 294920 | tf_op jit(solution)/shard_map/ppermute | solution.py:191
  38.3 10.5 %collective-permute-start.37 = (bf16[192,256]{1,0:T(8,128)(2,1)S(1)}, bf16[192,256]{1,0:T(8,128)(2,1)S(1)}, u32[]{:S(2)}, u32[]{:S(2)}) collective-permute-start(bf16[192,256]{1,0:T(8,128)(2,1)S(1)} %get-tuple-element.78), channel_id=1, source_target_pairs={{0,16},{4,20},{8,24},{12,28},{16,0},{20,4},{24,8},{28,12},{1,17},{... | collective-permute-start | bytes 294920 | tf_op jit(solution)/shard_map/ppermute | solution.py:191
  40.9 21.0 %collective-permute-start.12 = (bf16[128,1024]{1,0:T(8,128)(2,1)S(1)}, bf16[128,1024]{1,0:T(8,128)(2,1)S(1)}, u32[]{:S(2)}, u32[]{:S(2)}) collective-permute-start(bf16[128,1024]{1,0:T(8,128)(2,1)S(1)} %copy-done.3), channel_id=1, source_target_pairs={{0,2},{1,3},{2,0},{3,1},{4,6},{5,7},{6,4},{7,5},{8,10},{9,11},{10,... | collective-permute-start | bytes 786440 | tf_op jit(solution)/shard_map/ppermute | solution.py:191
  41.6 10.1 %collective-permute-start.38 = (bf16[192,256]{1,0:T(8,128)(2,1)S(1)}, bf16[192,256]{1,0:T(8,128)(2,1)S(1)}, u32[]{:S(2)}, u32[]{:S(2)}) collective-permute-start(bf16[192,256]{1,0:T(8,128)(2,1)S(1)} %get-tuple-element.79), channel_id=1, source_target_pairs={{0,24},{4,28},{8,16},{12,20},{16,8},{20,12},{24,0},{28,4},{1,25},{... | collective-permute-start | bytes 294920 | tf_op jit(solution)/shard_map/ppermute | solution.py:191
  47.3 4.7 %collective-permute-start.29 = (bf16[192,256]{1,0:T(8,128)(2,1)S(1)}, bf16[192,256]{1,0:T(8,128)(2,1)S(1)}, u32[]{:S(2)}, u32[]{:S(2)}) collective-permute-start(bf16[192,256]{1,0:T(8,128)(2,1)S(1)} %get-tuple-element.73), channel_id=1, source_target_pairs={{0,8},{4,12},{8,0},{12,4},{16,24},{20,28},{24,16},{28,20},{1,9},{5... | collective-permute-start | bytes 294920 | tf_op jit(solution)/shard_map/ppermute | solution.py:191
  48.1 16.0 %collective-permute-start.9 = (bf16[128,1024]{1,0:T(8,128)(2,1)S(1)}, bf16[128,1024]{1,0:T(8,128)(2,1)S(1)}, u32[]{:S(2)}, u32[]{:S(2)}) collective-permute-start(bf16[128,1024]{1,0:T(8,128)(2,1)S(1)} %copy-done.3), channel_id=1, source_target_pairs={{0,1},{1,0},{2,3},{3,2},{4,5},{5,4},{6,7},{7,6},{8,9},{9,8},{10,11... | collective-permute-start | bytes 786440 | tf_op jit(solution)/shard_map/ppermute | solution.py:191
  48.7 9.5 %collective-permute-start.30 = (bf16[192,256]{1,0:T(8,128)(2,1)S(1)}, bf16[192,256]{1,0:T(8,128)(2,1)S(1)}, u32[]{:S(2)}, u32[]{:S(2)}) collective-permute-start(bf16[192,256]{1,0:T(8,128)(2,1)S(1)} %get-tuple-element.74), channel_id=1, source_target_pairs={{0,16},{4,20},{8,24},{12,28},{16,0},{20,4},{24,8},{28,12},{1,17},{... | collective-permute-start | bytes 294920 | tf_op jit(solution)/shard_map/ppermute | solution.py:191
  51.6 21.0 %collective-permute-start.24 = (bf16[128,1024]{1,0:T(8,128)(2,1)S(1)}, bf16[128,1024]{1,0:T(8,128)(2,1)S(1)}, u32[]{:S(2)}, u32[]{:S(2)}) collective-permute-start(bf16[128,1024]{1,0:T(8,128)(2,1)S(1)} %get-tuple-element.69), channel_id=1, source_target_pairs={{0,1},{1,0},{2,3},{3,2},{4,5},{5,4},{6,7},{7,6},{8,9},{9,8},{10,11... | collective-permute-start | bytes 786440 | tf_op jit(solution)/shard_map/ppermute | solution.py:191
  52.0 7.7 %collective-permute-start.31 = (bf16[192,256]{1,0:T(8,128)(2,1)S(1)}, bf16[192,256]{1,0:T(8,128)(2,1)S(1)}, u32[]{:S(2)}, u32[]{:S(2)}) collective-permute-start(bf16[192,256]{1,0:T(8,128)(2,1)S(1)} %get-tuple-element.75), channel_id=1, source_target_pairs={{0,24},{4,28},{8,16},{12,20},{16,8},{20,12},{24,0},{28,4},{1,25},{... | collective-permute-start | bytes 294920 | tf_op jit(solution)/shard_map/ppermute | solution.py:191
  58.3 22.0 %collective-permute-start.14 = (bf16[128,1024]{1,0:T(8,128)(2,1)S(1)}, bf16[128,1024]{1,0:T(8,128)(2,1)S(1)}, u32[]{:S(2)}, u32[]{:S(2)}) collective-permute-start(bf16[128,1024]{1,0:T(8,128)(2,1)S(1)} %collective-permute-done.10.refs_2_), channel_id=1, source_target_pairs={{0,2},{1,3},{2,0},{3,1},{4,6},{5,7},{6,4},{7,5},{8,10},{9,11},{10,... | collective-permute-start | bytes 786440 | tf_op jit(solution)/shard_map/ppermute | solution.py:191
  59.7 5.4 %collective-permute-start.39 = (bf16[192,256]{1,0:T(8,128)(2,1)S(1)}, bf16[192,256]{1,0:T(8,128)(2,1)S(1)}, u32[]{:S(2)}, u32[]{:S(2)}) collective-permute-start(bf16[192,256]{1,0:T(8,128)(2,1)S(1)} %shard_map.116.refs_0_.refs_5_), channel_id=1, source_target_pairs={{0,8},{4,12},{8,0},{12,4},{16,24},{20,28},{24,16},{28,20},{1,9},{5... | collective-permute-start | bytes 294920 | tf_op jit(solution)/shard_map/ppermute | solution.py:191
  61.9 10.7 %collective-permute-start.40 = (bf16[192,256]{1,0:T(8,128)(2,1)S(1)}, bf16[192,256]{1,0:T(8,128)(2,1)S(1)}, u32[]{:S(2)}, u32[]{:S(2)}) collective-permute-start(bf16[192,256]{1,0:T(8,128)(2,1)S(1)} %shard_map.116.refs_0_.refs_5_), channel_id=1, source_target_pairs={{0,16},{4,20},{8,24},{12,28},{16,0},{20,4},{24,8},{28,12},{1,17},{... | collective-permute-start | bytes 294920 | tf_op jit(solution)/shard_map/ppermute | solution.py:191
  64.1 10.3 %collective-permute-start.41 = (bf16[192,256]{1,0:T(8,128)(2,1)S(1)}, bf16[192,256]{1,0:T(8,128)(2,1)S(1)}, u32[]{:S(2)}, u32[]{:S(2)}) collective-permute-start(bf16[192,256]{1,0:T(8,128)(2,1)S(1)} %shard_map.116.refs_0_.refs_5_), channel_id=1, source_target_pairs={{0,24},{4,28},{8,16},{12,20},{16,8},{20,12},{24,0},{28,4},{1,25},{... | collective-permute-start | bytes 294920 | tf_op jit(solution)/shard_map/ppermute | solution.py:191
  65.1 9.4 %collective-permute-start.32 = (bf16[192,256]{1,0:T(8,128)(2,1)S(1)}, bf16[192,256]{1,0:T(8,128)(2,1)S(1)}, u32[]{:S(2)}, u32[]{:S(2)}) collective-permute-start(bf16[192,256]{1,0:T(8,128)(2,1)S(1)} %shard_map.114.refs_0_), channel_id=1, source_target_pairs={{0,8},{4,12},{8,0},{12,4},{16,24},{20,28},{24,16},{28,20},{1,9},{5... | collective-permute-start | bytes 294920 | tf_op jit(solution)/shard_map/ppermute | solution.py:191
  72.6 7.7 %collective-permute-start.33 = (bf16[192,256]{1,0:T(8,128)(2,1)S(1)}, bf16[192,256]{1,0:T(8,128)(2,1)S(1)}, u32[]{:S(2)}, u32[]{:S(2)}) collective-permute-start(bf16[192,256]{1,0:T(8,128)(2,1)S(1)} %shard_map.114.refs_0_), channel_id=1, source_target_pairs={{0,16},{4,20},{8,24},{12,28},{16,0},{20,4},{24,8},{28,12},{1,17},{... | collective-permute-start | bytes 294920 | tf_op jit(solution)/shard_map/ppermute | solution.py:191
  72.6 8.2 %collective-permute-start.34 = (bf16[192,256]{1,0:T(8,128)(2,1)S(1)}, bf16[192,256]{1,0:T(8,128)(2,1)S(1)}, u32[]{:S(2)}, u32[]{:S(2)}) collective-permute-start(bf16[192,256]{1,0:T(8,128)(2,1)S(1)} %shard_map.114.refs_0_), channel_id=1, source_target_pairs={{0,24},{4,28},{8,16},{12,20},{16,8},{20,12},{24,0},{28,4},{1,25},{... | collective-permute-start | bytes 294920 | tf_op jit(solution)/shard_map/ppermute | solution.py:191
  74.4 7.8 %collective-permute-start.11 = (bf16[128,1024]{1,0:T(8,128)(2,1)S(1)}, bf16[128,1024]{1,0:T(8,128)(2,1)S(1)}, u32[]{:S(2)}, u32[]{:S(2)}) collective-permute-start(bf16[128,1024]{1,0:T(8,128)(2,1)S(1)} %collective-permute-done.10.refs_2_), channel_id=1, source_target_pairs={{0,1},{1,0},{2,3},{3,2},{4,5},{5,4},{6,7},{7,6},{8,9},{9,8},{10,11... | collective-permute-start | bytes 786440 | tf_op jit(solution)/shard_map/ppermute | solution.py:191
  74.5 8.7 %collective-permute-start.23 = (bf16[128,1024]{1,0:T(8,128)(2,1)S(1)}, bf16[128,1024]{1,0:T(8,128)(2,1)S(1)}, u32[]{:S(2)}, u32[]{:S(2)}) collective-permute-start(bf16[128,1024]{1,0:T(8,128)(2,1)S(1)} %get-tuple-element.67), channel_id=1, source_target_pairs={{0,1},{1,0},{2,3},{3,2},{4,5},{5,4},{6,7},{7,6},{8,9},{9,8},{10,11... | collective-permute-start | bytes 786440 | tf_op jit(solution)/shard_map/ppermute | solution.py:191
  80.3 4.0 %collective-permute-start.13 = (bf16[128,1024]{1,0:T(8,128)(2,1)S(1)}, bf16[128,1024]{1,0:T(8,128)(2,1)S(1)}, u32[]{:S(2)}, u32[]{:S(2)}) collective-permute-start(bf16[128,1024]{1,0:T(8,128)(2,1)S(1)} %collective-permute-done.12.refs_4_), channel_id=1, source_target_pairs={{0,1},{1,0},{2,3},{3,2},{4,5},{5,4},{6,7},{7,6},{8,9},{9,8},{10,11... | collective-permute-start | bytes 786440 | tf_op jit(solution)/shard_map/ppermute | solution.py:191
  80.3 4.0 %collective-permute-start.15 = (bf16[128,1024]{1,0:T(8,128)(2,1)S(1)}, bf16[128,1024]{1,0:T(8,128)(2,1)S(1)}, u32[]{:S(2)}, u32[]{:S(2)}) collective-permute-start(bf16[128,1024]{1,0:T(8,128)(2,1)S(1)} %collective-permute-done.14.refs_6_), channel_id=1, source_target_pairs={{0,1},{1,0},{2,3},{3,2},{4,5},{5,4},{6,7},{7,6},{8,9},{9,8},{10,11... | collective-permute-start | bytes 786440 | tf_op jit(solution)/shard_map/ppermute | solution.py:191
  80.8 8.3 %collective-permute-start.25 = (bf16[128,1024]{1,0:T(8,128)(2,1)S(1)}, bf16[128,1024]{1,0:T(8,128)(2,1)S(1)}, u32[]{:S(2)}, u32[]{:S(2)}) collective-permute-start(bf16[128,1024]{1,0:T(8,128)(2,1)S(1)} %shard_map.109), channel_id=1, source_target_pairs={{0,2},{1,3},{2,0},{3,1},{4,6},{5,7},{6,4},{7,5},{8,10},{9,11},{10,... | collective-permute-start | bytes 786440 | tf_op jit(solution)/shard_map/ppermute | solution.py:191
  82.1 41.7 %copy-start = (bf16[1024,1024]{1,0:T(8,128)(2,1)S(1)}, bf16[1024,1024]{1,0:T(8,128)(2,1)}, u32[]{:S(2)}) copy-start(bf16[1024,1024]{1,0:T(8,128)(2,1)} %wq_ref.1) | copy-start | bytes 6291460
  82.2 37.4 %collective-permute-start.42 = (bf16[768,256]{1,0:T(8,128)(2,1)S(1)}, bf16[768,256]{1,0:T(8,128)(2,1)S(1)}, u32[]{:S(2)}, u32[]{:S(2)}) collective-permute-start(bf16[768,256]{1,0:T(8,128)(2,1)S(1)} %shard_map.117), channel_id=1, source_target_pairs={{0,4},{4,0},{8,12},{12,8},{16,20},{20,16},{24,28},{28,24},{1,5},{5... | collective-permute-start | bytes 1179656 | tf_op jit(solution)/shard_map/ppermute | solution.py:191
  83.2 36.4 %collective-permute-start.35 = (bf16[768,256]{1,0:T(8,128)(2,1)S(1)}, bf16[768,256]{1,0:T(8,128)(2,1)S(1)}, u32[]{:S(2)}, u32[]{:S(2)}) collective-permute-start(bf16[768,256]{1,0:T(8,128)(2,1)S(1)} %shard_map.115), channel_id=1, source_target_pairs={{0,4},{4,0},{8,12},{12,8},{16,20},{20,16},{24,28},{28,24},{1,5},{5... | collective-permute-start | bytes 1179656 | tf_op jit(solution)/shard_map/ppermute | solution.py:191
  90.1 14.2 %collective-permute-start.26 = (bf16[128,512]{1,0:T(8,128)(2,1)S(1)}, bf16[128,512]{1,0:T(8,128)(2,1)S(1)}, u32[]{:S(2)}, u32[]{:S(2)}) collective-permute-start(bf16[128,512]{1,0:T(8,128)(2,1)S(1)} %get-tuple-element.71), channel_id=1, source_target_pairs={{0,4},{4,0},{8,12},{12,8},{16,20},{20,16},{24,28},{28,24},{1,5},{5... | collective-permute-start | bytes 393224 | tf_op jit(solution)/shard_map/ppermute | solution.py:191
  104.3 5.0 %collective-permute-start.27 = (bf16[256,256]{1,0:T(8,128)(2,1)S(1)}, bf16[256,256]{1,0:T(8,128)(2,1)S(1)}, u32[]{:S(2)}, u32[]{:S(2)}) collective-permute-start(bf16[256,256]{1,0:T(8,128)(2,1)S(1)} %shard_map.111), channel_id=1, source_target_pairs={{0,2},{1,3},{2,0},{3,1},{4,6},{5,7},{6,4},{7,5},{8,10},{9,11},{10,... | collective-permute-start | bytes 393224 | tf_op jit(solution)/shard_map/ppermute | solution.py:191
  105.1 4.6 %collective-permute-start.43 = (bf16[128,256]{1,0:T(8,128)(2,1)S(1)}, bf16[128,256]{1,0:T(8,128)(2,1)S(1)}, u32[]{:S(2)}, u32[]{:S(2)}) collective-permute-start(bf16[128,256]{1,0:T(8,128)(2,1)S(1)} %get-tuple-element.83), channel_id=1, source_target_pairs={{0,8},{4,12},{8,0},{12,4},{16,24},{20,28},{24,16},{28,20},{1,9},{5... | collective-permute-start | bytes 196616 | tf_op jit(solution)/shard_map/ppermute | solution.py:191
  109.4 14.5 %collective-permute-start.28 = (bf16[512,128]{1,0:T(8,128)(2,1)S(1)}, bf16[512,128]{1,0:T(8,128)(2,1)S(1)}, u32[]{:S(2)}, u32[]{:S(2)}) collective-permute-start(bf16[512,128]{1,0:T(8,128)(2,1)S(1)} %shard_map.112), channel_id=1, source_target_pairs={{0,1},{1,0},{2,3},{3,2},{4,5},{5,4},{6,7},{7,6},{8,9},{9,8},{10,11... | collective-permute-start | bytes 393224 | tf_op jit(solution)/shard_map/ppermute | solution.py:191
  109.5 8.5 %collective-permute-start.44 = (bf16[128,256]{1,0:T(8,128)(2,1)S(1)}, bf16[128,256]{1,0:T(8,128)(2,1)S(1)}, u32[]{:S(2)}, u32[]{:S(2)}) collective-permute-start(bf16[128,256]{1,0:T(8,128)(2,1)S(1)} %get-tuple-element.84), channel_id=1, source_target_pairs={{0,16},{4,20},{8,24},{12,28},{16,0},{20,4},{24,8},{28,12},{1,17},{... | collective-permute-start | bytes 196616 | tf_op jit(solution)/shard_map/ppermute | solution.py:191
  109.6 8.3 %collective-permute-start.45 = (bf16[128,256]{1,0:T(8,128)(2,1)S(1)}, bf16[128,256]{1,0:T(8,128)(2,1)S(1)}, u32[]{:S(2)}, u32[]{:S(2)}) collective-permute-start(bf16[128,256]{1,0:T(8,128)(2,1)S(1)} %get-tuple-element.85), channel_id=1, source_target_pairs={{0,24},{4,28},{8,16},{12,20},{16,8},{20,12},{24,0},{28,4},{1,25},{... | collective-permute-start | bytes 196616 | tf_op jit(solution)/shard_map/ppermute | solution.py:191
  118.6 4.0 %collective-permute-start.46 = (bf16[128,128]{1,0:T(8,128)(2,1)S(1)}, bf16[128,128]{1,0:T(8,128)(2,1)S(1)}, u32[]{:S(2)}, u32[]{:S(2)}) collective-permute-start(bf16[128,128]{1,0:T(8,128)(2,1)S(1)} %get-tuple-element.87), channel_id=1, source_target_pairs={{0,4},{4,0},{8,12},{12,8},{16,20},{20,16},{24,28},{28,24},{1,5},{5... | collective-permute-start | bytes 98312 | tf_op jit(solution)/shard_map/ppermute | solution.py:191

commit v4 on v3

--- a/solution.py
+++ b/solution.py
@@ -340,6 +340,7 @@
 
 X, Y, Z, CORE, SEQ = range(5)
 EXTRA = 16
+ORDERS = ((0, 2), (1, 3))
 
 
 def split_parts(d):
@@ -383,7 +384,7 @@
         in_specs=[SMEM] + [block] * 3,
         out_specs=[half(rows)] * 2 + [half(rows + EXTRA)] * 2,
         out_shape=[like((rows, cols // 2))] * 2 + [like((rows + EXTRA, cols // 2))] * 2,
-        compiler_params=params(),
+        compiler_params=params(60),
         cost_estimate=cost(),
     )(at, queries, grad_out, attn_out)
 
@@ -431,18 +432,36 @@
     )(*parts)
 
 
+def add_turned_kernel(own_ref, got_ref, out_ref):
+    rows = own_ref.shape[0] // 2
+    for n in range(2):
+        total = own_ref[span(n, rows)].astype(F32) + got_ref[span(1 - n, rows)].astype(F32)
+        out_ref[span(n, rows)] = total.astype(BF)
+
+
+def add_turned(own, got):
+    return pl.pallas_call(
+        add_turned_kernel,
+        in_specs=[VMEM] * 2,
+        out_specs=VMEM,
+        out_shape=like(own.shape),
+        compiler_params=params(),
+        cost_estimate=cost(),
+    )(own, got)
+
+
 def stack_kernel(cuts, *refs):
     out_ref, row = refs[-1], 0
     for r, cut in zip(refs[:-1], cuts, strict=True):
-        block = r[...] if cut is None else r[:, cut]
+        block = r[...] if cut is None else r[cut]
         out_ref[row : row + block.shape[0], :] = block
         row += block.shape[0]
 
 
 def stack(parts, cuts=None):
     cuts = cuts or [None] * len(parts)
-    rows = sum(t.shape[0] for t in parts)
-    width = parts[0].shape[1] if cuts[0] is None else cuts[0].stop - cuts[0].start
+    shapes = [jax.eval_shape(lambda t, c=c: t if c is None else t[c], t).shape for t, c in zip(parts, cuts, strict=True)]
+    rows, width = sum(t[0] for t in shapes), shapes[0][1]
     return pl.pallas_call(
         functools.partial(stack_kernel, cuts),
         in_specs=[VMEM] * len(parts),
@@ -568,15 +587,16 @@
         dqk_ref[...] = dq
 
     both = jnp.concatenate([dk.astype(BF), dv.astype(BF)], axis=0)
-    size = both.shape[0] // len(kv_refs)
-    for k, ref in enumerate(kv_refs):
-        out = both[:size]
-        for j in range(1, len(kv_refs)):
-            out = jnp.where((z ^ k) == j, both[span(j, size)], out)
-        ref[...] = out
-
-
-def half_of(at, own, high, q_pieces, g_pieces, pa, pb, vp, kt, ma, mb, sent, got):
+    size = both.shape[0] // 4
+    for ref, order in zip(kv_refs, ORDERS, strict=True):
+        for n, k in enumerate(order):
+            out = both[:size]
+            for j in range(1, 4):
+                out = jnp.where((z ^ k) == j, both[span(j, size)], out)
+            ref[span(n, size)] = out
+
+
+def half_of(at, own, q_pieces, g_pieces, pa, pb, vp, kt, ma, mb, sent, got):
     count = len(q_pieces)
     piece, cols = q_pieces[0].shape
     tokens = vp.shape[0]
@@ -587,7 +607,7 @@
     row_spec = pl.BlockSpec((piece, PAIR), lambda i, a: (0, pair(i, a)))
     p_spec = pl.BlockSpec((2, tokens, side), lambda i, a: (pair(i, a), 0, 0))
     stat_spec = lambda n: pl.BlockSpec((1, 2, n), lambda i, a: (pair(i, a), 0, 0))
-    block = 2 * tokens // high
+    block = tokens
     return pl.pallas_call(
         functools.partial(half_kernel, count),
         grid_spec=pltpu.PrefetchScalarGridSpec(
@@ -605,10 +625,10 @@
                 stat_spec(2 * side),
                 stat_spec(2 * side),
             ],
-            out_specs=[pl.BlockSpec((block, PAIR), lambda i, a: (0, bit(i, a)))] * high
+            out_specs=[pl.BlockSpec((block, PAIR), lambda i, a: (0, bit(i, a)))] * 2
             + [pl.BlockSpec((PAIR, 2 * side), lambda i, a: (0, 0))] * 2,
         ),
-        out_shape=[like((block, 2 * PAIR))] * high + [like((PAIR, 2 * side))] * 2,
+        out_shape=[like((block, 2 * PAIR))] * 2 + [like((PAIR, 2 * side))] * 2,
         compiler_params=params(),
         cost_estimate=cost(16 * side * tokens * 2 * PAIR * 2, 8 * side * tokens * 2, 0),
     )(at, *q_pieces, *g_pieces, pa, pb, vp, kt, ma, mb, sent, got)
@@ -627,9 +647,10 @@
     x = jnp.concatenate([r[...] for r in x_refs], axis=0)
     all_ref[...] = dot(dq, x, 1, 0)
     width = x.shape[1] // high
-    for k, ref in enumerate(w_refs):
-        start = pl.multiple_of((at_ref[Z] ^ k) * width, PAIR)
-        ref[...] = all_ref[:, pl.ds(start, width)].astype(BF)
+    for ref, order in zip(w_refs, ORDERS, strict=True):
+        for n, k in enumerate(order):
+            start = pl.multiple_of((at_ref[Z] ^ k) * width, PAIR)
+            ref[span(n, ref.shape[0] // 2)] = all_ref[:, pl.ds(start, width)].astype(BF)
 
 
 def columns_of(at, high, x_pieces, keep, core, y):
@@ -639,8 +660,8 @@
     return pl.pallas_call(
         functools.partial(columns_kernel, count, high),
         in_specs=[SMEM] + [VMEM] * (count + 3),
-        out_specs=[VMEM] * (high + 2),
-        out_shape=[like((width, cols // high))] * high + [like((width, rows // 2))] * 2,
+        out_specs=[VMEM] * 4,
+        out_shape=[like((2 * width, cols // high))] * 2 + [like((width, rows // 2))] * 2,
         scratch_shapes=[pltpu.VMEM((width, cols), F32)],
         compiler_params=params(),
         cost_estimate=cost(2 * rows * cols * width, 2 * rows * cols),
@@ -677,11 +698,26 @@
     )(at, back, x, y, core, wq)
 
 
-def weight_sum_kernel(at_ref, *refs):
-    total = refs[0][...].astype(F32)
-    for r in refs[1:-2]:
-        total = total + r[...].astype(F32)
-    keep_ref, send_ref = refs[-2:]
+def weight_near_kernel(own_ref, got_ref, keep_ref, send_ref):
+    rows = keep_ref.shape[0]
+    keep_ref[...] = own_ref[:rows].astype(F32) + got_ref[:rows].astype(F32)
+    send_ref[...] = (own_ref[rows:].astype(F32) + got_ref[rows:].astype(F32)).astype(BF)
+
+
+def weight_near(own, got):
+    rows, cols = own.shape[0] // 2, own.shape[1]
+    return pl.pallas_call(
+        weight_near_kernel,
+        in_specs=[VMEM] * 2,
+        out_specs=[VMEM] * 2,
+        out_shape=[like((rows, cols), F32), like((rows, cols))],
+        compiler_params=params(),
+        cost_estimate=cost(),
+    )(own, got)
+
+
+def weight_sum_kernel(at_ref, own_ref, got_ref, keep_ref, send_ref):
+    total = own_ref[...] + got_ref[...].astype(F32)
     size = keep_ref.shape[1]
     a, b = total[:, :size], total[:, size:]
     low = at_ref[X] == 0
@@ -689,16 +725,16 @@
     send_ref[...] = jnp.where(low, b, a).astype(BF)
 
 
-def weight_sum(at, parts):
-    rows, cols = parts[0].shape
+def weight_sum(at, own, got):
+    rows, cols = own.shape
     return pl.pallas_call(
         weight_sum_kernel,
-        in_specs=[SMEM] + [VMEM] * len(parts),
+        in_specs=[SMEM, VMEM, VMEM],
         out_specs=[VMEM] * 2,
         out_shape=[like((rows, cols // 2), F32), like((rows, cols // 2))],
         compiler_params=params(),
-        cost_estimate=cost(1000, 300000),
-    )(at, *parts)
+        cost_estimate=cost(),
+    )(at, own, got)
 
 
 def weight_out_kernel(at_ref, keep_ref, got_ref, out_ref):
@@ -721,35 +757,35 @@
     )(at, keep, got)
 
 
-def tokens_kernel(high, at_ref, *refs):
+def tokens_kernel(at_ref, *refs):
     y, x, z = at_ref[Y], at_ref[X], at_ref[Z]
     key_ref, val_ref = refs[-2:]
-    size = refs[0].shape[0]
-    each = high + 1
+    size = refs[0].shape[0] // 2
     for half in range(2):
         group = 2 * (y ^ (1 - half))
-        own, got = refs[half * each : half * each + high], refs[half * each + high]
-        for k in range(high):
+        keep, near, got = refs[3 * half : 3 * half + 3]
+        for i, k in enumerate(ORDERS[0] + ORDERS[1]):
             b = z ^ k
-            row = pl.multiple_of((b % (high // 2)) * size, 16)
+            row = pl.multiple_of((b % 2) * size, 16)
+            own = (keep if i < 2 else near)[span(i % 2, size)]
             for out_ref, which in ((key_ref, 0), (val_ref, 1)):
 
-                @pl.when(b // (high // 2) == which)
+                @pl.when(b // 2 == which)
                 def _():
                     for c in range(2):
-                        for odd, block in ((0, own[k][:, span(c)]), (1, got[span(k, size), span(c)])):
+                        for odd, block in ((0, own[:, span(c)]), (1, got[span(i, size), span(c)])):
                             col = pl.multiple_of((2 * (group + c) + (x ^ odd)) * PAIR, PAIR)
                             out_ref[pl.ds(row, size), pl.ds(col, PAIR)] = block
 
 
-def tokens_out(at, high, tokens, cols, parts):
-    return pl.pallas_call(
-        functools.partial(tokens_kernel, high),
+def tokens_out(at, tokens, cols, parts):
+    return pl.pallas_call(
+        tokens_kernel,
         in_specs=[SMEM] + [VMEM] * len(parts),
         out_specs=[VMEM] * 2,
         out_shape=[like((tokens, cols))] * 2,
         compiler_params=params(),
-        cost_estimate=cost(1000, 8 * tokens * cols),
+        cost_estimate=cost(),
     )(at, *parts)
 
 
@@ -766,45 +802,61 @@
     def rows_of(own, from_x):
         from_y, from_xy = over_y(own), over_y(from_x)
         a = [own, over_core(own), from_x, over_core(from_x)]
-        return a, [from_y, over_core(from_y), from_xy, over_core(from_xy)]
+        return a, from_y, from_xy
+
+    def far_rows(from_y, from_xy):
+        return [from_y, over_core(from_y), from_xy, over_core(from_xy)]
 
     qk, qs, gk, gs = pack(at, queries, grad_out, attn_out)
     kp, vp, kt = pack_tokens(at, keys, values)
     q_from_x = after(over_x(qs), kp)
-    qa, qb = rows_of(qk, q_from_x)
-    ga, gb = rows_of(after(gk, q_from_x), over_x(after(gs, q_from_x)))
+    qa, q_y, q_xy = rows_of(qk, q_from_x)
+    g_from_x = over_x(after(gs, q_from_x))
+    ga, g_y, g_xy = rows_of(after(gk, q_from_x), g_from_x)
+    gb = far_rows(g_y, g_xy)
     pa, ma, la = side_of(qa, kp)
+    qb = far_rows(q_y, after(q_xy, la))
     pb, mb, lb, sent = side_of(qb, kp, la)
     send = merge(la, lb, over_core(sent))
     got = over_y(send)
-
-    sums, dqs = [], []
-    for own in (False, True):
-        out = half_of(at, own, high, qa + qb, ga + gb, pa, pb, vp, kt, ma, mb, send, got)
-        sums.append(add(out[0], *[over_z(out[k], k) for k in range(1, high)]))
-        dqs.append((out[high + 1], over_core(out[high])))
-
-    far = over_y(add(*dqs[0]))
-    qx_from_x = over_x(after(qx, la))
-    xa, xb = rows_of(after(qx, got), after(qx_from_x, got))
-    *parts, back, back_s = columns_of(at, high, xa + xb, *dqs[1], far)
-    parts = parts[:1] + [over_z(parts[k], k) for k in range(1, high)]
-    keep, send_w = weight_sum(at, parts)
-    grad_weight = weight_out(at, keep, over_x(send_w))
-
+    x_from_x = over_x(after(qx, la))
+    xa, x_y, x_xy = rows_of(after(qx, got), after(x_from_x, got))
+
+    def half(own, pa):
+        return half_of(at, own, qa + qb, ga + gb, pa, pb, vp, kt, ma, mb, send, got)
+
+    def sum_near(keep, send):
+        return add(keep, over_z(send, 1))
+
+    def sum_far(near):
+        return add_turned(near, over_z(near, 2))
+
+    def spread(total):
+        near = over_z(total, 1)
+        return [total, near, over_x(stack([total, near]))]
+
+    kv_keep, kv_send, dq_send, dq_keep = half(False, pa)
+    first = sum_near(kv_keep, kv_send)
+    far = add(dq_keep, over_core(dq_send))
+    kv_keep, kv_send, dq_send, dq_keep = half(True, after(pa, far, x_y, x_from_x))
+    far = over_y(far)
+    second = sum_near(kv_keep, kv_send)
+    x_y, x_xy = after(x_y, dq_keep), after(x_xy, dq_keep)
+    w_keep, w_send, back, back_s = columns_of(
+        at, high, xa + far_rows(x_y, x_xy), dq_keep, over_core(dq_send), far
+    )
+    first, second = sum_far(first), sum_far(second)
+    w_keep, w_send = weight_near(w_keep, over_z(w_send, 1))
+    w_keep, w_send = weight_sum(at, w_keep, over_z(w_send, 2))
+    grad_weight = weight_out(at, w_keep, over_x(w_send))
+
+    from_x = over_x(back_s)
     size = back.shape[0]
-    from_x = over_x(back_s)
-    far_cut = slice(2 * size, 4 * size)
-    from_y = over_y(stack([back, from_x], [far_cut, far_cut]))
-    near = slice(size, 2 * size)
-    from_core = over_core(stack([back, from_x, from_y], [near, near, near]))
+    part = lambda i, n: (slice(None), slice(i * size, (i + n) * size))
+    from_y = over_y(stack([back, from_x], [part(2, 2)] * 2))
+    from_core = over_core(stack([back, from_x, from_y], [part(1, 1)] * 3))
     grad_input = input_of(at, back, from_x, from_y, from_core, wq)
-
-    parts = []
-    for total in sums:
-        blocks = [total] + [over_z(total, k) for k in range(1, high)]
-        parts += blocks + [over_x(stack(blocks))]
-    grad_keys, grad_values = tokens_out(at, high, *keys.shape, parts)
+    grad_keys, grad_values = tokens_out(at, *keys.shape, spread(first) + spread(second))
     return (grad_input, grad_keys, grad_values, grad_weight)
 
 

time: 126 us -> 106 us (0.84)
  starting transfers between devices: 46.4 us -> 32.5 us
  waiting for transfers between devices: 48.2 us -> 41.4 us
    ppermute x47 -> x40, starting transfers between devices: 46.4 us -> 32.5 us  [swap(): return lax.ppermute(x, axis, [(i, i ^ mask) for i in range(size)])]
    ppermute x47 -> x40, waiting for transfers between devices: 48.2 us -> 41.4 us  [swap(): return lax.ppermute(x, axis, [(i, i ^ mask) for i in range(size)])]
    unnamed x14 -> x18, local copies, waits for them, and re-layouts: 5.13 us -> 3.85 us
    pallas_call x2 -> x5, Pallas kernels: 2.73 us -> 2.79 us  [the longest x1 2.1 us: tokens_out(): pl.pallas_call(tokens_kernel, in_specs=[SMEM] + [VMEM] * len(parts), out_...]
  transfers between devices with their start and end apart: 47 -> 40, of which waited for: 16 -> 17; matrix products, arithmetic and copies ran while one was open for 0% -> 0% of each run, Pallas kernels for 18% -> 21%
where the time goes in v4:
time: 106 us; the launch traced here: 105 us
  waiting for transfers between devices  41.4 us (39%)
  starting transfers between devices  32.5 us (31%)
  Pallas kernels  26.2 us (25%)
  local copies, waits for them, and re-layouts  4.51 us (4%)
    ppermute x40, waiting for transfers between devices, swap(): return lax.ppermute(x, axis, [(i, i ^ mask) for i in range(size)])  41.4 us
    ppermute x40, starting transfers between devices, swap(): return lax.ppermute(x, axis, [(i, i ^ mask) for i in range(size)])  32.5 us
    pallas_call x2, Pallas kernels, half_of(): pl.pallas_call(functools.partial(half_kernel, count), grid_spec=pltpu.Pre...  10.8 us
    pallas_call x2, Pallas kernels, side_of(): pl.pallas_call(functools.partial(side_kernel, count, step, extra is not N...  4.7 us
    unnamed x18, local copies, waits for them, and re-layouts  3.85 us
  transfers between devices with their start and end apart: 40, of which 17 were waited for; matrix products, arithmetic and copies ran while one was open for 0% of the time, Pallas kernels for 21%

profile of v4, /device:TPU:0, one launch (start us, length us, event | category | flops | bytes accessed | tf_op | source)
XLA Modules:
  0.0 105.4 jit_solution(2087687415499533023)
XLA Ops:
  0.7 0.7 stack.23.at_ref
  1.3 2.1 %shard_map.102 = (bf16[128,512]{1,0:T(8,128)(2,1)}, bf16[128,512]{1,0:T(8,128)(2,1)}, bf16[144,512]{1,0:T(8,128)(2,1)}, bf16[144,512]{1,0:T(8,128)(2,1)}) custom-call(s32[5]{0:T(128)} %stack.23.at_ref, bf16[128,1024]{1,0:T(8,128)(2,1)} %q_ref.1, bf16[128,1024]{1,0:T(8,128)(2,1)} %g_ref.1, bf16[128,1024]{1,0:T(8,128)(2,1)} %o_ref.1), custom_call_target="tpu_custom_call" | custom-call | flops 1 | bytes 1 | tf_op jit(solution)/shard_map/pallas_call | solution.py:381
  3.5 3.0 %collective-permute-start.1 = (bf16[128,512]{1,0:T(8,128)(2,1)}, bf16[128,512]{1,0:T(8,128)(2,1)S(1)}, u32[]{:S(2)}, u32[]{:S(2)}) collective-permute-start(bf16[128,512]{1,0:T(8,128)(2,1)} %get-tuple-element.47), channel_id=1, source_target_pairs={{0,4},{4,0},{8,12},{12,8},{16,20},{20,16},{24,28},{28,24},{1,5},{5... | collective-permute-start | bytes 393224 | tf_op jit(solution)/shard_map/ppermute | solution.py:191
  6.5 1.5 %collective-permute-start.3 = (bf16[128,512]{1,0:T(8,128)(2,1)}, bf16[128,512]{1,0:T(8,128)(2,1)S(1)}, u32[]{:S(2)}, u32[]{:S(2)}) collective-permute-start(bf16[128,512]{1,0:T(8,128)(2,1)} %get-tuple-element.46.refs_0_), channel_id=1, source_target_pairs={{0,2},{1,3},{2,0},{3,1},{4,6},{5,7},{6,4},{7,5},{8,10},{9,11},{10,... | collective-permute-start | bytes 393224 | tf_op jit(solution)/shard_map/ppermute | solution.py:191
  8.0 1.1 %copy-done.3 = bf16[384,1024]{1,0:T(8,128)(2,1)S(1)} copy-done((bf16[384,1024]{1,0:T(8,128)(2,1)S(1)}, bf16[384,1024]{1,0:T(8,128)(2,1)}, u32[]{:S(2)}) %copy-start.3) | copy-done | bytes 786456
  9.1 1.1 %copy-done.4 = bf16[384,1024]{1,0:T(8,128)(2,1)S(1)} copy-done((bf16[384,1024]{1,0:T(8,128)(2,1)S(1)}, bf16[384,1024]{1,0:T(8,128)(2,1)}, u32[]{:S(2)}) %copy-start.4) | copy-done | bytes 786456
  10.2 0.7 copy-done.7
  10.9 1.1 %shard_map.103 = (bf16[384,512]{1,0:T(8,128)(2,1)S(1)}, bf16[384,512]{1,0:T(8,128)(2,1)S(1)}, bf16[512,384]{1,0:T(8,128)(2,1)S(1)}) custom-call(s32[5]{0:T(128)S(1)} %copy-done.7, bf16[384,1024]{1,0:T(8,128)(2,1)S(1)} %copy-done.3, bf16[384,1024]{1,0:T(8,128)(2,1)S(1)} %copy-done.4), custom_call_target="tpu_custom_call" | custom-call | flops 1 | bytes 1 | tf_op jit(solution)/shard_map/pallas_call | solution.py:406
  12.0 0.3 collective-permute-start.2
  12.3 0.5 collective-permute-start.5
  12.8 0.6 collective-permute-start.14
  13.5 0.9 copy-done.1
  14.4 2.3 %shard_map.104 = (bf16[8,384,512]{2,1,0:T(8,128)(2,1)S(1)}, f32[4,2,512]{2,1,0:T(2,128)S(1)}, f32[4,2,512]{2,1,0:T(2,128)S(1)}) custom-call(bf16[128,512]{1,0:T(8,128)(2,1)S(1)} %copy-done.1, bf16[128,512]{1,0:T(8,128)(2,1)S(1)} %collective-permute-done.refs_1_, bf16[128,512]{1,0:T(8,128)(2,1)S(1)} %collective-permute-done.1.refs_2_, ...), custom_call_target="tpu_custom_call" | custom-call | flops 1 | bytes 1 | tf_op jit(solution)/shard_map/pallas_call | solution.py:512
  16.7 1.3 %collective-permute-done.5.refs_2_.refs_6_ = bf16[128,512]{1,0:T(8,128)(2,1)S(1)} collective-permute-done((bf16[128,512]{1,0:T(8,128)(2,1)S(1)}, bf16[128,512]{1,0:T(8,128)(2,1)S(1)}, u32[]{:S(2)}, u32[]{:S(2)}) %collective-permute-start.5) | collective-permute-done | bytes 131104 | tf_op jit(solution)/shard_map/ppermute | solution.py:191
  18.0 0.7 collective-permute-start.16
  18.8 1.5 %collective-permute-start.18 = (bf16[144,512]{1,0:T(8,128)(2,1)S(1)}, bf16[144,512]{1,0:T(8,128)(2,1)S(1)}, u32[]{:S(2)}, u32[]{:S(2)}) collective-permute-start(bf16[144,512]{1,0:T(8,128)(2,1)S(1)} %collective-permute-done.14.refs_10_), channel_id=1, source_target_pairs={{0,2},{1,3},{2,0},{3,1},{4,6},{5,7},{6,4},{7,5},{8,10},{9,11},{10,... | collective-permute-start | bytes 442376 | tf_op jit(solution)/shard_map/ppermute | solution.py:191
  20.3 2.4 %shard_map.105 = (bf16[8,384,512]{2,1,0:T(8,128)(2,1)S(1)}, f32[4,2,512]{2,1,0:T(2,128)S(1)}, f32[4,2,512]{2,1,0:T(2,128)S(1)}, f32[4,2,1024]{2,1,0:T(2,128)S(1)}) custom-call(bf16[128,512]{1,0:T(8,128)(2,1)S(1)} %collective-permute-done.3.refs_0_.refs_4_, bf16[128,512]{1,0:T(8,128)(2,1)S(1)} %collective-permute-done.4.refs_1_.refs_5_, ...), custom_call_target="tpu_custom_call" | custom-call | flops 1 | bytes 1 | tf_op jit(solution)/shard_map/pallas_call | solution.py:512
  22.7 0.1 collective-permute-start.7
  22.7 1.2 %collective-permute-done.7.got_ref = f32[4,2,1024]{2,1,0:T(2,128)S(1)} collective-permute-done((f32[4,2,1024]{2,1,0:T(2,128)S(1)}, f32[4,2,1024]{2,1,0:T(2,128)S(1)}, u32[]{:S(2)}, u32[]{:S(2)}) %collective-permute-start.7) | collective-permute-done | bytes 32800 | tf_op jit(solution)/shard_map/ppermute | solution.py:191
  24.0 0.6 collective-permute-start.8
  24.5 0.5 collective-permute-start.15
  25.1 2.9 %collective-permute-done.18.refs_14_ = bf16[144,512]{1,0:T(8,128)(2,1)S(1)} collective-permute-done((bf16[144,512]{1,0:T(8,128)(2,1)S(1)}, bf16[144,512]{1,0:T(8,128)(2,1)S(1)}, u32[]{:S(2)}, u32[]{:S(2)}) %collective-permute-start.18) | collective-permute-done | bytes 147488 | tf_op jit(solution)/shard_map/ppermute | solution.py:191
  28.0 0.3 collective-permute-done.8.refs_23_
  28.3 0.5 collective-permute-start.10
  28.9 0.5 collective-permute-done.19.refs_15_
  29.3 5.4 %shard_map.107 = (bf16[384,256]{1,0:T(8,128)(2,1)S(1)}, bf16[384,256]{1,0:T(8,128)(2,1)S(1)}, bf16[128,1024]{1,0:T(8,128)(2,1)S(1)}, bf16[128,1024]{1,0:T(8,128)(2,1)S(1)}) custom-call(s32[5]{0:T(128)S(1)} %copy-done.8, bf16[128,512]{1,0:T(8,128)(2,1)S(1)} %copy-done.2, bf16[128,512]{1,0:T(8,128)(2,1)S(1)} %collective-permute-done.refs_1_, ...), custom_call_target="tpu_custom_call" | custom-call | flops 1 | bytes 1 | tf_op jit(solution)/shard_map/pallas_call | solution.py:611
  34.8 0.2 collective-permute-start.20
  35.0 0.8 collective-permute-start.12
  35.7 1.0 collective-permute-done.10.refs_2_
  36.7 0.5 collective-permute-start.22
  37.2 1.6 %collective-permute-start.29 = (bf16[384,256]{1,0:T(8,128)(2,1)S(1)}, bf16[384,256]{1,0:T(8,128)(2,1)S(1)}, u32[]{:S(2)}, u32[]{:S(2)}) collective-permute-start(bf16[384,256]{1,0:T(8,128)(2,1)S(1)} %get-tuple-element.77), channel_id=1, source_target_pairs={{0,8},{4,12},{8,0},{12,4},{16,24},{20,28},{24,16},{28,20},{1,9},{5... | collective-permute-start | bytes 589832 | tf_op jit(solution)/shard_map/ppermute | solution.py:191
  38.8 0.1 shard_map.108
  38.8 5.3 %collective-permute-done.12.refs_4_ = bf16[128,1024]{1,0:T(8,128)(2,1)S(1)} collective-permute-done((bf16[128,1024]{1,0:T(8,128)(2,1)S(1)}, bf16[128,1024]{1,0:T(8,128)(2,1)S(1)}, u32[]{:S(2)}, u32[]{:S(2)}) %collective-permute-start.12) | collective-permute-done | bytes 262176 | tf_op jit(solution)/shard_map/ppermute | solution.py:191
  44.1 5.4 %shard_map.109 = (bf16[384,256]{1,0:T(8,128)(2,1)S(1)}, bf16[384,256]{1,0:T(8,128)(2,1)S(1)}, bf16[128,1024]{1,0:T(8,128)(2,1)S(1)}, bf16[128,1024]{1,0:T(8,128)(2,1)S(1)}) custom-call(s32[5]{0:T(128)S(1)} %copy-done.8, bf16[128,512]{1,0:T(8,128)(2,1)S(1)} %copy-done.2, bf16[128,512]{1,0:T(8,128)(2,1)S(1)} %collective-permute-done.refs_1_, ...), custom_call_target="tpu_custom_call" | custom-call | flops 1 | bytes 1 | tf_op jit(solution)/shard_map/pallas_call | solution.py:611
  49.5 1.6 %collective-permute-start.33 = (bf16[384,256]{1,0:T(8,128)(2,1)S(1)}, bf16[384,256]{1,0:T(8,128)(2,1)S(1)}, u32[]{:S(2)}, u32[]{:S(2)}) collective-permute-start(bf16[384,256]{1,0:T(8,128)(2,1)S(1)} %get-tuple-element.79), channel_id=1, source_target_pairs={{0,8},{4,12},{8,0},{12,4},{16,24},{20,28},{24,16},{28,20},{1,9},{5... | collective-permute-start | bytes 589832 | tf_op jit(solution)/shard_map/ppermute | solution.py:191
  51.1 0.5 collective-permute-start.11
  51.7 2.7 %collective-permute-start.30 = (bf16[384,256]{1,0:T(8,128)(2,1)S(1)}, bf16[384,256]{1,0:T(8,128)(2,1)S(1)}, u32[]{:S(2)}, u32[]{:S(2)}) collective-permute-start(bf16[384,256]{1,0:T(8,128)(2,1)S(1)} %shard_map.114.own_ref), channel_id=1, source_target_pairs={{0,16},{4,20},{8,24},{12,28},{16,0},{20,4},{24,8},{28,12},{1,17},{... | collective-permute-start | bytes 589832 | tf_op jit(solution)/shard_map/ppermute | solution.py:191
  54.4 1.0 collective-permute-done.33.refs_1_
  55.4 4.7 %collective-permute-start.34 = (bf16[384,256]{1,0:T(8,128)(2,1)S(1)}, bf16[384,256]{1,0:T(8,128)(2,1)S(1)}, u32[]{:S(2)}, u32[]{:S(2)}) collective-permute-start(bf16[384,256]{1,0:T(8,128)(2,1)S(1)} %shard_map.117.own_ref), channel_id=1, source_target_pairs={{0,16},{4,20},{8,24},{12,28},{16,0},{20,4},{24,8},{28,12},{1,17},{... | collective-permute-start | bytes 589832 | tf_op jit(solution)/shard_map/ppermute | solution.py:191
  60.1 0.5 collective-permute-start.24
  60.6 7.8 %collective-permute-done.30.got_ref = bf16[384,256]{1,0:T(8,128)(2,1)S(1)} collective-permute-done((bf16[384,256]{1,0:T(8,128)(2,1)S(1)}, bf16[384,256]{1,0:T(8,128)(2,1)S(1)}, u32[]{:S(2)}, u32[]{:S(2)}) %collective-permute-start.30) | collective-permute-done | bytes 196640 | tf_op jit(solution)/shard_map/ppermute | solution.py:191
  68.4 1.0 collective-permute-start.25
  69.4 2.7 %collective-permute-done.34.got_ref = bf16[384,256]{1,0:T(8,128)(2,1)S(1)} collective-permute-done((bf16[384,256]{1,0:T(8,128)(2,1)S(1)}, bf16[384,256]{1,0:T(8,128)(2,1)S(1)}, u32[]{:S(2)}, u32[]{:S(2)}) %collective-permute-start.34) | collective-permute-done | bytes 196640 | tf_op jit(solution)/shard_map/ppermute | solution.py:191
  72.2 2.1 %collective-permute-start.35 = (bf16[384,256]{1,0:T(8,128)(2,1)S(1)}, bf16[384,256]{1,0:T(8,128)(2,1)S(1)}, u32[]{:S(2)}, u32[]{:S(2)}) collective-permute-start(bf16[384,256]{1,0:T(8,128)(2,1)S(1)} %shard_map.118.refs_0_.refs_3_), channel_id=1, source_target_pairs={{0,8},{4,12},{8,0},{12,4},{16,24},{20,28},{24,16},{28,20},{1,9},{5... | collective-permute-start | bytes 589832 | tf_op jit(solution)/shard_map/ppermute | solution.py:191
  74.3 1.4 %collective-permute-done.25.refs_10_ = bf16[128,1024]{1,0:T(8,128)(2,1)S(1)} collective-permute-done((bf16[128,1024]{1,0:T(8,128)(2,1)S(1)}, bf16[128,1024]{1,0:T(8,128)(2,1)S(1)}, u32[]{:S(2)}, u32[]{:S(2)}) %collective-permute-start.25) | collective-permute-done | bytes 262176 | tf_op jit(solution)/shard_map/ppermute | solution.py:191
  75.7 1.0 shard_map.110
  76.8 0.8 collective-permute-start.26
  77.6 2.4 %collective-permute-done.31.refs_1_ = bf16[384,256]{1,0:T(8,128)(2,1)S(1)} collective-permute-done((bf16[384,256]{1,0:T(8,128)(2,1)S(1)}, bf16[384,256]{1,0:T(8,128)(2,1)S(1)}, u32[]{:S(2)}, u32[]{:S(2)}) %collective-permute-start.31) | collective-permute-done | bytes 196640 | tf_op jit(solution)/shard_map/ppermute | solution.py:191
  80.0 1.1 %collective-permute-start.32 = (bf16[768,256]{1,0:T(8,128)(2,1)S(1)}, bf16[768,256]{1,0:T(8,128)(2,1)S(1)}, u32[]{:S(2)}, u32[]{:S(2)}) collective-permute-start(bf16[768,256]{1,0:T(8,128)(2,1)S(1)} %shard_map.116), channel_id=1, source_target_pairs={{0,4},{4,0},{8,12},{12,8},{16,20},{20,16},{24,28},{28,24},{1,5},{5... | collective-permute-start | bytes 1179656 | tf_op jit(solution)/shard_map/ppermute | solution.py:191
  81.0 1.7 %collective-permute-done.35.refs_1_.refs_4_ = bf16[384,256]{1,0:T(8,128)(2,1)S(1)} collective-permute-done((bf16[384,256]{1,0:T(8,128)(2,1)S(1)}, bf16[384,256]{1,0:T(8,128)(2,1)S(1)}, u32[]{:S(2)}, u32[]{:S(2)}) %collective-permute-start.35) | collective-permute-done | bytes 196640 | tf_op jit(solution)/shard_map/ppermute | solution.py:191
  82.8 0.8 collective-permute-start.36
  83.6 1.1 %collective-permute-start.27 = (bf16[256,256]{1,0:T(8,128)(2,1)S(1)}, bf16[256,256]{1,0:T(8,128)(2,1)S(1)}, u32[]{:S(2)}, u32[]{:S(2)}) collective-permute-start(bf16[256,256]{1,0:T(8,128)(2,1)S(1)} %shard_map.111), channel_id=1, source_target_pairs={{0,2},{1,3},{2,0},{3,1},{4,6},{5,7},{6,4},{7,5},{8,10},{9,11},{10,... | collective-permute-start | bytes 393224 | tf_op jit(solution)/shard_map/ppermute | solution.py:191
  84.7 0.3 collective-permute-start.37
  85.0 3.6 %collective-permute-done.27.refs_2_.y_ref = bf16[256,256]{1,0:T(8,128)(2,1)S(1)} collective-permute-done((bf16[256,256]{1,0:T(8,128)(2,1)S(1)}, bf16[256,256]{1,0:T(8,128)(2,1)S(1)}, u32[]{:S(2)}, u32[]{:S(2)}) %collective-permute-start.27) | collective-permute-done | bytes 131104 | tf_op jit(solution)/shard_map/ppermute | solution.py:191
  88.7 0.1 collective-permute-start.28
  88.8 0.9 collective-permute-done.37.got_ref
  89.7 1.0 collective-permute-start.38
  90.7 4.7 %collective-permute-done.38.got_ref = bf16[128,256]{1,0:T(8,128)(2,1)S(1)} collective-permute-done((bf16[128,256]{1,0:T(8,128)(2,1)S(1)}, bf16[128,256]{1,0:T(8,128)(2,1)S(1)}, u32[]{:S(2)}, u32[]{:S(2)}) %collective-permute-start.38) | collective-permute-done | bytes 65568 | tf_op jit(solution)/shard_map/ppermute | solution.py:191
  95.4 0.6 shard_map.122
  96.0 1.3 %collective-permute-start.39 = (bf16[128,128]{1,0:T(8,128)(2,1)S(1)}, bf16[128,128]{1,0:T(8,128)(2,1)S(1)}, u32[]{:S(2)}, u32[]{:S(2)}) collective-permute-start(bf16[128,128]{1,0:T(8,128)(2,1)S(1)} %get-tuple-element.87), channel_id=1, source_target_pairs={{0,4},{4,0},{8,12},{12,8},{16,20},{20,16},{24,28},{28,24},{1,5},{5... | collective-permute-start | bytes 98312 | tf_op jit(solution)/shard_map/ppermute | solution.py:191
  97.3 2.7 %collective-permute-done.39.got_ref = bf16[128,128]{1,0:T(8,128)(2,1)S(1)} collective-permute-done((bf16[128,128]{1,0:T(8,128)(2,1)S(1)}, bf16[128,128]{1,0:T(8,128)(2,1)S(1)}, u32[]{:S(2)}, u32[]{:S(2)}) %collective-permute-start.39) | collective-permute-done | bytes 32800 | tf_op jit(solution)/shard_map/ppermute | solution.py:191
  99.9 1.3 %shard_map.123 = f32[128,256]{1,0:T(8,128)} custom-call(s32[5]{0:T(128)S(1)} %copy-done.8, f32[128,128]{1,0:T(8,128)S(1)} %get-tuple-element.86.keep_ref, bf16[128,128]{1,0:T(8,128)(2,1)S(1)} %collective-permute-done.39.got_ref), custom_call_target="tpu_custom_call" | custom-call | flops 1 | bytes 1 | tf_op jit(solution)/shard_map/pallas_call | solution.py:750
  101.2 2.1 %shard_map.113 = bf16[128,1024]{1,0:T(8,128)(2,1)} custom-call(s32[5]{0:T(128)S(1)} %copy-done.8, bf16[128,512]{1,0:T(8,128)(2,1)S(1)} %get-tuple-element.74.refs_0_.back_ref, bf16[128,512]{1,0:T(8,128)(2,1)S(1)} %collective-permute-done.26.refs_1_.x_ref, bf16[256,256]{1,0:T(8,128)(2,1)S(1)} %collective-permute-done.27.refs_2_.y_ref, ...), custom_call_target="tpu_custom_call" | custom-call | flops 1 | bytes 1 | tf_op jit(solution)/shard_map/pallas_call | solution.py:690
  103.3 2.1 %shard_map.120 = (bf16[384,1024]{1,0:T(8,128)(2,1)}, bf16[384,1024]{1,0:T(8,128)(2,1)}) custom-call(s32[5]{0:T(128)S(1)} %copy-done.8, bf16[384,256]{1,0:T(8,128)(2,1)S(1)} %shard_map.115.refs_0_, bf16[384,256]{1,0:T(8,128)(2,1)S(1)} %collective-permute-done.31.refs_1_, bf16[768,256]{1,0:T(8,128)(2,1)S(1)} %collective-permute-done.32.refs_2_, ...), custom_call_target="tpu_custom_call" | custom-call | flops 1 | bytes 1 | tf_op jit(solution)/shard_map/pallas_call | solution.py:782
  (57 shorter events, 0.5 us)
Async XLA Ops:
  0.6 27.7 %copy-start.6 = (bf16[128,1024]{1,0:T(8,128)(2,1)S(1)}, bf16[128,1024]{1,0:T(8,128)(2,1)}, u32[]{:S(2)}) copy-start(bf16[128,1024]{1,0:T(8,128)(2,1)} %refs_0_) | copy-start | bytes 786436
  1.3 28.0 %copy-start.8 = (s32[5]{0:T(128)S(1)}, s32[5]{0:T(128)}, u32[]{:S(2)}) copy-start(s32[5]{0:T(128)} %stack.23.at_ref) | copy-start | bytes 64
  3.5 25.9 %copy-start.2 = (bf16[128,512]{1,0:T(8,128)(2,1)S(1)}, bf16[128,512]{1,0:T(8,128)(2,1)}, u32[]{:S(2)}) copy-start(bf16[128,512]{1,0:T(8,128)(2,1)} %get-tuple-element.46.refs_0_) | copy-start | bytes 393220
  3.5 8.5 %collective-permute-start.1 = (bf16[128,512]{1,0:T(8,128)(2,1)}, bf16[128,512]{1,0:T(8,128)(2,1)S(1)}, u32[]{:S(2)}, u32[]{:S(2)}) collective-permute-start(bf16[128,512]{1,0:T(8,128)(2,1)} %get-tuple-element.47), channel_id=1, source_target_pairs={{0,4},{4,0},{8,12},{12,8},{16,20},{20,16},{24,28},{28,24},{1,5},{5... | collective-permute-start | bytes 393224 | tf_op jit(solution)/shard_map/ppermute | solution.py:191
  6.5 7.0 %collective-permute-start = (bf16[128,512]{1,0:T(8,128)(2,1)}, bf16[128,512]{1,0:T(8,128)(2,1)S(1)}, u32[]{:S(2)}, u32[]{:S(2)}) collective-permute-start(bf16[128,512]{1,0:T(8,128)(2,1)} %get-tuple-element.46.refs_0_), channel_id=1, source_target_pairs={{0,1},{1,0},{2,3},{3,2},{4,5},{5,4},{6,7},{7,6},{8,9},{9,8},{10,11... | collective-permute-start | bytes 393224 | tf_op jit(solution)/shard_map/ppermute | solution.py:191
  6.5 7.0 %collective-permute-start.3 = (bf16[128,512]{1,0:T(8,128)(2,1)}, bf16[128,512]{1,0:T(8,128)(2,1)S(1)}, u32[]{:S(2)}, u32[]{:S(2)}) collective-permute-start(bf16[128,512]{1,0:T(8,128)(2,1)} %get-tuple-element.46.refs_0_), channel_id=1, source_target_pairs={{0,2},{1,3},{2,0},{3,1},{4,6},{5,7},{6,4},{7,5},{8,10},{9,11},{10,... | collective-permute-start | bytes 393224 | tf_op jit(solution)/shard_map/ppermute | solution.py:191
  8.0 1.1 %copy-start.3 = (bf16[384,1024]{1,0:T(8,128)(2,1)S(1)}, bf16[384,1024]{1,0:T(8,128)(2,1)}, u32[]{:S(2)}) copy-start(bf16[384,1024]{1,0:T(8,128)(2,1)} %k_ref.1) | copy-start | bytes 2359300
  9.1 1.1 %copy-start.4 = (bf16[384,1024]{1,0:T(8,128)(2,1)S(1)}, bf16[384,1024]{1,0:T(8,128)(2,1)}, u32[]{:S(2)}) copy-start(bf16[384,1024]{1,0:T(8,128)(2,1)} %v_ref.1) | copy-start | bytes 2359300
  10.2 0.7 copy-start.7
  10.9 13.6 %copy-start.5 = (bf16[144,512]{1,0:T(8,128)(2,1)S(1)}, bf16[144,512]{1,0:T(8,128)(2,1)}, u32[]{:S(2)}) copy-start(bf16[144,512]{1,0:T(8,128)(2,1)} %get-tuple-element.58.refs_8_) | copy-start | bytes 442372
  12.0 1.5 %collective-permute-start.2 = (bf16[128,512]{1,0:T(8,128)(2,1)S(1)}, bf16[128,512]{1,0:T(8,128)(2,1)S(1)}, u32[]{:S(2)}, u32[]{:S(2)}) collective-permute-start(bf16[128,512]{1,0:T(8,128)(2,1)S(1)} %collective-permute-done.1.refs_2_), channel_id=1, source_target_pairs={{0,1},{1,0},{2,3},{3,2},{4,5},{5,4},{6,7},{7,6},{8,9},{9,8},{10,11... | collective-permute-start | bytes 393224 | tf_op jit(solution)/shard_map/ppermute | solution.py:191
  12.3 5.7 %collective-permute-start.5 = (bf16[128,512]{1,0:T(8,128)(2,1)S(1)}, bf16[128,512]{1,0:T(8,128)(2,1)S(1)}, u32[]{:S(2)}, u32[]{:S(2)}) collective-permute-start(bf16[128,512]{1,0:T(8,128)(2,1)S(1)} %collective-permute-done.1.refs_2_), channel_id=1, source_target_pairs={{0,2},{1,3},{2,0},{3,1},{4,6},{5,7},{6,4},{7,5},{8,10},{9,11},{10,... | collective-permute-start | bytes 393224 | tf_op jit(solution)/shard_map/ppermute | solution.py:191
  12.8 6.0 %collective-permute-start.14 = (bf16[144,512]{1,0:T(8,128)(2,1)}, bf16[144,512]{1,0:T(8,128)(2,1)S(1)}, u32[]{:S(2)}, u32[]{:S(2)}) collective-permute-start(bf16[144,512]{1,0:T(8,128)(2,1)} %get-tuple-element.60), channel_id=1, source_target_pairs={{0,4},{4,0},{8,12},{12,8},{16,20},{20,16},{24,28},{28,24},{1,5},{5... | collective-permute-start | bytes 442376 | tf_op jit(solution)/shard_map/ppermute | solution.py:191
  13.4 6.9 %collective-permute-start.4 = (bf16[128,512]{1,0:T(8,128)(2,1)S(1)}, bf16[128,512]{1,0:T(8,128)(2,1)S(1)}, u32[]{:S(2)}, u32[]{:S(2)}) collective-permute-start(bf16[128,512]{1,0:T(8,128)(2,1)S(1)} %collective-permute-done.3.refs_0_.refs_4_), channel_id=1, source_target_pairs={{0,1},{1,0},{2,3},{3,2},{4,5},{5,4},{6,7},{7,6},{8,9},{9,8},{10,11... | collective-permute-start | bytes 393224 | tf_op jit(solution)/shard_map/ppermute | solution.py:191
  13.4 0.9 copy-start.1
  18.0 2.3 %collective-permute-start.6 = (bf16[128,512]{1,0:T(8,128)(2,1)S(1)}, bf16[128,512]{1,0:T(8,128)(2,1)S(1)}, u32[]{:S(2)}, u32[]{:S(2)}) collective-permute-start(bf16[128,512]{1,0:T(8,128)(2,1)S(1)} %collective-permute-done.5.refs_2_.refs_6_), channel_id=1, source_target_pairs={{0,1},{1,0},{2,3},{3,2},{4,5},{5,4},{6,7},{7,6},{8,9},{9,8},{10,11... | collective-permute-start | bytes 393224 | tf_op jit(solution)/shard_map/ppermute | solution.py:191
  18.0 7.1 %collective-permute-start.16 = (bf16[144,512]{1,0:T(8,128)(2,1)}, bf16[144,512]{1,0:T(8,128)(2,1)S(1)}, u32[]{:S(2)}, u32[]{:S(2)}) collective-permute-start(bf16[144,512]{1,0:T(8,128)(2,1)} %get-tuple-element.58.refs_8_), channel_id=1, source_target_pairs={{0,2},{1,3},{2,0},{3,1},{4,6},{5,7},{6,4},{7,5},{8,10},{9,11},{10,... | collective-permute-start | bytes 442376 | tf_op jit(solution)/shard_map/ppermute | solution.py:191
  18.8 9.2 %collective-permute-start.18 = (bf16[144,512]{1,0:T(8,128)(2,1)S(1)}, bf16[144,512]{1,0:T(8,128)(2,1)S(1)}, u32[]{:S(2)}, u32[]{:S(2)}) collective-permute-start(bf16[144,512]{1,0:T(8,128)(2,1)S(1)} %collective-permute-done.14.refs_10_), channel_id=1, source_target_pairs={{0,2},{1,3},{2,0},{3,1},{4,6},{5,7},{6,4},{7,5},{8,10},{9,11},{10,... | collective-permute-start | bytes 442376 | tf_op jit(solution)/shard_map/ppermute | solution.py:191
  22.7 1.3 %collective-permute-start.7 = (f32[4,2,1024]{2,1,0:T(2,128)S(1)}, f32[4,2,1024]{2,1,0:T(2,128)S(1)}, u32[]{:S(2)}, u32[]{:S(2)}) collective-permute-start(f32[4,2,1024]{2,1,0:T(2,128)S(1)} %get-tuple-element.53), channel_id=1, source_target_pairs={{0,1},{1,0},{2,3},{3,2},{4,5},{5,4},{6,7},{7,6},{8,9},{9,8},{10,11... | collective-permute-start | bytes 98312 | tf_op jit(solution)/shard_map/ppermute | solution.py:191
  24.0 4.3 %collective-permute-start.8 = (f32[4,2,1024]{2,1,0:T(2,128)S(1)}, f32[4,2,1024]{2,1,0:T(2,128)S(1)}, u32[]{:S(2)}, u32[]{:S(2)}) collective-permute-start(f32[4,2,1024]{2,1,0:T(2,128)S(1)} %shard_map.106.refs_22_), channel_id=1, source_target_pairs={{0,2},{1,3},{2,0},{3,1},{4,6},{5,7},{6,4},{7,5},{8,10},{9,11},{10,... | collective-permute-start | bytes 98312 | tf_op jit(solution)/shard_map/ppermute | solution.py:191
  24.5 4.3 %collective-permute-start.13 = (bf16[144,512]{1,0:T(8,128)(2,1)S(1)}, bf16[144,512]{1,0:T(8,128)(2,1)S(1)}, u32[]{:S(2)}, u32[]{:S(2)}) collective-permute-start(bf16[144,512]{1,0:T(8,128)(2,1)S(1)} %copy-done.5), channel_id=1, source_target_pairs={{0,1},{1,0},{2,3},{3,2},{4,5},{5,4},{6,7},{7,6},{8,9},{9,8},{10,11... | collective-permute-start | bytes 442376 | tf_op jit(solution)/shard_map/ppermute | solution.py:191
  24.5 4.3 %collective-permute-start.15 = (bf16[144,512]{1,0:T(8,128)(2,1)S(1)}, bf16[144,512]{1,0:T(8,128)(2,1)S(1)}, u32[]{:S(2)}, u32[]{:S(2)}) collective-permute-start(bf16[144,512]{1,0:T(8,128)(2,1)S(1)} %collective-permute-done.14.refs_10_), channel_id=1, source_target_pairs={{0,1},{1,0},{2,3},{3,2},{4,5},{5,4},{6,7},{7,6},{8,9},{9,8},{10,11... | collective-permute-start | bytes 442376 | tf_op jit(solution)/shard_map/ppermute | solution.py:191
  25.0 3.8 %collective-permute-start.17 = (bf16[144,512]{1,0:T(8,128)(2,1)S(1)}, bf16[144,512]{1,0:T(8,128)(2,1)S(1)}, u32[]{:S(2)}, u32[]{:S(2)}) collective-permute-start(bf16[144,512]{1,0:T(8,128)(2,1)S(1)} %collective-permute-done.16.refs_12_), channel_id=1, source_target_pairs={{0,1},{1,0},{2,3},{3,2},{4,5},{5,4},{6,7},{7,6},{8,9},{9,8},{10,11... | collective-permute-start | bytes 442376 | tf_op jit(solution)/shard_map/ppermute | solution.py:191
  28.0 1.4 %collective-permute-start.19 = (bf16[144,512]{1,0:T(8,128)(2,1)S(1)}, bf16[144,512]{1,0:T(8,128)(2,1)S(1)}, u32[]{:S(2)}, u32[]{:S(2)}) collective-permute-start(bf16[144,512]{1,0:T(8,128)(2,1)S(1)} %collective-permute-done.18.refs_14_), channel_id=1, source_target_pairs={{0,1},{1,0},{2,3},{3,2},{4,5},{5,4},{6,7},{7,6},{8,9},{9,8},{10,11... | collective-permute-start | bytes 442376 | tf_op jit(solution)/shard_map/ppermute | solution.py:191
  28.3 8.4 %collective-permute-start.10 = (bf16[128,1024]{1,0:T(8,128)(2,1)S(1)}, bf16[128,1024]{1,0:T(8,128)(2,1)S(1)}, u32[]{:S(2)}, u32[]{:S(2)}) collective-permute-start(bf16[128,1024]{1,0:T(8,128)(2,1)S(1)} %copy-done.6), channel_id=1, source_target_pairs={{0,4},{4,0},{8,12},{12,8},{16,20},{20,16},{24,28},{28,24},{1,5},{5... | collective-permute-start | bytes 786440 | tf_op jit(solution)/shard_map/ppermute | solution.py:191
  34.8 4.0 %collective-permute-start.20 = (bf16[128,1024]{1,0:T(8,128)(2,1)S(1)}, bf16[128,1024]{1,0:T(8,128)(2,1)S(1)}, u32[]{:S(2)}, u32[]{:S(2)}) collective-permute-start(bf16[128,1024]{1,0:T(8,128)(2,1)S(1)} %get-tuple-element.68), channel_id=1, source_target_pairs={{0,1},{1,0},{2,3},{3,2},{4,5},{5,4},{6,7},{7,6},{8,9},{9,8},{10,11... | collective-permute-start | bytes 786440 | tf_op jit(solution)/shard_map/ppermute | solution.py:191
  35.0 9.1 %collective-permute-start.12 = (bf16[128,1024]{1,0:T(8,128)(2,1)S(1)}, bf16[128,1024]{1,0:T(8,128)(2,1)S(1)}, u32[]{:S(2)}, u32[]{:S(2)}) collective-permute-start(bf16[128,1024]{1,0:T(8,128)(2,1)S(1)} %copy-done.6), channel_id=1, source_target_pairs={{0,2},{1,3},{2,0},{3,1},{4,6},{5,7},{6,4},{7,5},{8,10},{9,11},{10,... | collective-permute-start | bytes 786440 | tf_op jit(solution)/shard_map/ppermute | solution.py:191
  36.7 17.7 %collective-permute-start.22 = (bf16[128,1024]{1,0:T(8,128)(2,1)S(1)}, bf16[128,1024]{1,0:T(8,128)(2,1)S(1)}, u32[]{:S(2)}, u32[]{:S(2)}) collective-permute-start(bf16[128,1024]{1,0:T(8,128)(2,1)S(1)} %collective-permute-done.10.refs_2_), channel_id=1, source_target_pairs={{0,2},{1,3},{2,0},{3,1},{4,6},{5,7},{6,4},{7,5},{8,10},{9,11},{10,... | collective-permute-start | bytes 786440 | tf_op jit(solution)/shard_map/ppermute | solution.py:191
  37.2 14.5 %collective-permute-start.29 = (bf16[384,256]{1,0:T(8,128)(2,1)S(1)}, bf16[384,256]{1,0:T(8,128)(2,1)S(1)}, u32[]{:S(2)}, u32[]{:S(2)}) collective-permute-start(bf16[384,256]{1,0:T(8,128)(2,1)S(1)} %get-tuple-element.77), channel_id=1, source_target_pairs={{0,8},{4,12},{8,0},{12,4},{16,24},{20,28},{24,16},{28,20},{1,9},{5... | collective-permute-start | bytes 589832 | tf_op jit(solution)/shard_map/ppermute | solution.py:191
  49.5 5.9 %collective-permute-start.33 = (bf16[384,256]{1,0:T(8,128)(2,1)S(1)}, bf16[384,256]{1,0:T(8,128)(2,1)S(1)}, u32[]{:S(2)}, u32[]{:S(2)}) collective-permute-start(bf16[384,256]{1,0:T(8,128)(2,1)S(1)} %get-tuple-element.79), channel_id=1, source_target_pairs={{0,8},{4,12},{8,0},{12,4},{16,24},{20,28},{24,16},{28,20},{1,9},{5... | collective-permute-start | bytes 589832 | tf_op jit(solution)/shard_map/ppermute | solution.py:191
  51.1 9.0 %collective-permute-start.9 = (bf16[128,1024]{1,0:T(8,128)(2,1)S(1)}, bf16[128,1024]{1,0:T(8,128)(2,1)S(1)}, u32[]{:S(2)}, u32[]{:S(2)}) collective-permute-start(bf16[128,1024]{1,0:T(8,128)(2,1)S(1)} %copy-done.6), channel_id=1, source_target_pairs={{0,1},{1,0},{2,3},{3,2},{4,5},{5,4},{6,7},{7,6},{8,9},{9,8},{10,11... | collective-permute-start | bytes 786440 | tf_op jit(solution)/shard_map/ppermute | solution.py:191
  51.1 9.0 %collective-permute-start.11 = (bf16[128,1024]{1,0:T(8,128)(2,1)S(1)}, bf16[128,1024]{1,0:T(8,128)(2,1)S(1)}, u32[]{:S(2)}, u32[]{:S(2)}) collective-permute-start(bf16[128,1024]{1,0:T(8,128)(2,1)S(1)} %collective-permute-done.10.refs_2_), channel_id=1, source_target_pairs={{0,1},{1,0},{2,3},{3,2},{4,5},{5,4},{6,7},{7,6},{8,9},{9,8},{10,11... | collective-permute-start | bytes 786440 | tf_op jit(solution)/shard_map/ppermute | solution.py:191
  51.7 16.7 %collective-permute-start.30 = (bf16[384,256]{1,0:T(8,128)(2,1)S(1)}, bf16[384,256]{1,0:T(8,128)(2,1)S(1)}, u32[]{:S(2)}, u32[]{:S(2)}) collective-permute-start(bf16[384,256]{1,0:T(8,128)(2,1)S(1)} %shard_map.114.own_ref), channel_id=1, source_target_pairs={{0,16},{4,20},{8,24},{12,28},{16,0},{20,4},{24,8},{28,12},{1,17},{... | collective-permute-start | bytes 589832 | tf_op jit(solution)/shard_map/ppermute | solution.py:191
  54.4 17.8 %collective-permute-start.23 = (bf16[128,1024]{1,0:T(8,128)(2,1)S(1)}, bf16[128,1024]{1,0:T(8,128)(2,1)S(1)}, u32[]{:S(2)}, u32[]{:S(2)}) collective-permute-start(bf16[128,1024]{1,0:T(8,128)(2,1)S(1)} %collective-permute-done.22.refs_6_), channel_id=1, source_target_pairs={{0,1},{1,0},{2,3},{3,2},{4,5},{5,4},{6,7},{7,6},{8,9},{9,8},{10,11... | collective-permute-start | bytes 786440 | tf_op jit(solution)/shard_map/ppermute | solution.py:191
  55.4 16.7 %collective-permute-start.34 = (bf16[384,256]{1,0:T(8,128)(2,1)S(1)}, bf16[384,256]{1,0:T(8,128)(2,1)S(1)}, u32[]{:S(2)}, u32[]{:S(2)}) collective-permute-start(bf16[384,256]{1,0:T(8,128)(2,1)S(1)} %shard_map.117.own_ref), channel_id=1, source_target_pairs={{0,16},{4,20},{8,24},{12,28},{16,0},{20,4},{24,8},{28,12},{1,17},{... | collective-permute-start | bytes 589832 | tf_op jit(solution)/shard_map/ppermute | solution.py:191
  60.1 14.2 %collective-permute-start.21 = (bf16[128,1024]{1,0:T(8,128)(2,1)S(1)}, bf16[128,1024]{1,0:T(8,128)(2,1)S(1)}, u32[]{:S(2)}, u32[]{:S(2)}) collective-permute-start(bf16[128,1024]{1,0:T(8,128)(2,1)S(1)} %collective-permute-done.12.refs_4_), channel_id=1, source_target_pairs={{0,1},{1,0},{2,3},{3,2},{4,5},{5,4},{6,7},{7,6},{8,9},{9,8},{10,11... | collective-permute-start | bytes 786440 | tf_op jit(solution)/shard_map/ppermute | solution.py:191
  60.1 14.2 %collective-permute-start.24 = (bf16[128,1024]{1,0:T(8,128)(2,1)S(1)}, bf16[128,1024]{1,0:T(8,128)(2,1)S(1)}, u32[]{:S(2)}, u32[]{:S(2)}) collective-permute-start(bf16[128,1024]{1,0:T(8,128)(2,1)S(1)} %get-tuple-element.73), channel_id=1, source_target_pairs={{0,1},{1,0},{2,3},{3,2},{4,5},{5,4},{6,7},{7,6},{8,9},{9,8},{10,11... | collective-permute-start | bytes 786440 | tf_op jit(solution)/shard_map/ppermute | solution.py:191
  68.4 7.3 %collective-permute-start.25 = (bf16[128,1024]{1,0:T(8,128)(2,1)S(1)}, bf16[128,1024]{1,0:T(8,128)(2,1)S(1)}, u32[]{:S(2)}, u32[]{:S(2)}) collective-permute-start(bf16[128,1024]{1,0:T(8,128)(2,1)S(1)} %shard_map.108), channel_id=1, source_target_pairs={{0,2},{1,3},{2,0},{3,1},{4,6},{5,7},{6,4},{7,5},{8,10},{9,11},{10,... | collective-permute-start | bytes 786440 | tf_op jit(solution)/shard_map/ppermute | solution.py:191
  72.1 7.8 %collective-permute-start.31 = (bf16[384,256]{1,0:T(8,128)(2,1)S(1)}, bf16[384,256]{1,0:T(8,128)(2,1)S(1)}, u32[]{:S(2)}, u32[]{:S(2)}) collective-permute-start(bf16[384,256]{1,0:T(8,128)(2,1)S(1)} %shard_map.115.refs_0_), channel_id=1, source_target_pairs={{0,8},{4,12},{8,0},{12,4},{16,24},{20,28},{24,16},{28,20},{1,9},{5... | collective-permute-start | bytes 589832 | tf_op jit(solution)/shard_map/ppermute | solution.py:191
  72.2 29.0 %copy-start = (bf16[1024,1024]{1,0:T(8,128)(2,1)S(1)}, bf16[1024,1024]{1,0:T(8,128)(2,1)}, u32[]{:S(2)}) copy-start(bf16[1024,1024]{1,0:T(8,128)(2,1)} %wq_ref.1) | copy-start | bytes 6291460
  72.2 10.5 %collective-permute-start.35 = (bf16[384,256]{1,0:T(8,128)(2,1)S(1)}, bf16[384,256]{1,0:T(8,128)(2,1)S(1)}, u32[]{:S(2)}, u32[]{:S(2)}) collective-permute-start(bf16[384,256]{1,0:T(8,128)(2,1)S(1)} %shard_map.118.refs_0_.refs_3_), channel_id=1, source_target_pairs={{0,8},{4,12},{8,0},{12,4},{16,24},{20,28},{24,16},{28,20},{1,9},{5... | collective-permute-start | bytes 589832 | tf_op jit(solution)/shard_map/ppermute | solution.py:191
  76.8 6.8 %collective-permute-start.26 = (bf16[128,512]{1,0:T(8,128)(2,1)S(1)}, bf16[128,512]{1,0:T(8,128)(2,1)S(1)}, u32[]{:S(2)}, u32[]{:S(2)}) collective-permute-start(bf16[128,512]{1,0:T(8,128)(2,1)S(1)} %get-tuple-element.75), channel_id=1, source_target_pairs={{0,4},{4,0},{8,12},{12,8},{16,20},{20,16},{24,28},{28,24},{1,5},{5... | collective-permute-start | bytes 393224 | tf_op jit(solution)/shard_map/ppermute | solution.py:191
  80.0 23.3 %collective-permute-start.32 = (bf16[768,256]{1,0:T(8,128)(2,1)S(1)}, bf16[768,256]{1,0:T(8,128)(2,1)S(1)}, u32[]{:S(2)}, u32[]{:S(2)}) collective-permute-start(bf16[768,256]{1,0:T(8,128)(2,1)S(1)} %shard_map.116), channel_id=1, source_target_pairs={{0,4},{4,0},{8,12},{12,8},{16,20},{20,16},{24,28},{28,24},{1,5},{5... | collective-permute-start | bytes 1179656 | tf_op jit(solution)/shard_map/ppermute | solution.py:191
  82.8 20.5 %collective-permute-start.36 = (bf16[768,256]{1,0:T(8,128)(2,1)S(1)}, bf16[768,256]{1,0:T(8,128)(2,1)S(1)}, u32[]{:S(2)}, u32[]{:S(2)}) collective-permute-start(bf16[768,256]{1,0:T(8,128)(2,1)S(1)} %shard_map.119), channel_id=1, source_target_pairs={{0,4},{4,0},{8,12},{12,8},{16,20},{20,16},{24,28},{28,24},{1,5},{5... | collective-permute-start | bytes 1179656 | tf_op jit(solution)/shard_map/ppermute | solution.py:191
  83.6 5.0 %collective-permute-start.27 = (bf16[256,256]{1,0:T(8,128)(2,1)S(1)}, bf16[256,256]{1,0:T(8,128)(2,1)S(1)}, u32[]{:S(2)}, u32[]{:S(2)}) collective-permute-start(bf16[256,256]{1,0:T(8,128)(2,1)S(1)} %shard_map.111), channel_id=1, source_target_pairs={{0,2},{1,3},{2,0},{3,1},{4,6},{5,7},{6,4},{7,5},{8,10},{9,11},{10,... | collective-permute-start | bytes 393224 | tf_op jit(solution)/shard_map/ppermute | solution.py:191
  84.7 5.0 %collective-permute-start.37 = (bf16[256,256]{1,0:T(8,128)(2,1)S(1)}, bf16[256,256]{1,0:T(8,128)(2,1)S(1)}, u32[]{:S(2)}, u32[]{:S(2)}) collective-permute-start(bf16[256,256]{1,0:T(8,128)(2,1)S(1)} %get-tuple-element.83), channel_id=1, source_target_pairs={{0,8},{4,12},{8,0},{12,4},{16,24},{20,28},{24,16},{28,20},{1,9},{5... | collective-permute-start | bytes 393224 | tf_op jit(solution)/shard_map/ppermute | solution.py:191
  88.7 12.6 %collective-permute-start.28 = (bf16[512,128]{1,0:T(8,128)(2,1)S(1)}, bf16[512,128]{1,0:T(8,128)(2,1)S(1)}, u32[]{:S(2)}, u32[]{:S(2)}) collective-permute-start(bf16[512,128]{1,0:T(8,128)(2,1)S(1)} %shard_map.112), channel_id=1, source_target_pairs={{0,1},{1,0},{2,3},{3,2},{4,5},{5,4},{6,7},{7,6},{8,9},{9,8},{10,11... | collective-permute-start | bytes 393224 | tf_op jit(solution)/shard_map/ppermute | solution.py:191
  89.7 5.7 %collective-permute-start.38 = (bf16[128,256]{1,0:T(8,128)(2,1)S(1)}, bf16[128,256]{1,0:T(8,128)(2,1)S(1)}, u32[]{:S(2)}, u32[]{:S(2)}) collective-permute-start(bf16[128,256]{1,0:T(8,128)(2,1)S(1)} %get-tuple-element.85), channel_id=1, source_target_pairs={{0,16},{4,20},{8,24},{12,28},{16,0},{20,4},{24,8},{28,12},{1,17},{... | collective-permute-start | bytes 196616 | tf_op jit(solution)/shard_map/ppermute | solution.py:191
  96.0 4.0 %collective-permute-start.39 = (bf16[128,128]{1,0:T(8,128)(2,1)S(1)}, bf16[128,128]{1,0:T(8,128)(2,1)S(1)}, u32[]{:S(2)}, u32[]{:S(2)}) collective-permute-start(bf16[128,128]{1,0:T(8,128)(2,1)S(1)} %get-tuple-element.87), channel_id=1, source_target_pairs={{0,4},{4,0},{8,12},{12,8},{16,20},{20,16},{24,28},{28,24},{1,5},{5... | collective-permute-start | bytes 98312 | tf_op jit(solution)/shard_map/ppermute | solution.py:191

commit v5 on v4

--- a/solution.py
+++ b/solution.py
@@ -349,18 +349,18 @@
     return high, mid, d - high - mid
 
 
-def pack_kernel(at_ref, q_ref, g_ref, o_ref, qk_ref, qs_ref, gk_ref, gs_ref):
-    low = at_ref[X] == 0
+def pack_kernel(q_ref, g_ref, o_ref, keep_ref, send_ref):
+    low = lax.axis_index("dp") % 2 == 0
     rows = q_ref.shape[0]
-    pairs = qk_ref.shape[1] // PAIR
+    pairs = keep_ref.shape[1] // PAIR
     for p in range(pairs):
         scale = jnp.asarray(SCALE, BF)
         a, b = q_ref[:, span(2 * p)] * scale, q_ref[:, span(2 * p + 1)] * scale
-        qk_ref[:, span(p)] = jnp.where(low, a, b)
-        qs_ref[:, span(p)] = jnp.where(low, b, a)
+        keep_ref[:rows, span(p)] = jnp.where(low, a, b)
+        send_ref[:rows, span(p)] = jnp.where(low, b, a)
         a, b = g_ref[:, span(2 * p)], g_ref[:, span(2 * p + 1)]
-        gk_ref[:rows, span(p)] = jnp.where(low, a, b)
-        gs_ref[:rows, span(p)] = jnp.where(low, b, a)
+        keep_ref[rows : 2 * rows, span(p)] = jnp.where(low, a, b)
+        send_ref[rows : 2 * rows, span(p)] = jnp.where(low, b, a)
     cols = (g_ref[...].astype(F32) * o_ref[...].astype(F32)).T
     for p in range(pairs):
         both = []
@@ -369,24 +369,25 @@
         pad = [jnp.zeros((EXTRA - 6, rows), F32)]
         a = jnp.concatenate([both[h][n] for n in range(3) for h in (0, 1)] + pad, axis=0).astype(BF)
         b = jnp.concatenate([both[h][n] for n in range(3) for h in (2, 3)] + pad, axis=0).astype(BF)
-        gk_ref[rows:, span(p)] = jnp.where(low, a, b)
-        gs_ref[rows:, span(p)] = jnp.where(low, b, a)
-
-
-def pack(at, queries, grad_out, attn_out):
+        keep_ref[2 * rows :, span(p)] = jnp.where(low, a, b)
+        send_ref[2 * rows :, span(p)] = jnp.where(low, b, a)
+
+
+def pack(queries, grad_out, attn_out):
     rows, cols = queries.shape
     steps = 2
     block = pl.BlockSpec((rows, cols // steps), lambda i: (0, i))
-    half = lambda n: pl.BlockSpec((n, cols // 2 // steps), lambda i: (0, i))
+    total = 2 * rows + EXTRA
+    half = pl.BlockSpec((total, cols // 2 // steps), lambda i: (0, i))
     return pl.pallas_call(
         pack_kernel,
         grid=(steps,),
-        in_specs=[SMEM] + [block] * 3,
-        out_specs=[half(rows)] * 2 + [half(rows + EXTRA)] * 2,
-        out_shape=[like((rows, cols // 2))] * 2 + [like((rows + EXTRA, cols // 2))] * 2,
+        in_specs=[block] * 3,
+        out_specs=[half] * 2,
+        out_shape=[like((total, cols // 2))] * 2,
         compiler_params=params(60),
         cost_estimate=cost(),
-    )(at, queries, grad_out, attn_out)
+    )(queries, grad_out, attn_out)
 
 
 def pack_tokens_kernel(at_ref, k_ref, v_ref, kp_ref, vp_ref, kt_ref):
@@ -495,8 +496,9 @@
 
 def side_of(pieces, keys, extra=None, step=2):
     count = len(pieces)
-    piece, cols = pieces[0].shape
+    cols = pieces[0].shape[1]
     tokens = keys.shape[0]
+    piece = (pieces[0].shape[0] - EXTRA) // 2
     rows, pairs = piece * count, cols // PAIR
     stat_spec = lambda n: pl.BlockSpec((step, 2, n), lambda i: (i, 0, 0))
     in_specs = [pl.BlockSpec((piece, step * PAIR), lambda i: (0, i))] * count
@@ -544,9 +546,10 @@
 
 
 def half_kernel(count, at_ref, *refs):
-    q_refs, g_refs = refs[:count], refs[count : 2 * count]
-    pa_ref, pb_ref, v_ref, kt_ref, ma_ref, mb_ref, sent_ref, got_ref = refs[2 * count : 2 * count + 8]
-    kv_refs, dqs_ref, dqk_ref = refs[2 * count + 8 : -2], refs[-2], refs[-1]
+    row_refs = refs[:count]
+    piece = (row_refs[0].shape[0] - EXTRA) // 2
+    pa_ref, pb_ref, v_ref, kt_ref, ma_ref, mb_ref, sent_ref, got_ref = refs[count : count + 8]
+    kv_refs, dqs_ref, dqk_ref = refs[count + 8 : -2], refs[-2], refs[-1]
     side = ma_ref.shape[2]
     z = at_ref[Z]
     v = v_ref[...]
@@ -560,9 +563,9 @@
         w = jnp.exp(m_ref[0] - lse)
         wide = jnp.where(first, w[0:1], w[1:2]).T
         at = slice(b * count // 2, (b + 1) * count // 2)
-        q = jnp.concatenate([r[...] for r in q_refs[at]], axis=0)
-        g = jnp.concatenate([r[: r.shape[0] - EXTRA] for r in g_refs[at]], axis=0)
-        parts = [r[r.shape[0] - EXTRA :].astype(F32) for r in g_refs[at]]
+        q = jnp.concatenate([r[:piece] for r in row_refs[at]], axis=0)
+        g = jnp.concatenate([r[piece : 2 * piece] for r in row_refs[at]], axis=0)
+        parts = [r[2 * piece :].astype(F32) for r in row_refs[at]]
         delta = jnp.concatenate([d[0:2] + d[2:4] + d[4:6] for d in parts], axis=1)
         qw = (q.astype(F32) * wide).astype(BF)
         gw = (g.astype(F32) * wide).astype(BF)
@@ -596,15 +599,13 @@
             ref[span(n, size)] = out
 
 
-def half_of(at, own, q_pieces, g_pieces, pa, pb, vp, kt, ma, mb, sent, got):
-    count = len(q_pieces)
-    piece, cols = q_pieces[0].shape
+def half_of(at, own, pieces, pa, pb, vp, kt, ma, mb, sent, got):
+    count = len(pieces)
     tokens = vp.shape[0]
     side = ma.shape[2]
     bit = lambda i, a: (i + 1 + a[CORE]) % 2
     pair = lambda i, a: 2 * (a[Y] if own else 1 - a[Y]) + bit(i, a)
-    extra_spec = pl.BlockSpec((piece + EXTRA, PAIR), lambda i, a: (0, pair(i, a)))
-    row_spec = pl.BlockSpec((piece, PAIR), lambda i, a: (0, pair(i, a)))
+    row_spec = pl.BlockSpec((pieces[0].shape[0], PAIR), lambda i, a: (0, pair(i, a)))
     p_spec = pl.BlockSpec((2, tokens, side), lambda i, a: (pair(i, a), 0, 0))
     stat_spec = lambda n: pl.BlockSpec((1, 2, n), lambda i, a: (pair(i, a), 0, 0))
     block = tokens
@@ -614,7 +615,6 @@
             num_scalar_prefetch=1,
             grid=(2,),
             in_specs=[row_spec] * count
-            + [extra_spec] * count
             + [
                 p_spec,
                 p_spec,
@@ -631,7 +631,7 @@
         out_shape=[like((block, 2 * PAIR))] * 2 + [like((PAIR, 2 * side))] * 2,
         compiler_params=params(),
         cost_estimate=cost(16 * side * tokens * 2 * PAIR * 2, 8 * side * tokens * 2, 0),
-    )(at, *q_pieces, *g_pieces, pa, pb, vp, kt, ma, mb, sent, got)
+    )(at, *pieces, pa, pb, vp, kt, ma, mb, sent, got)
 
 
 def columns_kernel(count, high, at_ref, *refs):
@@ -807,23 +807,22 @@
     def far_rows(from_y, from_xy):
         return [from_y, over_core(from_y), from_xy, over_core(from_xy)]
 
-    qk, qs, gk, gs = pack(at, queries, grad_out, attn_out)
+    own, send = pack(queries, grad_out, attn_out)
     kp, vp, kt = pack_tokens(at, keys, values)
-    q_from_x = after(over_x(qs), kp)
-    qa, q_y, q_xy = rows_of(qk, q_from_x)
-    g_from_x = over_x(after(gs, q_from_x))
-    ga, g_y, g_xy = rows_of(after(gk, q_from_x), g_from_x)
-    gb = far_rows(g_y, g_xy)
-    pa, ma, la = side_of(qa, kp)
-    qb = far_rows(q_y, after(q_xy, la))
-    pb, mb, lb, sent = side_of(qb, kp, la)
+    from_x = after(over_x(send), kp)
+    ra, r_y, r_xy = rows_of(own, from_x)
+    x_from_x = over_x(after(qx, from_x))
+    pa, ma, la = side_of(ra, kp)
+    rb = far_rows(r_y, after(r_xy, la))
+    x_y = over_y(after(qx, r_xy))
+    pb, mb, lb, sent = side_of(rb, kp, la)
     send = merge(la, lb, over_core(sent))
     got = over_y(send)
-    x_from_x = over_x(after(qx, la))
-    xa, x_y, x_xy = rows_of(after(qx, got), after(x_from_x, got))
+    x_xy = over_y(after(x_from_x, got))
+    xa = [qx, over_core(after(qx, got)), x_from_x, over_core(after(x_from_x, got))]
 
     def half(own, pa):
-        return half_of(at, own, qa + qb, ga + gb, pa, pb, vp, kt, ma, mb, send, got)
+        return half_of(at, own, ra + rb, pa, pb, vp, kt, ma, mb, send, got)
 
     def sum_near(keep, send):
         return add(keep, over_z(send, 1))
@@ -835,10 +834,10 @@
         near = over_z(total, 1)
         return [total, near, over_x(stack([total, near]))]
 
-    kv_keep, kv_send, dq_send, dq_keep = half(False, pa)
+    kv_keep, kv_send, dq_send, dq_keep = half(False, after(pa, x_from_x, x_y))
     first = sum_near(kv_keep, kv_send)
     far = add(dq_keep, over_core(dq_send))
-    kv_keep, kv_send, dq_send, dq_keep = half(True, after(pa, far, x_y, x_from_x))
+    kv_keep, kv_send, dq_send, dq_keep = half(True, after(pa, far))
     far = over_y(far)
     second = sum_near(kv_keep, kv_send)
     x_y, x_xy = after(x_y, dq_keep), after(x_xy, dq_keep)

time: 106 us -> 101 us (0.953)
  starting transfers between devices: 32.5 us -> 27.1 us
  waiting for transfers between devices: 41.4 us -> 44.5 us
  local copies, waits for them, and re-layouts: 4.51 us -> 3.31 us
    ppermute x40 -> x33, starting transfers between devices: 32.5 us -> 27.1 us  [swap(): return lax.ppermute(x, axis, [(i, i ^ mask) for i in range(size)])]
    ppermute x40 -> x33, waiting for transfers between devices: 41.4 us -> 44.5 us  [swap(): return lax.ppermute(x, axis, [(i, i ^ mask) for i in range(size)])]
    unnamed x18 -> x12, local copies, waits for them, and re-layouts: 3.85 us -> 3.23 us
  transfers between devices with their start and end apart: 40 -> 33, of which waited for: 17 -> 16; matrix products, arithmetic and copies ran while one was open for 0% -> 0% of each run, Pallas kernels for 21% -> 16%
where the time goes in v5:
time: 101 us
  waiting for transfers between devices  44.5 us (44%)
  starting transfers between devices  27.1 us (27%)
  Pallas kernels  25.4 us (25%)
  local copies, waits for them, and re-layouts  3.31 us (3%)
    ppermute x33, waiting for transfers between devices, swap(): return lax.ppermute(x, axis, [(i, i ^ mask) for i in range(size)])  44.5 us
    ppermute x33, starting transfers between devices, swap(): return lax.ppermute(x, axis, [(i, i ^ mask) for i in range(size)])  27.1 us
    pallas_call x2, Pallas kernels, half_of(): pl.pallas_call(functools.partial(half_kernel, count), grid_spec=pltpu.Pre...  9.96 us
    pallas_call x2, Pallas kernels, side_of(): pl.pallas_call(functools.partial(side_kernel, count, step, extra is not N...  4.72 us
    unnamed x12, local copies, waits for them, and re-layouts  3.23 us
    pallas_call x1, Pallas kernels, pack(): pl.pallas_call(pack_kernel, grid=(steps,), in_specs=[block] * 3, out_spec...  2.19 us
    pallas_call x1, Pallas kernels, tokens_out(): pl.pallas_call(tokens_kernel, in_specs=[SMEM] + [VMEM] * len(parts), out_...  2.1 us
    pallas_call x1, Pallas kernels, input_of(): pl.pallas_call(input_kernel, in_specs=[SMEM] + [VMEM] * 5, out_specs=VMEM...  2.09 us
  transfers between devices with their start and end apart: 33, of which 16 were waited for; matrix products, arithmetic and copies ran while one was open for 0% of the time, Pallas kernels for 16%

profile of v5, /device:TPU:0, one launch (start us, length us, event | category | flops | bytes accessed | tf_op | source)
XLA Modules:
  0.0 101.2 jit_solution(17616521271481510449)
XLA Ops:
  0.6 2.2 %shard_map.102 = (bf16[272,512]{1,0:T(8,128)(2,1)}, bf16[272,512]{1,0:T(8,128)(2,1)}) custom-call(bf16[128,1024]{1,0:T(8,128)(2,1)} %q_ref.1, bf16[128,1024]{1,0:T(8,128)(2,1)} %g_ref.1, bf16[128,1024]{1,0:T(8,128)(2,1)} %o_ref.1), custom_call_target="tpu_custom_call" | custom-call | flops 1 | bytes 1 | tf_op jit(solution)/shard_map/pallas_call | solution.py:382
  2.8 2.9 %collective-permute-start.1 = (bf16[272,512]{1,0:T(8,128)(2,1)}, bf16[272,512]{1,0:T(8,128)(2,1)S(1)}, u32[]{:S(2)}, u32[]{:S(2)}) collective-permute-start(bf16[272,512]{1,0:T(8,128)(2,1)} %get-tuple-element.45), channel_id=1, source_target_pairs={{0,4},{4,0},{8,12},{12,8},{16,20},{20,16},{24,28},{28,24},{1,5},{5... | collective-permute-start | bytes 835592 | tf_op jit(solution)/shard_map/ppermute | solution.py:191
  5.8 1.5 %collective-permute-start.3 = (bf16[272,512]{1,0:T(8,128)(2,1)}, bf16[272,512]{1,0:T(8,128)(2,1)S(1)}, u32[]{:S(2)}, u32[]{:S(2)}) collective-permute-start(bf16[272,512]{1,0:T(8,128)(2,1)} %get-tuple-element.44.refs_0_), channel_id=1, source_target_pairs={{0,2},{1,3},{2,0},{3,1},{4,6},{5,7},{6,4},{7,5},{8,10},{9,11},{10,... | collective-permute-start | bytes 835592 | tf_op jit(solution)/shard_map/ppermute | solution.py:191
  7.3 0.1 stack.23.at_ref
  7.4 1.1 %copy-done.3 = bf16[384,1024]{1,0:T(8,128)(2,1)S(1)} copy-done((bf16[384,1024]{1,0:T(8,128)(2,1)S(1)}, bf16[384,1024]{1,0:T(8,128)(2,1)}, u32[]{:S(2)}) %copy-start.3) | copy-done | bytes 786456
  8.5 1.1 %copy-done.4 = bf16[384,1024]{1,0:T(8,128)(2,1)S(1)} copy-done((bf16[384,1024]{1,0:T(8,128)(2,1)S(1)}, bf16[384,1024]{1,0:T(8,128)(2,1)}, u32[]{:S(2)}) %copy-start.4) | copy-done | bytes 786456
  9.6 1.1 %shard_map.103 = (bf16[384,512]{1,0:T(8,128)(2,1)S(1)}, bf16[384,512]{1,0:T(8,128)(2,1)S(1)}, bf16[512,384]{1,0:T(8,128)(2,1)S(1)}) custom-call(s32[5]{0:T(128)S(1)} %stack.23.at_ref, bf16[384,1024]{1,0:T(8,128)(2,1)S(1)} %copy-done.3, bf16[384,1024]{1,0:T(8,128)(2,1)S(1)} %copy-done.4), custom_call_target="tpu_custom_call" | custom-call | flops 1 | bytes 1 | tf_op jit(solution)/shard_map/pallas_call | solution.py:407
  10.7 1.9 %collective-permute-done.1.refs_2_ = bf16[272,512]{1,0:T(8,128)(2,1)S(1)} collective-permute-done((bf16[272,512]{1,0:T(8,128)(2,1)}, bf16[272,512]{1,0:T(8,128)(2,1)S(1)}, u32[]{:S(2)}, u32[]{:S(2)}) %collective-permute-start.1) | collective-permute-done | bytes 278560 | tf_op jit(solution)/shard_map/ppermute | solution.py:191
  12.6 1.8 %collective-permute-start.5 = (bf16[272,512]{1,0:T(8,128)(2,1)S(1)}, bf16[272,512]{1,0:T(8,128)(2,1)S(1)}, u32[]{:S(2)}, u32[]{:S(2)}) collective-permute-start(bf16[272,512]{1,0:T(8,128)(2,1)S(1)} %collective-permute-done.1.refs_2_), channel_id=1, source_target_pairs={{0,2},{1,3},{2,0},{3,1},{4,6},{5,7},{6,4},{7,5},{8,10},{9,11},{10,... | collective-permute-start | bytes 835592 | tf_op jit(solution)/shard_map/ppermute | solution.py:191
  14.4 0.6 collective-permute-done.3.refs_0_.refs_4_
  15.1 0.0 copy-start
  15.1 0.9 copy-done
  16.0 2.4 %shard_map.104 = (bf16[8,384,512]{2,1,0:T(8,128)(2,1)S(1)}, f32[4,2,512]{2,1,0:T(2,128)S(1)}, f32[4,2,512]{2,1,0:T(2,128)S(1)}) custom-call(bf16[272,512]{1,0:T(8,128)(2,1)S(1)} %copy-done, bf16[272,512]{1,0:T(8,128)(2,1)S(1)} %collective-permute-done.refs_1_, bf16[272,512]{1,0:T(8,128)(2,1)S(1)} %collective-permute-done.1.refs_2_, ...), custom_call_target="tpu_custom_call" | custom-call | flops 1 | bytes 1 | tf_op jit(solution)/shard_map/pallas_call | solution.py:514
  18.4 3.3 %collective-permute-done.5.refs_2_.refs_6_ = bf16[272,512]{1,0:T(8,128)(2,1)S(1)} collective-permute-done((bf16[272,512]{1,0:T(8,128)(2,1)S(1)}, bf16[272,512]{1,0:T(8,128)(2,1)S(1)}, u32[]{:S(2)}, u32[]{:S(2)}) %collective-permute-start.5) | collective-permute-done | bytes 278560 | tf_op jit(solution)/shard_map/ppermute | solution.py:191
  21.7 1.7 %collective-permute-start.10 = (bf16[128,1024]{1,0:T(8,128)(2,1)S(1)}, bf16[128,1024]{1,0:T(8,128)(2,1)S(1)}, u32[]{:S(2)}, u32[]{:S(2)}) collective-permute-start(bf16[128,1024]{1,0:T(8,128)(2,1)S(1)} %copy-done.5), channel_id=1, source_target_pairs={{0,4},{4,0},{8,12},{12,8},{16,20},{20,16},{24,28},{28,24},{1,5},{5... | collective-permute-start | bytes 786440 | tf_op jit(solution)/shard_map/ppermute | solution.py:191
  23.5 1.5 %collective-permute-start.12 = (bf16[128,1024]{1,0:T(8,128)(2,1)S(1)}, bf16[128,1024]{1,0:T(8,128)(2,1)S(1)}, u32[]{:S(2)}, u32[]{:S(2)}) collective-permute-start(bf16[128,1024]{1,0:T(8,128)(2,1)S(1)} %copy-done.5), channel_id=1, source_target_pairs={{0,2},{1,3},{2,0},{3,1},{4,6},{5,7},{6,4},{7,5},{8,10},{9,11},{10,... | collective-permute-start | bytes 786440 | tf_op jit(solution)/shard_map/ppermute | solution.py:191
  25.0 2.4 %shard_map.105 = (bf16[8,384,512]{2,1,0:T(8,128)(2,1)S(1)}, f32[4,2,512]{2,1,0:T(2,128)S(1)}, f32[4,2,512]{2,1,0:T(2,128)S(1)}, f32[4,2,1024]{2,1,0:T(2,128)S(1)}) custom-call(bf16[272,512]{1,0:T(8,128)(2,1)S(1)} %collective-permute-done.3.refs_0_.refs_4_, bf16[272,512]{1,0:T(8,128)(2,1)S(1)} %collective-permute-done.4.refs_1_.refs_5_, ...), custom_call_target="tpu_custom_call" | custom-call | flops 1 | bytes 1 | tf_op jit(solution)/shard_map/pallas_call | solution.py:514
  27.4 0.1 collective-permute-start.7
  27.4 1.2 %collective-permute-done.7.got_ref = f32[4,2,1024]{2,1,0:T(2,128)S(1)} collective-permute-done((f32[4,2,1024]{2,1,0:T(2,128)S(1)}, f32[4,2,1024]{2,1,0:T(2,128)S(1)}, u32[]{:S(2)}, u32[]{:S(2)}) %collective-permute-start.7) | collective-permute-done | bytes 32800 | tf_op jit(solution)/shard_map/ppermute | solution.py:191
  28.7 0.6 collective-permute-start.8
  29.2 1.2 %collective-permute-done.10.refs_2_ = bf16[128,1024]{1,0:T(8,128)(2,1)S(1)} collective-permute-done((bf16[128,1024]{1,0:T(8,128)(2,1)S(1)}, bf16[128,1024]{1,0:T(8,128)(2,1)S(1)}, u32[]{:S(2)}, u32[]{:S(2)}) %collective-permute-start.10) | collective-permute-done | bytes 262176 | tf_op jit(solution)/shard_map/ppermute | solution.py:191
  30.5 1.8 %collective-permute-done.12.refs_4_ = bf16[128,1024]{1,0:T(8,128)(2,1)S(1)} collective-permute-done((bf16[128,1024]{1,0:T(8,128)(2,1)S(1)}, bf16[128,1024]{1,0:T(8,128)(2,1)S(1)}, u32[]{:S(2)}, u32[]{:S(2)}) %collective-permute-start.12) | collective-permute-done | bytes 262176 | tf_op jit(solution)/shard_map/ppermute | solution.py:191
  32.2 0.4 collective-permute-done.8.refs_15_
  32.6 5.0 %shard_map.107 = (bf16[384,256]{1,0:T(8,128)(2,1)S(1)}, bf16[384,256]{1,0:T(8,128)(2,1)S(1)}, bf16[128,1024]{1,0:T(8,128)(2,1)S(1)}, bf16[128,1024]{1,0:T(8,128)(2,1)S(1)}) custom-call(s32[5]{0:T(128)S(1)} %stack.23.at_ref, bf16[272,512]{1,0:T(8,128)(2,1)S(1)} %copy-done.1, bf16[272,512]{1,0:T(8,128)(2,1)S(1)} %collective-permute-done.refs_1_, ...), custom_call_target="tpu_custom_call" | custom-call | flops 1 | bytes 1 | tf_op jit(solution)/shard_map/pallas_call | solution.py:612
  37.6 0.1 collective-permute-start.13
  37.7 1.5 %collective-permute-start.15 = (bf16[128,1024]{1,0:T(8,128)(2,1)S(1)}, bf16[128,1024]{1,0:T(8,128)(2,1)S(1)}, u32[]{:S(2)}, u32[]{:S(2)}) collective-permute-start(bf16[128,1024]{1,0:T(8,128)(2,1)S(1)} %collective-permute-done.10.refs_2_), channel_id=1, source_target_pairs={{0,2},{1,3},{2,0},{3,1},{4,6},{5,7},{6,4},{7,5},{8,10},{9,11},{10,... | collective-permute-start | bytes 786440 | tf_op jit(solution)/shard_map/ppermute | solution.py:191
  39.2 1.6 %collective-permute-start.22 = (bf16[384,256]{1,0:T(8,128)(2,1)S(1)}, bf16[384,256]{1,0:T(8,128)(2,1)S(1)}, u32[]{:S(2)}, u32[]{:S(2)}) collective-permute-start(bf16[384,256]{1,0:T(8,128)(2,1)S(1)} %get-tuple-element.73), channel_id=1, source_target_pairs={{0,8},{4,12},{8,0},{12,4},{16,24},{20,28},{24,16},{28,20},{1,9},{5... | collective-permute-start | bytes 589832 | tf_op jit(solution)/shard_map/ppermute | solution.py:191
  40.8 0.1 shard_map.108
  40.9 5.0 %shard_map.109 = (bf16[384,256]{1,0:T(8,128)(2,1)S(1)}, bf16[384,256]{1,0:T(8,128)(2,1)S(1)}, bf16[128,1024]{1,0:T(8,128)(2,1)S(1)}, bf16[128,1024]{1,0:T(8,128)(2,1)S(1)}) custom-call(s32[5]{0:T(128)S(1)} %stack.23.at_ref, bf16[272,512]{1,0:T(8,128)(2,1)S(1)} %copy-done.1, bf16[272,512]{1,0:T(8,128)(2,1)S(1)} %collective-permute-done.refs_1_, ...), custom_call_target="tpu_custom_call" | custom-call | flops 1 | bytes 1 | tf_op jit(solution)/shard_map/pallas_call | solution.py:612
  45.9 0.5 collective-permute-start.26
  46.4 0.5 collective-permute-start.9
  47.0 2.7 %collective-permute-start.23 = (bf16[384,256]{1,0:T(8,128)(2,1)S(1)}, bf16[384,256]{1,0:T(8,128)(2,1)S(1)}, u32[]{:S(2)}, u32[]{:S(2)}) collective-permute-start(bf16[384,256]{1,0:T(8,128)(2,1)S(1)} %shard_map.114.own_ref), channel_id=1, source_target_pairs={{0,16},{4,20},{8,24},{12,28},{16,0},{20,4},{24,8},{28,12},{1,17},{... | collective-permute-start | bytes 589832 | tf_op jit(solution)/shard_map/ppermute | solution.py:191
  49.6 7.2 %collective-permute-done.26.refs_1_ = bf16[384,256]{1,0:T(8,128)(2,1)S(1)} collective-permute-done((bf16[384,256]{1,0:T(8,128)(2,1)S(1)}, bf16[384,256]{1,0:T(8,128)(2,1)S(1)}, u32[]{:S(2)}, u32[]{:S(2)}) %collective-permute-start.26) | collective-permute-done | bytes 196640 | tf_op jit(solution)/shard_map/ppermute | solution.py:191
  56.8 0.1 shard_map.117.own_ref
  56.9 0.1 collective-permute-start.27
  57.0 0.1 collective-permute-start.14
  57.1 0.5 collective-permute-start.17
  57.6 5.6 %collective-permute-done.23.got_ref = bf16[384,256]{1,0:T(8,128)(2,1)S(1)} collective-permute-done((bf16[384,256]{1,0:T(8,128)(2,1)S(1)}, bf16[384,256]{1,0:T(8,128)(2,1)S(1)}, u32[]{:S(2)}, u32[]{:S(2)}) %collective-permute-start.23) | collective-permute-done | bytes 196640 | tf_op jit(solution)/shard_map/ppermute | solution.py:191
  63.2 1.4 %collective-permute-start.18 = (bf16[128,1024]{1,0:T(8,128)(2,1)S(1)}, bf16[128,1024]{1,0:T(8,128)(2,1)S(1)}, u32[]{:S(2)}, u32[]{:S(2)}) collective-permute-start(bf16[128,1024]{1,0:T(8,128)(2,1)S(1)} %shard_map.108), channel_id=1, source_target_pairs={{0,2},{1,3},{2,0},{3,1},{4,6},{5,7},{6,4},{7,5},{8,10},{9,11},{10,... | collective-permute-start | bytes 786440 | tf_op jit(solution)/shard_map/ppermute | solution.py:191
  64.6 0.1 shard_map.115.refs_0_
  64.7 2.7 %collective-permute-done.27.got_ref = bf16[384,256]{1,0:T(8,128)(2,1)S(1)} collective-permute-done((bf16[384,256]{1,0:T(8,128)(2,1)S(1)}, bf16[384,256]{1,0:T(8,128)(2,1)S(1)}, u32[]{:S(2)}, u32[]{:S(2)}) %collective-permute-start.27) | collective-permute-done | bytes 196640 | tf_op jit(solution)/shard_map/ppermute | solution.py:191
  67.4 0.8 collective-permute-start.24
  68.2 0.0 copy-start.2
  68.2 1.3 %collective-permute-start.28 = (bf16[384,256]{1,0:T(8,128)(2,1)S(1)}, bf16[384,256]{1,0:T(8,128)(2,1)S(1)}, u32[]{:S(2)}, u32[]{:S(2)}) collective-permute-start(bf16[384,256]{1,0:T(8,128)(2,1)S(1)} %shard_map.118.refs_0_.refs_3_), channel_id=1, source_target_pairs={{0,8},{4,12},{8,0},{12,4},{16,24},{20,28},{24,16},{28,20},{1,9},{5... | collective-permute-start | bytes 589832 | tf_op jit(solution)/shard_map/ppermute | solution.py:191
  69.5 0.0 collective-permute-done.18.refs_10_
  69.6 1.0 %shard_map.110 = (bf16[256,256]{1,0:T(8,128)(2,1)S(1)}, bf16[256,256]{1,0:T(8,128)(2,1)S(1)}, bf16[128,512]{1,0:T(8,128)(2,1)S(1)}, bf16[128,512]{1,0:T(8,128)(2,1)S(1)}) custom-call(s32[5]{0:T(128)S(1)} %stack.23.at_ref, bf16[128,1024]{1,0:T(8,128)(2,1)S(1)} %copy-done.5, bf16[128,1024]{1,0:T(8,128)(2,1)S(1)} %collective-permute-done.9.refs_1_, ...), custom_call_target="tpu_custom_call" | custom-call | flops 1 | bytes 1 | tf_op jit(solution)/shard_map/pallas_call | solution.py:660
  70.6 0.6 collective-permute-start.19
  71.2 3.9 %collective-permute-done.24.refs_1_ = bf16[384,256]{1,0:T(8,128)(2,1)S(1)} collective-permute-done((bf16[384,256]{1,0:T(8,128)(2,1)S(1)}, bf16[384,256]{1,0:T(8,128)(2,1)S(1)}, u32[]{:S(2)}, u32[]{:S(2)}) %collective-permute-start.24) | collective-permute-done | bytes 196640 | tf_op jit(solution)/shard_map/ppermute | solution.py:191
  75.2 0.6 collective-permute-start.25
  75.8 2.8 %collective-permute-done.28.refs_1_.refs_4_ = bf16[384,256]{1,0:T(8,128)(2,1)S(1)} collective-permute-done((bf16[384,256]{1,0:T(8,128)(2,1)S(1)}, bf16[384,256]{1,0:T(8,128)(2,1)S(1)}, u32[]{:S(2)}, u32[]{:S(2)}) %collective-permute-start.28) | collective-permute-done | bytes 196640 | tf_op jit(solution)/shard_map/ppermute | solution.py:191
  78.5 0.6 collective-permute-start.29
  79.2 0.7 collective-permute-start.20
  79.9 0.3 collective-permute-start.30
  80.2 4.0 %collective-permute-done.20.refs_2_.y_ref = bf16[256,256]{1,0:T(8,128)(2,1)S(1)} collective-permute-done((bf16[256,256]{1,0:T(8,128)(2,1)S(1)}, bf16[256,256]{1,0:T(8,128)(2,1)S(1)}, u32[]{:S(2)}, u32[]{:S(2)}) %collective-permute-start.20) | collective-permute-done | bytes 131104 | tf_op jit(solution)/shard_map/ppermute | solution.py:191
  84.2 0.1 collective-permute-start.21
  84.3 0.5 collective-permute-done.30.got_ref
  84.9 1.6 %collective-permute-start.31 = (bf16[128,256]{1,0:T(8,128)(2,1)S(1)}, bf16[128,256]{1,0:T(8,128)(2,1)S(1)}, u32[]{:S(2)}, u32[]{:S(2)}) collective-permute-start(bf16[128,256]{1,0:T(8,128)(2,1)S(1)} %get-tuple-element.81), channel_id=1, source_target_pairs={{0,16},{4,20},{8,24},{12,28},{16,0},{20,4},{24,8},{28,12},{1,17},{... | collective-permute-start | bytes 196616 | tf_op jit(solution)/shard_map/ppermute | solution.py:191
  86.5 4.7 %collective-permute-done.31.got_ref = bf16[128,256]{1,0:T(8,128)(2,1)S(1)} collective-permute-done((bf16[128,256]{1,0:T(8,128)(2,1)S(1)}, bf16[128,256]{1,0:T(8,128)(2,1)S(1)}, u32[]{:S(2)}, u32[]{:S(2)}) %collective-permute-start.31) | collective-permute-done | bytes 65568 | tf_op jit(solution)/shard_map/ppermute | solution.py:191
  91.2 0.6 shard_map.122
  91.8 1.6 %collective-permute-start.32 = (bf16[128,128]{1,0:T(8,128)(2,1)S(1)}, bf16[128,128]{1,0:T(8,128)(2,1)S(1)}, u32[]{:S(2)}, u32[]{:S(2)}) collective-permute-start(bf16[128,128]{1,0:T(8,128)(2,1)S(1)} %get-tuple-element.83), channel_id=1, source_target_pairs={{0,4},{4,0},{8,12},{12,8},{16,20},{20,16},{24,28},{28,24},{1,5},{5... | collective-permute-start | bytes 98312 | tf_op jit(solution)/shard_map/ppermute | solution.py:191
  93.3 2.4 %collective-permute-done.32.got_ref = bf16[128,128]{1,0:T(8,128)(2,1)S(1)} collective-permute-done((bf16[128,128]{1,0:T(8,128)(2,1)S(1)}, bf16[128,128]{1,0:T(8,128)(2,1)S(1)}, u32[]{:S(2)}, u32[]{:S(2)}) %collective-permute-start.32) | collective-permute-done | bytes 32800 | tf_op jit(solution)/shard_map/ppermute | solution.py:191
  95.7 1.3 %shard_map.123 = f32[128,256]{1,0:T(8,128)} custom-call(s32[5]{0:T(128)S(1)} %stack.23.at_ref, f32[128,128]{1,0:T(8,128)S(1)} %get-tuple-element.82.keep_ref, bf16[128,128]{1,0:T(8,128)(2,1)S(1)} %collective-permute-done.32.got_ref), custom_call_target="tpu_custom_call" | custom-call | flops 1 | bytes 1 | tf_op jit(solution)/shard_map/pallas_call | solution.py:750
  97.0 2.1 %shard_map.113 = bf16[128,1024]{1,0:T(8,128)(2,1)} custom-call(s32[5]{0:T(128)S(1)} %stack.23.at_ref, bf16[128,512]{1,0:T(8,128)(2,1)S(1)} %get-tuple-element.70.refs_0_.back_ref, bf16[128,512]{1,0:T(8,128)(2,1)S(1)} %collective-permute-done.19.refs_1_.x_ref, bf16[256,256]{1,0:T(8,128)(2,1)S(1)} %collective-permute-done.20.refs_2_.y_ref, ...), custom_call_target="tpu_custom_call" | custom-call | flops 1 | bytes 1 | tf_op jit(solution)/shard_map/pallas_call | solution.py:690
  99.1 2.1 %shard_map.120 = (bf16[384,1024]{1,0:T(8,128)(2,1)}, bf16[384,1024]{1,0:T(8,128)(2,1)}) custom-call(s32[5]{0:T(128)S(1)} %stack.23.at_ref, bf16[384,256]{1,0:T(8,128)(2,1)S(1)} %shard_map.115.refs_0_, bf16[384,256]{1,0:T(8,128)(2,1)S(1)} %collective-permute-done.24.refs_1_, bf16[768,256]{1,0:T(8,128)(2,1)S(1)} %collective-permute-done.25.refs_2_, ...), custom_call_target="tpu_custom_call" | custom-call | flops 1 | bytes 1 | tf_op jit(solution)/shard_map/pallas_call | solution.py:782
  (37 shorter events, 0.3 us)
Async XLA Ops:
  0.6 21.1 %copy-start.5 = (bf16[128,1024]{1,0:T(8,128)(2,1)S(1)}, bf16[128,1024]{1,0:T(8,128)(2,1)}, u32[]{:S(2)}) copy-start(bf16[128,1024]{1,0:T(8,128)(2,1)} %refs_0_.1) | copy-start | bytes 786436
  2.8 29.8 %copy-start.1 = (bf16[272,512]{1,0:T(8,128)(2,1)S(1)}, bf16[272,512]{1,0:T(8,128)(2,1)}, u32[]{:S(2)}) copy-start(bf16[272,512]{1,0:T(8,128)(2,1)} %get-tuple-element.44.refs_0_) | copy-start | bytes 835588
  2.8 9.8 %collective-permute-start.1 = (bf16[272,512]{1,0:T(8,128)(2,1)}, bf16[272,512]{1,0:T(8,128)(2,1)S(1)}, u32[]{:S(2)}, u32[]{:S(2)}) collective-permute-start(bf16[272,512]{1,0:T(8,128)(2,1)} %get-tuple-element.45), channel_id=1, source_target_pairs={{0,4},{4,0},{8,12},{12,8},{16,20},{20,16},{24,28},{28,24},{1,5},{5... | collective-permute-start | bytes 835592 | tf_op jit(solution)/shard_map/ppermute | solution.py:191
  5.8 9.3 %collective-permute-start = (bf16[272,512]{1,0:T(8,128)(2,1)}, bf16[272,512]{1,0:T(8,128)(2,1)S(1)}, u32[]{:S(2)}, u32[]{:S(2)}) collective-permute-start(bf16[272,512]{1,0:T(8,128)(2,1)} %get-tuple-element.44.refs_0_), channel_id=1, source_target_pairs={{0,1},{1,0},{2,3},{3,2},{4,5},{5,4},{6,7},{7,6},{8,9},{9,8},{10,11... | collective-permute-start | bytes 835592 | tf_op jit(solution)/shard_map/ppermute | solution.py:191
  5.8 9.3 %collective-permute-start.3 = (bf16[272,512]{1,0:T(8,128)(2,1)}, bf16[272,512]{1,0:T(8,128)(2,1)S(1)}, u32[]{:S(2)}, u32[]{:S(2)}) collective-permute-start(bf16[272,512]{1,0:T(8,128)(2,1)} %get-tuple-element.44.refs_0_), channel_id=1, source_target_pairs={{0,2},{1,3},{2,0},{3,1},{4,6},{5,7},{6,4},{7,5},{8,10},{9,11},{10,... | collective-permute-start | bytes 835592 | tf_op jit(solution)/shard_map/ppermute | solution.py:191
  7.4 1.1 %copy-start.3 = (bf16[384,1024]{1,0:T(8,128)(2,1)S(1)}, bf16[384,1024]{1,0:T(8,128)(2,1)}, u32[]{:S(2)}) copy-start(bf16[384,1024]{1,0:T(8,128)(2,1)} %k_ref.1) | copy-start | bytes 2359300
  8.5 1.1 %copy-start.4 = (bf16[384,1024]{1,0:T(8,128)(2,1)S(1)}, bf16[384,1024]{1,0:T(8,128)(2,1)}, u32[]{:S(2)}) copy-start(bf16[384,1024]{1,0:T(8,128)(2,1)} %v_ref.1) | copy-start | bytes 2359300
  12.6 2.4 %collective-permute-start.2 = (bf16[272,512]{1,0:T(8,128)(2,1)S(1)}, bf16[272,512]{1,0:T(8,128)(2,1)S(1)}, u32[]{:S(2)}, u32[]{:S(2)}) collective-permute-start(bf16[272,512]{1,0:T(8,128)(2,1)S(1)} %collective-permute-done.1.refs_2_), channel_id=1, source_target_pairs={{0,1},{1,0},{2,3},{3,2},{4,5},{5,4},{6,7},{7,6},{8,9},{9,8},{10,11... | collective-permute-start | bytes 835592 | tf_op jit(solution)/shard_map/ppermute | solution.py:191
  12.6 9.1 %collective-permute-start.5 = (bf16[272,512]{1,0:T(8,128)(2,1)S(1)}, bf16[272,512]{1,0:T(8,128)(2,1)S(1)}, u32[]{:S(2)}, u32[]{:S(2)}) collective-permute-start(bf16[272,512]{1,0:T(8,128)(2,1)S(1)} %collective-permute-done.1.refs_2_), channel_id=1, source_target_pairs={{0,2},{1,3},{2,0},{3,1},{4,6},{5,7},{6,4},{7,5},{8,10},{9,11},{10,... | collective-permute-start | bytes 835592 | tf_op jit(solution)/shard_map/ppermute | solution.py:191
  15.1 9.9 %collective-permute-start.4 = (bf16[272,512]{1,0:T(8,128)(2,1)S(1)}, bf16[272,512]{1,0:T(8,128)(2,1)S(1)}, u32[]{:S(2)}, u32[]{:S(2)}) collective-permute-start(bf16[272,512]{1,0:T(8,128)(2,1)S(1)} %collective-permute-done.3.refs_0_.refs_4_), channel_id=1, source_target_pairs={{0,1},{1,0},{2,3},{3,2},{4,5},{5,4},{6,7},{7,6},{8,9},{9,8},{10,11... | collective-permute-start | bytes 835592 | tf_op jit(solution)/shard_map/ppermute | solution.py:191
  15.1 1.0 copy-start
  21.7 3.2 %collective-permute-start.6 = (bf16[272,512]{1,0:T(8,128)(2,1)S(1)}, bf16[272,512]{1,0:T(8,128)(2,1)S(1)}, u32[]{:S(2)}, u32[]{:S(2)}) collective-permute-start(bf16[272,512]{1,0:T(8,128)(2,1)S(1)} %collective-permute-done.5.refs_2_.refs_6_), channel_id=1, source_target_pairs={{0,1},{1,0},{2,3},{3,2},{4,5},{5,4},{6,7},{7,6},{8,9},{9,8},{10,11... | collective-permute-start | bytes 835592 | tf_op jit(solution)/shard_map/ppermute | solution.py:191
  21.7 8.7 %collective-permute-start.10 = (bf16[128,1024]{1,0:T(8,128)(2,1)S(1)}, bf16[128,1024]{1,0:T(8,128)(2,1)S(1)}, u32[]{:S(2)}, u32[]{:S(2)}) collective-permute-start(bf16[128,1024]{1,0:T(8,128)(2,1)S(1)} %copy-done.5), channel_id=1, source_target_pairs={{0,4},{4,0},{8,12},{12,8},{16,20},{20,16},{24,28},{28,24},{1,5},{5... | collective-permute-start | bytes 786440 | tf_op jit(solution)/shard_map/ppermute | solution.py:191
  23.5 8.8 %collective-permute-start.12 = (bf16[128,1024]{1,0:T(8,128)(2,1)S(1)}, bf16[128,1024]{1,0:T(8,128)(2,1)S(1)}, u32[]{:S(2)}, u32[]{:S(2)}) collective-permute-start(bf16[128,1024]{1,0:T(8,128)(2,1)S(1)} %copy-done.5), channel_id=1, source_target_pairs={{0,2},{1,3},{2,0},{3,1},{4,6},{5,7},{6,4},{7,5},{8,10},{9,11},{10,... | collective-permute-start | bytes 786440 | tf_op jit(solution)/shard_map/ppermute | solution.py:191
  27.4 1.3 %collective-permute-start.7 = (f32[4,2,1024]{2,1,0:T(2,128)S(1)}, f32[4,2,1024]{2,1,0:T(2,128)S(1)}, u32[]{:S(2)}, u32[]{:S(2)}) collective-permute-start(f32[4,2,1024]{2,1,0:T(2,128)S(1)} %get-tuple-element.51), channel_id=1, source_target_pairs={{0,1},{1,0},{2,3},{3,2},{4,5},{5,4},{6,7},{7,6},{8,9},{9,8},{10,11... | collective-permute-start | bytes 98312 | tf_op jit(solution)/shard_map/ppermute | solution.py:191
  28.7 4.0 %collective-permute-start.8 = (f32[4,2,1024]{2,1,0:T(2,128)S(1)}, f32[4,2,1024]{2,1,0:T(2,128)S(1)}, u32[]{:S(2)}, u32[]{:S(2)}) collective-permute-start(f32[4,2,1024]{2,1,0:T(2,128)S(1)} %shard_map.106.refs_14_), channel_id=1, source_target_pairs={{0,2},{1,3},{2,0},{3,1},{4,6},{5,7},{6,4},{7,5},{8,10},{9,11},{10,... | collective-permute-start | bytes 98312 | tf_op jit(solution)/shard_map/ppermute | solution.py:191
  37.6 3.2 %collective-permute-start.13 = (bf16[128,1024]{1,0:T(8,128)(2,1)S(1)}, bf16[128,1024]{1,0:T(8,128)(2,1)S(1)}, u32[]{:S(2)}, u32[]{:S(2)}) collective-permute-start(bf16[128,1024]{1,0:T(8,128)(2,1)S(1)} %get-tuple-element.64), channel_id=1, source_target_pairs={{0,1},{1,0},{2,3},{3,2},{4,5},{5,4},{6,7},{7,6},{8,9},{9,8},{10,11... | collective-permute-start | bytes 786440 | tf_op jit(solution)/shard_map/ppermute | solution.py:191
  37.7 11.9 %collective-permute-start.15 = (bf16[128,1024]{1,0:T(8,128)(2,1)S(1)}, bf16[128,1024]{1,0:T(8,128)(2,1)S(1)}, u32[]{:S(2)}, u32[]{:S(2)}) collective-permute-start(bf16[128,1024]{1,0:T(8,128)(2,1)S(1)} %collective-permute-done.10.refs_2_), channel_id=1, source_target_pairs={{0,2},{1,3},{2,0},{3,1},{4,6},{5,7},{6,4},{7,5},{8,10},{9,11},{10,... | collective-permute-start | bytes 786440 | tf_op jit(solution)/shard_map/ppermute | solution.py:191
  39.2 7.7 %collective-permute-start.22 = (bf16[384,256]{1,0:T(8,128)(2,1)S(1)}, bf16[384,256]{1,0:T(8,128)(2,1)S(1)}, u32[]{:S(2)}, u32[]{:S(2)}) collective-permute-start(bf16[384,256]{1,0:T(8,128)(2,1)S(1)} %get-tuple-element.73), channel_id=1, source_target_pairs={{0,8},{4,12},{8,0},{12,4},{16,24},{20,28},{24,16},{28,20},{1,9},{5... | collective-permute-start | bytes 589832 | tf_op jit(solution)/shard_map/ppermute | solution.py:191
  45.9 11.0 %collective-permute-start.26 = (bf16[384,256]{1,0:T(8,128)(2,1)S(1)}, bf16[384,256]{1,0:T(8,128)(2,1)S(1)}, u32[]{:S(2)}, u32[]{:S(2)}) collective-permute-start(bf16[384,256]{1,0:T(8,128)(2,1)S(1)} %get-tuple-element.75), channel_id=1, source_target_pairs={{0,8},{4,12},{8,0},{12,4},{16,24},{20,28},{24,16},{28,20},{1,9},{5... | collective-permute-start | bytes 589832 | tf_op jit(solution)/shard_map/ppermute | solution.py:191
  46.4 10.6 %collective-permute-start.11 = (bf16[128,1024]{1,0:T(8,128)(2,1)S(1)}, bf16[128,1024]{1,0:T(8,128)(2,1)S(1)}, u32[]{:S(2)}, u32[]{:S(2)}) collective-permute-start(bf16[128,1024]{1,0:T(8,128)(2,1)S(1)} %collective-permute-done.10.refs_2_), channel_id=1, source_target_pairs={{0,1},{1,0},{2,3},{3,2},{4,5},{5,4},{6,7},{7,6},{8,9},{9,8},{10,11... | collective-permute-start | bytes 786440 | tf_op jit(solution)/shard_map/ppermute | solution.py:191
  46.4 10.7 %collective-permute-start.9 = (bf16[128,1024]{1,0:T(8,128)(2,1)S(1)}, bf16[128,1024]{1,0:T(8,128)(2,1)S(1)}, u32[]{:S(2)}, u32[]{:S(2)}) collective-permute-start(bf16[128,1024]{1,0:T(8,128)(2,1)S(1)} %copy-done.5), channel_id=1, source_target_pairs={{0,1},{1,0},{2,3},{3,2},{4,5},{5,4},{6,7},{7,6},{8,9},{9,8},{10,11... | collective-permute-start | bytes 786440 | tf_op jit(solution)/shard_map/ppermute | solution.py:191
  47.0 16.2 %collective-permute-start.23 = (bf16[384,256]{1,0:T(8,128)(2,1)S(1)}, bf16[384,256]{1,0:T(8,128)(2,1)S(1)}, u32[]{:S(2)}, u32[]{:S(2)}) collective-permute-start(bf16[384,256]{1,0:T(8,128)(2,1)S(1)} %shard_map.114.own_ref), channel_id=1, source_target_pairs={{0,16},{4,20},{8,24},{12,28},{16,0},{20,4},{24,8},{28,12},{1,17},{... | collective-permute-start | bytes 589832 | tf_op jit(solution)/shard_map/ppermute | solution.py:191
  49.6 18.6 %collective-permute-start.16 = (bf16[128,1024]{1,0:T(8,128)(2,1)S(1)}, bf16[128,1024]{1,0:T(8,128)(2,1)S(1)}, u32[]{:S(2)}, u32[]{:S(2)}) collective-permute-start(bf16[128,1024]{1,0:T(8,128)(2,1)S(1)} %collective-permute-done.15.refs_6_), channel_id=1, source_target_pairs={{0,1},{1,0},{2,3},{3,2},{4,5},{5,4},{6,7},{7,6},{8,9},{9,8},{10,11... | collective-permute-start | bytes 786440 | tf_op jit(solution)/shard_map/ppermute | solution.py:191
  56.9 10.5 %collective-permute-start.27 = (bf16[384,256]{1,0:T(8,128)(2,1)S(1)}, bf16[384,256]{1,0:T(8,128)(2,1)S(1)}, u32[]{:S(2)}, u32[]{:S(2)}) collective-permute-start(bf16[384,256]{1,0:T(8,128)(2,1)S(1)} %shard_map.117.own_ref), channel_id=1, source_target_pairs={{0,16},{4,20},{8,24},{12,28},{16,0},{20,4},{24,8},{28,12},{1,17},{... | collective-permute-start | bytes 589832 | tf_op jit(solution)/shard_map/ppermute | solution.py:191
  57.0 12.5 %collective-permute-start.14 = (bf16[128,1024]{1,0:T(8,128)(2,1)S(1)}, bf16[128,1024]{1,0:T(8,128)(2,1)S(1)}, u32[]{:S(2)}, u32[]{:S(2)}) collective-permute-start(bf16[128,1024]{1,0:T(8,128)(2,1)S(1)} %collective-permute-done.12.refs_4_), channel_id=1, source_target_pairs={{0,1},{1,0},{2,3},{3,2},{4,5},{5,4},{6,7},{7,6},{8,9},{9,8},{10,11... | collective-permute-start | bytes 786440 | tf_op jit(solution)/shard_map/ppermute | solution.py:191
  57.1 12.5 %collective-permute-start.17 = (bf16[128,1024]{1,0:T(8,128)(2,1)S(1)}, bf16[128,1024]{1,0:T(8,128)(2,1)S(1)}, u32[]{:S(2)}, u32[]{:S(2)}) collective-permute-start(bf16[128,1024]{1,0:T(8,128)(2,1)S(1)} %get-tuple-element.69), channel_id=1, source_target_pairs={{0,1},{1,0},{2,3},{3,2},{4,5},{5,4},{6,7},{7,6},{8,9},{9,8},{10,11... | collective-permute-start | bytes 786440 | tf_op jit(solution)/shard_map/ppermute | solution.py:191
  63.2 6.4 %collective-permute-start.18 = (bf16[128,1024]{1,0:T(8,128)(2,1)S(1)}, bf16[128,1024]{1,0:T(8,128)(2,1)S(1)}, u32[]{:S(2)}, u32[]{:S(2)}) collective-permute-start(bf16[128,1024]{1,0:T(8,128)(2,1)S(1)} %shard_map.108), channel_id=1, source_target_pairs={{0,2},{1,3},{2,0},{3,1},{4,6},{5,7},{6,4},{7,5},{8,10},{9,11},{10,... | collective-permute-start | bytes 786440 | tf_op jit(solution)/shard_map/ppermute | solution.py:191
  67.4 7.8 %collective-permute-start.24 = (bf16[384,256]{1,0:T(8,128)(2,1)S(1)}, bf16[384,256]{1,0:T(8,128)(2,1)S(1)}, u32[]{:S(2)}, u32[]{:S(2)}) collective-permute-start(bf16[384,256]{1,0:T(8,128)(2,1)S(1)} %shard_map.115.refs_0_), channel_id=1, source_target_pairs={{0,8},{4,12},{8,0},{12,4},{16,24},{20,28},{24,16},{28,20},{1,9},{5... | collective-permute-start | bytes 589832 | tf_op jit(solution)/shard_map/ppermute | solution.py:191
  68.2 28.9 %copy-start.2 = (bf16[1024,1024]{1,0:T(8,128)(2,1)S(1)}, bf16[1024,1024]{1,0:T(8,128)(2,1)}, u32[]{:S(2)}) copy-start(bf16[1024,1024]{1,0:T(8,128)(2,1)} %wq_ref.1) | copy-start | bytes 6291460
  68.2 10.3 %collective-permute-start.28 = (bf16[384,256]{1,0:T(8,128)(2,1)S(1)}, bf16[384,256]{1,0:T(8,128)(2,1)S(1)}, u32[]{:S(2)}, u32[]{:S(2)}) collective-permute-start(bf16[384,256]{1,0:T(8,128)(2,1)S(1)} %shard_map.118.refs_0_.refs_3_), channel_id=1, source_target_pairs={{0,8},{4,12},{8,0},{12,4},{16,24},{20,28},{24,16},{28,20},{1,9},{5... | collective-permute-start | bytes 589832 | tf_op jit(solution)/shard_map/ppermute | solution.py:191
  70.6 8.5 %collective-permute-start.19 = (bf16[128,512]{1,0:T(8,128)(2,1)S(1)}, bf16[128,512]{1,0:T(8,128)(2,1)S(1)}, u32[]{:S(2)}, u32[]{:S(2)}) collective-permute-start(bf16[128,512]{1,0:T(8,128)(2,1)S(1)} %get-tuple-element.71), channel_id=1, source_target_pairs={{0,4},{4,0},{8,12},{12,8},{16,20},{20,16},{24,28},{28,24},{1,5},{5... | collective-permute-start | bytes 393224 | tf_op jit(solution)/shard_map/ppermute | solution.py:191
  75.2 24.0 %collective-permute-start.25 = (bf16[768,256]{1,0:T(8,128)(2,1)S(1)}, bf16[768,256]{1,0:T(8,128)(2,1)S(1)}, u32[]{:S(2)}, u32[]{:S(2)}) collective-permute-start(bf16[768,256]{1,0:T(8,128)(2,1)S(1)} %shard_map.116), channel_id=1, source_target_pairs={{0,4},{4,0},{8,12},{12,8},{16,20},{20,16},{24,28},{28,24},{1,5},{5... | collective-permute-start | bytes 1179656 | tf_op jit(solution)/shard_map/ppermute | solution.py:191
  78.5 20.6 %collective-permute-start.29 = (bf16[768,256]{1,0:T(8,128)(2,1)S(1)}, bf16[768,256]{1,0:T(8,128)(2,1)S(1)}, u32[]{:S(2)}, u32[]{:S(2)}) collective-permute-start(bf16[768,256]{1,0:T(8,128)(2,1)S(1)} %shard_map.119), channel_id=1, source_target_pairs={{0,4},{4,0},{8,12},{12,8},{16,20},{20,16},{24,28},{28,24},{1,5},{5... | collective-permute-start | bytes 1179656 | tf_op jit(solution)/shard_map/ppermute | solution.py:191
  79.2 5.0 %collective-permute-start.20 = (bf16[256,256]{1,0:T(8,128)(2,1)S(1)}, bf16[256,256]{1,0:T(8,128)(2,1)S(1)}, u32[]{:S(2)}, u32[]{:S(2)}) collective-permute-start(bf16[256,256]{1,0:T(8,128)(2,1)S(1)} %shard_map.111), channel_id=1, source_target_pairs={{0,2},{1,3},{2,0},{3,1},{4,6},{5,7},{6,4},{7,5},{8,10},{9,11},{10,... | collective-permute-start | bytes 393224 | tf_op jit(solution)/shard_map/ppermute | solution.py:191
  79.9 5.0 %collective-permute-start.30 = (bf16[256,256]{1,0:T(8,128)(2,1)S(1)}, bf16[256,256]{1,0:T(8,128)(2,1)S(1)}, u32[]{:S(2)}, u32[]{:S(2)}) collective-permute-start(bf16[256,256]{1,0:T(8,128)(2,1)S(1)} %get-tuple-element.79), channel_id=1, source_target_pairs={{0,8},{4,12},{8,0},{12,4},{16,24},{20,28},{24,16},{28,20},{1,9},{5... | collective-permute-start | bytes 393224 | tf_op jit(solution)/shard_map/ppermute | solution.py:191
  84.2 12.8 %collective-permute-start.21 = (bf16[512,128]{1,0:T(8,128)(2,1)S(1)}, bf16[512,128]{1,0:T(8,128)(2,1)S(1)}, u32[]{:S(2)}, u32[]{:S(2)}) collective-permute-start(bf16[512,128]{1,0:T(8,128)(2,1)S(1)} %shard_map.112), channel_id=1, source_target_pairs={{0,1},{1,0},{2,3},{3,2},{4,5},{5,4},{6,7},{7,6},{8,9},{9,8},{10,11... | collective-permute-start | bytes 393224 | tf_op jit(solution)/shard_map/ppermute | solution.py:191
  84.9 6.3 %collective-permute-start.31 = (bf16[128,256]{1,0:T(8,128)(2,1)S(1)}, bf16[128,256]{1,0:T(8,128)(2,1)S(1)}, u32[]{:S(2)}, u32[]{:S(2)}) collective-permute-start(bf16[128,256]{1,0:T(8,128)(2,1)S(1)} %get-tuple-element.81), channel_id=1, source_target_pairs={{0,16},{4,20},{8,24},{12,28},{16,0},{20,4},{24,8},{28,12},{1,17},{... | collective-permute-start | bytes 196616 | tf_op jit(solution)/shard_map/ppermute | solution.py:191
  91.8 4.0 %collective-permute-start.32 = (bf16[128,128]{1,0:T(8,128)(2,1)S(1)}, bf16[128,128]{1,0:T(8,128)(2,1)S(1)}, u32[]{:S(2)}, u32[]{:S(2)}) collective-permute-start(bf16[128,128]{1,0:T(8,128)(2,1)S(1)} %get-tuple-element.83), channel_id=1, source_target_pairs={{0,4},{4,0},{8,12},{12,8},{16,20},{20,16},{24,28},{28,24},{1,5},{5... | collective-permute-start | bytes 98312 | tf_op jit(solution)/shard_map/ppermute | solution.py:191

commit v6 on v5

--- a/solution.py
+++ b/solution.py
@@ -763,17 +763,18 @@
     size = refs[0].shape[0] // 2
     for half in range(2):
         group = 2 * (y ^ (1 - half))
-        keep, near, got = refs[3 * half : 3 * half + 3]
+        keep, near, keep_x, near_x = refs[4 * half : 4 * half + 4]
         for i, k in enumerate(ORDERS[0] + ORDERS[1]):
             b = z ^ k
             row = pl.multiple_of((b % 2) * size, 16)
             own = (keep if i < 2 else near)[span(i % 2, size)]
+            got = (keep_x if i < 2 else near_x)[span(i % 2, size)]
             for out_ref, which in ((key_ref, 0), (val_ref, 1)):
 
                 @pl.when(b // 2 == which)
                 def _():
                     for c in range(2):
-                        for odd, block in ((0, own[:, span(c)]), (1, got[span(i, size), span(c)])):
+                        for odd, block in ((0, own[:, span(c)]), (1, got[:, span(c)])):
                             col = pl.multiple_of((2 * (group + c) + (x ^ odd)) * PAIR, PAIR)
                             out_ref[pl.ds(row, size), pl.ds(col, PAIR)] = block
 
@@ -811,35 +812,36 @@
     kp, vp, kt = pack_tokens(at, keys, values)
     from_x = after(over_x(send), kp)
     ra, r_y, r_xy = rows_of(own, from_x)
-    x_from_x = over_x(after(qx, from_x))
+    x_from_x = over_x(after(qx, own))
     pa, ma, la = side_of(ra, kp)
-    rb = far_rows(r_y, after(r_xy, la))
+    rb = far_rows(r_y, after(r_xy, la, x_from_x))
     x_y = over_y(after(qx, r_xy))
     pb, mb, lb, sent = side_of(rb, kp, la)
     send = merge(la, lb, over_core(sent))
     got = over_y(send)
-    x_xy = over_y(after(x_from_x, got))
+    x_xy = over_y(after(x_from_x, send))
     xa = [qx, over_core(after(qx, got)), x_from_x, over_core(after(x_from_x, got))]
 
     def half(own, pa):
         return half_of(at, own, ra + rb, pa, pb, vp, kt, ma, mb, send, got)
 
-    def sum_near(keep, send):
-        return add(keep, over_z(send, 1))
+    def sum_near(keep, send, *deps):
+        return add(after(keep, *deps), over_z(send, 1))
 
     def sum_far(near):
         return add_turned(near, over_z(near, 2))
 
     def spread(total):
         near = over_z(total, 1)
-        return [total, near, over_x(stack([total, near]))]
+        return [total, near, over_x(total), over_x(near)]
 
     kv_keep, kv_send, dq_send, dq_keep = half(False, after(pa, x_from_x, x_y))
-    first = sum_near(kv_keep, kv_send)
+    first = (kv_keep, kv_send)
     far = add(dq_keep, over_core(dq_send))
     kv_keep, kv_send, dq_send, dq_keep = half(True, after(pa, far))
     far = over_y(far)
-    second = sum_near(kv_keep, kv_send)
+    first = sum_near(after(first[0], dq_keep), first[1])
+    second = sum_near(kv_keep, kv_send, far)
     x_y, x_xy = after(x_y, dq_keep), after(x_xy, dq_keep)
     w_keep, w_send, back, back_s = columns_of(
         at, high, xa + far_rows(x_y, x_xy), dq_keep, over_core(dq_send), far
@@ -847,7 +849,7 @@
     first, second = sum_far(first), sum_far(second)
     w_keep, w_send = weight_near(w_keep, over_z(w_send, 1))
     w_keep, w_send = weight_sum(at, w_keep, over_z(w_send, 2))
-    grad_weight = weight_out(at, w_keep, over_x(w_send))
+    w_got = over_x(w_send)
 
     from_x = over_x(back_s)
     size = back.shape[0]
@@ -855,7 +857,10 @@
     from_y = over_y(stack([back, from_x], [part(2, 2)] * 2))
     from_core = over_core(stack([back, from_x, from_y], [part(1, 1)] * 3))
     grad_input = input_of(at, back, from_x, from_y, from_core, wq)
-    grad_keys, grad_values = tokens_out(at, *keys.shape, spread(first) + spread(second))
+    first = spread(first)
+    second = spread(after(second, first[2]))
+    grad_keys, grad_values = tokens_out(at, *keys.shape, first + second)
+    grad_weight = weight_out(at, after(w_keep, grad_input, grad_keys), w_got)
     return (grad_input, grad_keys, grad_values, grad_weight)
 
 

time: 101 us -> 94.1 us (0.932)
  waiting for transfers between devices: 44.5 us -> 31.1 us
  starting transfers between devices: 27.1 us -> 33.3 us
    ppermute x33 -> x35, waiting for transfers between devices: 44.5 us -> 31.1 us  [swap(): return lax.ppermute(x, axis, [(i, i ^ mask) for i in range(size)])]
    ppermute x33 -> x35, starting transfers between devices: 27.1 us -> 33.3 us  [swap(): return lax.ppermute(x, axis, [(i, i ^ mask) for i in range(size)])]
  transfers between devices with their start and end apart: 33 -> 35, of which waited for: 16 -> 12; matrix products, arithmetic and copies ran while one was open for 0% -> 0% of each run, Pallas kernels for 16% -> 18%
where the time goes in v6:
time: 94.1 us; the launch traced here: 93.9 us
  starting transfers between devices  33.3 us (35%)
  waiting for transfers between devices  31.1 us (33%)
  Pallas kernels  25.4 us (27%)
  local copies, waits for them, and re-layouts  3.32 us (4%)
    ppermute x35, starting transfers between devices, swap(): return lax.ppermute(x, axis, [(i, i ^ mask) for i in range(size)])  33.3 us
    ppermute x35, waiting for transfers between devices, swap(): return lax.ppermute(x, axis, [(i, i ^ mask) for i in range(size)])  31.1 us
    pallas_call x2, Pallas kernels, half_of(): pl.pallas_call(functools.partial(half_kernel, count), grid_spec=pltpu.Pre...  9.95 us
    pallas_call x2, Pallas kernels, side_of(): pl.pallas_call(functools.partial(side_kernel, count, step, extra is not N...  4.71 us
    unnamed x12, local copies, waits for them, and re-layouts  3.23 us
    pallas_call x1, Pallas kernels, pack(): pl.pallas_call(pack_kernel, grid=(steps,), in_specs=[block] * 3, out_spec...  2.19 us
    pallas_call x1, Pallas kernels, tokens_out(): pl.pallas_call(tokens_kernel, in_specs=[SMEM] + [VMEM] * len(parts), out_...  2.12 us
    pallas_call x1, Pallas kernels, input_of(): pl.pallas_call(input_kernel, in_specs=[SMEM] + [VMEM] * 5, out_specs=VMEM...  2.09 us
  transfers between devices with their start and end apart: 35, of which 12 were waited for; matrix products, arithmetic and copies ran while one was open for 0% of the time, Pallas kernels for 18%

profile of v6, /device:TPU:0, one launch (start us, length us, event | category | flops | bytes accessed | tf_op | source)
XLA Modules:
  0.0 93.9 jit_solution(10254660013085989513)
XLA Ops:
  0.6 0.0 copy-start.5
  0.6 2.2 %shard_map.102 = (bf16[272,512]{1,0:T(8,128)(2,1)}, bf16[272,512]{1,0:T(8,128)(2,1)}) custom-call(bf16[128,1024]{1,0:T(8,128)(2,1)} %q_ref.1, bf16[128,1024]{1,0:T(8,128)(2,1)} %g_ref.1, bf16[128,1024]{1,0:T(8,128)(2,1)} %o_ref.1), custom_call_target="tpu_custom_call" | custom-call | flops 1 | bytes 1 | tf_op jit(solution)/shard_map/pallas_call | solution.py:382
  2.8 2.9 %collective-permute-start.1 = (bf16[272,512]{1,0:T(8,128)(2,1)}, bf16[272,512]{1,0:T(8,128)(2,1)S(1)}, u32[]{:S(2)}, u32[]{:S(2)}) collective-permute-start(bf16[272,512]{1,0:T(8,128)(2,1)} %get-tuple-element.50), channel_id=1, source_target_pairs={{0,4},{4,0},{8,12},{12,8},{16,20},{20,16},{24,28},{28,24},{1,5},{5... | collective-permute-start | bytes 835592 | tf_op jit(solution)/shard_map/ppermute | solution.py:191
  5.8 1.5 %collective-permute-start.3 = (bf16[272,512]{1,0:T(8,128)(2,1)}, bf16[272,512]{1,0:T(8,128)(2,1)S(1)}, u32[]{:S(2)}, u32[]{:S(2)}) collective-permute-start(bf16[272,512]{1,0:T(8,128)(2,1)} %get-tuple-element.49.refs_0_), channel_id=1, source_target_pairs={{0,2},{1,3},{2,0},{3,1},{4,6},{5,7},{6,4},{7,5},{8,10},{9,11},{10,... | collective-permute-start | bytes 835592 | tf_op jit(solution)/shard_map/ppermute | solution.py:191
  7.3 0.1 stack.23.at_ref
  7.4 1.1 %copy-done.3 = bf16[384,1024]{1,0:T(8,128)(2,1)S(1)} copy-done((bf16[384,1024]{1,0:T(8,128)(2,1)S(1)}, bf16[384,1024]{1,0:T(8,128)(2,1)}, u32[]{:S(2)}) %copy-start.3) | copy-done | bytes 786456
  8.5 1.1 %copy-done.4 = bf16[384,1024]{1,0:T(8,128)(2,1)S(1)} copy-done((bf16[384,1024]{1,0:T(8,128)(2,1)S(1)}, bf16[384,1024]{1,0:T(8,128)(2,1)}, u32[]{:S(2)}) %copy-start.4) | copy-done | bytes 786456
  9.6 1.1 %shard_map.103 = (bf16[384,512]{1,0:T(8,128)(2,1)S(1)}, bf16[384,512]{1,0:T(8,128)(2,1)S(1)}, bf16[512,384]{1,0:T(8,128)(2,1)S(1)}) custom-call(s32[5]{0:T(128)S(1)} %stack.23.at_ref, bf16[384,1024]{1,0:T(8,128)(2,1)S(1)} %copy-done.3, bf16[384,1024]{1,0:T(8,128)(2,1)S(1)} %copy-done.4), custom_call_target="tpu_custom_call" | custom-call | flops 1 | bytes 1 | tf_op jit(solution)/shard_map/pallas_call | solution.py:407
  10.7 1.9 %collective-permute-done.1.refs_2_ = bf16[272,512]{1,0:T(8,128)(2,1)S(1)} collective-permute-done((bf16[272,512]{1,0:T(8,128)(2,1)}, bf16[272,512]{1,0:T(8,128)(2,1)S(1)}, u32[]{:S(2)}, u32[]{:S(2)}) %collective-permute-start.1) | collective-permute-done | bytes 278560 | tf_op jit(solution)/shard_map/ppermute | solution.py:191
  12.6 0.0 collective-permute-start.2
  12.6 1.8 %collective-permute-start.5 = (bf16[272,512]{1,0:T(8,128)(2,1)S(1)}, bf16[272,512]{1,0:T(8,128)(2,1)S(1)}, u32[]{:S(2)}, u32[]{:S(2)}) collective-permute-start(bf16[272,512]{1,0:T(8,128)(2,1)S(1)} %collective-permute-done.1.refs_2_), channel_id=1, source_target_pairs={{0,2},{1,3},{2,0},{3,1},{4,6},{5,7},{6,4},{7,5},{8,10},{9,11},{10,... | collective-permute-start | bytes 835592 | tf_op jit(solution)/shard_map/ppermute | solution.py:191
  14.4 1.5 %collective-permute-start.6 = (bf16[128,1024]{1,0:T(8,128)(2,1)}, bf16[128,1024]{1,0:T(8,128)(2,1)S(1)}, u32[]{:S(2)}, u32[]{:S(2)}) collective-permute-start(bf16[128,1024]{1,0:T(8,128)(2,1)} %refs_0_.1), channel_id=1, source_target_pairs={{0,4},{4,0},{8,12},{12,8},{16,20},{20,16},{24,28},{28,24},{1,5},{5... | collective-permute-start | bytes 786440 | tf_op jit(solution)/shard_map/ppermute | solution.py:191
  15.9 0.0 collective-permute-start.4
  15.9 0.0 collective-permute-done.refs_1_
  15.9 0.0 copy-start
  15.9 0.9 %copy-done = bf16[272,512]{1,0:T(8,128)(2,1)S(1)} copy-done((bf16[272,512]{1,0:T(8,128)(2,1)S(1)}, bf16[272,512]{1,0:T(8,128)(2,1)}, u32[]{:S(2)}) %copy-start) | copy-done | bytes 278552
  16.9 2.4 %shard_map.104 = (bf16[8,384,512]{2,1,0:T(8,128)(2,1)S(1)}, f32[4,2,512]{2,1,0:T(2,128)S(1)}, f32[4,2,512]{2,1,0:T(2,128)S(1)}) custom-call(bf16[272,512]{1,0:T(8,128)(2,1)S(1)} %copy-done, bf16[272,512]{1,0:T(8,128)(2,1)S(1)} %collective-permute-done.refs_1_, bf16[272,512]{1,0:T(8,128)(2,1)S(1)} %collective-permute-done.1.refs_2_, ...), custom_call_target="tpu_custom_call" | custom-call | flops 1 | bytes 1 | tf_op jit(solution)/shard_map/pallas_call | solution.py:514
  19.2 3.8 %collective-permute-done.6.refs_2_ = bf16[128,1024]{1,0:T(8,128)(2,1)S(1)} collective-permute-done((bf16[128,1024]{1,0:T(8,128)(2,1)}, bf16[128,1024]{1,0:T(8,128)(2,1)S(1)}, u32[]{:S(2)}, u32[]{:S(2)}) %collective-permute-start.6) | collective-permute-done | bytes 262176 | tf_op jit(solution)/shard_map/ppermute | solution.py:191
  23.1 0.4 collective-permute-start.12
  23.5 1.1 %collective-permute-done.7.refs_3_.refs_7_ = bf16[272,512]{1,0:T(8,128)(2,1)S(1)} collective-permute-done((bf16[272,512]{1,0:T(8,128)(2,1)S(1)}, bf16[272,512]{1,0:T(8,128)(2,1)S(1)}, u32[]{:S(2)}, u32[]{:S(2)}) %collective-permute-start.7) | collective-permute-done | bytes 278560 | tf_op jit(solution)/shard_map/ppermute | solution.py:191
  24.6 2.4 %shard_map.105 = (bf16[8,384,512]{2,1,0:T(8,128)(2,1)S(1)}, f32[4,2,512]{2,1,0:T(2,128)S(1)}, f32[4,2,512]{2,1,0:T(2,128)S(1)}, f32[4,2,1024]{2,1,0:T(2,128)S(1)}) custom-call(bf16[272,512]{1,0:T(8,128)(2,1)S(1)} %collective-permute-done.3.refs_0_.refs_4_, bf16[272,512]{1,0:T(8,128)(2,1)S(1)} %collective-permute-done.4.refs_1_.refs_5_, ...), custom_call_target="tpu_custom_call" | custom-call | flops 1 | bytes 1 | tf_op jit(solution)/shard_map/pallas_call | solution.py:514
  27.0 0.2 collective-permute-start.8
  27.2 1.1 %collective-permute-done.8.got_ref = f32[4,2,1024]{2,1,0:T(2,128)S(1)} collective-permute-done((f32[4,2,1024]{2,1,0:T(2,128)S(1)}, f32[4,2,1024]{2,1,0:T(2,128)S(1)}, u32[]{:S(2)}, u32[]{:S(2)}) %collective-permute-start.8) | collective-permute-done | bytes 32800 | tf_op jit(solution)/shard_map/ppermute | solution.py:191
  28.3 0.6 collective-permute-start.9
  28.9 3.2 %collective-permute-done.12.refs_4_ = bf16[128,1024]{1,0:T(8,128)(2,1)S(1)} collective-permute-done((bf16[128,1024]{1,0:T(8,128)(2,1)S(1)}, bf16[128,1024]{1,0:T(8,128)(2,1)S(1)}, u32[]{:S(2)}, u32[]{:S(2)}) %collective-permute-start.12) | collective-permute-done | bytes 262176 | tf_op jit(solution)/shard_map/ppermute | solution.py:191
  32.1 0.4 collective-permute-done.9.refs_15_
  32.5 5.0 %shard_map.107 = (bf16[384,256]{1,0:T(8,128)(2,1)S(1)}, bf16[384,256]{1,0:T(8,128)(2,1)S(1)}, bf16[128,1024]{1,0:T(8,128)(2,1)S(1)}, bf16[128,1024]{1,0:T(8,128)(2,1)S(1)}) custom-call(s32[5]{0:T(128)S(1)} %stack.23.at_ref, bf16[272,512]{1,0:T(8,128)(2,1)S(1)} %copy-done.1, bf16[272,512]{1,0:T(8,128)(2,1)S(1)} %collective-permute-done.refs_1_, ...), custom_call_target="tpu_custom_call" | custom-call | flops 1 | bytes 1 | tf_op jit(solution)/shard_map/pallas_call | solution.py:612
  37.5 0.1 collective-permute-start.13
  37.6 0.5 collective-permute-start.15
  38.0 1.7 %collective-permute-start.22 = (bf16[384,256]{1,0:T(8,128)(2,1)S(1)}, bf16[384,256]{1,0:T(8,128)(2,1)S(1)}, u32[]{:S(2)}, u32[]{:S(2)}) collective-permute-start(bf16[384,256]{1,0:T(8,128)(2,1)S(1)} %get-tuple-element.80), channel_id=1, source_target_pairs={{0,8},{4,12},{8,0},{12,4},{16,24},{20,28},{24,16},{28,20},{1,9},{5... | collective-permute-start | bytes 589832 | tf_op jit(solution)/shard_map/ppermute | solution.py:191
  39.7 0.1 shard_map.108
  39.8 1.6 %collective-permute-start.18 = (bf16[128,1024]{1,0:T(8,128)(2,1)S(1)}, bf16[128,1024]{1,0:T(8,128)(2,1)S(1)}, u32[]{:S(2)}, u32[]{:S(2)}) collective-permute-start(bf16[128,1024]{1,0:T(8,128)(2,1)S(1)} %shard_map.108), channel_id=1, source_target_pairs={{0,2},{1,3},{2,0},{3,1},{4,6},{5,7},{6,4},{7,5},{8,10},{9,11},{10,... | collective-permute-start | bytes 786440 | tf_op jit(solution)/shard_map/ppermute | solution.py:191
  41.4 5.0 %shard_map.109 = (bf16[384,256]{1,0:T(8,128)(2,1)S(1)}, bf16[384,256]{1,0:T(8,128)(2,1)S(1)}, bf16[128,1024]{1,0:T(8,128)(2,1)S(1)}, bf16[128,1024]{1,0:T(8,128)(2,1)S(1)}) custom-call(s32[5]{0:T(128)S(1)} %stack.23.at_ref, bf16[272,512]{1,0:T(8,128)(2,1)S(1)} %copy-done.1, bf16[272,512]{1,0:T(8,128)(2,1)S(1)} %collective-permute-done.refs_1_, ...), custom_call_target="tpu_custom_call" | custom-call | flops 1 | bytes 1 | tf_op jit(solution)/shard_map/pallas_call | solution.py:612
  46.3 0.5 collective-permute-start.27
  46.9 0.0 copy-start.2
  46.9 2.6 %collective-permute-start.23 = (bf16[384,256]{1,0:T(8,128)(2,1)S(1)}, bf16[384,256]{1,0:T(8,128)(2,1)S(1)}, u32[]{:S(2)}, u32[]{:S(2)}) collective-permute-start(bf16[384,256]{1,0:T(8,128)(2,1)S(1)} %shard_map.114.own_ref), channel_id=1, source_target_pairs={{0,16},{4,20},{8,24},{12,28},{16,0},{20,4},{24,8},{28,12},{1,17},{... | collective-permute-start | bytes 589832 | tf_op jit(solution)/shard_map/ppermute | solution.py:191
  49.6 0.5 collective-permute-start.10
  50.1 6.9 %collective-permute-done.27.refs_1_ = bf16[384,256]{1,0:T(8,128)(2,1)S(1)} collective-permute-done((bf16[384,256]{1,0:T(8,128)(2,1)S(1)}, bf16[384,256]{1,0:T(8,128)(2,1)S(1)}, u32[]{:S(2)}, u32[]{:S(2)}) %collective-permute-start.27) | collective-permute-done | bytes 196640 | tf_op jit(solution)/shard_map/ppermute | solution.py:191
  57.0 0.5 collective-permute-start.14
  57.5 0.1 collective-permute-start.17
  57.6 0.1 shard_map.115.refs_0_
  57.7 1.5 %collective-permute-start.28 = (bf16[384,256]{1,0:T(8,128)(2,1)S(1)}, bf16[384,256]{1,0:T(8,128)(2,1)S(1)}, u32[]{:S(2)}, u32[]{:S(2)}) collective-permute-start(bf16[384,256]{1,0:T(8,128)(2,1)S(1)} %shard_map.116.own_ref), channel_id=1, source_target_pairs={{0,16},{4,20},{8,24},{12,28},{16,0},{20,4},{24,8},{28,12},{1,17},{... | collective-permute-start | bytes 589832 | tf_op jit(solution)/shard_map/ppermute | solution.py:191
  59.2 1.5 %collective-permute-start.25 = (bf16[384,256]{1,0:T(8,128)(2,1)S(1)}, bf16[384,256]{1,0:T(8,128)(2,1)S(1)}, u32[]{:S(2)}, u32[]{:S(2)}) collective-permute-start(bf16[384,256]{1,0:T(8,128)(2,1)S(1)} %shard_map.115.refs_0_), channel_id=1, source_target_pairs={{0,4},{4,0},{8,12},{12,8},{16,20},{20,16},{24,28},{28,24},{1,5},{5... | collective-permute-start | bytes 589832 | tf_op jit(solution)/shard_map/ppermute | solution.py:191
  60.7 1.0 %shard_map.110 = (bf16[256,256]{1,0:T(8,128)(2,1)S(1)}, bf16[256,256]{1,0:T(8,128)(2,1)S(1)}, bf16[128,512]{1,0:T(8,128)(2,1)S(1)}, bf16[128,512]{1,0:T(8,128)(2,1)S(1)}) custom-call(s32[5]{0:T(128)S(1)} %stack.23.at_ref, bf16[128,1024]{1,0:T(8,128)(2,1)S(1)} %copy-done.5, bf16[128,1024]{1,0:T(8,128)(2,1)S(1)} %collective-permute-done.10.refs_1_, ...), custom_call_target="tpu_custom_call" | custom-call | flops 1 | bytes 1 | tf_op jit(solution)/shard_map/pallas_call | solution.py:660
  61.7 0.6 collective-permute-start.19
  62.3 3.9 %collective-permute-start.24 = (bf16[384,256]{1,0:T(8,128)(2,1)S(1)}, bf16[384,256]{1,0:T(8,128)(2,1)S(1)}, u32[]{:S(2)}, u32[]{:S(2)}) collective-permute-start(bf16[384,256]{1,0:T(8,128)(2,1)S(1)} %shard_map.115.refs_0_), channel_id=1, source_target_pairs={{0,8},{4,12},{8,0},{12,4},{16,24},{20,28},{24,16},{28,20},{1,9},{5... | collective-permute-start | bytes 589832 | tf_op jit(solution)/shard_map/ppermute | solution.py:191
  66.3 4.0 %collective-permute-done.28.got_ref = bf16[384,256]{1,0:T(8,128)(2,1)S(1)} collective-permute-done((bf16[384,256]{1,0:T(8,128)(2,1)S(1)}, bf16[384,256]{1,0:T(8,128)(2,1)S(1)}, u32[]{:S(2)}, u32[]{:S(2)}) %collective-permute-start.28) | collective-permute-done | bytes 196640 | tf_op jit(solution)/shard_map/ppermute | solution.py:191
  70.3 0.6 collective-permute-start.29
  70.9 0.6 collective-permute-start.20
  71.5 1.5 %collective-permute-start.32 = (bf16[256,256]{1,0:T(8,128)(2,1)S(1)}, bf16[256,256]{1,0:T(8,128)(2,1)S(1)}, u32[]{:S(2)}, u32[]{:S(2)}) collective-permute-start(bf16[256,256]{1,0:T(8,128)(2,1)S(1)} %get-tuple-element.88), channel_id=1, source_target_pairs={{0,8},{4,12},{8,0},{12,4},{16,24},{20,28},{24,16},{28,20},{1,9},{5... | collective-permute-start | bytes 393224 | tf_op jit(solution)/shard_map/ppermute | solution.py:191
  73.1 0.2 collective-permute-done.24.refs_1_
  73.2 1.5 %collective-permute-start.26 = (bf16[384,256]{1,0:T(8,128)(2,1)S(1)}, bf16[384,256]{1,0:T(8,128)(2,1)S(1)}, u32[]{:S(2)}, u32[]{:S(2)}) collective-permute-start(bf16[384,256]{1,0:T(8,128)(2,1)S(1)} %collective-permute-done.24.refs_1_), channel_id=1, source_target_pairs={{0,4},{4,0},{8,12},{12,8},{16,20},{20,16},{24,28},{28,24},{1,5},{5... | collective-permute-start | bytes 589832 | tf_op jit(solution)/shard_map/ppermute | solution.py:191
  74.7 0.5 collective-permute-start.30
  75.3 2.9 %collective-permute-done.29.refs_5_ = bf16[384,256]{1,0:T(8,128)(2,1)S(1)} collective-permute-done((bf16[384,256]{1,0:T(8,128)(2,1)S(1)}, bf16[384,256]{1,0:T(8,128)(2,1)S(1)}, u32[]{:S(2)}, u32[]{:S(2)}) %collective-permute-start.29) | collective-permute-done | bytes 196640 | tf_op jit(solution)/shard_map/ppermute | solution.py:191
  78.2 1.5 %collective-permute-start.31 = (bf16[384,256]{1,0:T(8,128)(2,1)S(1)}, bf16[384,256]{1,0:T(8,128)(2,1)S(1)}, u32[]{:S(2)}, u32[]{:S(2)}) collective-permute-start(bf16[384,256]{1,0:T(8,128)(2,1)S(1)} %collective-permute-done.29.refs_5_), channel_id=1, source_target_pairs={{0,4},{4,0},{8,12},{12,8},{16,20},{20,16},{24,28},{28,24},{1,5},{5... | collective-permute-start | bytes 589832 | tf_op jit(solution)/shard_map/ppermute | solution.py:191
  79.7 0.1 collective-permute-start.21
  79.8 0.1 collective-permute-done.32.got_ref
  80.0 1.4 %collective-permute-start.33 = (bf16[128,256]{1,0:T(8,128)(2,1)S(1)}, bf16[128,256]{1,0:T(8,128)(2,1)S(1)}, u32[]{:S(2)}, u32[]{:S(2)}) collective-permute-start(bf16[128,256]{1,0:T(8,128)(2,1)S(1)} %get-tuple-element.90), channel_id=1, source_target_pairs={{0,16},{4,20},{8,24},{12,28},{16,0},{20,4},{24,8},{28,12},{1,17},{... | collective-permute-start | bytes 196616 | tf_op jit(solution)/shard_map/ppermute | solution.py:191
  81.4 5.3 %collective-permute-done.33.got_ref = bf16[128,256]{1,0:T(8,128)(2,1)S(1)} collective-permute-done((bf16[128,256]{1,0:T(8,128)(2,1)S(1)}, bf16[128,256]{1,0:T(8,128)(2,1)S(1)}, u32[]{:S(2)}, u32[]{:S(2)}) %collective-permute-start.33) | collective-permute-done | bytes 65568 | tf_op jit(solution)/shard_map/ppermute | solution.py:191
  86.7 0.6 shard_map.120
  87.3 1.0 %collective-permute-start.34 = (bf16[128,128]{1,0:T(8,128)(2,1)S(1)}, bf16[128,128]{1,0:T(8,128)(2,1)S(1)}, u32[]{:S(2)}, u32[]{:S(2)}) collective-permute-start(bf16[128,128]{1,0:T(8,128)(2,1)S(1)} %get-tuple-element.93), channel_id=1, source_target_pairs={{0,4},{4,0},{8,12},{12,8},{16,20},{20,16},{24,28},{28,24},{1,5},{5... | collective-permute-start | bytes 98312 | tf_op jit(solution)/shard_map/ppermute | solution.py:191
  88.3 2.1 %shard_map.113 = bf16[128,1024]{1,0:T(8,128)(2,1)} custom-call(s32[5]{0:T(128)S(1)} %stack.23.at_ref, bf16[128,512]{1,0:T(8,128)(2,1)S(1)} %get-tuple-element.76.refs_0_.back_ref, bf16[128,512]{1,0:T(8,128)(2,1)S(1)} %collective-permute-done.19.refs_1_.x_ref, bf16[256,256]{1,0:T(8,128)(2,1)S(1)} %collective-permute-done.20.refs_2_.y_ref, ...), custom_call_target="tpu_custom_call" | custom-call | flops 1 | bytes 1 | tf_op jit(solution)/shard_map/pallas_call | solution.py:690
  90.4 2.1 %shard_map.118 = (bf16[384,1024]{1,0:T(8,128)(2,1)}, bf16[384,1024]{1,0:T(8,128)(2,1)}) custom-call(s32[5]{0:T(128)S(1)} %stack.23.at_ref, bf16[384,256]{1,0:T(8,128)(2,1)S(1)} %shard_map.115.refs_0_, bf16[384,256]{1,0:T(8,128)(2,1)S(1)} %collective-permute-done.24.refs_1_, bf16[384,256]{1,0:T(8,128)(2,1)S(1)} %collective-permute-done.25.refs_2_, ...), custom_call_target="tpu_custom_call" | custom-call | flops 1 | bytes 1 | tf_op jit(solution)/shard_map/pallas_call | solution.py:783
  92.6 1.3 %shard_map.121 = f32[128,256]{1,0:T(8,128)} custom-call(s32[5]{0:T(128)S(1)} %stack.23.at_ref, f32[128,128]{1,0:T(8,128)S(1)} %get-tuple-element.92.keep_ref, bf16[128,128]{1,0:T(8,128)(2,1)S(1)} %collective-permute-done.34.got_ref), custom_call_target="tpu_custom_call" | custom-call | flops 1 | bytes 1 | tf_op jit(solution)/shard_map/pallas_call | solution.py:750
  (39 shorter events, 0.3 us)
Async XLA Ops:
  0.6 22.4 %copy-start.5 = (bf16[128,1024]{1,0:T(8,128)(2,1)S(1)}, bf16[128,1024]{1,0:T(8,128)(2,1)}, u32[]{:S(2)}) copy-start(bf16[128,1024]{1,0:T(8,128)(2,1)} %refs_0_.1) | copy-start | bytes 786436
  2.8 29.7 %copy-start.1 = (bf16[272,512]{1,0:T(8,128)(2,1)S(1)}, bf16[272,512]{1,0:T(8,128)(2,1)}, u32[]{:S(2)}) copy-start(bf16[272,512]{1,0:T(8,128)(2,1)} %get-tuple-element.49.refs_0_) | copy-start | bytes 835588
  2.8 9.8 %collective-permute-start.1 = (bf16[272,512]{1,0:T(8,128)(2,1)}, bf16[272,512]{1,0:T(8,128)(2,1)S(1)}, u32[]{:S(2)}, u32[]{:S(2)}) collective-permute-start(bf16[272,512]{1,0:T(8,128)(2,1)} %get-tuple-element.50), channel_id=1, source_target_pairs={{0,4},{4,0},{8,12},{12,8},{16,20},{20,16},{24,28},{28,24},{1,5},{5... | collective-permute-start | bytes 835592 | tf_op jit(solution)/shard_map/ppermute | solution.py:191
  5.8 10.1 %collective-permute-start = (bf16[272,512]{1,0:T(8,128)(2,1)}, bf16[272,512]{1,0:T(8,128)(2,1)S(1)}, u32[]{:S(2)}, u32[]{:S(2)}) collective-permute-start(bf16[272,512]{1,0:T(8,128)(2,1)} %get-tuple-element.49.refs_0_), channel_id=1, source_target_pairs={{0,1},{1,0},{2,3},{3,2},{4,5},{5,4},{6,7},{7,6},{8,9},{9,8},{10,11... | collective-permute-start | bytes 835592 | tf_op jit(solution)/shard_map/ppermute | solution.py:191
  5.8 10.1 %collective-permute-start.3 = (bf16[272,512]{1,0:T(8,128)(2,1)}, bf16[272,512]{1,0:T(8,128)(2,1)S(1)}, u32[]{:S(2)}, u32[]{:S(2)}) collective-permute-start(bf16[272,512]{1,0:T(8,128)(2,1)} %get-tuple-element.49.refs_0_), channel_id=1, source_target_pairs={{0,2},{1,3},{2,0},{3,1},{4,6},{5,7},{6,4},{7,5},{8,10},{9,11},{10,... | collective-permute-start | bytes 835592 | tf_op jit(solution)/shard_map/ppermute | solution.py:191
  7.4 1.1 %copy-start.3 = (bf16[384,1024]{1,0:T(8,128)(2,1)S(1)}, bf16[384,1024]{1,0:T(8,128)(2,1)}, u32[]{:S(2)}) copy-start(bf16[384,1024]{1,0:T(8,128)(2,1)} %k_ref.1) | copy-start | bytes 2359300
  8.5 1.1 %copy-start.4 = (bf16[384,1024]{1,0:T(8,128)(2,1)S(1)}, bf16[384,1024]{1,0:T(8,128)(2,1)}, u32[]{:S(2)}) copy-start(bf16[384,1024]{1,0:T(8,128)(2,1)} %v_ref.1) | copy-start | bytes 2359300
  12.6 3.3 %collective-permute-start.2 = (bf16[272,512]{1,0:T(8,128)(2,1)S(1)}, bf16[272,512]{1,0:T(8,128)(2,1)S(1)}, u32[]{:S(2)}, u32[]{:S(2)}) collective-permute-start(bf16[272,512]{1,0:T(8,128)(2,1)S(1)} %collective-permute-done.1.refs_2_), channel_id=1, source_target_pairs={{0,1},{1,0},{2,3},{3,2},{4,5},{5,4},{6,7},{7,6},{8,9},{9,8},{10,11... | collective-permute-start | bytes 835592 | tf_op jit(solution)/shard_map/ppermute | solution.py:191
  12.6 10.4 %collective-permute-start.5 = (bf16[272,512]{1,0:T(8,128)(2,1)S(1)}, bf16[272,512]{1,0:T(8,128)(2,1)S(1)}, u32[]{:S(2)}, u32[]{:S(2)}) collective-permute-start(bf16[272,512]{1,0:T(8,128)(2,1)S(1)} %collective-permute-done.1.refs_2_), channel_id=1, source_target_pairs={{0,2},{1,3},{2,0},{3,1},{4,6},{5,7},{6,4},{7,5},{8,10},{9,11},{10,... | collective-permute-start | bytes 835592 | tf_op jit(solution)/shard_map/ppermute | solution.py:191
  14.4 8.6 %collective-permute-start.6 = (bf16[128,1024]{1,0:T(8,128)(2,1)}, bf16[128,1024]{1,0:T(8,128)(2,1)S(1)}, u32[]{:S(2)}, u32[]{:S(2)}) collective-permute-start(bf16[128,1024]{1,0:T(8,128)(2,1)} %refs_0_.1), channel_id=1, source_target_pairs={{0,4},{4,0},{8,12},{12,8},{16,20},{20,16},{24,28},{28,24},{1,5},{5... | collective-permute-start | bytes 786440 | tf_op jit(solution)/shard_map/ppermute | solution.py:191
  15.9 7.6 %collective-permute-start.4 = (bf16[272,512]{1,0:T(8,128)(2,1)S(1)}, bf16[272,512]{1,0:T(8,128)(2,1)S(1)}, u32[]{:S(2)}, u32[]{:S(2)}) collective-permute-start(bf16[272,512]{1,0:T(8,128)(2,1)S(1)} %collective-permute-done.3.refs_0_.refs_4_), channel_id=1, source_target_pairs={{0,1},{1,0},{2,3},{3,2},{4,5},{5,4},{6,7},{7,6},{8,9},{9,8},{10,11... | collective-permute-start | bytes 835592 | tf_op jit(solution)/shard_map/ppermute | solution.py:191
  15.9 1.0 %copy-start = (bf16[272,512]{1,0:T(8,128)(2,1)S(1)}, bf16[272,512]{1,0:T(8,128)(2,1)}, u32[]{:S(2)}) copy-start(bf16[272,512]{1,0:T(8,128)(2,1)} %get-tuple-element.49.refs_0_) | copy-start | bytes 835588
  23.1 1.6 %collective-permute-start.7 = (bf16[272,512]{1,0:T(8,128)(2,1)S(1)}, bf16[272,512]{1,0:T(8,128)(2,1)S(1)}, u32[]{:S(2)}, u32[]{:S(2)}) collective-permute-start(bf16[272,512]{1,0:T(8,128)(2,1)S(1)} %collective-permute-done.5.refs_2_.refs_6_), channel_id=1, source_target_pairs={{0,1},{1,0},{2,3},{3,2},{4,5},{5,4},{6,7},{7,6},{8,9},{9,8},{10,11... | collective-permute-start | bytes 835592 | tf_op jit(solution)/shard_map/ppermute | solution.py:191
  23.1 9.1 %collective-permute-start.12 = (bf16[128,1024]{1,0:T(8,128)(2,1)S(1)}, bf16[128,1024]{1,0:T(8,128)(2,1)S(1)}, u32[]{:S(2)}, u32[]{:S(2)}) collective-permute-start(bf16[128,1024]{1,0:T(8,128)(2,1)S(1)} %copy-done.5), channel_id=1, source_target_pairs={{0,2},{1,3},{2,0},{3,1},{4,6},{5,7},{6,4},{7,5},{8,10},{9,11},{10,... | collective-permute-start | bytes 786440 | tf_op jit(solution)/shard_map/ppermute | solution.py:191
  27.0 1.3 %collective-permute-start.8 = (f32[4,2,1024]{2,1,0:T(2,128)S(1)}, f32[4,2,1024]{2,1,0:T(2,128)S(1)}, u32[]{:S(2)}, u32[]{:S(2)}) collective-permute-start(f32[4,2,1024]{2,1,0:T(2,128)S(1)} %get-tuple-element.57), channel_id=1, source_target_pairs={{0,1},{1,0},{2,3},{3,2},{4,5},{5,4},{6,7},{7,6},{8,9},{9,8},{10,11... | collective-permute-start | bytes 98312 | tf_op jit(solution)/shard_map/ppermute | solution.py:191
  28.3 4.2 %collective-permute-start.9 = (f32[4,2,1024]{2,1,0:T(2,128)S(1)}, f32[4,2,1024]{2,1,0:T(2,128)S(1)}, u32[]{:S(2)}, u32[]{:S(2)}) collective-permute-start(f32[4,2,1024]{2,1,0:T(2,128)S(1)} %shard_map.106.refs_14_), channel_id=1, source_target_pairs={{0,2},{1,3},{2,0},{3,1},{4,6},{5,7},{6,4},{7,5},{8,10},{9,11},{10,... | collective-permute-start | bytes 98312 | tf_op jit(solution)/shard_map/ppermute | solution.py:191
  37.5 2.2 %collective-permute-start.13 = (bf16[128,1024]{1,0:T(8,128)(2,1)S(1)}, bf16[128,1024]{1,0:T(8,128)(2,1)S(1)}, u32[]{:S(2)}, u32[]{:S(2)}) collective-permute-start(bf16[128,1024]{1,0:T(8,128)(2,1)S(1)} %get-tuple-element.69), channel_id=1, source_target_pairs={{0,1},{1,0},{2,3},{3,2},{4,5},{5,4},{6,7},{7,6},{8,9},{9,8},{10,11... | collective-permute-start | bytes 786440 | tf_op jit(solution)/shard_map/ppermute | solution.py:191
  37.6 12.0 %collective-permute-start.15 = (bf16[128,1024]{1,0:T(8,128)(2,1)S(1)}, bf16[128,1024]{1,0:T(8,128)(2,1)S(1)}, u32[]{:S(2)}, u32[]{:S(2)}) collective-permute-start(bf16[128,1024]{1,0:T(8,128)(2,1)S(1)} %collective-permute-done.6.refs_2_), channel_id=1, source_target_pairs={{0,2},{1,3},{2,0},{3,1},{4,6},{5,7},{6,4},{7,5},{8,10},{9,11},{10,... | collective-permute-start | bytes 786440 | tf_op jit(solution)/shard_map/ppermute | solution.py:191
  38.0 8.8 %collective-permute-start.22 = (bf16[384,256]{1,0:T(8,128)(2,1)S(1)}, bf16[384,256]{1,0:T(8,128)(2,1)S(1)}, u32[]{:S(2)}, u32[]{:S(2)}) collective-permute-start(bf16[384,256]{1,0:T(8,128)(2,1)S(1)} %get-tuple-element.80), channel_id=1, source_target_pairs={{0,8},{4,12},{8,0},{12,4},{16,24},{20,28},{24,16},{28,20},{1,9},{5... | collective-permute-start | bytes 589832 | tf_op jit(solution)/shard_map/ppermute | solution.py:191
  39.8 17.8 %collective-permute-start.18 = (bf16[128,1024]{1,0:T(8,128)(2,1)S(1)}, bf16[128,1024]{1,0:T(8,128)(2,1)S(1)}, u32[]{:S(2)}, u32[]{:S(2)}) collective-permute-start(bf16[128,1024]{1,0:T(8,128)(2,1)S(1)} %shard_map.108), channel_id=1, source_target_pairs={{0,2},{1,3},{2,0},{3,1},{4,6},{5,7},{6,4},{7,5},{8,10},{9,11},{10,... | collective-permute-start | bytes 786440 | tf_op jit(solution)/shard_map/ppermute | solution.py:191
  46.3 10.7 %collective-permute-start.27 = (bf16[384,256]{1,0:T(8,128)(2,1)S(1)}, bf16[384,256]{1,0:T(8,128)(2,1)S(1)}, u32[]{:S(2)}, u32[]{:S(2)}) collective-permute-start(bf16[384,256]{1,0:T(8,128)(2,1)S(1)} %get-tuple-element.83), channel_id=1, source_target_pairs={{0,8},{4,12},{8,0},{12,4},{16,24},{20,28},{24,16},{28,20},{1,9},{5... | collective-permute-start | bytes 589832 | tf_op jit(solution)/shard_map/ppermute | solution.py:191
  46.9 41.4 %copy-start.2 = (bf16[1024,1024]{1,0:T(8,128)(2,1)S(1)}, bf16[1024,1024]{1,0:T(8,128)(2,1)}, u32[]{:S(2)}) copy-start(bf16[1024,1024]{1,0:T(8,128)(2,1)} %wq_ref.1) | copy-start | bytes 6291460
  46.9 10.1 %collective-permute-start.23 = (bf16[384,256]{1,0:T(8,128)(2,1)S(1)}, bf16[384,256]{1,0:T(8,128)(2,1)S(1)}, u32[]{:S(2)}, u32[]{:S(2)}) collective-permute-start(bf16[384,256]{1,0:T(8,128)(2,1)S(1)} %shard_map.114.own_ref), channel_id=1, source_target_pairs={{0,16},{4,20},{8,24},{12,28},{16,0},{20,4},{24,8},{28,12},{1,17},{... | collective-permute-start | bytes 589832 | tf_op jit(solution)/shard_map/ppermute | solution.py:191
  49.6 8.2 %collective-permute-start.11 = (bf16[128,1024]{1,0:T(8,128)(2,1)S(1)}, bf16[128,1024]{1,0:T(8,128)(2,1)S(1)}, u32[]{:S(2)}, u32[]{:S(2)}) collective-permute-start(bf16[128,1024]{1,0:T(8,128)(2,1)S(1)} %collective-permute-done.6.refs_2_), channel_id=1, source_target_pairs={{0,1},{1,0},{2,3},{3,2},{4,5},{5,4},{6,7},{7,6},{8,9},{9,8},{10,11... | collective-permute-start | bytes 786440 | tf_op jit(solution)/shard_map/ppermute | solution.py:191
  49.6 9.6 %collective-permute-start.10 = (bf16[128,1024]{1,0:T(8,128)(2,1)S(1)}, bf16[128,1024]{1,0:T(8,128)(2,1)S(1)}, u32[]{:S(2)}, u32[]{:S(2)}) collective-permute-start(bf16[128,1024]{1,0:T(8,128)(2,1)S(1)} %copy-done.5), channel_id=1, source_target_pairs={{0,1},{1,0},{2,3},{3,2},{4,5},{5,4},{6,7},{7,6},{8,9},{9,8},{10,11... | collective-permute-start | bytes 786440 | tf_op jit(solution)/shard_map/ppermute | solution.py:191
  57.0 3.7 %collective-permute-start.16 = (bf16[128,1024]{1,0:T(8,128)(2,1)S(1)}, bf16[128,1024]{1,0:T(8,128)(2,1)S(1)}, u32[]{:S(2)}, u32[]{:S(2)}) collective-permute-start(bf16[128,1024]{1,0:T(8,128)(2,1)S(1)} %collective-permute-done.15.refs_6_), channel_id=1, source_target_pairs={{0,1},{1,0},{2,3},{3,2},{4,5},{5,4},{6,7},{7,6},{8,9},{9,8},{10,11... | collective-permute-start | bytes 786440 | tf_op jit(solution)/shard_map/ppermute | solution.py:191
  57.0 3.7 %collective-permute-start.14 = (bf16[128,1024]{1,0:T(8,128)(2,1)S(1)}, bf16[128,1024]{1,0:T(8,128)(2,1)S(1)}, u32[]{:S(2)}, u32[]{:S(2)}) collective-permute-start(bf16[128,1024]{1,0:T(8,128)(2,1)S(1)} %collective-permute-done.12.refs_4_), channel_id=1, source_target_pairs={{0,1},{1,0},{2,3},{3,2},{4,5},{5,4},{6,7},{7,6},{8,9},{9,8},{10,11... | collective-permute-start | bytes 786440 | tf_op jit(solution)/shard_map/ppermute | solution.py:191
  57.5 3.1 %collective-permute-start.17 = (bf16[128,1024]{1,0:T(8,128)(2,1)S(1)}, bf16[128,1024]{1,0:T(8,128)(2,1)S(1)}, u32[]{:S(2)}, u32[]{:S(2)}) collective-permute-start(bf16[128,1024]{1,0:T(8,128)(2,1)S(1)} %get-tuple-element.75), channel_id=1, source_target_pairs={{0,1},{1,0},{2,3},{3,2},{4,5},{5,4},{6,7},{7,6},{8,9},{9,8},{10,11... | collective-permute-start | bytes 786440 | tf_op jit(solution)/shard_map/ppermute | solution.py:191
  57.7 12.5 %collective-permute-start.28 = (bf16[384,256]{1,0:T(8,128)(2,1)S(1)}, bf16[384,256]{1,0:T(8,128)(2,1)S(1)}, u32[]{:S(2)}, u32[]{:S(2)}) collective-permute-start(bf16[384,256]{1,0:T(8,128)(2,1)S(1)} %shard_map.116.own_ref), channel_id=1, source_target_pairs={{0,16},{4,20},{8,24},{12,28},{16,0},{20,4},{24,8},{28,12},{1,17},{... | collective-permute-start | bytes 589832 | tf_op jit(solution)/shard_map/ppermute | solution.py:191
  59.2 11.1 %collective-permute-start.25 = (bf16[384,256]{1,0:T(8,128)(2,1)S(1)}, bf16[384,256]{1,0:T(8,128)(2,1)S(1)}, u32[]{:S(2)}, u32[]{:S(2)}) collective-permute-start(bf16[384,256]{1,0:T(8,128)(2,1)S(1)} %shard_map.115.refs_0_), channel_id=1, source_target_pairs={{0,4},{4,0},{8,12},{12,8},{16,20},{20,16},{24,28},{28,24},{1,5},{5... | collective-permute-start | bytes 589832 | tf_op jit(solution)/shard_map/ppermute | solution.py:191
  61.7 9.2 %collective-permute-start.19 = (bf16[128,512]{1,0:T(8,128)(2,1)S(1)}, bf16[128,512]{1,0:T(8,128)(2,1)S(1)}, u32[]{:S(2)}, u32[]{:S(2)}) collective-permute-start(bf16[128,512]{1,0:T(8,128)(2,1)S(1)} %get-tuple-element.77), channel_id=1, source_target_pairs={{0,4},{4,0},{8,12},{12,8},{16,20},{20,16},{24,28},{28,24},{1,5},{5... | collective-permute-start | bytes 393224 | tf_op jit(solution)/shard_map/ppermute | solution.py:191
  62.3 10.9 %collective-permute-start.24 = (bf16[384,256]{1,0:T(8,128)(2,1)S(1)}, bf16[384,256]{1,0:T(8,128)(2,1)S(1)}, u32[]{:S(2)}, u32[]{:S(2)}) collective-permute-start(bf16[384,256]{1,0:T(8,128)(2,1)S(1)} %shard_map.115.refs_0_), channel_id=1, source_target_pairs={{0,8},{4,12},{8,0},{12,4},{16,24},{20,28},{24,16},{28,20},{1,9},{5... | collective-permute-start | bytes 589832 | tf_op jit(solution)/shard_map/ppermute | solution.py:191
  70.3 7.9 %collective-permute-start.29 = (bf16[384,256]{1,0:T(8,128)(2,1)S(1)}, bf16[384,256]{1,0:T(8,128)(2,1)S(1)}, u32[]{:S(2)}, u32[]{:S(2)}) collective-permute-start(bf16[384,256]{1,0:T(8,128)(2,1)S(1)} %shard_map.117.refs_4_), channel_id=1, source_target_pairs={{0,8},{4,12},{8,0},{12,4},{16,24},{20,28},{24,16},{28,20},{1,9},{5... | collective-permute-start | bytes 589832 | tf_op jit(solution)/shard_map/ppermute | solution.py:191
  70.9 8.8 %collective-permute-start.20 = (bf16[256,256]{1,0:T(8,128)(2,1)S(1)}, bf16[256,256]{1,0:T(8,128)(2,1)S(1)}, u32[]{:S(2)}, u32[]{:S(2)}) collective-permute-start(bf16[256,256]{1,0:T(8,128)(2,1)S(1)} %shard_map.111), channel_id=1, source_target_pairs={{0,2},{1,3},{2,0},{3,1},{4,6},{5,7},{6,4},{7,5},{8,10},{9,11},{10,... | collective-permute-start | bytes 393224 | tf_op jit(solution)/shard_map/ppermute | solution.py:191
  71.5 8.4 %collective-permute-start.32 = (bf16[256,256]{1,0:T(8,128)(2,1)S(1)}, bf16[256,256]{1,0:T(8,128)(2,1)S(1)}, u32[]{:S(2)}, u32[]{:S(2)}) collective-permute-start(bf16[256,256]{1,0:T(8,128)(2,1)S(1)} %get-tuple-element.88), channel_id=1, source_target_pairs={{0,8},{4,12},{8,0},{12,4},{16,24},{20,28},{24,16},{28,20},{1,9},{5... | collective-permute-start | bytes 393224 | tf_op jit(solution)/shard_map/ppermute | solution.py:191
  73.2 17.2 %collective-permute-start.26 = (bf16[384,256]{1,0:T(8,128)(2,1)S(1)}, bf16[384,256]{1,0:T(8,128)(2,1)S(1)}, u32[]{:S(2)}, u32[]{:S(2)}) collective-permute-start(bf16[384,256]{1,0:T(8,128)(2,1)S(1)} %collective-permute-done.24.refs_1_), channel_id=1, source_target_pairs={{0,4},{4,0},{8,12},{12,8},{16,20},{20,16},{24,28},{28,24},{1,5},{5... | collective-permute-start | bytes 589832 | tf_op jit(solution)/shard_map/ppermute | solution.py:191
  74.7 15.7 %collective-permute-start.30 = (bf16[384,256]{1,0:T(8,128)(2,1)S(1)}, bf16[384,256]{1,0:T(8,128)(2,1)S(1)}, u32[]{:S(2)}, u32[]{:S(2)}) collective-permute-start(bf16[384,256]{1,0:T(8,128)(2,1)S(1)} %shard_map.117.refs_4_), channel_id=1, source_target_pairs={{0,4},{4,0},{8,12},{12,8},{16,20},{20,16},{24,28},{28,24},{1,5},{5... | collective-permute-start | bytes 589832 | tf_op jit(solution)/shard_map/ppermute | solution.py:191
  78.2 12.2 %collective-permute-start.31 = (bf16[384,256]{1,0:T(8,128)(2,1)S(1)}, bf16[384,256]{1,0:T(8,128)(2,1)S(1)}, u32[]{:S(2)}, u32[]{:S(2)}) collective-permute-start(bf16[384,256]{1,0:T(8,128)(2,1)S(1)} %collective-permute-done.29.refs_5_), channel_id=1, source_target_pairs={{0,4},{4,0},{8,12},{12,8},{16,20},{20,16},{24,28},{28,24},{1,5},{5... | collective-permute-start | bytes 589832 | tf_op jit(solution)/shard_map/ppermute | solution.py:191
  79.7 8.6 %collective-permute-start.21 = (bf16[512,128]{1,0:T(8,128)(2,1)S(1)}, bf16[512,128]{1,0:T(8,128)(2,1)S(1)}, u32[]{:S(2)}, u32[]{:S(2)}) collective-permute-start(bf16[512,128]{1,0:T(8,128)(2,1)S(1)} %shard_map.112), channel_id=1, source_target_pairs={{0,1},{1,0},{2,3},{3,2},{4,5},{5,4},{6,7},{7,6},{8,9},{9,8},{10,11... | collective-permute-start | bytes 393224 | tf_op jit(solution)/shard_map/ppermute | solution.py:191
  80.0 6.7 %collective-permute-start.33 = (bf16[128,256]{1,0:T(8,128)(2,1)S(1)}, bf16[128,256]{1,0:T(8,128)(2,1)S(1)}, u32[]{:S(2)}, u32[]{:S(2)}) collective-permute-start(bf16[128,256]{1,0:T(8,128)(2,1)S(1)} %get-tuple-element.90), channel_id=1, source_target_pairs={{0,16},{4,20},{8,24},{12,28},{16,0},{20,4},{24,8},{28,12},{1,17},{... | collective-permute-start | bytes 196616 | tf_op jit(solution)/shard_map/ppermute | solution.py:191
  87.3 5.3 %collective-permute-start.34 = (bf16[128,128]{1,0:T(8,128)(2,1)S(1)}, bf16[128,128]{1,0:T(8,128)(2,1)S(1)}, u32[]{:S(2)}, u32[]{:S(2)}) collective-permute-start(bf16[128,128]{1,0:T(8,128)(2,1)S(1)} %get-tuple-element.93), channel_id=1, source_target_pairs={{0,4},{4,0},{8,12},{12,8},{16,20},{20,16},{24,28},{28,24},{1,5},{5... | collective-permute-start | bytes 98312 | tf_op jit(solution)/shard_map/ppermute | solution.py:191

commit v7 on v6

--- a/solution.py
+++ b/solution.py
@@ -812,11 +812,11 @@
     kp, vp, kt = pack_tokens(at, keys, values)
     from_x = after(over_x(send), kp)
     ra, r_y, r_xy = rows_of(own, from_x)
-    x_from_x = over_x(after(qx, own))
     pa, ma, la = side_of(ra, kp)
-    rb = far_rows(r_y, after(r_xy, la, x_from_x))
+    rb = far_rows(r_y, after(r_xy, la))
     x_y = over_y(after(qx, r_xy))
     pb, mb, lb, sent = side_of(rb, kp, la)
+    x_from_x = over_x(after(qx, lb))
     send = merge(la, lb, over_core(sent))
     got = over_y(send)
     x_xy = over_y(after(x_from_x, send))
@@ -835,9 +835,9 @@
         near = over_z(total, 1)
         return [total, near, over_x(total), over_x(near)]
 
-    kv_keep, kv_send, dq_send, dq_keep = half(False, after(pa, x_from_x, x_y))
+    kv_keep, kv_send, dq_send, dq_keep = half(False, after(pa, x_y))
     first = (kv_keep, kv_send)
-    far = add(dq_keep, over_core(dq_send))
+    far = add(dq_keep, over_core(after(dq_send, x_from_x)))
     kv_keep, kv_send, dq_send, dq_keep = half(True, after(pa, far))
     far = over_y(far)
     first = sum_near(after(first[0], dq_keep), first[1])
@@ -848,8 +848,7 @@
     )
     first, second = sum_far(first), sum_far(second)
     w_keep, w_send = weight_near(w_keep, over_z(w_send, 1))
-    w_keep, w_send = weight_sum(at, w_keep, over_z(w_send, 2))
-    w_got = over_x(w_send)
+    w_got = over_z(w_send, 2)
 
     from_x = over_x(back_s)
     size = back.shape[0]
@@ -857,10 +856,12 @@
     from_y = over_y(stack([back, from_x], [part(2, 2)] * 2))
     from_core = over_core(stack([back, from_x, from_y], [part(1, 1)] * 3))
     grad_input = input_of(at, back, from_x, from_y, from_core, wq)
+    w_keep, w_send = weight_sum(at, after(w_keep, grad_input), w_got)
+    w_got = over_x(w_send)
     first = spread(first)
     second = spread(after(second, first[2]))
     grad_keys, grad_values = tokens_out(at, *keys.shape, first + second)
-    grad_weight = weight_out(at, after(w_keep, grad_input, grad_keys), w_got)
+    grad_weight = weight_out(at, after(w_keep, grad_keys), w_got)
     return (grad_input, grad_keys, grad_values, grad_weight)
 
 

time: 94.1 us -> 92.2 us (0.980)
  waiting for transfers between devices: 31.1 us -> 26.1 us
  starting transfers between devices: 33.3 us -> 36.4 us
    ppermute x35, waiting for transfers between devices: 31.1 us -> 26.1 us  [swap(): return lax.ppermute(x, axis, [(i, i ^ mask) for i in range(size)])]
    ppermute x35, starting transfers between devices: 33.3 us -> 36.4 us  [swap(): return lax.ppermute(x, axis, [(i, i ^ mask) for i in range(size)])]
  transfers between devices with their start and end apart: 35 -> 35, of which waited for: 12 -> 12; matrix products, arithmetic and copies ran while one was open for 0% -> 0% of each run, Pallas kernels for 18% -> 24%
where the time goes in v7:
time: 92.2 us; the launch traced here: 92 us
  starting transfers between devices  36.4 us (39%)
  waiting for transfers between devices  26.1 us (28%)
  Pallas kernels  25.4 us (28%)
  local copies, waits for them, and re-layouts  3.31 us (4%)
    ppermute x35, starting transfers between devices, swap(): return lax.ppermute(x, axis, [(i, i ^ mask) for i in range(size)])  36.4 us
    ppermute x35, waiting for transfers between devices, swap(): return lax.ppermute(x, axis, [(i, i ^ mask) for i in range(size)])  26.1 us
    pallas_call x2, Pallas kernels, half_of(): pl.pallas_call(functools.partial(half_kernel, count), grid_spec=pltpu.Pre...  9.95 us
    pallas_call x2, Pallas kernels, side_of(): pl.pallas_call(functools.partial(side_kernel, count, step, extra is not N...  4.72 us
    unnamed x12, local copies, waits for them, and re-layouts  3.23 us
    pallas_call x1, Pallas kernels, pack(): pl.pallas_call(pack_kernel, grid=(steps,), in_specs=[block] * 3, out_spec...  2.19 us
    pallas_call x1, Pallas kernels, tokens_out(): pl.pallas_call(tokens_kernel, in_specs=[SMEM] + [VMEM] * len(parts), out_...  2.12 us
    pallas_call x1, Pallas kernels, input_of(): pl.pallas_call(input_kernel, in_specs=[SMEM] + [VMEM] * 5, out_specs=VMEM...  2.09 us
  transfers between devices with their start and end apart: 35, of which 12 were waited for; matrix products, arithmetic and copies ran while one was open for 0% of the time, Pallas kernels for 24%

profile of v7, /device:TPU:0, one launch (start us, length us, event | category | flops | bytes accessed | tf_op | source)
XLA Modules:
  0.0 92.0 jit_solution(1732312662233718494)
XLA Ops:
  0.6 2.2 %shard_map.102 = (bf16[272,512]{1,0:T(8,128)(2,1)}, bf16[272,512]{1,0:T(8,128)(2,1)}) custom-call(bf16[128,1024]{1,0:T(8,128)(2,1)} %q_ref.1, bf16[128,1024]{1,0:T(8,128)(2,1)} %g_ref.1, bf16[128,1024]{1,0:T(8,128)(2,1)} %o_ref.1), custom_call_target="tpu_custom_call" | custom-call | flops 1 | bytes 1 | tf_op jit(solution)/shard_map/pallas_call | solution.py:382
  2.8 2.9 %collective-permute-start.1 = (bf16[272,512]{1,0:T(8,128)(2,1)}, bf16[272,512]{1,0:T(8,128)(2,1)S(1)}, u32[]{:S(2)}, u32[]{:S(2)}) collective-permute-start(bf16[272,512]{1,0:T(8,128)(2,1)} %get-tuple-element.52), channel_id=1, source_target_pairs={{0,4},{4,0},{8,12},{12,8},{16,20},{20,16},{24,28},{28,24},{1,5},{5... | collective-permute-start | bytes 835592 | tf_op jit(solution)/shard_map/ppermute | solution.py:191
  5.8 1.5 %collective-permute-start.3 = (bf16[272,512]{1,0:T(8,128)(2,1)}, bf16[272,512]{1,0:T(8,128)(2,1)S(1)}, u32[]{:S(2)}, u32[]{:S(2)}) collective-permute-start(bf16[272,512]{1,0:T(8,128)(2,1)} %get-tuple-element.51.refs_0_), channel_id=1, source_target_pairs={{0,2},{1,3},{2,0},{3,1},{4,6},{5,7},{6,4},{7,5},{8,10},{9,11},{10,... | collective-permute-start | bytes 835592 | tf_op jit(solution)/shard_map/ppermute | solution.py:191
  7.3 0.1 stack.23.at_ref
  7.4 1.1 %copy-done.3 = bf16[384,1024]{1,0:T(8,128)(2,1)S(1)} copy-done((bf16[384,1024]{1,0:T(8,128)(2,1)S(1)}, bf16[384,1024]{1,0:T(8,128)(2,1)}, u32[]{:S(2)}) %copy-start.3) | copy-done | bytes 786456
  8.5 1.1 %copy-done.4 = bf16[384,1024]{1,0:T(8,128)(2,1)S(1)} copy-done((bf16[384,1024]{1,0:T(8,128)(2,1)S(1)}, bf16[384,1024]{1,0:T(8,128)(2,1)}, u32[]{:S(2)}) %copy-start.4) | copy-done | bytes 786456
  9.6 1.1 %shard_map.103 = (bf16[384,512]{1,0:T(8,128)(2,1)S(1)}, bf16[384,512]{1,0:T(8,128)(2,1)S(1)}, bf16[512,384]{1,0:T(8,128)(2,1)S(1)}) custom-call(s32[5]{0:T(128)S(1)} %stack.23.at_ref, bf16[384,1024]{1,0:T(8,128)(2,1)S(1)} %copy-done.3, bf16[384,1024]{1,0:T(8,128)(2,1)S(1)} %copy-done.4), custom_call_target="tpu_custom_call" | custom-call | flops 1 | bytes 1 | tf_op jit(solution)/shard_map/pallas_call | solution.py:407
  10.7 1.9 %collective-permute-done.1.refs_2_ = bf16[272,512]{1,0:T(8,128)(2,1)S(1)} collective-permute-done((bf16[272,512]{1,0:T(8,128)(2,1)}, bf16[272,512]{1,0:T(8,128)(2,1)S(1)}, u32[]{:S(2)}, u32[]{:S(2)}) %collective-permute-start.1) | collective-permute-done | bytes 278560 | tf_op jit(solution)/shard_map/ppermute | solution.py:191
  12.6 0.0 collective-permute-start.2
  12.6 1.8 %collective-permute-start.5 = (bf16[272,512]{1,0:T(8,128)(2,1)S(1)}, bf16[272,512]{1,0:T(8,128)(2,1)S(1)}, u32[]{:S(2)}, u32[]{:S(2)}) collective-permute-start(bf16[272,512]{1,0:T(8,128)(2,1)S(1)} %collective-permute-done.1.refs_2_), channel_id=1, source_target_pairs={{0,2},{1,3},{2,0},{3,1},{4,6},{5,7},{6,4},{7,5},{8,10},{9,11},{10,... | collective-permute-start | bytes 835592 | tf_op jit(solution)/shard_map/ppermute | solution.py:191
  14.4 0.6 collective-permute-done.3.refs_0_.refs_4_
  15.1 0.0 collective-permute-start.4
  15.1 0.0 collective-permute-done.refs_1_
  15.1 0.0 copy-start
  15.1 0.9 %copy-done = bf16[272,512]{1,0:T(8,128)(2,1)S(1)} copy-done((bf16[272,512]{1,0:T(8,128)(2,1)S(1)}, bf16[272,512]{1,0:T(8,128)(2,1)}, u32[]{:S(2)}) %copy-start) | copy-done | bytes 278552
  16.0 2.4 %shard_map.104 = (bf16[8,384,512]{2,1,0:T(8,128)(2,1)S(1)}, f32[4,2,512]{2,1,0:T(2,128)S(1)}, f32[4,2,512]{2,1,0:T(2,128)S(1)}) custom-call(bf16[272,512]{1,0:T(8,128)(2,1)S(1)} %copy-done, bf16[272,512]{1,0:T(8,128)(2,1)S(1)} %collective-permute-done.refs_1_, bf16[272,512]{1,0:T(8,128)(2,1)S(1)} %collective-permute-done.1.refs_2_, ...), custom_call_target="tpu_custom_call" | custom-call | flops 1 | bytes 1 | tf_op jit(solution)/shard_map/pallas_call | solution.py:514
  18.4 3.3 %collective-permute-done.5.refs_2_.refs_6_ = bf16[272,512]{1,0:T(8,128)(2,1)S(1)} collective-permute-done((bf16[272,512]{1,0:T(8,128)(2,1)S(1)}, bf16[272,512]{1,0:T(8,128)(2,1)S(1)}, u32[]{:S(2)}, u32[]{:S(2)}) %collective-permute-start.5) | collective-permute-done | bytes 278560 | tf_op jit(solution)/shard_map/ppermute | solution.py:191
  21.7 0.0 collective-permute-start.6
  21.7 1.7 %collective-permute-start.12 = (bf16[128,1024]{1,0:T(8,128)(2,1)S(1)}, bf16[128,1024]{1,0:T(8,128)(2,1)S(1)}, u32[]{:S(2)}, u32[]{:S(2)}) collective-permute-start(bf16[128,1024]{1,0:T(8,128)(2,1)S(1)} %copy-done.5), channel_id=1, source_target_pairs={{0,2},{1,3},{2,0},{3,1},{4,6},{5,7},{6,4},{7,5},{8,10},{9,11},{10,... | collective-permute-start | bytes 786440 | tf_op jit(solution)/shard_map/ppermute | solution.py:191
  23.5 2.4 %shard_map.105 = (bf16[8,384,512]{2,1,0:T(8,128)(2,1)S(1)}, f32[4,2,512]{2,1,0:T(2,128)S(1)}, f32[4,2,512]{2,1,0:T(2,128)S(1)}, f32[4,2,1024]{2,1,0:T(2,128)S(1)}) custom-call(bf16[272,512]{1,0:T(8,128)(2,1)S(1)} %collective-permute-done.3.refs_0_.refs_4_, bf16[272,512]{1,0:T(8,128)(2,1)S(1)} %collective-permute-done.4.refs_1_.refs_5_, ...), custom_call_target="tpu_custom_call" | custom-call | flops 1 | bytes 1 | tf_op jit(solution)/shard_map/pallas_call | solution.py:514
  25.9 1.6 %collective-permute-start.10 = (bf16[128,1024]{1,0:T(8,128)(2,1)S(1)}, bf16[128,1024]{1,0:T(8,128)(2,1)S(1)}, u32[]{:S(2)}, u32[]{:S(2)}) collective-permute-start(bf16[128,1024]{1,0:T(8,128)(2,1)S(1)} %copy-done.5), channel_id=1, source_target_pairs={{0,4},{4,0},{8,12},{12,8},{16,20},{20,16},{24,28},{28,24},{1,5},{5... | collective-permute-start | bytes 786440 | tf_op jit(solution)/shard_map/ppermute | solution.py:191
  27.4 0.0 collective-permute-start.7
  27.4 1.2 %collective-permute-done.7.got_ref = f32[4,2,1024]{2,1,0:T(2,128)S(1)} collective-permute-done((f32[4,2,1024]{2,1,0:T(2,128)S(1)}, f32[4,2,1024]{2,1,0:T(2,128)S(1)}, u32[]{:S(2)}, u32[]{:S(2)}) %collective-permute-start.7) | collective-permute-done | bytes 32800 | tf_op jit(solution)/shard_map/ppermute | solution.py:191
  28.7 1.6 %collective-permute-start.8 = (f32[4,2,1024]{2,1,0:T(2,128)S(1)}, f32[4,2,1024]{2,1,0:T(2,128)S(1)}, u32[]{:S(2)}, u32[]{:S(2)}) collective-permute-start(f32[4,2,1024]{2,1,0:T(2,128)S(1)} %shard_map.106.refs_14_), channel_id=1, source_target_pairs={{0,2},{1,3},{2,0},{3,1},{4,6},{5,7},{6,4},{7,5},{8,10},{9,11},{10,... | collective-permute-start | bytes 98312 | tf_op jit(solution)/shard_map/ppermute | solution.py:191
  30.3 0.2 collective-permute-done.12.refs_4_
  30.5 2.2 %collective-permute-done.8.refs_15_ = f32[4,2,1024]{2,1,0:T(2,128)S(1)} collective-permute-done((f32[4,2,1024]{2,1,0:T(2,128)S(1)}, f32[4,2,1024]{2,1,0:T(2,128)S(1)}, u32[]{:S(2)}, u32[]{:S(2)}) %collective-permute-start.8) | collective-permute-done | bytes 32800 | tf_op jit(solution)/shard_map/ppermute | solution.py:191
  32.7 5.0 %shard_map.107 = (bf16[384,256]{1,0:T(8,128)(2,1)S(1)}, bf16[384,256]{1,0:T(8,128)(2,1)S(1)}, bf16[128,1024]{1,0:T(8,128)(2,1)S(1)}, bf16[128,1024]{1,0:T(8,128)(2,1)S(1)}) custom-call(s32[5]{0:T(128)S(1)} %stack.23.at_ref, bf16[272,512]{1,0:T(8,128)(2,1)S(1)} %copy-done.1, bf16[272,512]{1,0:T(8,128)(2,1)S(1)} %collective-permute-done.refs_1_, ...), custom_call_target="tpu_custom_call" | custom-call | flops 1 | bytes 1 | tf_op jit(solution)/shard_map/pallas_call | solution.py:612
  37.7 0.1 collective-permute-start.13
  37.7 1.6 %collective-permute-start.15 = (bf16[128,1024]{1,0:T(8,128)(2,1)S(1)}, bf16[128,1024]{1,0:T(8,128)(2,1)S(1)}, u32[]{:S(2)}, u32[]{:S(2)}) collective-permute-start(bf16[128,1024]{1,0:T(8,128)(2,1)S(1)} %collective-permute-done.10.refs_2_), channel_id=1, source_target_pairs={{0,2},{1,3},{2,0},{3,1},{4,6},{5,7},{6,4},{7,5},{8,10},{9,11},{10,... | collective-permute-start | bytes 786440 | tf_op jit(solution)/shard_map/ppermute | solution.py:191
  39.3 1.6 %collective-permute-start.22 = (bf16[384,256]{1,0:T(8,128)(2,1)S(1)}, bf16[384,256]{1,0:T(8,128)(2,1)S(1)}, u32[]{:S(2)}, u32[]{:S(2)}) collective-permute-start(bf16[384,256]{1,0:T(8,128)(2,1)S(1)} %get-tuple-element.83), channel_id=1, source_target_pairs={{0,8},{4,12},{8,0},{12,4},{16,24},{20,28},{24,16},{28,20},{1,9},{5... | collective-permute-start | bytes 589832 | tf_op jit(solution)/shard_map/ppermute | solution.py:191
  40.9 0.1 shard_map.108
  41.0 0.6 collective-permute-start.18
  41.5 5.0 %shard_map.109 = (bf16[384,256]{1,0:T(8,128)(2,1)S(1)}, bf16[384,256]{1,0:T(8,128)(2,1)S(1)}, bf16[128,1024]{1,0:T(8,128)(2,1)S(1)}, bf16[128,1024]{1,0:T(8,128)(2,1)S(1)}) custom-call(s32[5]{0:T(128)S(1)} %stack.23.at_ref, bf16[272,512]{1,0:T(8,128)(2,1)S(1)} %copy-done.1, bf16[272,512]{1,0:T(8,128)(2,1)S(1)} %collective-permute-done.refs_1_, ...), custom_call_target="tpu_custom_call" | custom-call | flops 1 | bytes 1 | tf_op jit(solution)/shard_map/pallas_call | solution.py:612
  46.5 1.0 %collective-permute-start.27 = (bf16[384,256]{1,0:T(8,128)(2,1)S(1)}, bf16[384,256]{1,0:T(8,128)(2,1)S(1)}, u32[]{:S(2)}, u32[]{:S(2)}) collective-permute-start(bf16[384,256]{1,0:T(8,128)(2,1)S(1)} %get-tuple-element.86), channel_id=1, source_target_pairs={{0,8},{4,12},{8,0},{12,4},{16,24},{20,28},{24,16},{28,20},{1,9},{5... | collective-permute-start | bytes 589832 | tf_op jit(solution)/shard_map/ppermute | solution.py:191
  47.6 2.7 %collective-permute-start.23 = (bf16[384,256]{1,0:T(8,128)(2,1)S(1)}, bf16[384,256]{1,0:T(8,128)(2,1)S(1)}, u32[]{:S(2)}, u32[]{:S(2)}) collective-permute-start(bf16[384,256]{1,0:T(8,128)(2,1)S(1)} %shard_map.114.own_ref), channel_id=1, source_target_pairs={{0,16},{4,20},{8,24},{12,28},{16,0},{20,4},{24,8},{28,12},{1,17},{... | collective-permute-start | bytes 589832 | tf_op jit(solution)/shard_map/ppermute | solution.py:191
  50.3 0.5 collective-permute-start.11
  50.8 6.4 %collective-permute-done.27.refs_1_ = bf16[384,256]{1,0:T(8,128)(2,1)S(1)} collective-permute-done((bf16[384,256]{1,0:T(8,128)(2,1)S(1)}, bf16[384,256]{1,0:T(8,128)(2,1)S(1)}, u32[]{:S(2)}, u32[]{:S(2)}) %collective-permute-start.27) | collective-permute-done | bytes 196640 | tf_op jit(solution)/shard_map/ppermute | solution.py:191
  57.2 0.5 collective-permute-start.14
  57.7 0.1 collective-permute-start.17
  57.8 0.1 shard_map.115.refs_0_
  57.9 2.2 %collective-permute-start.28 = (bf16[384,256]{1,0:T(8,128)(2,1)S(1)}, bf16[384,256]{1,0:T(8,128)(2,1)S(1)}, u32[]{:S(2)}, u32[]{:S(2)}) collective-permute-start(bf16[384,256]{1,0:T(8,128)(2,1)S(1)} %shard_map.116.own_ref), channel_id=1, source_target_pairs={{0,16},{4,20},{8,24},{12,28},{16,0},{20,4},{24,8},{28,12},{1,17},{... | collective-permute-start | bytes 589832 | tf_op jit(solution)/shard_map/ppermute | solution.py:191
  60.1 0.5 collective-permute-start.25
  60.7 1.0 %shard_map.110 = (bf16[256,256]{1,0:T(8,128)(2,1)S(1)}, bf16[256,256]{1,0:T(8,128)(2,1)S(1)}, bf16[128,512]{1,0:T(8,128)(2,1)S(1)}, bf16[128,512]{1,0:T(8,128)(2,1)S(1)}) custom-call(s32[5]{0:T(128)S(1)} %stack.23.at_ref, bf16[128,1024]{1,0:T(8,128)(2,1)S(1)} %copy-done.5, bf16[128,1024]{1,0:T(8,128)(2,1)S(1)} %collective-permute-done.9.refs_1_, ...), custom_call_target="tpu_custom_call" | custom-call | flops 1 | bytes 1 | tf_op jit(solution)/shard_map/pallas_call | solution.py:660
  61.7 1.5 %collective-permute-start.19 = (bf16[128,512]{1,0:T(8,128)(2,1)S(1)}, bf16[128,512]{1,0:T(8,128)(2,1)S(1)}, u32[]{:S(2)}, u32[]{:S(2)}) collective-permute-start(bf16[128,512]{1,0:T(8,128)(2,1)S(1)} %get-tuple-element.80), channel_id=1, source_target_pairs={{0,4},{4,0},{8,12},{12,8},{16,20},{20,16},{24,28},{28,24},{1,5},{5... | collective-permute-start | bytes 393224 | tf_op jit(solution)/shard_map/ppermute | solution.py:191
  63.3 3.2 %collective-permute-start.24 = (bf16[384,256]{1,0:T(8,128)(2,1)S(1)}, bf16[384,256]{1,0:T(8,128)(2,1)S(1)}, u32[]{:S(2)}, u32[]{:S(2)}) collective-permute-start(bf16[384,256]{1,0:T(8,128)(2,1)S(1)} %shard_map.115.refs_0_), channel_id=1, source_target_pairs={{0,8},{4,12},{8,0},{12,4},{16,24},{20,28},{24,16},{28,20},{1,9},{5... | collective-permute-start | bytes 589832 | tf_op jit(solution)/shard_map/ppermute | solution.py:191
  66.5 4.0 %collective-permute-done.28.got_ref = bf16[384,256]{1,0:T(8,128)(2,1)S(1)} collective-permute-done((bf16[384,256]{1,0:T(8,128)(2,1)S(1)}, bf16[384,256]{1,0:T(8,128)(2,1)S(1)}, u32[]{:S(2)}, u32[]{:S(2)}) %collective-permute-start.28) | collective-permute-done | bytes 196640 | tf_op jit(solution)/shard_map/ppermute | solution.py:191
  70.5 0.6 collective-permute-start.29
  71.1 1.5 %collective-permute-start.20 = (bf16[256,256]{1,0:T(8,128)(2,1)S(1)}, bf16[256,256]{1,0:T(8,128)(2,1)S(1)}, u32[]{:S(2)}, u32[]{:S(2)}) collective-permute-start(bf16[256,256]{1,0:T(8,128)(2,1)S(1)} %shard_map.111), channel_id=1, source_target_pairs={{0,2},{1,3},{2,0},{3,1},{4,6},{5,7},{6,4},{7,5},{8,10},{9,11},{10,... | collective-permute-start | bytes 393224 | tf_op jit(solution)/shard_map/ppermute | solution.py:191
  72.7 1.5 %collective-permute-start.32 = (bf16[256,256]{1,0:T(8,128)(2,1)S(1)}, bf16[256,256]{1,0:T(8,128)(2,1)S(1)}, u32[]{:S(2)}, u32[]{:S(2)}) collective-permute-start(bf16[256,256]{1,0:T(8,128)(2,1)S(1)} %get-tuple-element.91), channel_id=1, source_target_pairs={{0,8},{4,12},{8,0},{12,4},{16,24},{20,28},{24,16},{28,20},{1,9},{5... | collective-permute-start | bytes 393224 | tf_op jit(solution)/shard_map/ppermute | solution.py:191
  74.2 0.5 collective-permute-start.26
  74.8 1.5 %collective-permute-start.30 = (bf16[384,256]{1,0:T(8,128)(2,1)S(1)}, bf16[384,256]{1,0:T(8,128)(2,1)S(1)}, u32[]{:S(2)}, u32[]{:S(2)}) collective-permute-start(bf16[384,256]{1,0:T(8,128)(2,1)S(1)} %shard_map.117.refs_4_), channel_id=1, source_target_pairs={{0,4},{4,0},{8,12},{12,8},{16,20},{20,16},{24,28},{28,24},{1,5},{5... | collective-permute-start | bytes 589832 | tf_op jit(solution)/shard_map/ppermute | solution.py:191
  76.3 2.2 %collective-permute-done.29.refs_5_ = bf16[384,256]{1,0:T(8,128)(2,1)S(1)} collective-permute-done((bf16[384,256]{1,0:T(8,128)(2,1)S(1)}, bf16[384,256]{1,0:T(8,128)(2,1)S(1)}, u32[]{:S(2)}, u32[]{:S(2)}) %collective-permute-start.29) | collective-permute-done | bytes 196640 | tf_op jit(solution)/shard_map/ppermute | solution.py:191
  78.4 0.5 collective-permute-start.31
  79.0 0.1 collective-permute-start.21
  79.1 1.1 %collective-permute-done.32.got_ref = bf16[256,256]{1,0:T(8,128)(2,1)S(1)} collective-permute-done((bf16[256,256]{1,0:T(8,128)(2,1)S(1)}, bf16[256,256]{1,0:T(8,128)(2,1)S(1)}, u32[]{:S(2)}, u32[]{:S(2)}) %collective-permute-start.32) | collective-permute-done | bytes 131104 | tf_op jit(solution)/shard_map/ppermute | solution.py:191
  80.2 1.5 %collective-permute-start.33 = (bf16[128,256]{1,0:T(8,128)(2,1)S(1)}, bf16[128,256]{1,0:T(8,128)(2,1)S(1)}, u32[]{:S(2)}, u32[]{:S(2)}) collective-permute-start(bf16[128,256]{1,0:T(8,128)(2,1)S(1)} %get-tuple-element.94), channel_id=1, source_target_pairs={{0,16},{4,20},{8,24},{12,28},{16,0},{20,4},{24,8},{28,12},{1,17},{... | collective-permute-start | bytes 196616 | tf_op jit(solution)/shard_map/ppermute | solution.py:191
  81.7 2.1 %shard_map.113 = bf16[128,1024]{1,0:T(8,128)(2,1)} custom-call(s32[5]{0:T(128)S(1)} %stack.23.at_ref, bf16[128,512]{1,0:T(8,128)(2,1)S(1)} %get-tuple-element.79.refs_0_.back_ref, bf16[128,512]{1,0:T(8,128)(2,1)S(1)} %collective-permute-done.19.refs_1_.x_ref, bf16[256,256]{1,0:T(8,128)(2,1)S(1)} %collective-permute-done.20.refs_2_.y_ref, ...), custom_call_target="tpu_custom_call" | custom-call | flops 1 | bytes 1 | tf_op jit(solution)/shard_map/pallas_call | solution.py:690
  83.8 2.4 %collective-permute-done.33.got_ref = bf16[128,256]{1,0:T(8,128)(2,1)S(1)} collective-permute-done((bf16[128,256]{1,0:T(8,128)(2,1)S(1)}, bf16[128,256]{1,0:T(8,128)(2,1)S(1)}, u32[]{:S(2)}, u32[]{:S(2)}) %collective-permute-start.33) | collective-permute-done | bytes 65568 | tf_op jit(solution)/shard_map/ppermute | solution.py:191
  86.1 0.6 shard_map.120
  86.7 1.4 %collective-permute-start.34 = (bf16[128,128]{1,0:T(8,128)(2,1)S(1)}, bf16[128,128]{1,0:T(8,128)(2,1)S(1)}, u32[]{:S(2)}, u32[]{:S(2)}) collective-permute-start(bf16[128,128]{1,0:T(8,128)(2,1)S(1)} %get-tuple-element.97), channel_id=1, source_target_pairs={{0,4},{4,0},{8,12},{12,8},{16,20},{20,16},{24,28},{28,24},{1,5},{5... | collective-permute-start | bytes 98312 | tf_op jit(solution)/shard_map/ppermute | solution.py:191
  88.1 0.5 collective-permute-done.31.refs_7_
  88.5 2.1 %shard_map.118 = (bf16[384,1024]{1,0:T(8,128)(2,1)}, bf16[384,1024]{1,0:T(8,128)(2,1)}) custom-call(s32[5]{0:T(128)S(1)} %stack.23.at_ref, bf16[384,256]{1,0:T(8,128)(2,1)S(1)} %shard_map.115.refs_0_, bf16[384,256]{1,0:T(8,128)(2,1)S(1)} %collective-permute-done.24.refs_1_, bf16[384,256]{1,0:T(8,128)(2,1)S(1)} %collective-permute-done.25.refs_2_, ...), custom_call_target="tpu_custom_call" | custom-call | flops 1 | bytes 1 | tf_op jit(solution)/shard_map/pallas_call | solution.py:783
  90.7 0.0 collective-permute-done.34.got_ref
  90.7 1.3 %shard_map.121 = f32[128,256]{1,0:T(8,128)} custom-call(s32[5]{0:T(128)S(1)} %stack.23.at_ref, f32[128,128]{1,0:T(8,128)S(1)} %get-tuple-element.96.keep_ref, bf16[128,128]{1,0:T(8,128)(2,1)S(1)} %collective-permute-done.34.got_ref), custom_call_target="tpu_custom_call" | custom-call | flops 1 | bytes 1 | tf_op jit(solution)/shard_map/pallas_call | solution.py:750
  (39 shorter events, 0.3 us)
Async XLA Ops:
  0.6 21.1 %copy-start.5 = (bf16[128,1024]{1,0:T(8,128)(2,1)S(1)}, bf16[128,1024]{1,0:T(8,128)(2,1)}, u32[]{:S(2)}) copy-start(bf16[128,1024]{1,0:T(8,128)(2,1)} %refs_0_.1) | copy-start | bytes 786436
  2.8 29.8 %copy-start.1 = (bf16[272,512]{1,0:T(8,128)(2,1)S(1)}, bf16[272,512]{1,0:T(8,128)(2,1)}, u32[]{:S(2)}) copy-start(bf16[272,512]{1,0:T(8,128)(2,1)} %get-tuple-element.51.refs_0_) | copy-start | bytes 835588
  2.8 9.8 %collective-permute-start.1 = (bf16[272,512]{1,0:T(8,128)(2,1)}, bf16[272,512]{1,0:T(8,128)(2,1)S(1)}, u32[]{:S(2)}, u32[]{:S(2)}) collective-permute-start(bf16[272,512]{1,0:T(8,128)(2,1)} %get-tuple-element.52), channel_id=1, source_target_pairs={{0,4},{4,0},{8,12},{12,8},{16,20},{20,16},{24,28},{28,24},{1,5},{5... | collective-permute-start | bytes 835592 | tf_op jit(solution)/shard_map/ppermute | solution.py:191
  5.8 9.3 %collective-permute-start = (bf16[272,512]{1,0:T(8,128)(2,1)}, bf16[272,512]{1,0:T(8,128)(2,1)S(1)}, u32[]{:S(2)}, u32[]{:S(2)}) collective-permute-start(bf16[272,512]{1,0:T(8,128)(2,1)} %get-tuple-element.51.refs_0_), channel_id=1, source_target_pairs={{0,1},{1,0},{2,3},{3,2},{4,5},{5,4},{6,7},{7,6},{8,9},{9,8},{10,11... | collective-permute-start | bytes 835592 | tf_op jit(solution)/shard_map/ppermute | solution.py:191
  5.8 9.3 %collective-permute-start.3 = (bf16[272,512]{1,0:T(8,128)(2,1)}, bf16[272,512]{1,0:T(8,128)(2,1)S(1)}, u32[]{:S(2)}, u32[]{:S(2)}) collective-permute-start(bf16[272,512]{1,0:T(8,128)(2,1)} %get-tuple-element.51.refs_0_), channel_id=1, source_target_pairs={{0,2},{1,3},{2,0},{3,1},{4,6},{5,7},{6,4},{7,5},{8,10},{9,11},{10,... | collective-permute-start | bytes 835592 | tf_op jit(solution)/shard_map/ppermute | solution.py:191
  7.4 1.1 %copy-start.3 = (bf16[384,1024]{1,0:T(8,128)(2,1)S(1)}, bf16[384,1024]{1,0:T(8,128)(2,1)}, u32[]{:S(2)}) copy-start(bf16[384,1024]{1,0:T(8,128)(2,1)} %k_ref.1) | copy-start | bytes 2359300
  8.5 1.1 %copy-start.4 = (bf16[384,1024]{1,0:T(8,128)(2,1)S(1)}, bf16[384,1024]{1,0:T(8,128)(2,1)}, u32[]{:S(2)}) copy-start(bf16[384,1024]{1,0:T(8,128)(2,1)} %v_ref.1) | copy-start | bytes 2359300
  12.6 2.4 %collective-permute-start.2 = (bf16[272,512]{1,0:T(8,128)(2,1)S(1)}, bf16[272,512]{1,0:T(8,128)(2,1)S(1)}, u32[]{:S(2)}, u32[]{:S(2)}) collective-permute-start(bf16[272,512]{1,0:T(8,128)(2,1)S(1)} %collective-permute-done.1.refs_2_), channel_id=1, source_target_pairs={{0,1},{1,0},{2,3},{3,2},{4,5},{5,4},{6,7},{7,6},{8,9},{9,8},{10,11... | collective-permute-start | bytes 835592 | tf_op jit(solution)/shard_map/ppermute | solution.py:191
  12.6 9.1 %collective-permute-start.5 = (bf16[272,512]{1,0:T(8,128)(2,1)S(1)}, bf16[272,512]{1,0:T(8,128)(2,1)S(1)}, u32[]{:S(2)}, u32[]{:S(2)}) collective-permute-start(bf16[272,512]{1,0:T(8,128)(2,1)S(1)} %collective-permute-done.1.refs_2_), channel_id=1, source_target_pairs={{0,2},{1,3},{2,0},{3,1},{4,6},{5,7},{6,4},{7,5},{8,10},{9,11},{10,... | collective-permute-start | bytes 835592 | tf_op jit(solution)/shard_map/ppermute | solution.py:191
  15.1 8.4 %collective-permute-start.4 = (bf16[272,512]{1,0:T(8,128)(2,1)S(1)}, bf16[272,512]{1,0:T(8,128)(2,1)S(1)}, u32[]{:S(2)}, u32[]{:S(2)}) collective-permute-start(bf16[272,512]{1,0:T(8,128)(2,1)S(1)} %collective-permute-done.3.refs_0_.refs_4_), channel_id=1, source_target_pairs={{0,1},{1,0},{2,3},{3,2},{4,5},{5,4},{6,7},{7,6},{8,9},{9,8},{10,11... | collective-permute-start | bytes 835592 | tf_op jit(solution)/shard_map/ppermute | solution.py:191
  15.1 1.0 %copy-start = (bf16[272,512]{1,0:T(8,128)(2,1)S(1)}, bf16[272,512]{1,0:T(8,128)(2,1)}, u32[]{:S(2)}) copy-start(bf16[272,512]{1,0:T(8,128)(2,1)} %get-tuple-element.51.refs_0_) | copy-start | bytes 835588
  21.7 1.8 %collective-permute-start.6 = (bf16[272,512]{1,0:T(8,128)(2,1)S(1)}, bf16[272,512]{1,0:T(8,128)(2,1)S(1)}, u32[]{:S(2)}, u32[]{:S(2)}) collective-permute-start(bf16[272,512]{1,0:T(8,128)(2,1)S(1)} %collective-permute-done.5.refs_2_.refs_6_), channel_id=1, source_target_pairs={{0,1},{1,0},{2,3},{3,2},{4,5},{5,4},{6,7},{7,6},{8,9},{9,8},{10,11... | collective-permute-start | bytes 835592 | tf_op jit(solution)/shard_map/ppermute | solution.py:191
  21.7 8.7 %collective-permute-start.12 = (bf16[128,1024]{1,0:T(8,128)(2,1)S(1)}, bf16[128,1024]{1,0:T(8,128)(2,1)S(1)}, u32[]{:S(2)}, u32[]{:S(2)}) collective-permute-start(bf16[128,1024]{1,0:T(8,128)(2,1)S(1)} %copy-done.5), channel_id=1, source_target_pairs={{0,2},{1,3},{2,0},{3,1},{4,6},{5,7},{6,4},{7,5},{8,10},{9,11},{10,... | collective-permute-start | bytes 786440 | tf_op jit(solution)/shard_map/ppermute | solution.py:191
  25.9 11.8 %collective-permute-start.10 = (bf16[128,1024]{1,0:T(8,128)(2,1)S(1)}, bf16[128,1024]{1,0:T(8,128)(2,1)S(1)}, u32[]{:S(2)}, u32[]{:S(2)}) collective-permute-start(bf16[128,1024]{1,0:T(8,128)(2,1)S(1)} %copy-done.5), channel_id=1, source_target_pairs={{0,4},{4,0},{8,12},{12,8},{16,20},{20,16},{24,28},{28,24},{1,5},{5... | collective-permute-start | bytes 786440 | tf_op jit(solution)/shard_map/ppermute | solution.py:191
  27.4 1.2 %collective-permute-start.7 = (f32[4,2,1024]{2,1,0:T(2,128)S(1)}, f32[4,2,1024]{2,1,0:T(2,128)S(1)}, u32[]{:S(2)}, u32[]{:S(2)}) collective-permute-start(f32[4,2,1024]{2,1,0:T(2,128)S(1)} %get-tuple-element.58), channel_id=1, source_target_pairs={{0,1},{1,0},{2,3},{3,2},{4,5},{5,4},{6,7},{7,6},{8,9},{9,8},{10,11... | collective-permute-start | bytes 98312 | tf_op jit(solution)/shard_map/ppermute | solution.py:191
  28.7 4.0 %collective-permute-start.8 = (f32[4,2,1024]{2,1,0:T(2,128)S(1)}, f32[4,2,1024]{2,1,0:T(2,128)S(1)}, u32[]{:S(2)}, u32[]{:S(2)}) collective-permute-start(f32[4,2,1024]{2,1,0:T(2,128)S(1)} %shard_map.106.refs_14_), channel_id=1, source_target_pairs={{0,2},{1,3},{2,0},{3,1},{4,6},{5,7},{6,4},{7,5},{8,10},{9,11},{10,... | collective-permute-start | bytes 98312 | tf_op jit(solution)/shard_map/ppermute | solution.py:191
  37.7 3.2 %collective-permute-start.13 = (bf16[128,1024]{1,0:T(8,128)(2,1)S(1)}, bf16[128,1024]{1,0:T(8,128)(2,1)S(1)}, u32[]{:S(2)}, u32[]{:S(2)}) collective-permute-start(bf16[128,1024]{1,0:T(8,128)(2,1)S(1)} %get-tuple-element.72), channel_id=1, source_target_pairs={{0,1},{1,0},{2,3},{3,2},{4,5},{5,4},{6,7},{7,6},{8,9},{9,8},{10,11... | collective-permute-start | bytes 786440 | tf_op jit(solution)/shard_map/ppermute | solution.py:191
  37.7 12.5 %collective-permute-start.15 = (bf16[128,1024]{1,0:T(8,128)(2,1)S(1)}, bf16[128,1024]{1,0:T(8,128)(2,1)S(1)}, u32[]{:S(2)}, u32[]{:S(2)}) collective-permute-start(bf16[128,1024]{1,0:T(8,128)(2,1)S(1)} %collective-permute-done.10.refs_2_), channel_id=1, source_target_pairs={{0,2},{1,3},{2,0},{3,1},{4,6},{5,7},{6,4},{7,5},{8,10},{9,11},{10,... | collective-permute-start | bytes 786440 | tf_op jit(solution)/shard_map/ppermute | solution.py:191
  39.3 8.2 %collective-permute-start.22 = (bf16[384,256]{1,0:T(8,128)(2,1)S(1)}, bf16[384,256]{1,0:T(8,128)(2,1)S(1)}, u32[]{:S(2)}, u32[]{:S(2)}) collective-permute-start(bf16[384,256]{1,0:T(8,128)(2,1)S(1)} %get-tuple-element.83), channel_id=1, source_target_pairs={{0,8},{4,12},{8,0},{12,4},{16,24},{20,28},{24,16},{28,20},{1,9},{5... | collective-permute-start | bytes 589832 | tf_op jit(solution)/shard_map/ppermute | solution.py:191
  41.0 16.8 %collective-permute-start.18 = (bf16[128,1024]{1,0:T(8,128)(2,1)S(1)}, bf16[128,1024]{1,0:T(8,128)(2,1)S(1)}, u32[]{:S(2)}, u32[]{:S(2)}) collective-permute-start(bf16[128,1024]{1,0:T(8,128)(2,1)S(1)} %shard_map.108), channel_id=1, source_target_pairs={{0,2},{1,3},{2,0},{3,1},{4,6},{5,7},{6,4},{7,5},{8,10},{9,11},{10,... | collective-permute-start | bytes 786440 | tf_op jit(solution)/shard_map/ppermute | solution.py:191
  46.5 10.7 %collective-permute-start.27 = (bf16[384,256]{1,0:T(8,128)(2,1)S(1)}, bf16[384,256]{1,0:T(8,128)(2,1)S(1)}, u32[]{:S(2)}, u32[]{:S(2)}) collective-permute-start(bf16[384,256]{1,0:T(8,128)(2,1)S(1)} %get-tuple-element.86), channel_id=1, source_target_pairs={{0,8},{4,12},{8,0},{12,4},{16,24},{20,28},{24,16},{28,20},{1,9},{5... | collective-permute-start | bytes 589832 | tf_op jit(solution)/shard_map/ppermute | solution.py:191
  47.5 34.1 %copy-start.2 = (bf16[1024,1024]{1,0:T(8,128)(2,1)S(1)}, bf16[1024,1024]{1,0:T(8,128)(2,1)}, u32[]{:S(2)}) copy-start(bf16[1024,1024]{1,0:T(8,128)(2,1)} %wq_ref.1) | copy-start | bytes 6291460
  47.6 9.6 %collective-permute-start.23 = (bf16[384,256]{1,0:T(8,128)(2,1)S(1)}, bf16[384,256]{1,0:T(8,128)(2,1)S(1)}, u32[]{:S(2)}, u32[]{:S(2)}) collective-permute-start(bf16[384,256]{1,0:T(8,128)(2,1)S(1)} %shard_map.114.own_ref), channel_id=1, source_target_pairs={{0,16},{4,20},{8,24},{12,28},{16,0},{20,4},{24,8},{28,12},{1,17},{... | collective-permute-start | bytes 589832 | tf_op jit(solution)/shard_map/ppermute | solution.py:191
  50.2 7.7 %collective-permute-start.9 = (bf16[128,1024]{1,0:T(8,128)(2,1)S(1)}, bf16[128,1024]{1,0:T(8,128)(2,1)S(1)}, u32[]{:S(2)}, u32[]{:S(2)}) collective-permute-start(bf16[128,1024]{1,0:T(8,128)(2,1)S(1)} %copy-done.5), channel_id=1, source_target_pairs={{0,1},{1,0},{2,3},{3,2},{4,5},{5,4},{6,7},{7,6},{8,9},{9,8},{10,11... | collective-permute-start | bytes 786440 | tf_op jit(solution)/shard_map/ppermute | solution.py:191
  50.3 9.9 %collective-permute-start.11 = (bf16[128,1024]{1,0:T(8,128)(2,1)S(1)}, bf16[128,1024]{1,0:T(8,128)(2,1)S(1)}, u32[]{:S(2)}, u32[]{:S(2)}) collective-permute-start(bf16[128,1024]{1,0:T(8,128)(2,1)S(1)} %collective-permute-done.10.refs_2_), channel_id=1, source_target_pairs={{0,1},{1,0},{2,3},{3,2},{4,5},{5,4},{6,7},{7,6},{8,9},{9,8},{10,11... | collective-permute-start | bytes 786440 | tf_op jit(solution)/shard_map/ppermute | solution.py:191
  57.2 3.5 %collective-permute-start.16 = (bf16[128,1024]{1,0:T(8,128)(2,1)S(1)}, bf16[128,1024]{1,0:T(8,128)(2,1)S(1)}, u32[]{:S(2)}, u32[]{:S(2)}) collective-permute-start(bf16[128,1024]{1,0:T(8,128)(2,1)S(1)} %collective-permute-done.15.refs_6_), channel_id=1, source_target_pairs={{0,1},{1,0},{2,3},{3,2},{4,5},{5,4},{6,7},{7,6},{8,9},{9,8},{10,11... | collective-permute-start | bytes 786440 | tf_op jit(solution)/shard_map/ppermute | solution.py:191
  57.2 3.5 %collective-permute-start.14 = (bf16[128,1024]{1,0:T(8,128)(2,1)S(1)}, bf16[128,1024]{1,0:T(8,128)(2,1)S(1)}, u32[]{:S(2)}, u32[]{:S(2)}) collective-permute-start(bf16[128,1024]{1,0:T(8,128)(2,1)S(1)} %collective-permute-done.12.refs_4_), channel_id=1, source_target_pairs={{0,1},{1,0},{2,3},{3,2},{4,5},{5,4},{6,7},{7,6},{8,9},{9,8},{10,11... | collective-permute-start | bytes 786440 | tf_op jit(solution)/shard_map/ppermute | solution.py:191
  57.7 2.9 %collective-permute-start.17 = (bf16[128,1024]{1,0:T(8,128)(2,1)S(1)}, bf16[128,1024]{1,0:T(8,128)(2,1)S(1)}, u32[]{:S(2)}, u32[]{:S(2)}) collective-permute-start(bf16[128,1024]{1,0:T(8,128)(2,1)S(1)} %get-tuple-element.78), channel_id=1, source_target_pairs={{0,1},{1,0},{2,3},{3,2},{4,5},{5,4},{6,7},{7,6},{8,9},{9,8},{10,11... | collective-permute-start | bytes 786440 | tf_op jit(solution)/shard_map/ppermute | solution.py:191
  57.9 12.5 %collective-permute-start.28 = (bf16[384,256]{1,0:T(8,128)(2,1)S(1)}, bf16[384,256]{1,0:T(8,128)(2,1)S(1)}, u32[]{:S(2)}, u32[]{:S(2)}) collective-permute-start(bf16[384,256]{1,0:T(8,128)(2,1)S(1)} %shard_map.116.own_ref), channel_id=1, source_target_pairs={{0,16},{4,20},{8,24},{12,28},{16,0},{20,4},{24,8},{28,12},{1,17},{... | collective-permute-start | bytes 589832 | tf_op jit(solution)/shard_map/ppermute | solution.py:191
  60.1 10.4 %collective-permute-start.25 = (bf16[384,256]{1,0:T(8,128)(2,1)S(1)}, bf16[384,256]{1,0:T(8,128)(2,1)S(1)}, u32[]{:S(2)}, u32[]{:S(2)}) collective-permute-start(bf16[384,256]{1,0:T(8,128)(2,1)S(1)} %shard_map.115.refs_0_), channel_id=1, source_target_pairs={{0,4},{4,0},{8,12},{12,8},{16,20},{20,16},{24,28},{28,24},{1,5},{5... | collective-permute-start | bytes 589832 | tf_op jit(solution)/shard_map/ppermute | solution.py:191
  61.7 9.4 %collective-permute-start.19 = (bf16[128,512]{1,0:T(8,128)(2,1)S(1)}, bf16[128,512]{1,0:T(8,128)(2,1)S(1)}, u32[]{:S(2)}, u32[]{:S(2)}) collective-permute-start(bf16[128,512]{1,0:T(8,128)(2,1)S(1)} %get-tuple-element.80), channel_id=1, source_target_pairs={{0,4},{4,0},{8,12},{12,8},{16,20},{20,16},{24,28},{28,24},{1,5},{5... | collective-permute-start | bytes 393224 | tf_op jit(solution)/shard_map/ppermute | solution.py:191
  63.3 11.0 %collective-permute-start.24 = (bf16[384,256]{1,0:T(8,128)(2,1)S(1)}, bf16[384,256]{1,0:T(8,128)(2,1)S(1)}, u32[]{:S(2)}, u32[]{:S(2)}) collective-permute-start(bf16[384,256]{1,0:T(8,128)(2,1)S(1)} %shard_map.115.refs_0_), channel_id=1, source_target_pairs={{0,8},{4,12},{8,0},{12,4},{16,24},{20,28},{24,16},{28,20},{1,9},{5... | collective-permute-start | bytes 589832 | tf_op jit(solution)/shard_map/ppermute | solution.py:191
  70.5 7.9 %collective-permute-start.29 = (bf16[384,256]{1,0:T(8,128)(2,1)S(1)}, bf16[384,256]{1,0:T(8,128)(2,1)S(1)}, u32[]{:S(2)}, u32[]{:S(2)}) collective-permute-start(bf16[384,256]{1,0:T(8,128)(2,1)S(1)} %shard_map.117.refs_4_), channel_id=1, source_target_pairs={{0,8},{4,12},{8,0},{12,4},{16,24},{20,28},{24,16},{28,20},{1,9},{5... | collective-permute-start | bytes 589832 | tf_op jit(solution)/shard_map/ppermute | solution.py:191
  71.1 7.8 %collective-permute-start.20 = (bf16[256,256]{1,0:T(8,128)(2,1)S(1)}, bf16[256,256]{1,0:T(8,128)(2,1)S(1)}, u32[]{:S(2)}, u32[]{:S(2)}) collective-permute-start(bf16[256,256]{1,0:T(8,128)(2,1)S(1)} %shard_map.111), channel_id=1, source_target_pairs={{0,2},{1,3},{2,0},{3,1},{4,6},{5,7},{6,4},{7,5},{8,10},{9,11},{10,... | collective-permute-start | bytes 393224 | tf_op jit(solution)/shard_map/ppermute | solution.py:191
  72.7 7.5 %collective-permute-start.32 = (bf16[256,256]{1,0:T(8,128)(2,1)S(1)}, bf16[256,256]{1,0:T(8,128)(2,1)S(1)}, u32[]{:S(2)}, u32[]{:S(2)}) collective-permute-start(bf16[256,256]{1,0:T(8,128)(2,1)S(1)} %get-tuple-element.91), channel_id=1, source_target_pairs={{0,8},{4,12},{8,0},{12,4},{16,24},{20,28},{24,16},{28,20},{1,9},{5... | collective-permute-start | bytes 393224 | tf_op jit(solution)/shard_map/ppermute | solution.py:191
  74.2 13.9 %collective-permute-start.26 = (bf16[384,256]{1,0:T(8,128)(2,1)S(1)}, bf16[384,256]{1,0:T(8,128)(2,1)S(1)}, u32[]{:S(2)}, u32[]{:S(2)}) collective-permute-start(bf16[384,256]{1,0:T(8,128)(2,1)S(1)} %collective-permute-done.24.refs_1_), channel_id=1, source_target_pairs={{0,4},{4,0},{8,12},{12,8},{16,20},{20,16},{24,28},{28,24},{1,5},{5... | collective-permute-start | bytes 589832 | tf_op jit(solution)/shard_map/ppermute | solution.py:191
  74.8 13.3 %collective-permute-start.30 = (bf16[384,256]{1,0:T(8,128)(2,1)S(1)}, bf16[384,256]{1,0:T(8,128)(2,1)S(1)}, u32[]{:S(2)}, u32[]{:S(2)}) collective-permute-start(bf16[384,256]{1,0:T(8,128)(2,1)S(1)} %shard_map.117.refs_4_), channel_id=1, source_target_pairs={{0,4},{4,0},{8,12},{12,8},{16,20},{20,16},{24,28},{28,24},{1,5},{5... | collective-permute-start | bytes 589832 | tf_op jit(solution)/shard_map/ppermute | solution.py:191
  78.4 10.1 %collective-permute-start.31 = (bf16[384,256]{1,0:T(8,128)(2,1)S(1)}, bf16[384,256]{1,0:T(8,128)(2,1)S(1)}, u32[]{:S(2)}, u32[]{:S(2)}) collective-permute-start(bf16[384,256]{1,0:T(8,128)(2,1)S(1)} %collective-permute-done.29.refs_5_), channel_id=1, source_target_pairs={{0,4},{4,0},{8,12},{12,8},{16,20},{20,16},{24,28},{28,24},{1,5},{5... | collective-permute-start | bytes 589832 | tf_op jit(solution)/shard_map/ppermute | solution.py:191
  79.0 2.7 %collective-permute-start.21 = (bf16[512,128]{1,0:T(8,128)(2,1)S(1)}, bf16[512,128]{1,0:T(8,128)(2,1)S(1)}, u32[]{:S(2)}, u32[]{:S(2)}) collective-permute-start(bf16[512,128]{1,0:T(8,128)(2,1)S(1)} %shard_map.112), channel_id=1, source_target_pairs={{0,1},{1,0},{2,3},{3,2},{4,5},{5,4},{6,7},{7,6},{8,9},{9,8},{10,11... | collective-permute-start | bytes 393224 | tf_op jit(solution)/shard_map/ppermute | solution.py:191
  80.2 5.9 %collective-permute-start.33 = (bf16[128,256]{1,0:T(8,128)(2,1)S(1)}, bf16[128,256]{1,0:T(8,128)(2,1)S(1)}, u32[]{:S(2)}, u32[]{:S(2)}) collective-permute-start(bf16[128,256]{1,0:T(8,128)(2,1)S(1)} %get-tuple-element.94), channel_id=1, source_target_pairs={{0,16},{4,20},{8,24},{12,28},{16,0},{20,4},{24,8},{28,12},{1,17},{... | collective-permute-start | bytes 196616 | tf_op jit(solution)/shard_map/ppermute | solution.py:191
  86.7 4.0 %collective-permute-start.34 = (bf16[128,128]{1,0:T(8,128)(2,1)S(1)}, bf16[128,128]{1,0:T(8,128)(2,1)S(1)}, u32[]{:S(2)}, u32[]{:S(2)}) collective-permute-start(bf16[128,128]{1,0:T(8,128)(2,1)S(1)} %get-tuple-element.97), channel_id=1, source_target_pairs={{0,4},{4,0},{8,12},{12,8},{16,20},{20,16},{24,28},{28,24},{1,5},{5... | collective-permute-start | bytes 98312 | tf_op jit(solution)/shard_map/ppermute | solution.py:191

commit v8 on v7

--- a/solution.py
+++ b/solution.py
@@ -480,7 +480,7 @@
     else:
         p_ref, m_ref, lse_ref = refs[count + 1 :]
     for j in range(step):
-        q = jnp.concatenate([r[:, span(j)] for r in q_refs], axis=0)
+        q = jnp.concatenate([r[: (r.shape[0] - EXTRA) // 2, span(j)] for r in q_refs], axis=0)
         k = k_ref[:, span(j)]
         for head in range(2):
             s = dot(own_lanes(k, head), q, 1, 1)
@@ -494,26 +494,22 @@
         send_ref[...] = jnp.concatenate([flip_core(la_ref[...]), flip_core(lse_ref[...])], axis=-1)
 
 
-def side_of(pieces, keys, extra=None, step=2):
+def side_of(pieces, keys, extra=None):
     count = len(pieces)
     cols = pieces[0].shape[1]
     tokens = keys.shape[0]
     piece = (pieces[0].shape[0] - EXTRA) // 2
     rows, pairs = piece * count, cols // PAIR
-    stat_spec = lambda n: pl.BlockSpec((step, 2, n), lambda i: (i, 0, 0))
-    in_specs = [pl.BlockSpec((piece, step * PAIR), lambda i: (0, i))] * count
-    in_specs += [pl.BlockSpec((tokens, step * PAIR), lambda i: (0, i))]
-    out_specs = [pl.BlockSpec((2 * step, tokens, rows), lambda i: (i, 0, 0)), stat_spec(rows), stat_spec(rows)]
+    in_specs, out_specs = [VMEM] * (count + 1), [VMEM] * 3
     out_shape = [like((2 * pairs, tokens, rows)), like((pairs, 2, rows), F32), like((pairs, 2, rows), F32)]
     args = [*pieces, keys]
     if extra is not None:
-        in_specs += [stat_spec(rows)]
-        out_specs += [stat_spec(2 * rows)]
+        in_specs += [VMEM]
+        out_specs += [VMEM]
         out_shape += [like((pairs, 2, 2 * rows), F32)]
         args += [extra]
     return pl.pallas_call(
-        functools.partial(side_kernel, count, step, extra is not None),
-        grid=(pairs // step,),
+        functools.partial(side_kernel, count, pairs, extra is not None),
         in_specs=in_specs,
         out_specs=out_specs,
         out_shape=out_shape,
@@ -545,92 +541,71 @@
     )(la, lb, got)
 
 
-def half_kernel(count, at_ref, *refs):
+def half_kernel(count, own, at_ref, *refs):
     row_refs = refs[:count]
     piece = (row_refs[0].shape[0] - EXTRA) // 2
     pa_ref, pb_ref, v_ref, kt_ref, ma_ref, mb_ref, sent_ref, got_ref = refs[count : count + 8]
     kv_refs, dqs_ref, dqk_ref = refs[count + 8 : -2], refs[-2], refs[-1]
     side = ma_ref.shape[2]
     z = at_ref[Z]
-    v = v_ref[...]
-    tokens = v.shape[0]
-    dk = jnp.zeros((tokens, PAIR), F32)
-    dv = jnp.zeros((tokens, PAIR), F32)
     first = lax.broadcasted_iota(jnp.int32, (PAIR, side), 0) < HD
-    halves = []
-    for b, p_ref, m_ref in ((0, pa_ref, ma_ref), (1, pb_ref, mb_ref)):
-        lse = log_add(sent_ref[0, :, span(1 - b, side)], got_ref[0, :, span(b, side)])
-        w = jnp.exp(m_ref[0] - lse)
-        wide = jnp.where(first, w[0:1], w[1:2]).T
-        at = slice(b * count // 2, (b + 1) * count // 2)
-        q = jnp.concatenate([r[:piece] for r in row_refs[at]], axis=0)
-        g = jnp.concatenate([r[piece : 2 * piece] for r in row_refs[at]], axis=0)
-        parts = [r[2 * piece :].astype(F32) for r in row_refs[at]]
-        delta = jnp.concatenate([d[0:2] + d[2:4] + d[4:6] for d in parts], axis=1)
-        qw = (q.astype(F32) * wide).astype(BF)
-        gw = (g.astype(F32) * wide).astype(BF)
-        parts = []
-        for head in range(2):
-            p = p_ref[head]
-            dp = dot(v, own_lanes(g, head), 1, 1)
-            t = (p.astype(F32) * (dp - delta[head : head + 1])).astype(BF)
-            dv = dv + dot(p, own_lanes(gw, head), 1, 0)
-            dk = dk + dot(t, own_lanes(qw, head), 1, 0)
-            dq = dot(kt_ref[span(head, HD)], t, 1, 0)
-            parts.append((dq * (w[head : head + 1] * SCALE)).astype(BF))
-        halves.append(jnp.concatenate(parts, axis=0))
-    dq = jnp.concatenate(halves, axis=1)
-
-    @pl.when(pl.program_id(0) == 0)
-    def _():
-        dqs_ref[...] = flip_core(dq)
-
-    @pl.when(pl.program_id(0) == 1)
-    def _():
-        dqk_ref[...] = dq
-
-    both = jnp.concatenate([dk.astype(BF), dv.astype(BF)], axis=0)
-    size = both.shape[0] // 4
-    for ref, order in zip(kv_refs, ORDERS, strict=True):
-        for n, k in enumerate(order):
-            out = both[:size]
-            for j in range(1, 4):
-                out = jnp.where((z ^ k) == j, both[span(j, size)], out)
-            ref[span(n, size)] = out
+    for i in range(2):
+        bit = (i + 1 + at_ref[CORE]) % 2
+        pair = 2 * (at_ref[Y] if own else 1 - at_ref[Y]) + bit
+        lanes = pl.ds(pl.multiple_of(pair * PAIR, PAIR), PAIR)
+        v = v_ref[:, lanes]
+        tokens = v.shape[0]
+        dk = jnp.zeros((tokens, PAIR), F32)
+        dv = jnp.zeros((tokens, PAIR), F32)
+        halves = []
+        for b, p_ref, m_ref in ((0, pa_ref, ma_ref), (1, pb_ref, mb_ref)):
+            lse = log_add(sent_ref[pair, :, span(1 - b, side)], got_ref[pair, :, span(b, side)])
+            w = jnp.exp(m_ref[pair] - lse)
+            wide = jnp.where(first, w[0:1], w[1:2]).T
+            at = slice(b * count // 2, (b + 1) * count // 2)
+            rows = [r[:, lanes] for r in row_refs[at]]
+            q = jnp.concatenate([r[:piece] for r in rows], axis=0)
+            g = jnp.concatenate([r[piece : 2 * piece] for r in rows], axis=0)
+            parts = [r[2 * piece :].astype(F32) for r in rows]
+            delta = jnp.concatenate([d[0:2] + d[2:4] + d[4:6] for d in parts], axis=1)
+            qw = (q.astype(F32) * wide).astype(BF)
+            gw = (g.astype(F32) * wide).astype(BF)
+            parts = []
+            for head in range(2):
+                p = p_ref[2 * pair + head]
+                dp = dot(v, own_lanes(g, head), 1, 1)
+                t = (p.astype(F32) * (dp - delta[head : head + 1])).astype(BF)
+                dv = dv + dot(p, own_lanes(gw, head), 1, 0)
+                dk = dk + dot(t, own_lanes(qw, head), 1, 0)
+                dq = dot(kt_ref[pl.ds(pl.multiple_of(pair * PAIR, PAIR) + head * HD, HD), :], t, 1, 0)
+                parts.append((dq * (w[head : head + 1] * SCALE)).astype(BF))
+            halves.append(jnp.concatenate(parts, axis=0))
+        dq = jnp.concatenate(halves, axis=1)
+        if i == 0:
+            dqs_ref[...] = flip_core(dq)
+        else:
+            dqk_ref[...] = dq
+        both = jnp.concatenate([dk.astype(BF), dv.astype(BF)], axis=0)
+        size = both.shape[0] // 4
+        out_lanes = pl.ds(pl.multiple_of(bit * PAIR, PAIR), PAIR)
+        for ref, order in zip(kv_refs, ORDERS, strict=True):
+            for n, k in enumerate(order):
+                out = both[:size]
+                for j in range(1, 4):
+                    out = jnp.where((z ^ k) == j, both[span(j, size)], out)
+                ref[span(n, size), out_lanes] = out
 
 
 def half_of(at, own, pieces, pa, pb, vp, kt, ma, mb, sent, got):
     count = len(pieces)
-    tokens = vp.shape[0]
-    side = ma.shape[2]
-    bit = lambda i, a: (i + 1 + a[CORE]) % 2
-    pair = lambda i, a: 2 * (a[Y] if own else 1 - a[Y]) + bit(i, a)
-    row_spec = pl.BlockSpec((pieces[0].shape[0], PAIR), lambda i, a: (0, pair(i, a)))
-    p_spec = pl.BlockSpec((2, tokens, side), lambda i, a: (pair(i, a), 0, 0))
-    stat_spec = lambda n: pl.BlockSpec((1, 2, n), lambda i, a: (pair(i, a), 0, 0))
-    block = tokens
-    return pl.pallas_call(
-        functools.partial(half_kernel, count),
-        grid_spec=pltpu.PrefetchScalarGridSpec(
-            num_scalar_prefetch=1,
-            grid=(2,),
-            in_specs=[row_spec] * count
-            + [
-                p_spec,
-                p_spec,
-                pl.BlockSpec((tokens, PAIR), lambda i, a: (0, pair(i, a))),
-                pl.BlockSpec((PAIR, tokens), lambda i, a: (pair(i, a), 0)),
-                stat_spec(side),
-                stat_spec(side),
-                stat_spec(2 * side),
-                stat_spec(2 * side),
-            ],
-            out_specs=[pl.BlockSpec((block, PAIR), lambda i, a: (0, bit(i, a)))] * 2
-            + [pl.BlockSpec((PAIR, 2 * side), lambda i, a: (0, 0))] * 2,
-        ),
-        out_shape=[like((block, 2 * PAIR))] * 2 + [like((PAIR, 2 * side))] * 2,
-        compiler_params=params(),
-        cost_estimate=cost(16 * side * tokens * 2 * PAIR * 2, 8 * side * tokens * 2, 0),
+    tokens, side = vp.shape[0], ma.shape[2]
+    return pl.pallas_call(
+        functools.partial(half_kernel, count, own),
+        in_specs=[SMEM] + [VMEM] * (count + 8),
+        out_specs=[VMEM] * 4,
+        out_shape=[like((tokens, 2 * PAIR))] * 2 + [like((PAIR, 2 * side))] * 2,
+        compiler_params=params(),
+        cost_estimate=cost(),
     )(at, *pieces, pa, pb, vp, kt, ma, mb, sent, got)
 
 

time: 92.2 us -> 90.1 us (0.977)
  Pallas kernels: 25.4 us -> 22.8 us
    pallas_call x4, Pallas kernels: 14.7 us -> 12.1 us  [the longest x2 7.89 us: half_of(): pl.pallas_call(functools.partial(half_kernel, count, own), in_specs=[SMEM...]
  transfers between devices with their start and end apart: 35 -> 35, of which waited for: 12 -> 13; matrix products, arithmetic and copies ran while one was open for 0% -> 0% of each run, Pallas kernels for 24% -> 21%
where the time goes in v8:
time: 90.1 us; the launch traced here: 89.9 us
  starting transfers between devices  36.7 us (41%)
  waiting for transfers between devices  26.3 us (29%)
  Pallas kernels  22.8 us (25%)
  local copies, waits for them, and re-layouts  3.31 us (4%)
    ppermute x35, starting transfers between devices, swap(): return lax.ppermute(x, axis, [(i, i ^ mask) for i in range(size)])  36.7 us
    ppermute x35, waiting for transfers between devices, swap(): return lax.ppermute(x, axis, [(i, i ^ mask) for i in range(size)])  26.3 us
    pallas_call x2, Pallas kernels, half_of(): pl.pallas_call(functools.partial(half_kernel, count, own), in_specs=[SMEM...  7.89 us
    pallas_call x2, Pallas kernels, side_of(): pl.pallas_call(functools.partial(side_kernel, count, pairs, extra is not...  4.2 us
    unnamed x12, local copies, waits for them, and re-layouts  3.23 us
    pallas_call x1, Pallas kernels, pack(): pl.pallas_call(pack_kernel, grid=(steps,), in_specs=[block] * 3, out_spec...  2.19 us
    pallas_call x1, Pallas kernels, tokens_out(): pl.pallas_call(tokens_kernel, in_specs=[SMEM] + [VMEM] * len(parts), out_...  2.12 us
    pallas_call x1, Pallas kernels, input_of(): pl.pallas_call(input_kernel, in_specs=[SMEM] + [VMEM] * 5, out_specs=VMEM...  2.09 us
  transfers between devices with their start and end apart: 35, of which 13 were waited for; matrix products, arithmetic and copies ran while one was open for 0% of the time, Pallas kernels for 21%

profile of v8, /device:TPU:0, one launch (start us, length us, event | category | flops | bytes accessed | tf_op | source)
XLA Modules:
  0.0 89.9 jit_solution(12323117859766796330)
XLA Ops:
  0.6 2.2 %shard_map.102 = (bf16[272,512]{1,0:T(8,128)(2,1)}, bf16[272,512]{1,0:T(8,128)(2,1)}) custom-call(bf16[128,1024]{1,0:T(8,128)(2,1)} %q_ref.1, bf16[128,1024]{1,0:T(8,128)(2,1)} %g_ref.1, bf16[128,1024]{1,0:T(8,128)(2,1)} %o_ref.1), custom_call_target="tpu_custom_call" | custom-call | flops 1 | bytes 1 | tf_op jit(solution)/shard_map/pallas_call | solution.py:382
  2.8 2.9 %collective-permute-start.1 = (bf16[272,512]{1,0:T(8,128)(2,1)}, bf16[272,512]{1,0:T(8,128)(2,1)S(1)}, u32[]{:S(2)}, u32[]{:S(2)}) collective-permute-start(bf16[272,512]{1,0:T(8,128)(2,1)} %get-tuple-element.52), channel_id=1, source_target_pairs={{0,4},{4,0},{8,12},{12,8},{16,20},{20,16},{24,28},{28,24},{1,5},{5... | collective-permute-start | bytes 835592 | tf_op jit(solution)/shard_map/ppermute | solution.py:191
  5.8 0.0 collective-permute-start
  5.8 1.5 %collective-permute-start.3 = (bf16[272,512]{1,0:T(8,128)(2,1)}, bf16[272,512]{1,0:T(8,128)(2,1)S(1)}, u32[]{:S(2)}, u32[]{:S(2)}) collective-permute-start(bf16[272,512]{1,0:T(8,128)(2,1)} %get-tuple-element.51.refs_0_), channel_id=1, source_target_pairs={{0,2},{1,3},{2,0},{3,1},{4,6},{5,7},{6,4},{7,5},{8,10},{9,11},{10,... | collective-permute-start | bytes 835592 | tf_op jit(solution)/shard_map/ppermute | solution.py:191
  7.3 0.1 stack.23.at_ref
  7.4 1.1 %copy-done.3 = bf16[384,1024]{1,0:T(8,128)(2,1)S(1)} copy-done((bf16[384,1024]{1,0:T(8,128)(2,1)S(1)}, bf16[384,1024]{1,0:T(8,128)(2,1)}, u32[]{:S(2)}) %copy-start.3) | copy-done | bytes 786456
  8.5 1.1 %copy-done.4 = bf16[384,1024]{1,0:T(8,128)(2,1)S(1)} copy-done((bf16[384,1024]{1,0:T(8,128)(2,1)S(1)}, bf16[384,1024]{1,0:T(8,128)(2,1)}, u32[]{:S(2)}) %copy-start.4) | copy-done | bytes 786456
  9.6 1.1 %shard_map.103 = (bf16[384,512]{1,0:T(8,128)(2,1)S(1)}, bf16[384,512]{1,0:T(8,128)(2,1)S(1)}, bf16[512,384]{1,0:T(8,128)(2,1)S(1)}) custom-call(s32[5]{0:T(128)S(1)} %stack.23.at_ref, bf16[384,1024]{1,0:T(8,128)(2,1)S(1)} %copy-done.3, bf16[384,1024]{1,0:T(8,128)(2,1)S(1)} %copy-done.4), custom_call_target="tpu_custom_call" | custom-call | flops 1 | bytes 1 | tf_op jit(solution)/shard_map/pallas_call | solution.py:407
  10.7 1.9 %collective-permute-done.1.refs_2_ = bf16[272,512]{1,0:T(8,128)(2,1)S(1)} collective-permute-done((bf16[272,512]{1,0:T(8,128)(2,1)}, bf16[272,512]{1,0:T(8,128)(2,1)S(1)}, u32[]{:S(2)}, u32[]{:S(2)}) %collective-permute-start.1) | collective-permute-done | bytes 278560 | tf_op jit(solution)/shard_map/ppermute | solution.py:191
  12.6 1.8 %collective-permute-start.5 = (bf16[272,512]{1,0:T(8,128)(2,1)S(1)}, bf16[272,512]{1,0:T(8,128)(2,1)S(1)}, u32[]{:S(2)}, u32[]{:S(2)}) collective-permute-start(bf16[272,512]{1,0:T(8,128)(2,1)S(1)} %collective-permute-done.1.refs_2_), channel_id=1, source_target_pairs={{0,2},{1,3},{2,0},{3,1},{4,6},{5,7},{6,4},{7,5},{8,10},{9,11},{10,... | collective-permute-start | bytes 835592 | tf_op jit(solution)/shard_map/ppermute | solution.py:191
  14.4 0.6 collective-permute-done.3.refs_0_.refs_4_
  15.1 0.0 collective-permute-start.4
  15.1 0.0 collective-permute-done.refs_1_
  15.1 0.0 collective-permute-done.2.refs_3_
  15.1 0.0 copy-start
  15.1 0.9 %copy-done = bf16[272,512]{1,0:T(8,128)(2,1)S(1)} copy-done((bf16[272,512]{1,0:T(8,128)(2,1)S(1)}, bf16[272,512]{1,0:T(8,128)(2,1)}, u32[]{:S(2)}) %copy-start) | copy-done | bytes 278552
  16.0 2.1 %shard_map.104 = (bf16[8,384,512]{2,1,0:T(8,128)(2,1)S(1)}, f32[4,2,512]{2,1,0:T(2,128)S(1)}, f32[4,2,512]{2,1,0:T(2,128)S(1)}) custom-call(bf16[272,512]{1,0:T(8,128)(2,1)S(1)} %copy-done, bf16[272,512]{1,0:T(8,128)(2,1)S(1)} %collective-permute-done.refs_1_, bf16[272,512]{1,0:T(8,128)(2,1)S(1)} %collective-permute-done.1.refs_2_, ...), custom_call_target="tpu_custom_call" | custom-call | flops 1 | bytes 1 | tf_op jit(solution)/shard_map/pallas_call | solution.py:511
  18.1 3.6 %collective-permute-done.5.refs_2_.refs_6_ = bf16[272,512]{1,0:T(8,128)(2,1)S(1)} collective-permute-done((bf16[272,512]{1,0:T(8,128)(2,1)S(1)}, bf16[272,512]{1,0:T(8,128)(2,1)S(1)}, u32[]{:S(2)}, u32[]{:S(2)}) %collective-permute-start.5) | collective-permute-done | bytes 278560 | tf_op jit(solution)/shard_map/ppermute | solution.py:191
  21.7 1.7 %collective-permute-start.12 = (bf16[128,1024]{1,0:T(8,128)(2,1)S(1)}, bf16[128,1024]{1,0:T(8,128)(2,1)S(1)}, u32[]{:S(2)}, u32[]{:S(2)}) collective-permute-start(bf16[128,1024]{1,0:T(8,128)(2,1)S(1)} %copy-done.5), channel_id=1, source_target_pairs={{0,2},{1,3},{2,0},{3,1},{4,6},{5,7},{6,4},{7,5},{8,10},{9,11},{10,... | collective-permute-start | bytes 786440 | tf_op jit(solution)/shard_map/ppermute | solution.py:191
  23.5 0.0 collective-permute-done.4.refs_1_.refs_5_
  23.5 2.1 %shard_map.105 = (bf16[8,384,512]{2,1,0:T(8,128)(2,1)S(1)}, f32[4,2,512]{2,1,0:T(2,128)S(1)}, f32[4,2,512]{2,1,0:T(2,128)S(1)}, f32[4,2,1024]{2,1,0:T(2,128)S(1)}) custom-call(bf16[272,512]{1,0:T(8,128)(2,1)S(1)} %collective-permute-done.3.refs_0_.refs_4_, bf16[272,512]{1,0:T(8,128)(2,1)S(1)} %collective-permute-done.4.refs_1_.refs_5_, ...), custom_call_target="tpu_custom_call" | custom-call | flops 1 | bytes 1 | tf_op jit(solution)/shard_map/pallas_call | solution.py:511
  25.6 1.6 %collective-permute-start.10 = (bf16[128,1024]{1,0:T(8,128)(2,1)S(1)}, bf16[128,1024]{1,0:T(8,128)(2,1)S(1)}, u32[]{:S(2)}, u32[]{:S(2)}) collective-permute-start(bf16[128,1024]{1,0:T(8,128)(2,1)S(1)} %copy-done.5), channel_id=1, source_target_pairs={{0,4},{4,0},{8,12},{12,8},{16,20},{20,16},{24,28},{28,24},{1,5},{5... | collective-permute-start | bytes 786440 | tf_op jit(solution)/shard_map/ppermute | solution.py:191
  27.2 1.2 %collective-permute-done.7.got_ref = f32[4,2,1024]{2,1,0:T(2,128)S(1)} collective-permute-done((f32[4,2,1024]{2,1,0:T(2,128)S(1)}, f32[4,2,1024]{2,1,0:T(2,128)S(1)}, u32[]{:S(2)}, u32[]{:S(2)}) %collective-permute-start.7) | collective-permute-done | bytes 32800 | tf_op jit(solution)/shard_map/ppermute | solution.py:191
  28.4 1.6 %collective-permute-start.8 = (f32[4,2,1024]{2,1,0:T(2,128)S(1)}, f32[4,2,1024]{2,1,0:T(2,128)S(1)}, u32[]{:S(2)}, u32[]{:S(2)}) collective-permute-start(f32[4,2,1024]{2,1,0:T(2,128)S(1)} %shard_map.106.refs_14_), channel_id=1, source_target_pairs={{0,2},{1,3},{2,0},{3,1},{4,6},{5,7},{6,4},{7,5},{8,10},{9,11},{10,... | collective-permute-start | bytes 98312 | tf_op jit(solution)/shard_map/ppermute | solution.py:191
  30.0 0.5 collective-permute-done.12.refs_4_
  30.5 1.9 %collective-permute-done.8.refs_15_ = f32[4,2,1024]{2,1,0:T(2,128)S(1)} collective-permute-done((f32[4,2,1024]{2,1,0:T(2,128)S(1)}, f32[4,2,1024]{2,1,0:T(2,128)S(1)}, u32[]{:S(2)}, u32[]{:S(2)}) %collective-permute-start.8) | collective-permute-done | bytes 32800 | tf_op jit(solution)/shard_map/ppermute | solution.py:191
  32.4 3.9 %shard_map.107 = (bf16[384,256]{1,0:T(8,128)(2,1)S(1)}, bf16[384,256]{1,0:T(8,128)(2,1)S(1)}, bf16[128,1024]{1,0:T(8,128)(2,1)S(1)}, bf16[128,1024]{1,0:T(8,128)(2,1)S(1)}) custom-call(s32[5]{0:T(128)S(1)} %stack.23.at_ref, bf16[272,512]{1,0:T(8,128)(2,1)S(1)} %copy-done.1, bf16[272,512]{1,0:T(8,128)(2,1)S(1)} %collective-permute-done.refs_1_, ...), custom_call_target="tpu_custom_call" | custom-call | flops 1 | bytes 1 | tf_op jit(solution)/shard_map/pallas_call | solution.py:602
  36.4 0.1 collective-permute-start.13
  36.4 1.6 %collective-permute-start.15 = (bf16[128,1024]{1,0:T(8,128)(2,1)S(1)}, bf16[128,1024]{1,0:T(8,128)(2,1)S(1)}, u32[]{:S(2)}, u32[]{:S(2)}) collective-permute-start(bf16[128,1024]{1,0:T(8,128)(2,1)S(1)} %collective-permute-done.10.refs_2_), channel_id=1, source_target_pairs={{0,2},{1,3},{2,0},{3,1},{4,6},{5,7},{6,4},{7,5},{8,10},{9,11},{10,... | collective-permute-start | bytes 786440 | tf_op jit(solution)/shard_map/ppermute | solution.py:191
  38.0 1.6 %collective-permute-start.22 = (bf16[384,256]{1,0:T(8,128)(2,1)S(1)}, bf16[384,256]{1,0:T(8,128)(2,1)S(1)}, u32[]{:S(2)}, u32[]{:S(2)}) collective-permute-start(bf16[384,256]{1,0:T(8,128)(2,1)S(1)} %get-tuple-element.83), channel_id=1, source_target_pairs={{0,8},{4,12},{8,0},{12,4},{16,24},{20,28},{24,16},{28,20},{1,9},{5... | collective-permute-start | bytes 589832 | tf_op jit(solution)/shard_map/ppermute | solution.py:191
  39.6 0.1 shard_map.108
  39.7 0.6 collective-permute-start.18
  40.2 3.9 %shard_map.109 = (bf16[384,256]{1,0:T(8,128)(2,1)S(1)}, bf16[384,256]{1,0:T(8,128)(2,1)S(1)}, bf16[128,1024]{1,0:T(8,128)(2,1)S(1)}, bf16[128,1024]{1,0:T(8,128)(2,1)S(1)}) custom-call(s32[5]{0:T(128)S(1)} %stack.23.at_ref, bf16[272,512]{1,0:T(8,128)(2,1)S(1)} %copy-done.1, bf16[272,512]{1,0:T(8,128)(2,1)S(1)} %collective-permute-done.refs_1_, ...), custom_call_target="tpu_custom_call" | custom-call | flops 1 | bytes 1 | tf_op jit(solution)/shard_map/pallas_call | solution.py:602
  44.2 1.0 %collective-permute-start.27 = (bf16[384,256]{1,0:T(8,128)(2,1)S(1)}, bf16[384,256]{1,0:T(8,128)(2,1)S(1)}, u32[]{:S(2)}, u32[]{:S(2)}) collective-permute-start(bf16[384,256]{1,0:T(8,128)(2,1)S(1)} %get-tuple-element.86), channel_id=1, source_target_pairs={{0,8},{4,12},{8,0},{12,4},{16,24},{20,28},{24,16},{28,20},{1,9},{5... | collective-permute-start | bytes 589832 | tf_op jit(solution)/shard_map/ppermute | solution.py:191
  45.3 2.7 %collective-permute-start.23 = (bf16[384,256]{1,0:T(8,128)(2,1)S(1)}, bf16[384,256]{1,0:T(8,128)(2,1)S(1)}, u32[]{:S(2)}, u32[]{:S(2)}) collective-permute-start(bf16[384,256]{1,0:T(8,128)(2,1)S(1)} %shard_map.114.own_ref), channel_id=1, source_target_pairs={{0,16},{4,20},{8,24},{12,28},{16,0},{20,4},{24,8},{28,12},{1,17},{... | collective-permute-start | bytes 589832 | tf_op jit(solution)/shard_map/ppermute | solution.py:191
  47.9 0.5 collective-permute-start.11
  48.4 6.4 %collective-permute-done.27.refs_1_ = bf16[384,256]{1,0:T(8,128)(2,1)S(1)} collective-permute-done((bf16[384,256]{1,0:T(8,128)(2,1)S(1)}, bf16[384,256]{1,0:T(8,128)(2,1)S(1)}, u32[]{:S(2)}, u32[]{:S(2)}) %collective-permute-start.27) | collective-permute-done | bytes 196640 | tf_op jit(solution)/shard_map/ppermute | solution.py:191
  54.9 0.5 collective-permute-start.14
  55.4 0.1 collective-permute-start.17
  55.5 0.1 shard_map.115.refs_0_
  55.6 2.1 %collective-permute-start.28 = (bf16[384,256]{1,0:T(8,128)(2,1)S(1)}, bf16[384,256]{1,0:T(8,128)(2,1)S(1)}, u32[]{:S(2)}, u32[]{:S(2)}) collective-permute-start(bf16[384,256]{1,0:T(8,128)(2,1)S(1)} %shard_map.116.own_ref), channel_id=1, source_target_pairs={{0,16},{4,20},{8,24},{12,28},{16,0},{20,4},{24,8},{28,12},{1,17},{... | collective-permute-start | bytes 589832 | tf_op jit(solution)/shard_map/ppermute | solution.py:191
  57.7 0.5 collective-permute-start.25
  58.2 1.0 %shard_map.110 = (bf16[256,256]{1,0:T(8,128)(2,1)S(1)}, bf16[256,256]{1,0:T(8,128)(2,1)S(1)}, bf16[128,512]{1,0:T(8,128)(2,1)S(1)}, bf16[128,512]{1,0:T(8,128)(2,1)S(1)}) custom-call(s32[5]{0:T(128)S(1)} %stack.23.at_ref, bf16[128,1024]{1,0:T(8,128)(2,1)S(1)} %copy-done.5, bf16[128,1024]{1,0:T(8,128)(2,1)S(1)} %collective-permute-done.9.refs_1_, ...), custom_call_target="tpu_custom_call" | custom-call | flops 1 | bytes 1 | tf_op jit(solution)/shard_map/pallas_call | solution.py:635
  59.3 1.6 %collective-permute-start.19 = (bf16[128,512]{1,0:T(8,128)(2,1)S(1)}, bf16[128,512]{1,0:T(8,128)(2,1)S(1)}, u32[]{:S(2)}, u32[]{:S(2)}) collective-permute-start(bf16[128,512]{1,0:T(8,128)(2,1)S(1)} %get-tuple-element.80), channel_id=1, source_target_pairs={{0,4},{4,0},{8,12},{12,8},{16,20},{20,16},{24,28},{28,24},{1,5},{5... | collective-permute-start | bytes 393224 | tf_op jit(solution)/shard_map/ppermute | solution.py:191
  60.8 3.6 %collective-permute-start.24 = (bf16[384,256]{1,0:T(8,128)(2,1)S(1)}, bf16[384,256]{1,0:T(8,128)(2,1)S(1)}, u32[]{:S(2)}, u32[]{:S(2)}) collective-permute-start(bf16[384,256]{1,0:T(8,128)(2,1)S(1)} %shard_map.115.refs_0_), channel_id=1, source_target_pairs={{0,8},{4,12},{8,0},{12,4},{16,24},{20,28},{24,16},{28,20},{1,9},{5... | collective-permute-start | bytes 589832 | tf_op jit(solution)/shard_map/ppermute | solution.py:191
  64.4 3.7 %collective-permute-done.28.got_ref = bf16[384,256]{1,0:T(8,128)(2,1)S(1)} collective-permute-done((bf16[384,256]{1,0:T(8,128)(2,1)S(1)}, bf16[384,256]{1,0:T(8,128)(2,1)S(1)}, u32[]{:S(2)}, u32[]{:S(2)}) %collective-permute-start.28) | collective-permute-done | bytes 196640 | tf_op jit(solution)/shard_map/ppermute | solution.py:191
  68.2 0.9 %collective-permute-start.29 = (bf16[384,256]{1,0:T(8,128)(2,1)S(1)}, bf16[384,256]{1,0:T(8,128)(2,1)S(1)}, u32[]{:S(2)}, u32[]{:S(2)}) collective-permute-start(bf16[384,256]{1,0:T(8,128)(2,1)S(1)} %shard_map.117.refs_4_), channel_id=1, source_target_pairs={{0,8},{4,12},{8,0},{12,4},{16,24},{20,28},{24,16},{28,20},{1,9},{5... | collective-permute-start | bytes 589832 | tf_op jit(solution)/shard_map/ppermute | solution.py:191
  69.1 1.2 %collective-permute-start.20 = (bf16[256,256]{1,0:T(8,128)(2,1)S(1)}, bf16[256,256]{1,0:T(8,128)(2,1)S(1)}, u32[]{:S(2)}, u32[]{:S(2)}) collective-permute-start(bf16[256,256]{1,0:T(8,128)(2,1)S(1)} %shard_map.111), channel_id=1, source_target_pairs={{0,2},{1,3},{2,0},{3,1},{4,6},{5,7},{6,4},{7,5},{8,10},{9,11},{10,... | collective-permute-start | bytes 393224 | tf_op jit(solution)/shard_map/ppermute | solution.py:191
  70.4 1.5 %collective-permute-start.32 = (bf16[256,256]{1,0:T(8,128)(2,1)S(1)}, bf16[256,256]{1,0:T(8,128)(2,1)S(1)}, u32[]{:S(2)}, u32[]{:S(2)}) collective-permute-start(bf16[256,256]{1,0:T(8,128)(2,1)S(1)} %get-tuple-element.91), channel_id=1, source_target_pairs={{0,8},{4,12},{8,0},{12,4},{16,24},{20,28},{24,16},{28,20},{1,9},{5... | collective-permute-start | bytes 393224 | tf_op jit(solution)/shard_map/ppermute | solution.py:191
  71.9 0.5 collective-permute-start.26
  72.4 1.5 %collective-permute-start.30 = (bf16[384,256]{1,0:T(8,128)(2,1)S(1)}, bf16[384,256]{1,0:T(8,128)(2,1)S(1)}, u32[]{:S(2)}, u32[]{:S(2)}) collective-permute-start(bf16[384,256]{1,0:T(8,128)(2,1)S(1)} %shard_map.117.refs_4_), channel_id=1, source_target_pairs={{0,4},{4,0},{8,12},{12,8},{16,20},{20,16},{24,28},{28,24},{1,5},{5... | collective-permute-start | bytes 589832 | tf_op jit(solution)/shard_map/ppermute | solution.py:191
  73.9 2.2 %collective-permute-done.29.refs_5_ = bf16[384,256]{1,0:T(8,128)(2,1)S(1)} collective-permute-done((bf16[384,256]{1,0:T(8,128)(2,1)S(1)}, bf16[384,256]{1,0:T(8,128)(2,1)S(1)}, u32[]{:S(2)}, u32[]{:S(2)}) %collective-permute-start.29) | collective-permute-done | bytes 196640 | tf_op jit(solution)/shard_map/ppermute | solution.py:191
  76.1 0.5 collective-permute-start.31
  76.6 0.1 collective-permute-start.21
  76.7 1.1 %collective-permute-done.32.got_ref = bf16[256,256]{1,0:T(8,128)(2,1)S(1)} collective-permute-done((bf16[256,256]{1,0:T(8,128)(2,1)S(1)}, bf16[256,256]{1,0:T(8,128)(2,1)S(1)}, u32[]{:S(2)}, u32[]{:S(2)}) %collective-permute-start.32) | collective-permute-done | bytes 131104 | tf_op jit(solution)/shard_map/ppermute | solution.py:191
  77.9 1.7 %collective-permute-start.33 = (bf16[128,256]{1,0:T(8,128)(2,1)S(1)}, bf16[128,256]{1,0:T(8,128)(2,1)S(1)}, u32[]{:S(2)}, u32[]{:S(2)}) collective-permute-start(bf16[128,256]{1,0:T(8,128)(2,1)S(1)} %get-tuple-element.94), channel_id=1, source_target_pairs={{0,16},{4,20},{8,24},{12,28},{16,0},{20,4},{24,8},{28,12},{1,17},{... | collective-permute-start | bytes 196616 | tf_op jit(solution)/shard_map/ppermute | solution.py:191
  79.6 2.1 %shard_map.113 = bf16[128,1024]{1,0:T(8,128)(2,1)} custom-call(s32[5]{0:T(128)S(1)} %stack.23.at_ref, bf16[128,512]{1,0:T(8,128)(2,1)S(1)} %get-tuple-element.79.refs_0_.back_ref, bf16[128,512]{1,0:T(8,128)(2,1)S(1)} %collective-permute-done.19.refs_1_.x_ref, bf16[256,256]{1,0:T(8,128)(2,1)S(1)} %collective-permute-done.20.refs_2_.y_ref, ...), custom_call_target="tpu_custom_call" | custom-call | flops 1 | bytes 1 | tf_op jit(solution)/shard_map/pallas_call | solution.py:665
  81.7 2.4 %collective-permute-done.33.got_ref = bf16[128,256]{1,0:T(8,128)(2,1)S(1)} collective-permute-done((bf16[128,256]{1,0:T(8,128)(2,1)S(1)}, bf16[128,256]{1,0:T(8,128)(2,1)S(1)}, u32[]{:S(2)}, u32[]{:S(2)}) %collective-permute-start.33) | collective-permute-done | bytes 65568 | tf_op jit(solution)/shard_map/ppermute | solution.py:191
  84.0 0.6 shard_map.120
  84.6 1.1 %collective-permute-start.34 = (bf16[128,128]{1,0:T(8,128)(2,1)S(1)}, bf16[128,128]{1,0:T(8,128)(2,1)S(1)}, u32[]{:S(2)}, u32[]{:S(2)}) collective-permute-start(bf16[128,128]{1,0:T(8,128)(2,1)S(1)} %get-tuple-element.97), channel_id=1, source_target_pairs={{0,4},{4,0},{8,12},{12,8},{16,20},{20,16},{24,28},{28,24},{1,5},{5... | collective-permute-start | bytes 98312 | tf_op jit(solution)/shard_map/ppermute | solution.py:191
  85.7 0.5 collective-permute-done.31.refs_7_
  86.2 2.1 %shard_map.118 = (bf16[384,1024]{1,0:T(8,128)(2,1)}, bf16[384,1024]{1,0:T(8,128)(2,1)}) custom-call(s32[5]{0:T(128)S(1)} %stack.23.at_ref, bf16[384,256]{1,0:T(8,128)(2,1)S(1)} %shard_map.115.refs_0_, bf16[384,256]{1,0:T(8,128)(2,1)S(1)} %collective-permute-done.24.refs_1_, bf16[384,256]{1,0:T(8,128)(2,1)S(1)} %collective-permute-done.25.refs_2_, ...), custom_call_target="tpu_custom_call" | custom-call | flops 1 | bytes 1 | tf_op jit(solution)/shard_map/pallas_call | solution.py:758
  88.3 0.2 collective-permute-done.34.got_ref
  88.6 1.3 %shard_map.121 = f32[128,256]{1,0:T(8,128)} custom-call(s32[5]{0:T(128)S(1)} %stack.23.at_ref, f32[128,128]{1,0:T(8,128)S(1)} %get-tuple-element.96.keep_ref, bf16[128,128]{1,0:T(8,128)(2,1)S(1)} %collective-permute-done.34.got_ref), custom_call_target="tpu_custom_call" | custom-call | flops 1 | bytes 1 | tf_op jit(solution)/shard_map/pallas_call | solution.py:725
  (39 shorter events, 0.3 us)
Async XLA Ops:
  0.6 21.1 %copy-start.5 = (bf16[128,1024]{1,0:T(8,128)(2,1)S(1)}, bf16[128,1024]{1,0:T(8,128)(2,1)}, u32[]{:S(2)}) copy-start(bf16[128,1024]{1,0:T(8,128)(2,1)} %refs_0_.1) | copy-start | bytes 786436
  2.8 29.6 %copy-start.1 = (bf16[272,512]{1,0:T(8,128)(2,1)S(1)}, bf16[272,512]{1,0:T(8,128)(2,1)}, u32[]{:S(2)}) copy-start(bf16[272,512]{1,0:T(8,128)(2,1)} %get-tuple-element.51.refs_0_) | copy-start | bytes 835588
  2.8 9.8 %collective-permute-start.1 = (bf16[272,512]{1,0:T(8,128)(2,1)}, bf16[272,512]{1,0:T(8,128)(2,1)S(1)}, u32[]{:S(2)}, u32[]{:S(2)}) collective-permute-start(bf16[272,512]{1,0:T(8,128)(2,1)} %get-tuple-element.52), channel_id=1, source_target_pairs={{0,4},{4,0},{8,12},{12,8},{16,20},{20,16},{24,28},{28,24},{1,5},{5... | collective-permute-start | bytes 835592 | tf_op jit(solution)/shard_map/ppermute | solution.py:191
  5.8 9.3 %collective-permute-start = (bf16[272,512]{1,0:T(8,128)(2,1)}, bf16[272,512]{1,0:T(8,128)(2,1)S(1)}, u32[]{:S(2)}, u32[]{:S(2)}) collective-permute-start(bf16[272,512]{1,0:T(8,128)(2,1)} %get-tuple-element.51.refs_0_), channel_id=1, source_target_pairs={{0,1},{1,0},{2,3},{3,2},{4,5},{5,4},{6,7},{7,6},{8,9},{9,8},{10,11... | collective-permute-start | bytes 835592 | tf_op jit(solution)/shard_map/ppermute | solution.py:191
  5.8 9.3 %collective-permute-start.3 = (bf16[272,512]{1,0:T(8,128)(2,1)}, bf16[272,512]{1,0:T(8,128)(2,1)S(1)}, u32[]{:S(2)}, u32[]{:S(2)}) collective-permute-start(bf16[272,512]{1,0:T(8,128)(2,1)} %get-tuple-element.51.refs_0_), channel_id=1, source_target_pairs={{0,2},{1,3},{2,0},{3,1},{4,6},{5,7},{6,4},{7,5},{8,10},{9,11},{10,... | collective-permute-start | bytes 835592 | tf_op jit(solution)/shard_map/ppermute | solution.py:191
  7.4 1.1 %copy-start.3 = (bf16[384,1024]{1,0:T(8,128)(2,1)S(1)}, bf16[384,1024]{1,0:T(8,128)(2,1)}, u32[]{:S(2)}) copy-start(bf16[384,1024]{1,0:T(8,128)(2,1)} %k_ref.1) | copy-start | bytes 2359300
  8.5 1.1 %copy-start.4 = (bf16[384,1024]{1,0:T(8,128)(2,1)S(1)}, bf16[384,1024]{1,0:T(8,128)(2,1)}, u32[]{:S(2)}) copy-start(bf16[384,1024]{1,0:T(8,128)(2,1)} %v_ref.1) | copy-start | bytes 2359300
  12.6 2.4 %collective-permute-start.2 = (bf16[272,512]{1,0:T(8,128)(2,1)S(1)}, bf16[272,512]{1,0:T(8,128)(2,1)S(1)}, u32[]{:S(2)}, u32[]{:S(2)}) collective-permute-start(bf16[272,512]{1,0:T(8,128)(2,1)S(1)} %collective-permute-done.1.refs_2_), channel_id=1, source_target_pairs={{0,1},{1,0},{2,3},{3,2},{4,5},{5,4},{6,7},{7,6},{8,9},{9,8},{10,11... | collective-permute-start | bytes 835592 | tf_op jit(solution)/shard_map/ppermute | solution.py:191
  12.6 9.1 %collective-permute-start.5 = (bf16[272,512]{1,0:T(8,128)(2,1)S(1)}, bf16[272,512]{1,0:T(8,128)(2,1)S(1)}, u32[]{:S(2)}, u32[]{:S(2)}) collective-permute-start(bf16[272,512]{1,0:T(8,128)(2,1)S(1)} %collective-permute-done.1.refs_2_), channel_id=1, source_target_pairs={{0,2},{1,3},{2,0},{3,1},{4,6},{5,7},{6,4},{7,5},{8,10},{9,11},{10,... | collective-permute-start | bytes 835592 | tf_op jit(solution)/shard_map/ppermute | solution.py:191
  15.1 8.4 %collective-permute-start.4 = (bf16[272,512]{1,0:T(8,128)(2,1)S(1)}, bf16[272,512]{1,0:T(8,128)(2,1)S(1)}, u32[]{:S(2)}, u32[]{:S(2)}) collective-permute-start(bf16[272,512]{1,0:T(8,128)(2,1)S(1)} %collective-permute-done.3.refs_0_.refs_4_), channel_id=1, source_target_pairs={{0,1},{1,0},{2,3},{3,2},{4,5},{5,4},{6,7},{7,6},{8,9},{9,8},{10,11... | collective-permute-start | bytes 835592 | tf_op jit(solution)/shard_map/ppermute | solution.py:191
  15.1 1.0 %copy-start = (bf16[272,512]{1,0:T(8,128)(2,1)S(1)}, bf16[272,512]{1,0:T(8,128)(2,1)}, u32[]{:S(2)}) copy-start(bf16[272,512]{1,0:T(8,128)(2,1)} %get-tuple-element.51.refs_0_) | copy-start | bytes 835588
  21.7 1.8 %collective-permute-start.6 = (bf16[272,512]{1,0:T(8,128)(2,1)S(1)}, bf16[272,512]{1,0:T(8,128)(2,1)S(1)}, u32[]{:S(2)}, u32[]{:S(2)}) collective-permute-start(bf16[272,512]{1,0:T(8,128)(2,1)S(1)} %collective-permute-done.5.refs_2_.refs_6_), channel_id=1, source_target_pairs={{0,1},{1,0},{2,3},{3,2},{4,5},{5,4},{6,7},{7,6},{8,9},{9,8},{10,11... | collective-permute-start | bytes 835592 | tf_op jit(solution)/shard_map/ppermute | solution.py:191
  21.7 8.7 %collective-permute-start.12 = (bf16[128,1024]{1,0:T(8,128)(2,1)S(1)}, bf16[128,1024]{1,0:T(8,128)(2,1)S(1)}, u32[]{:S(2)}, u32[]{:S(2)}) collective-permute-start(bf16[128,1024]{1,0:T(8,128)(2,1)S(1)} %copy-done.5), channel_id=1, source_target_pairs={{0,2},{1,3},{2,0},{3,1},{4,6},{5,7},{6,4},{7,5},{8,10},{9,11},{10,... | collective-permute-start | bytes 786440 | tf_op jit(solution)/shard_map/ppermute | solution.py:191
  25.6 10.7 %collective-permute-start.10 = (bf16[128,1024]{1,0:T(8,128)(2,1)S(1)}, bf16[128,1024]{1,0:T(8,128)(2,1)S(1)}, u32[]{:S(2)}, u32[]{:S(2)}) collective-permute-start(bf16[128,1024]{1,0:T(8,128)(2,1)S(1)} %copy-done.5), channel_id=1, source_target_pairs={{0,4},{4,0},{8,12},{12,8},{16,20},{20,16},{24,28},{28,24},{1,5},{5... | collective-permute-start | bytes 786440 | tf_op jit(solution)/shard_map/ppermute | solution.py:191
  27.2 1.2 %collective-permute-start.7 = (f32[4,2,1024]{2,1,0:T(2,128)S(1)}, f32[4,2,1024]{2,1,0:T(2,128)S(1)}, u32[]{:S(2)}, u32[]{:S(2)}) collective-permute-start(f32[4,2,1024]{2,1,0:T(2,128)S(1)} %get-tuple-element.58), channel_id=1, source_target_pairs={{0,1},{1,0},{2,3},{3,2},{4,5},{5,4},{6,7},{7,6},{8,9},{9,8},{10,11... | collective-permute-start | bytes 98312 | tf_op jit(solution)/shard_map/ppermute | solution.py:191
  28.4 4.0 %collective-permute-start.8 = (f32[4,2,1024]{2,1,0:T(2,128)S(1)}, f32[4,2,1024]{2,1,0:T(2,128)S(1)}, u32[]{:S(2)}, u32[]{:S(2)}) collective-permute-start(f32[4,2,1024]{2,1,0:T(2,128)S(1)} %shard_map.106.refs_14_), channel_id=1, source_target_pairs={{0,2},{1,3},{2,0},{3,1},{4,6},{5,7},{6,4},{7,5},{8,10},{9,11},{10,... | collective-permute-start | bytes 98312 | tf_op jit(solution)/shard_map/ppermute | solution.py:191
  36.4 3.2 %collective-permute-start.13 = (bf16[128,1024]{1,0:T(8,128)(2,1)S(1)}, bf16[128,1024]{1,0:T(8,128)(2,1)S(1)}, u32[]{:S(2)}, u32[]{:S(2)}) collective-permute-start(bf16[128,1024]{1,0:T(8,128)(2,1)S(1)} %get-tuple-element.72), channel_id=1, source_target_pairs={{0,1},{1,0},{2,3},{3,2},{4,5},{5,4},{6,7},{7,6},{8,9},{9,8},{10,11... | collective-permute-start | bytes 786440 | tf_op jit(solution)/shard_map/ppermute | solution.py:191
  36.4 11.5 %collective-permute-start.15 = (bf16[128,1024]{1,0:T(8,128)(2,1)S(1)}, bf16[128,1024]{1,0:T(8,128)(2,1)S(1)}, u32[]{:S(2)}, u32[]{:S(2)}) collective-permute-start(bf16[128,1024]{1,0:T(8,128)(2,1)S(1)} %collective-permute-done.10.refs_2_), channel_id=1, source_target_pairs={{0,2},{1,3},{2,0},{3,1},{4,6},{5,7},{6,4},{7,5},{8,10},{9,11},{10,... | collective-permute-start | bytes 786440 | tf_op jit(solution)/shard_map/ppermute | solution.py:191
  38.0 7.2 %collective-permute-start.22 = (bf16[384,256]{1,0:T(8,128)(2,1)S(1)}, bf16[384,256]{1,0:T(8,128)(2,1)S(1)}, u32[]{:S(2)}, u32[]{:S(2)}) collective-permute-start(bf16[384,256]{1,0:T(8,128)(2,1)S(1)} %get-tuple-element.83), channel_id=1, source_target_pairs={{0,8},{4,12},{8,0},{12,4},{16,24},{20,28},{24,16},{28,20},{1,9},{5... | collective-permute-start | bytes 589832 | tf_op jit(solution)/shard_map/ppermute | solution.py:191
  39.7 15.7 %collective-permute-start.18 = (bf16[128,1024]{1,0:T(8,128)(2,1)S(1)}, bf16[128,1024]{1,0:T(8,128)(2,1)S(1)}, u32[]{:S(2)}, u32[]{:S(2)}) collective-permute-start(bf16[128,1024]{1,0:T(8,128)(2,1)S(1)} %shard_map.108), channel_id=1, source_target_pairs={{0,2},{1,3},{2,0},{3,1},{4,6},{5,7},{6,4},{7,5},{8,10},{9,11},{10,... | collective-permute-start | bytes 786440 | tf_op jit(solution)/shard_map/ppermute | solution.py:191
  44.2 10.7 %collective-permute-start.27 = (bf16[384,256]{1,0:T(8,128)(2,1)S(1)}, bf16[384,256]{1,0:T(8,128)(2,1)S(1)}, u32[]{:S(2)}, u32[]{:S(2)}) collective-permute-start(bf16[384,256]{1,0:T(8,128)(2,1)S(1)} %get-tuple-element.86), channel_id=1, source_target_pairs={{0,8},{4,12},{8,0},{12,4},{16,24},{20,28},{24,16},{28,20},{1,9},{5... | collective-permute-start | bytes 589832 | tf_op jit(solution)/shard_map/ppermute | solution.py:191
  45.2 34.4 %copy-start.2 = (bf16[1024,1024]{1,0:T(8,128)(2,1)S(1)}, bf16[1024,1024]{1,0:T(8,128)(2,1)}, u32[]{:S(2)}) copy-start(bf16[1024,1024]{1,0:T(8,128)(2,1)} %wq_ref.1) | copy-start | bytes 6291460
  45.3 9.6 %collective-permute-start.23 = (bf16[384,256]{1,0:T(8,128)(2,1)S(1)}, bf16[384,256]{1,0:T(8,128)(2,1)S(1)}, u32[]{:S(2)}, u32[]{:S(2)}) collective-permute-start(bf16[384,256]{1,0:T(8,128)(2,1)S(1)} %shard_map.114.own_ref), channel_id=1, source_target_pairs={{0,16},{4,20},{8,24},{12,28},{16,0},{20,4},{24,8},{28,12},{1,17},{... | collective-permute-start | bytes 589832 | tf_op jit(solution)/shard_map/ppermute | solution.py:191
  47.9 7.7 %collective-permute-start.9 = (bf16[128,1024]{1,0:T(8,128)(2,1)S(1)}, bf16[128,1024]{1,0:T(8,128)(2,1)S(1)}, u32[]{:S(2)}, u32[]{:S(2)}) collective-permute-start(bf16[128,1024]{1,0:T(8,128)(2,1)S(1)} %copy-done.5), channel_id=1, source_target_pairs={{0,1},{1,0},{2,3},{3,2},{4,5},{5,4},{6,7},{7,6},{8,9},{9,8},{10,11... | collective-permute-start | bytes 786440 | tf_op jit(solution)/shard_map/ppermute | solution.py:191
  47.9 9.8 %collective-permute-start.11 = (bf16[128,1024]{1,0:T(8,128)(2,1)S(1)}, bf16[128,1024]{1,0:T(8,128)(2,1)S(1)}, u32[]{:S(2)}, u32[]{:S(2)}) collective-permute-start(bf16[128,1024]{1,0:T(8,128)(2,1)S(1)} %collective-permute-done.10.refs_2_), channel_id=1, source_target_pairs={{0,1},{1,0},{2,3},{3,2},{4,5},{5,4},{6,7},{7,6},{8,9},{9,8},{10,11... | collective-permute-start | bytes 786440 | tf_op jit(solution)/shard_map/ppermute | solution.py:191
  54.9 3.3 %collective-permute-start.16 = (bf16[128,1024]{1,0:T(8,128)(2,1)S(1)}, bf16[128,1024]{1,0:T(8,128)(2,1)S(1)}, u32[]{:S(2)}, u32[]{:S(2)}) collective-permute-start(bf16[128,1024]{1,0:T(8,128)(2,1)S(1)} %collective-permute-done.15.refs_6_), channel_id=1, source_target_pairs={{0,1},{1,0},{2,3},{3,2},{4,5},{5,4},{6,7},{7,6},{8,9},{9,8},{10,11... | collective-permute-start | bytes 786440 | tf_op jit(solution)/shard_map/ppermute | solution.py:191
  54.9 3.3 %collective-permute-start.14 = (bf16[128,1024]{1,0:T(8,128)(2,1)S(1)}, bf16[128,1024]{1,0:T(8,128)(2,1)S(1)}, u32[]{:S(2)}, u32[]{:S(2)}) collective-permute-start(bf16[128,1024]{1,0:T(8,128)(2,1)S(1)} %collective-permute-done.12.refs_4_), channel_id=1, source_target_pairs={{0,1},{1,0},{2,3},{3,2},{4,5},{5,4},{6,7},{7,6},{8,9},{9,8},{10,11... | collective-permute-start | bytes 786440 | tf_op jit(solution)/shard_map/ppermute | solution.py:191
  55.4 2.8 %collective-permute-start.17 = (bf16[128,1024]{1,0:T(8,128)(2,1)S(1)}, bf16[128,1024]{1,0:T(8,128)(2,1)S(1)}, u32[]{:S(2)}, u32[]{:S(2)}) collective-permute-start(bf16[128,1024]{1,0:T(8,128)(2,1)S(1)} %get-tuple-element.78), channel_id=1, source_target_pairs={{0,1},{1,0},{2,3},{3,2},{4,5},{5,4},{6,7},{7,6},{8,9},{9,8},{10,11... | collective-permute-start | bytes 786440 | tf_op jit(solution)/shard_map/ppermute | solution.py:191
  55.6 12.5 %collective-permute-start.28 = (bf16[384,256]{1,0:T(8,128)(2,1)S(1)}, bf16[384,256]{1,0:T(8,128)(2,1)S(1)}, u32[]{:S(2)}, u32[]{:S(2)}) collective-permute-start(bf16[384,256]{1,0:T(8,128)(2,1)S(1)} %shard_map.116.own_ref), channel_id=1, source_target_pairs={{0,16},{4,20},{8,24},{12,28},{16,0},{20,4},{24,8},{28,12},{1,17},{... | collective-permute-start | bytes 589832 | tf_op jit(solution)/shard_map/ppermute | solution.py:191
  57.7 10.5 %collective-permute-start.25 = (bf16[384,256]{1,0:T(8,128)(2,1)S(1)}, bf16[384,256]{1,0:T(8,128)(2,1)S(1)}, u32[]{:S(2)}, u32[]{:S(2)}) collective-permute-start(bf16[384,256]{1,0:T(8,128)(2,1)S(1)} %shard_map.115.refs_0_), channel_id=1, source_target_pairs={{0,4},{4,0},{8,12},{12,8},{16,20},{20,16},{24,28},{28,24},{1,5},{5... | collective-permute-start | bytes 589832 | tf_op jit(solution)/shard_map/ppermute | solution.py:191
  59.3 9.8 %collective-permute-start.19 = (bf16[128,512]{1,0:T(8,128)(2,1)S(1)}, bf16[128,512]{1,0:T(8,128)(2,1)S(1)}, u32[]{:S(2)}, u32[]{:S(2)}) collective-permute-start(bf16[128,512]{1,0:T(8,128)(2,1)S(1)} %get-tuple-element.80), channel_id=1, source_target_pairs={{0,4},{4,0},{8,12},{12,8},{16,20},{20,16},{24,28},{28,24},{1,5},{5... | collective-permute-start | bytes 393224 | tf_op jit(solution)/shard_map/ppermute | solution.py:191
  60.8 11.0 %collective-permute-start.24 = (bf16[384,256]{1,0:T(8,128)(2,1)S(1)}, bf16[384,256]{1,0:T(8,128)(2,1)S(1)}, u32[]{:S(2)}, u32[]{:S(2)}) collective-permute-start(bf16[384,256]{1,0:T(8,128)(2,1)S(1)} %shard_map.115.refs_0_), channel_id=1, source_target_pairs={{0,8},{4,12},{8,0},{12,4},{16,24},{20,28},{24,16},{28,20},{1,9},{5... | collective-permute-start | bytes 589832 | tf_op jit(solution)/shard_map/ppermute | solution.py:191
  68.2 7.9 %collective-permute-start.29 = (bf16[384,256]{1,0:T(8,128)(2,1)S(1)}, bf16[384,256]{1,0:T(8,128)(2,1)S(1)}, u32[]{:S(2)}, u32[]{:S(2)}) collective-permute-start(bf16[384,256]{1,0:T(8,128)(2,1)S(1)} %shard_map.117.refs_4_), channel_id=1, source_target_pairs={{0,8},{4,12},{8,0},{12,4},{16,24},{20,28},{24,16},{28,20},{1,9},{5... | collective-permute-start | bytes 589832 | tf_op jit(solution)/shard_map/ppermute | solution.py:191
  69.1 7.5 %collective-permute-start.20 = (bf16[256,256]{1,0:T(8,128)(2,1)S(1)}, bf16[256,256]{1,0:T(8,128)(2,1)S(1)}, u32[]{:S(2)}, u32[]{:S(2)}) collective-permute-start(bf16[256,256]{1,0:T(8,128)(2,1)S(1)} %shard_map.111), channel_id=1, source_target_pairs={{0,2},{1,3},{2,0},{3,1},{4,6},{5,7},{6,4},{7,5},{8,10},{9,11},{10,... | collective-permute-start | bytes 393224 | tf_op jit(solution)/shard_map/ppermute | solution.py:191
  70.4 7.5 %collective-permute-start.32 = (bf16[256,256]{1,0:T(8,128)(2,1)S(1)}, bf16[256,256]{1,0:T(8,128)(2,1)S(1)}, u32[]{:S(2)}, u32[]{:S(2)}) collective-permute-start(bf16[256,256]{1,0:T(8,128)(2,1)S(1)} %get-tuple-element.91), channel_id=1, source_target_pairs={{0,8},{4,12},{8,0},{12,4},{16,24},{20,28},{24,16},{28,20},{1,9},{5... | collective-permute-start | bytes 393224 | tf_op jit(solution)/shard_map/ppermute | solution.py:191
  71.9 13.9 %collective-permute-start.26 = (bf16[384,256]{1,0:T(8,128)(2,1)S(1)}, bf16[384,256]{1,0:T(8,128)(2,1)S(1)}, u32[]{:S(2)}, u32[]{:S(2)}) collective-permute-start(bf16[384,256]{1,0:T(8,128)(2,1)S(1)} %collective-permute-done.24.refs_1_), channel_id=1, source_target_pairs={{0,4},{4,0},{8,12},{12,8},{16,20},{20,16},{24,28},{28,24},{1,5},{5... | collective-permute-start | bytes 589832 | tf_op jit(solution)/shard_map/ppermute | solution.py:191
  72.4 13.3 %collective-permute-start.30 = (bf16[384,256]{1,0:T(8,128)(2,1)S(1)}, bf16[384,256]{1,0:T(8,128)(2,1)S(1)}, u32[]{:S(2)}, u32[]{:S(2)}) collective-permute-start(bf16[384,256]{1,0:T(8,128)(2,1)S(1)} %shard_map.117.refs_4_), channel_id=1, source_target_pairs={{0,4},{4,0},{8,12},{12,8},{16,20},{20,16},{24,28},{28,24},{1,5},{5... | collective-permute-start | bytes 589832 | tf_op jit(solution)/shard_map/ppermute | solution.py:191
  76.1 10.1 %collective-permute-start.31 = (bf16[384,256]{1,0:T(8,128)(2,1)S(1)}, bf16[384,256]{1,0:T(8,128)(2,1)S(1)}, u32[]{:S(2)}, u32[]{:S(2)}) collective-permute-start(bf16[384,256]{1,0:T(8,128)(2,1)S(1)} %collective-permute-done.29.refs_5_), channel_id=1, source_target_pairs={{0,4},{4,0},{8,12},{12,8},{16,20},{20,16},{24,28},{28,24},{1,5},{5... | collective-permute-start | bytes 589832 | tf_op jit(solution)/shard_map/ppermute | solution.py:191
  76.6 2.9 %collective-permute-start.21 = (bf16[512,128]{1,0:T(8,128)(2,1)S(1)}, bf16[512,128]{1,0:T(8,128)(2,1)S(1)}, u32[]{:S(2)}, u32[]{:S(2)}) collective-permute-start(bf16[512,128]{1,0:T(8,128)(2,1)S(1)} %shard_map.112), channel_id=1, source_target_pairs={{0,1},{1,0},{2,3},{3,2},{4,5},{5,4},{6,7},{7,6},{8,9},{9,8},{10,11... | collective-permute-start | bytes 393224 | tf_op jit(solution)/shard_map/ppermute | solution.py:191
  77.9 6.2 %collective-permute-start.33 = (bf16[128,256]{1,0:T(8,128)(2,1)S(1)}, bf16[128,256]{1,0:T(8,128)(2,1)S(1)}, u32[]{:S(2)}, u32[]{:S(2)}) collective-permute-start(bf16[128,256]{1,0:T(8,128)(2,1)S(1)} %get-tuple-element.94), channel_id=1, source_target_pairs={{0,16},{4,20},{8,24},{12,28},{16,0},{20,4},{24,8},{28,12},{1,17},{... | collective-permute-start | bytes 196616 | tf_op jit(solution)/shard_map/ppermute | solution.py:191
  84.6 4.0 %collective-permute-start.34 = (bf16[128,128]{1,0:T(8,128)(2,1)S(1)}, bf16[128,128]{1,0:T(8,128)(2,1)S(1)}, u32[]{:S(2)}, u32[]{:S(2)}) collective-permute-start(bf16[128,128]{1,0:T(8,128)(2,1)S(1)} %get-tuple-element.97), channel_id=1, source_target_pairs={{0,4},{4,0},{8,12},{12,8},{16,20},{20,16},{24,28},{28,24},{1,5},{5... | collective-permute-start | bytes 98312 | tf_op jit(solution)/shard_map/ppermute | solution.py:191
